TPU v7x, 32 devices: a whole 2x2x4 slice. The times are simulated.
32 devices in a mesh: groups: 2 (over y), wide: 4 (over z), tp: 4 (over x, core).
Axes of the slice: x: 2, y: 2, z: 4, core: 2. Of those that a mesh axis runs over, the one named last changes fastest.
Arguments:
- hidden: bfloat16 [4, 64, 8192], P(None, ('groups', 'wide'), 'tp'), parts along dimension 1, may hold values from -6 to 6
- input_norm_gain: bfloat16 [8192], replicated, may hold values from 0.099609375 to 1.8984375
- key_value_weight: bfloat16 [8192, 2, 1024], P(None, None, 'tp'), may hold values from -0.0625 to 0.0625
- key_value_bias: bfloat16 [2, 1024], P(None, 'tp'), may hold values from -3 to 3
- adapter_down_factor: bfloat16 [4, 64, 8192], P('groups', None, 'wide'), parts along dimension 0, may hold values from -0.0625 to 0.0625
- adapter_up_factor: bfloat16 [4, 1024, 64], P('groups', 'tp', 'wide'), parts along dimension 0, may hold values from -0.375 to 0.375
- queries: bfloat16 [4, 64, 8192], P(None, ('groups', 'wide'), 'tp'), parts along dimension 1, may hold values from -180 to 180
- stored_rotated_keys: bfloat16 [64, 512, 1024], P(('groups', 'wide'), None, 'tp'), parts along dimension 0, may hold values from -6 to 6
- stored_value_rows: bfloat16 [64, 512, 1024], P(('groups', 'wide'), None, 'tp'), parts along dimension 0, may hold values from -6 to 6
- lengths: int32 [64], P(('groups', 'wide')), parts along dimension 0, may hold values from 1 to 512, 8192 in all
Outputs:
- new_keys: bfloat16 [4, 64, 1024], P(None, ('groups', 'wide'), 'tp'), parts along dimension 1
- new_values: bfloat16 [4, 64, 1024], P(None, ('groups', 'wide'), 'tp'), parts along dimension 1
- attended: bfloat16 [4, 64, 8192], P(None, ('groups', 'wide'), 'tp'), parts along dimension 1
There are 2 independent parts, one for each index of `groups`. A program takes and returns all parts, laid end to end along the dimension named above; an argument that names none is the same for every part. Nothing has to cross between parts.
Inputs may be any that keep to these rules, and one draw needn't show every extreme that they name: The lengths of each part sum to 8192; some row holds exactly 512 cached positions in every draw.
All inputs are finite; a program needn't handle non-finite values. No bound on the sum of `lengths` on one device may be relied on, other than what follows from the above.
Results may differ from a plain program's by a relative error of at most 0.0095.
Values may be sent and summed in bfloat16 or wider, within the bound.
No kernel may reach another device: no remote copies, remote signals or barrier semaphores. Data moves between devices by JAX's collectives and lax.ppermute only.
A program may use at most 64 MiB of HBM per device.

v0:
```python
import math

import jax
import jax.numpy as jnp
from jax import lax
from jax.sharding import PartitionSpec as P

HD = 128


norm_eps = 1e-06
adapter_scale = 2.0
rope_base = 1000000.0
masked_score = -1e30


def rotate_keys(key_rows, positions):
    step_count, row_count, row_width = key_rows.shape
    head_count = row_width // HD
    half_dim = HD // 2
    split_keys = key_rows.reshape(step_count, row_count, head_count, HD)
    inv_freq = rope_base ** (-(2.0 * jnp.arange(half_dim, dtype=jnp.float32)) / HD)
    angles = positions.astype(jnp.float32)[:, :, None] * inv_freq
    cosine = jnp.cos(angles)[:, :, None, :]
    sine_part = jnp.sin(angles)[:, :, None, :]
    first_half = split_keys[..., :half_dim]
    second = split_keys[..., half_dim:]
    turned = jnp.concatenate(
        [first_half * cosine - second * sine_part, second * cosine + first_half * sine_part],
        axis=-1,
    )
    return turned.reshape(step_count, row_count, row_width)


def attend(queries, stored_rotated_keys, stored_value_rows, new_keys, new_values, lengths):
    step_count, row_count, query_width = queries.shape
    cache_span = stored_rotated_keys.shape[1]
    group_count = stored_rotated_keys.shape[2] // HD
    per_group = query_width // HD // group_count
    score_scale = 1.0 / math.sqrt(HD)
    query_split = queries.reshape(step_count, row_count, group_count, per_group, HD)
    old_keys = stored_rotated_keys.reshape(row_count, cache_span, group_count, HD)
    old_values = stored_value_rows.reshape(row_count, cache_span, group_count, HD)
    fresh_keys = new_keys.reshape(step_count, row_count, group_count, HD)
    fresh_values = new_values.reshape(step_count, row_count, group_count, HD)
    old_scores = (
        jnp.einsum("srgqd,rlgd->srgql", query_split, old_keys, preferred_element_type=jnp.float32)
        * score_scale
    )
    fresh_scores = (
        jnp.einsum("srgqd,trgd->srgqt", query_split, fresh_keys, preferred_element_type=jnp.float32)
        * score_scale
    )
    old_live = jnp.arange(cache_span, dtype=jnp.int32)[None, :] < lengths[:, None]
    fresh_live = (
        jnp.arange(step_count, dtype=jnp.int32)[None, :]
        <= jnp.arange(step_count, dtype=jnp.int32)[:, None]
    )
    old_scores = jnp.where(old_live[None, :, None, None, :], old_scores, masked_score)
    fresh_scores = jnp.where(fresh_live[:, None, None, None, :], fresh_scores, masked_score)
    score_top = jnp.maximum(
        jnp.max(old_scores, axis=-1, keepdims=True), jnp.max(fresh_scores, axis=-1, keepdims=True)
    )
    old_exp = jnp.exp(old_scores - score_top)
    fresh_exp = jnp.exp(fresh_scores - score_top)
    totals = jnp.sum(old_exp, axis=-1, keepdims=True) + jnp.sum(fresh_exp, axis=-1, keepdims=True)
    old_prob = (old_exp / totals).astype(jnp.bfloat16)
    fresh_prob = (fresh_exp / totals).astype(jnp.bfloat16)
    attended = jnp.einsum(
        "srgql,rlgd->srgqd", old_prob, old_values, preferred_element_type=jnp.float32
    )
    attended = attended + jnp.einsum(
        "srgqt,trgd->srgqd", fresh_prob, fresh_values, preferred_element_type=jnp.float32
    )
    return attended.astype(jnp.bfloat16).reshape(step_count, row_count, query_width)


def on_device(
    hidden,
    input_norm_gain,
    key_value_weight,
    key_value_bias,
    adapter_down_factor,
    adapter_up_factor,
    queries,
    stored_rotated_keys,
    stored_value_rows,
    lengths,
):
    full_rows = lax.all_gather(hidden, "tp", axis=2, tiled=True)
    widened = full_rows.astype(jnp.float32)
    mean_square = jnp.mean(widened * widened, axis=-1, keepdims=True)
    normed = (
        widened * lax.rsqrt(mean_square + norm_eps) * input_norm_gain.astype(jnp.float32)
    ).astype(jnp.bfloat16)
    step_count, row_count = (normed.shape[0], normed.shape[1])
    down_full, rank_full = (
        lax.all_gather(adapter_down_factor, "wide", axis=2, tiled=True),
        lax.all_gather(adapter_up_factor, "wide", axis=2, tiled=True),
    )
    factor_product = jnp.einsum(
        "kca,kad->dkc", rank_full, down_full, preferred_element_type=jnp.float32
    )
    combined_output = key_value_weight.astype(jnp.float32) + adapter_scale * factor_product
    merged_high = combined_output.astype(jnp.bfloat16)
    merged_low = (combined_output - merged_high.astype(jnp.float32)).astype(jnp.bfloat16)
    projected_output = jnp.einsum(
        "srd,dkc->srkc", normed, merged_high, preferred_element_type=jnp.float32
    )
    projected_output = projected_output + jnp.einsum(
        "srd,dkc->srkc", normed, merged_low, preferred_element_type=jnp.float32
    )
    projected_output = projected_output + key_value_bias.astype(jnp.float32)
    positions = lengths[None, :] + jnp.arange(step_count, dtype=jnp.int32)[:, None]
    new_keys = rotate_keys(projected_output[:, :, 0, :], positions).astype(jnp.bfloat16)
    new_values = projected_output[:, :, 1, :].astype(jnp.bfloat16)
    attended = attend(
        queries, stored_rotated_keys, stored_value_rows, new_keys, new_values, lengths
    )
    return (new_keys, new_values, attended)


def solution(mesh):
    in_specs = (
        P(None, ("groups", "wide"), "tp"),
        P(),
        P(None, None, "tp"),
        P(None, "tp"),
        P("groups", None, "wide"),
        P("groups", "tp", "wide"),
        P(None, ("groups", "wide"), "tp"),
        P(("groups", "wide"), None, "tp"),
        P(("groups", "wide"), None, "tp"),
        P(("groups", "wide")),
    )
    out_specs = (
        P(None, ("groups", "wide"), "tp"),
        P(None, ("groups", "wide"), "tp"),
        P(None, ("groups", "wide"), "tp"),
    )
    return jax.shard_map(
        on_device, mesh=mesh, in_specs=in_specs, out_specs=out_specs, check_vma=False
    )
```

profile of v0, /device:TPU:0, one launch (start us, length us, event | category | flops | bytes accessed | tf_op | source)
XLA Modules:
  0.0 79.7 jit_solution(16583041609217512452)
XLA Ops:
  7.2 0.0 copy-start
  7.2 0.0 copy-start.3
  7.2 0.0 copy-start.2
  7.2 0.0 copy-start.4
  7.2 0.0 all-gather.2.cloned.1.call-start
  7.3 0.7 all-gather.2.cloned.1.call-update
  7.9 0.7 convert_element_type.58
  8.7 0.7 convert_element_type.64
  9.3 4.0 %reshape.105 = bf16[8,512,2,128]{3,2,1,0:T(2,128)(2,1)} reshape(bf16[8,512,256]{2,1,0:T(8,128)(2,1)} %param.17) | data formatting | bytes 4194304 | tf_op jit(solution)/shard_map/reshape | solution.py:42
  13.3 2.5 %reshape.107 = bf16[8,512,2,128]{3,2,1,0:T(2,128)(2,1)S(1)} reshape(bf16[8,512,256]{2,1,0:T(8,128)(2,1)} %param.18) | data formatting | bytes 4194304 | tf_op jit(solution)/shard_map/reshape | solution.py:43
  15.9 0.0 copy-done.3
  15.9 15.2 %all_gather.11 = bf16[2,256,64]{1,2,0:T(8,128)(2,1)S(1)} all-gather(bf16[2,256,16]{1,2,0:T(8,128)(2,1)S(1)} %copy-done.3), channel_id=1, replica_groups=mesh['groups'=2,'wide'=4,'tp'=4] {'wide'}, dimensions={2}, use_global_device_ids=true | all-gather | bytes 81920 | tf_op jit(solution)/shard_map/all_gather | solution.py:99
  31.2 0.0 copy-done.2
  31.2 7.2 %all_gather.9 = bf16[4,8,8192]{2,1,0:T(8,128)(2,1)S(1)} all-gather(bf16[4,8,2048]{2,1,0:T(8,128)(2,1)S(1)} %copy-done.2), channel_id=1, replica_groups=mesh['groups'=2,'wide'=4,'tp'=4] {'tp'}, dimensions={2}, use_global_device_ids=true | all-gather | bytes 655360 | tf_op jit(solution)/shard_map/all_gather | solution.py:90
  38.3 0.2 fusion.37
  38.6 0.0 copy-done.4
  38.6 0.1 add_convert_fusion
  38.6 0.1 iota_compare_fusion
  38.7 0.2 multiply_cosine_fusion
  38.9 0.0 copy-done
  38.9 3.4 %fusion.56 = (f32[4,8,2,8]{3,0,2,1:T(4,128)S(1)}, f32[4,8,2,8,512]{4,3,0,2,1:T(8,128)}) fusion(bf16[4,8,2,8,128]{4,1,3,2,0:T(8,128)(2,1)S(1)} %bitcast.57, bf16[8,512,2,128,1]{3,2,1,0,4:T(2,128)(2,1)} %bitcast.60, pred[8,512]{1,0:T(8,128)(4,1)S(1)} %iota_compare_fusion), kind=kOutput, calls=%fused_computation.60 | convolution fusion | flops 67894784 | bytes 3282944 | tf_op jit(solution)/shard_map/srgqd,rlgd->srgql/dot_general | solution.py:47
  42.3 16.6 %all-gather.2.cloned.1.call-done = bf16[2,64,8192]{2,1,0:T(8,128)(2,1)} async-done(((bf16[2,64,2048]{2,1,0:T(8,128)(2,1)}), bf16[2,64,8192]{2,1,0:T(8,128)(2,1)}) %all-gather.2.cloned.1.call-update) | async-done | bytes 2097168 | tf_op jit(solution)/shard_map/all_gather | solution.py:98
  58.9 6.4 %bitcast_add_fusion = f32[8192,2,256]{2,0,1:T(8,128)S(1)} fusion(bf16[2,64,8192]{2,1,0:T(8,128)(2,1)} %all-gather.2.cloned.1.call-done, bf16[2,256,64]{1,2,0:T(8,128)(2,1)S(1)} %all_gather.11, bf16[8192,2,256]{2,1,0:T(2,128)(2,1)} %param.12), kind=kOutput, calls=%fused_computation | convolution fusion | flops 549453824 | bytes 27328512 | tf_op jit(solution)/shard_map/kca,kad->dkc/dot_general | solution.py:101
  65.3 1.6 %fusion.1 = f32[4,8,2,256]{3,1,2,0:T(8,128)S(1)} fusion(f32[8192,2,256]{2,0,1:T(8,128)S(1)} %bitcast_add_fusion, bf16[4,8,8192]{2,1,0:T(8,128)(2,1)S(1)} %all_gather.9, f32[8192]{0:T(1024)S(1)} %convert_element_type.58, f32[4,8]{1,0:T(4,128)S(1)} %add_rsqrt_fusion), kind=kOutput, calls=%fused_computation.3 | convolution fusion | flops 273678336 | bytes 17399936 | tf_op jit(solution)/shard_map/srd,dkc->srkc/dot_general | solution.py:107
  66.9 0.0 copy-start.1
  66.9 1.6 %fusion.34 = f32[4,8,2,256]{3,1,2,0:T(8,128)S(1)} fusion(f32[4,8,2,256]{3,1,2,0:T(8,128)S(1)} %fusion.1, f32[8192,2,256]{2,0,1:T(8,128)S(1)} %bitcast_add_fusion, bf16[4,8,8192]{2,1,0:T(8,128)(2,1)S(1)} %all_gather.9, f32[8192]{0:T(1024)S(1)} %convert_element_type.58, f32[4,8]{1,0:T(4,128)S(1)} %add_rsqrt_fusion, f32[2,256]{1,0:T(2,128)S(1)} %convert_element_type.64), kind=kOutput, calls=%fused_computation.25 | convolution fusion | flops 286294016 | bytes 17467520 | tf_op jit(solution)/shard_map/srd,dkc->srkc/dot_general | solution.py:110
  68.5 0.6 fusion.53
  69.1 0.1 fusion.55
  69.2 0.1 maximum_convert_fusion
  69.3 0.6 copy.78
  69.9 0.7 fusion.57
  70.6 0.0 copy-done.1
  70.6 0.4 fusion.40
  71.0 0.1 fusion.48
  71.2 0.3 convolution_bitcast_fusion
  71.5 0.6 fusion.26
  72.1 0.7 reshape.108
  (8 shorter events, 0.1 us)
Async XLA Ops:
  7.2 31.8 %copy-start = (bf16[4,8,2048]{2,1,0:T(8,128)(2,1)S(1)}, bf16[4,8,2048]{2,1,0:T(8,128)(2,1)}, u32[]{:S(2)}) copy-start(bf16[4,8,2048]{2,1,0:T(8,128)(2,1)} %param.16) | copy-start | bytes 393220
  7.2 8.7 %copy-start.3 = (bf16[2,256,16]{1,2,0:T(8,128)(2,1)S(1)}, bf16[2,256,16]{1,2,0:T(8,128)(2,1)}, u32[]{:S(2)}) copy-start(bf16[2,256,16]{1,2,0:T(8,128)(2,1)} %param.15) | copy-start | bytes 49156
  7.2 24.0 %copy-start.2 = (bf16[4,8,2048]{2,1,0:T(8,128)(2,1)S(1)}, bf16[4,8,2048]{2,1,0:T(8,128)(2,1)}, u32[]{:S(2)}) copy-start(bf16[4,8,2048]{2,1,0:T(8,128)(2,1)} %param.10) | copy-start | bytes 393220
  7.2 31.4 %copy-start.4 = (s32[8]{0:T(128)S(1)}, s32[8]{0:T(128)}, u32[]{:S(2)}) copy-start(s32[8]{0:T(128)} %param.19) | copy-start | bytes 100
  7.2 51.7 %all-gather.2.cloned.1.call-start = ((), (), s32[]{:S(2)}) async-start(), calls=%async_computation | async-start | bytes 2621440 | tf_op jit(solution)/shard_map/all_gather | solution.py:98
  66.9 3.8 %copy-start.1 = (f32[4,8,2,8,512]{4,3,0,2,1:T(8,128)S(1)}, f32[4,8,2,8,512]{4,3,0,2,1:T(8,128)}, u32[]{:S(2)}) copy-start(f32[4,8,2,8,512]{4,3,0,2,1:T(8,128)} %get-tuple-element.12) | copy-start | bytes 3145732
Sparse Core Ops, SparseCore 0:
  9.6 49.2 all-gather.1
where the time goes:
time: 80 us; the launch traced here: 79.7 us
  blocking collectives  22.4 us (28%)
  waiting for transfers between devices  17.2 us (22%)
  matrix products  14.5 us (18%)
  between operations  14.2 us (18%)
  local copies, waits for them, and re-layouts  8.59 us (11%)
  other arithmetic  2.66 us (3%)
    all_gather x1, waiting for transfers between devices, on_device(): lax.all_gather(adapter_down_factor, 'wide', axis=2, tiled=True)  16.6 us
    all_gather x1, blocking collectives, on_device(): lax.all_gather(adapter_up_factor, 'wide', axis=2, tiled=True)  15.2 us
    all_gather x1, blocking collectives, on_device(): full_rows = lax.all_gather(hidden, 'tp', axis=2, tiled=True)  7.17 us
    dot_general x1, matrix products, on_device(): jnp.einsum('kca,kad->dkc', rank_full, down_full, preferred_element_type=j...  6.4 us
    reshape x1, local copies, waits for them, and re-layouts, attend(): stored_rotated_keys.reshape(row_count, cache_span, group_count, HD)  3.98 us
    dot_general x1, matrix products, attend(): jnp.einsum('srgqd,rlgd->srgql', query_split, old_keys, preferred_element_...  3.38 us
    reshape x1, local copies, waits for them, and re-layouts, attend(): stored_value_rows.reshape(row_count, cache_span, group_count, HD)  2.54 us
  transfers between devices with their start and end apart: 1, of which 1 were waited for; matrix products, arithmetic and copies ran while one was open for 15% of the time, Pallas kernels for 0%

commit v1 on v0

--- a/solution.py
+++ b/solution.py
@@ -1,3 +1,4 @@
+import functools
 import math
 
 import jax
@@ -75,7 +76,44 @@
     return attended.astype(jnp.bfloat16).reshape(step_count, row_count, query_width)
 
 
+def lora_inner(hidden, scaled_gain_rows, adapter_down_factor, wide_count, tp_count):
+    step_count, row_count, part_width = hidden.shape
+    if wide_count == tp_count and tp_count == 4:
+        there = []
+        for w in range(4):
+            for t in range(4):
+                there.append((w * 4 + t, t * 4 + 2 * ((t // 2) ^ ((w + t) & 1)) + w // 2))
+        moved = lax.ppermute(hidden, ("wide", "tp"), there)
+        block = lax.axis_index("wide")
+        gain_part = lax.dynamic_slice(scaled_gain_rows, (block * part_width,), (part_width,))
+        moved = (moved.astype(jnp.float32) * gain_part.astype(jnp.float32)).astype(jnp.bfloat16)
+        inner = jnp.einsum(
+            "srd,kad->srka", moved, adapter_down_factor, preferred_element_type=jnp.float32
+        )
+        parts = []
+        for j in range(4):
+            back = []
+            for source, dest in there:
+                w, f = source // 4, source % 4
+                back.append((dest, w * 4 + (f + j) % 4))
+            parts.append(lax.ppermute(inner, ("wide", "tp"), back))
+        return parts
+    rows = lax.all_gather(hidden, "tp", axis=2, tiled=True).astype(jnp.float32)
+    rows = (rows * scaled_gain_rows.astype(jnp.float32)).astype(jnp.bfloat16)
+    down = lax.all_gather(adapter_down_factor, "wide", axis=2, tiled=True)
+    return [jnp.einsum("srd,kad->srka", rows, down, preferred_element_type=jnp.float32)]
+
+
+def gather_parts(block, axis, count):
+    parts = [block]
+    for j in range(1, count):
+        parts.append(lax.ppermute(block, axis, [(i, (i + j) % count) for i in range(count)]))
+    return parts
+
+
 def on_device(
+    wide_count,
+    tp_count,
     hidden,
     input_norm_gain,
     key_value_weight,
@@ -87,29 +125,39 @@
     stored_value_rows,
     lengths,
 ):
-    full_rows = lax.all_gather(hidden, "tp", axis=2, tiled=True)
-    widened = full_rows.astype(jnp.float32)
-    mean_square = jnp.mean(widened * widened, axis=-1, keepdims=True)
-    normed = (
-        widened * lax.rsqrt(mean_square + norm_eps) * input_norm_gain.astype(jnp.float32)
-    ).astype(jnp.bfloat16)
-    step_count, row_count = (normed.shape[0], normed.shape[1])
-    down_full, rank_full = (
-        lax.all_gather(adapter_down_factor, "wide", axis=2, tiled=True),
-        lax.all_gather(adapter_up_factor, "wide", axis=2, tiled=True),
-    )
-    factor_product = jnp.einsum(
-        "kca,kad->dkc", rank_full, down_full, preferred_element_type=jnp.float32
-    )
-    combined_output = key_value_weight.astype(jnp.float32) + adapter_scale * factor_product
-    merged_high = combined_output.astype(jnp.bfloat16)
-    merged_low = (combined_output - merged_high.astype(jnp.float32)).astype(jnp.bfloat16)
-    projected_output = jnp.einsum(
-        "srd,dkc->srkc", normed, merged_high, preferred_element_type=jnp.float32
-    )
-    projected_output = projected_output + jnp.einsum(
-        "srd,dkc->srkc", normed, merged_low, preferred_element_type=jnp.float32
-    )
+    step_count, row_count, part_width = hidden.shape
+    inner_parts = lora_inner(hidden, input_norm_gain, adapter_down_factor, wide_count, tp_count)
+    width = part_width * tp_count
+    me = lax.axis_index("tp")
+    my_wide = lax.axis_index("wide")
+    square_sum = 0.0
+    base = 0.0
+    for j, part in enumerate(gather_parts(hidden, "tp", tp_count)):
+        start = (me - j) % tp_count * part_width
+        part = part.astype(jnp.float32)
+        square_sum = square_sum + jnp.sum(part * part, axis=-1)
+        gain_part = lax.dynamic_slice(input_norm_gain, (start,), (part_width,))
+        scaled = (part * gain_part.astype(jnp.float32)).astype(jnp.bfloat16)
+        weight_part = lax.dynamic_slice(
+            key_value_weight, (start, 0, 0), (part_width,) + key_value_weight.shape[1:]
+        )
+        base = base + jnp.einsum(
+            "srd,dkc->srkc", scaled, weight_part, preferred_element_type=jnp.float32
+        )
+    row_scale = lax.rsqrt(square_sum / width + norm_eps)
+    inner = sum(inner_parts[1:], inner_parts[0])
+    up_parts = gather_parts(adapter_up_factor, "wide", wide_count)
+    rank_part = adapter_up_factor.shape[2]
+    lora = 0.0
+    for j, part in enumerate(up_parts):
+        start = (my_wide - j) % wide_count * rank_part
+        lora = lora + jnp.einsum(
+            "srka,kca->srkc",
+            lax.dynamic_slice(inner, (0, 0, 0, start), inner.shape[:3] + (rank_part,)),
+            part.astype(jnp.float32),
+            precision=lax.Precision.HIGHEST,
+        )
+    projected_output = (base + adapter_scale * lora) * row_scale[:, :, None, None]
     projected_output = projected_output + key_value_bias.astype(jnp.float32)
     positions = lengths[None, :] + jnp.arange(step_count, dtype=jnp.int32)[:, None]
     new_keys = rotate_keys(projected_output[:, :, 0, :], positions).astype(jnp.bfloat16)
@@ -138,6 +186,7 @@
         P(None, ("groups", "wide"), "tp"),
         P(None, ("groups", "wide"), "tp"),
     )
+    body = functools.partial(on_device, mesh.shape["wide"], mesh.shape["tp"])
     return jax.shard_map(
-        on_device, mesh=mesh, in_specs=in_specs, out_specs=out_specs, check_vma=False
+        body, mesh=mesh, in_specs=in_specs, out_specs=out_specs, check_vma=False
     )

time: 80 us -> 60 us (0.75)
  starting transfers between devices: 0.04 us -> 23.1 us
  blocking collectives: 22.4 us -> 0 us
  between operations: 14.2 us -> 0.97 us
  waiting for transfers between devices: 17.2 us -> 4.35 us
  local copies, waits for them, and re-layouts: 8.59 us -> 19.6 us
  matrix products: 14.5 us -> 8.63 us
    ppermute x0 -> x11, starting transfers between devices: none -> 23.1 us  [the longest x6 11.6 us: gather_parts(): lax.ppermute(block, axis, [(i, (i + j) % count) for i in range(count)])]
    all_gather x2 -> x0, blocking collectives: 22.4 us -> none  [the longest x1 15.2 us: on_device(): lax.all_gather(adapter_up_factor, 'wide', axis=2, tiled=True)]
    all_gather x1 -> x0, waiting for transfers between devices: 16.6 us -> none  [on_device(): lax.all_gather(adapter_down_factor, 'wide', axis=2, tiled=True)]
    dynamic_slice x0 -> x1, local copies, waits for them, and re-layouts: none -> 8.89 us  [on_device(): lax.dynamic_slice(key_value_weight, (start, 0, 0), (part_width,) + key_va...]
    ppermute x0 -> x11, waiting for transfers between devices: none -> 4.35 us  [the longest x6 4.34 us: gather_parts(): lax.ppermute(block, axis, [(i, (i + j) % count) for i in range(count)])]
    dot_general x3 -> x9, matrix products: 9.56 us -> 5.26 us  [the longest x4 3.99 us: on_device(): jnp.einsum('srd,dkc->srkc', scaled, weight_part, preferred_element_type=j...]
    dot_general x1, matrix products: 3.38 us -> 1.82 us  [attend(): jnp.einsum('srgqd,rlgd->srgql', query_split, old_keys, preferred_element_...]
    reshape x1, local copies, waits for them, and re-layouts: 2.54 us -> 3.97 us  [attend(): stored_value_rows.reshape(row_count, cache_span, group_count, HD)]
  transfers between devices with their start and end apart: 1 -> 11, of which waited for: 1 -> 2; matrix products, arithmetic and copies ran while one was open for 15% -> 43% of each run, Pallas kernels for 0% -> 0%
where the time goes in v1:
time: 60 us; the launch traced here: 59.4 us
  starting transfers between devices  23.1 us (38%)
  local copies, waits for them, and re-layouts  19.6 us (33%)
  matrix products  8.63 us (14%)
  waiting for transfers between devices  4.35 us (7%)
  other arithmetic  2.85 us (5%)
  between operations  0.97 us (2%)
    ppermute x6, starting transfers between devices, gather_parts(): lax.ppermute(block, axis, [(i, (i + j) % count) for i in range(count)])  11.6 us
    ppermute x4, starting transfers between devices, lora_inner(): parts.append(lax.ppermute(inner, ('wide', 'tp'), back))  9.89 us
    dynamic_slice x1, local copies, waits for them, and re-layouts, on_device(): lax.dynamic_slice(key_value_weight, (start, 0, 0), (part_width,) + key_va...  8.89 us
    ppermute x6, waiting for transfers between devices, gather_parts(): lax.ppermute(block, axis, [(i, (i + j) % count) for i in range(count)])  4.34 us
    dot_general x4, matrix products, on_device(): jnp.einsum('srd,dkc->srkc', scaled, weight_part, preferred_element_type=j...  3.99 us
    reshape x1, local copies, waits for them, and re-layouts, attend(): stored_value_rows.reshape(row_count, cache_span, group_count, HD)  3.97 us
    reshape x1, local copies, waits for them, and re-layouts, attend(): stored_rotated_keys.reshape(row_count, cache_span, group_count, HD)  3.96 us
    dot_general x1, matrix products, attend(): jnp.einsum('srgqd,rlgd->srgql', query_split, old_keys, preferred_element_...  1.82 us
  transfers between devices with their start and end apart: 11, of which 2 were waited for; matrix products, arithmetic and copies ran while one was open for 43% of the time, Pallas kernels for 0%

profile of v1, /device:TPU:0, one launch (start us, length us, event | category | flops | bytes accessed | tf_op | source)
XLA Modules:
  0.0 59.4 jit_solution(6100133873351252585)
XLA Ops:
  0.6 0.0 copy-start
  0.6 3.0 %collective-permute-start.1 = (bf16[4,8,2048]{2,1,0:T(8,128)(2,1)}, bf16[4,8,2048]{2,1,0:T(8,128)(2,1)S(1)}, u32[]{:S(2)}, u32[]{:S(2)}) collective-permute-start(bf16[4,8,2048]{2,1,0:T(8,128)(2,1)} %param.10), channel_id=1, source_target_pairs={{0,2},{1,3},{2,0},{3,1},{4,6},{5,7},{6,4},{7,5},{8,10},{9,11},{10,... | collective-permute-start | bytes 393224 | tf_op jit(solution)/shard_map/ppermute | solution.py:110
  3.6 0.0 collective-permute-start.2
  3.7 0.5 collective-permute-start
  4.2 1.6 %collective-permute-start.3 = (bf16[4,8,2048]{2,1,0:T(8,128)(2,1)}, bf16[4,8,2048]{2,1,0:T(8,128)(2,1)S(1)}, u32[]{:S(2)}, u32[]{:S(2)}) collective-permute-start(bf16[4,8,2048]{2,1,0:T(8,128)(2,1)} %param.10), channel_id=1, source_target_pairs={{0,0},{1,6},{2,10},{3,12},{4,2},{5,4},{6,8},{7,14},{8,1},{9,7},{10... | collective-permute-start | bytes 393224 | tf_op jit(solution)/shard_map/ppermute | solution.py:86
  5.7 4.9 %collective-permute-start.10 = (bf16[2,256,16]{1,2,0:T(8,128)(2,1)}, bf16[2,256,16]{1,2,0:T(8,128)(2,1)S(1)}, u32[]{:S(2)}, u32[]{:S(2)}) collective-permute-start(bf16[2,256,16]{1,2,0:T(8,128)(2,1)} %param.15), channel_id=1, source_target_pairs={{0,12},{4,0},{8,4},{12,8},{1,13},{5,1},{9,5},{13,9},{2,14},{6,2},{... | collective-permute-start | bytes 49160 | tf_op jit(solution)/shard_map/ppermute | solution.py:110
  10.6 0.7 %add_convert_fusion = f32[4,8]{0,1:T(8,128)S(1)} fusion(s32[8]{0:T(128)} %param.19), kind=kLoop, calls=%fused_computation.99 | loop fusion | flops 64 | bytes 160 | tf_op jit(solution)/shard_map/convert_element_type | solution.py:24
  11.4 0.7 %iota_compare_fusion = pred[8,512]{1,0:T(8,128)(4,1)S(1)} fusion(s32[8]{0:T(128)} %param.19), kind=kLoop, calls=%fused_computation.96 | loop fusion | flops 4096 | bytes 4128 | tf_op jit(solution)/shard_map/lt | solution.py:55
  12.1 4.0 %reshape.115 = bf16[8,512,2,128]{3,2,1,0:T(2,128)(2,1)} reshape(bf16[8,512,256]{2,1,0:T(8,128)(2,1)} %param.17) | data formatting | bytes 4194304 | tf_op jit(solution)/shard_map/reshape | solution.py:43
  16.1 8.9 %constant_dynamic-slice_fusion.2 = (bf16[2048,2,256]{2,1,0:T(2,128)(2,1)S(1)}, bf16[2048,2,256]{2,1,0:T(2,128)(2,1)}, bf16[2048,2,256]{2,1,0:T(2,128)(2,1)S(1)}, bf16[2048,2,256]{2,1,0:T(2,128)(2,1)}) fusion(bf16[8192,2,256]{2,1,0:T(2,128)(2,1)} %param.12, s32[]{:T(128)S(6)} %select_n.80, s32[]{:T(128)S(6)} %select_n.82, s32[]{:T(128)S(6)} %select_n.78, ...), kind=kLoop, calls=%fused_computation.113 | loop fusion | bytes 16777232 | tf_op jit(solution)/shard_map/dynamic_slice | solution.py:141
  24.9 0.0 copy-start.9
  25.0 1.1 %fusion.3 = f32[4,8,2,256]{3,1,2,0:T(8,128)} fusion(bf16[2048,2,256]{2,1,0:T(2,128)(2,1)S(1)} %get-tuple-element.5, bf16[4,8,2048]{2,1,0:T(8,128)(2,1)S(1)} %copy-done.5, f32[2048]{0:T(1024)S(1)} %get-tuple-element.16), kind=kOutput, calls=%fused_computation.7 | convolution fusion | flops 67305472 | bytes 2301952 | tf_op jit(solution)/shard_map/srd,dkc->srkc/dot_general | solution.py:144
  26.1 0.2 multiply_cosine_fusion
  26.3 0.3 copy-done.3
  26.6 1.8 %fusion.91 = (f32[4,8,2,8]{3,0,2,1:T(4,128)S(1)}, f32[4,8,2,8,512]{4,3,0,2,1:T(8,128)}) fusion(bf16[4,8,2,8,128]{4,1,3,2,0:T(8,128)(2,1)S(1)} %bitcast.106, bf16[8,512,2,128,1]{3,2,1,0,4:T(2,128)(2,1)S(1)} %bitcast.104, pred[8,512]{1,0:T(8,128)(4,1)S(1)} %iota_compare_fusion), kind=kOutput, calls=%fused_computation.117 | convolution fusion | flops 67894784 | bytes 3282944 | tf_op jit(solution)/shard_map/srgqd,rlgd->srgql/dot_general | solution.py:48
  28.5 4.0 %reshape.117 = bf16[8,512,2,128]{3,2,1,0:T(2,128)(2,1)} reshape(bf16[8,512,256]{2,1,0:T(8,128)(2,1)} %param.18) | data formatting | bytes 4194304 | tf_op jit(solution)/shard_map/reshape | solution.py:44
  32.5 0.1 fusion.44
  32.6 0.3 fusion.39
  32.9 0.7 %collective-permute-start.4 = (f32[4,8,2,64]{3,1,2,0:T(8,128)S(1)}, f32[4,8,2,64]{3,1,2,0:T(8,128)S(1)}, u32[]{:S(2)}, u32[]{:S(2)}) collective-permute-start(f32[4,8,2,64]{3,1,2,0:T(8,128)S(1)} %fusion.39), channel_id=1, source_target_pairs={{0,0},{6,1},{10,2},{12,3},{2,4},{4,5},{8,6},{14,7},{1,8},{7,9},{11... | collective-permute-start | bytes 49160 | tf_op jit(solution)/shard_map/ppermute | solution.py:99
  33.6 2.8 %collective-permute-start.5 = (f32[4,8,2,64]{3,1,2,0:T(8,128)S(1)}, f32[4,8,2,64]{3,1,2,0:T(8,128)S(1)}, u32[]{:S(2)}, u32[]{:S(2)}) collective-permute-start(f32[4,8,2,64]{3,1,2,0:T(8,128)S(1)} %fusion.39), channel_id=1, source_target_pairs={{0,1},{6,2},{10,3},{12,0},{2,5},{4,6},{8,7},{14,4},{1,9},{7,10},{1... | collective-permute-start | bytes 49160 | tf_op jit(solution)/shard_map/ppermute | solution.py:99
  36.5 0.1 fusion.46
  36.6 2.2 %collective-permute-start.6 = (f32[4,8,2,64]{3,1,2,0:T(8,128)S(1)}, f32[4,8,2,64]{3,1,2,0:T(8,128)S(1)}, u32[]{:S(2)}, u32[]{:S(2)}) collective-permute-start(f32[4,8,2,64]{3,1,2,0:T(8,128)S(1)} %fusion.39), channel_id=1, source_target_pairs={{0,2},{6,3},{10,0},{12,1},{2,6},{4,7},{8,4},{14,5},{1,10},{7,11},{... | collective-permute-start | bytes 49160 | tf_op jit(solution)/shard_map/ppermute | solution.py:99
  38.8 0.1 fusion.48
  38.9 4.2 %collective-permute-start.7 = (f32[4,8,2,64]{3,1,2,0:T(8,128)S(1)}, f32[4,8,2,64]{3,1,2,0:T(8,128)S(1)}, u32[]{:S(2)}, u32[]{:S(2)}) collective-permute-start(f32[4,8,2,64]{3,1,2,0:T(8,128)S(1)} %fusion.39), channel_id=1, source_target_pairs={{0,3},{6,0},{10,1},{12,2},{2,7},{4,4},{8,5},{14,6},{1,11},{7,8},{1... | collective-permute-start | bytes 49160 | tf_op jit(solution)/shard_map/ppermute | solution.py:99
  43.1 0.1 fusion.50
  43.2 2.0 %fusion.1 = f32[4,8,2,256]{3,1,2,0:T(8,128)S(1)} fusion(bf16[2048,2,256]{2,1,0:T(2,128)(2,1)} %get-tuple-element.4, bf16[4,8,2048]{2,1,0:T(8,128)(2,1)S(1)} %collective-permute-done.1, f32[2048]{0:T(1024)S(1)} %get-tuple-element.14), kind=kOutput, calls=%fused_computation.3 | convolution fusion | flops 67305472 | bytes 2301952 | tf_op jit(solution)/shard_map/srd,dkc->srkc/dot_general | solution.py:144
  45.2 0.0 copy-done.1
  45.3 0.4 fusion
  45.7 0.4 copy-done.10
  46.1 0.4 fusion.37
  46.6 2.5 %collective-permute-start.9 = (bf16[2,256,16]{1,2,0:T(8,128)(2,1)S(1)}, bf16[2,256,16]{1,2,0:T(8,128)(2,1)S(1)}, u32[]{:S(2)}, u32[]{:S(2)}) collective-permute-start(bf16[2,256,16]{1,2,0:T(8,128)(2,1)S(1)} %copy-done.7), channel_id=1, source_target_pairs={{0,8},{4,12},{8,0},{12,4},{1,9},{5,13},{9,1},{13,5},{2,10},{6,14},... | collective-permute-start | bytes 49160 | tf_op jit(solution)/shard_map/ppermute | solution.py:110
  49.1 0.7 %collective-permute-start.8 = (bf16[2,256,16]{1,2,0:T(8,128)(2,1)S(1)}, bf16[2,256,16]{1,2,0:T(8,128)(2,1)S(1)}, u32[]{:S(2)}, u32[]{:S(2)}) collective-permute-start(bf16[2,256,16]{1,2,0:T(8,128)(2,1)S(1)} %copy-done.7), channel_id=1, source_target_pairs={{0,4},{4,8},{8,12},{12,0},{1,5},{5,9},{9,13},{13,1},{2,6},{6,10},{... | collective-permute-start | bytes 49160 | tf_op jit(solution)/shard_map/ppermute | solution.py:110
  49.8 0.2 fusion.71
  50.1 1.4 %collective-permute-done.9 = bf16[2,256,16]{1,2,0:T(8,128)(2,1)S(1)} collective-permute-done((bf16[2,256,16]{1,2,0:T(8,128)(2,1)S(1)}, bf16[2,256,16]{1,2,0:T(8,128)(2,1)S(1)}, u32[]{:S(2)}, u32[]{:S(2)}) %collective-permute-start.9) | collective-permute-done | bytes 16416 | tf_op jit(solution)/shard_map/ppermute | solution.py:110
  51.5 0.2 fusion.73
  51.7 2.9 %collective-permute-done.8 = bf16[2,256,16]{1,2,0:T(8,128)(2,1)S(1)} collective-permute-done((bf16[2,256,16]{1,2,0:T(8,128)(2,1)S(1)}, bf16[2,256,16]{1,2,0:T(8,128)(2,1)S(1)}, u32[]{:S(2)}, u32[]{:S(2)}) %collective-permute-start.8) | collective-permute-done | bytes 16416 | tf_op jit(solution)/shard_map/ppermute | solution.py:110
  54.6 0.2 fusion.75
  54.9 0.2 fusion.34
  55.1 0.6 %fusion.84 = (bf16[4,8,2,128,1]{3,1,2,0,4:T(8,128)(2,1)S(1)}, bf16[4,8,256]{2,1,0:T(8,128)(2,1)}) fusion(f32[4,8,2,256]{3,1,2,0:T(8,128)S(1)} %fusion.34), kind=kLoop, calls=%fused_computation.97 | loop fusion | bytes 49152 | tf_op jit(solution)/shard_map/convert_element_type | solution.py:164
  55.7 0.1 fusion.90
  55.9 0.1 maximum_convert_fusion
  55.9 0.6 %copy.129 = bf16[4,8,2,128]{3,1,2,0:T(8,128)(2,1)} copy(bf16[4,8,2,128]{3,0,2,1:T(4,128)(2,1)S(1)} %maximum_convert_fusion) | data formatting | bytes 32768 | tf_op jit(solution)/shard_map/convert_element_type | solution.py:163
  56.6 0.7 %fusion.92 = (f32[4,8,2,8]{3,0,2,1:T(4,128)S(1)}, f32[4,8,2,8,4]{3,4,0,2,1:T(4,128)S(1)}) fusion(bf16[4,8,2,8,128]{4,1,3,2,0:T(8,128)(2,1)S(1)} %bitcast.107, bf16[4,8,2,128]{3,0,2,1:T(4,128)(2,1)S(1)} %maximum_convert_fusion, pred[4,4]{1,0:T(4,128)(4,1)S(1)} %iota_compare_fusion.1), kind=kOutput, calls=%fused_computation.118 | convolution fusion | flops 529920 | bytes 157712 | tf_op jit(solution)/shard_map/srgqd,trgd->srgqt/dot_general | solution.py:52
  57.3 0.1 fusion.68
  57.4 0.4 fusion.38
  57.8 0.3 convolution_bitcast_fusion
  58.1 0.6 fusion.23
  58.7 0.7 %reshape.118 = bf16[4,8,2048]{2,1,0:T(8,128)(2,1)} reshape(bf16[4,8,2,8,128]{4,3,2,1,0:T(8,128)(2,1)S(1)} %copy.52) | data formatting | bytes 262144 | tf_op jit(solution)/shard_map/reshape | solution.py:76
  (37 shorter events, 0.2 us)
Async XLA Ops:
  0.6 31.9 %copy-start = (bf16[2,64,2048]{2,1,0:T(8,128)(2,1)S(1)}, bf16[2,64,2048]{2,1,0:T(8,128)(2,1)}, u32[]{:S(2)}) copy-start(bf16[2,64,2048]{2,1,0:T(8,128)(2,1)} %param.14) | copy-start | bytes 1572868
  0.6 35.9 %collective-permute-start.1 = (bf16[4,8,2048]{2,1,0:T(8,128)(2,1)}, bf16[4,8,2048]{2,1,0:T(8,128)(2,1)S(1)}, u32[]{:S(2)}, u32[]{:S(2)}) collective-permute-start(bf16[4,8,2048]{2,1,0:T(8,128)(2,1)} %param.10), channel_id=1, source_target_pairs={{0,2},{1,3},{2,0},{3,1},{4,6},{5,7},{6,4},{7,5},{8,10},{9,11},{10,... | collective-permute-start | bytes 393224 | tf_op jit(solution)/shard_map/ppermute | solution.py:110
  3.6 35.3 %collective-permute-start.2 = (bf16[4,8,2048]{2,1,0:T(8,128)(2,1)}, bf16[4,8,2048]{2,1,0:T(8,128)(2,1)S(1)}, u32[]{:S(2)}, u32[]{:S(2)}) collective-permute-start(bf16[4,8,2048]{2,1,0:T(8,128)(2,1)} %param.10), channel_id=1, source_target_pairs={{0,3},{1,0},{2,1},{3,2},{4,7},{5,4},{6,5},{7,6},{8,11},{9,8},{10,9... | collective-permute-start | bytes 393224 | tf_op jit(solution)/shard_map/ppermute | solution.py:110
  3.7 30.0 %collective-permute-start = (bf16[4,8,2048]{2,1,0:T(8,128)(2,1)}, bf16[4,8,2048]{2,1,0:T(8,128)(2,1)S(1)}, u32[]{:S(2)}, u32[]{:S(2)}) collective-permute-start(bf16[4,8,2048]{2,1,0:T(8,128)(2,1)} %param.10), channel_id=1, source_target_pairs={{0,1},{1,2},{2,3},{3,0},{4,5},{5,6},{6,7},{7,4},{8,9},{9,10},{10,1... | collective-permute-start | bytes 393224 | tf_op jit(solution)/shard_map/ppermute | solution.py:110
  4.2 28.4 %collective-permute-start.3 = (bf16[4,8,2048]{2,1,0:T(8,128)(2,1)}, bf16[4,8,2048]{2,1,0:T(8,128)(2,1)S(1)}, u32[]{:S(2)}, u32[]{:S(2)}) collective-permute-start(bf16[4,8,2048]{2,1,0:T(8,128)(2,1)} %param.10), channel_id=1, source_target_pairs={{0,0},{1,6},{2,10},{3,12},{4,2},{5,4},{6,8},{7,14},{8,1},{9,7},{10... | collective-permute-start | bytes 393224 | tf_op jit(solution)/shard_map/ppermute | solution.py:86
  5.7 44.1 %collective-permute-start.10 = (bf16[2,256,16]{1,2,0:T(8,128)(2,1)}, bf16[2,256,16]{1,2,0:T(8,128)(2,1)S(1)}, u32[]{:S(2)}, u32[]{:S(2)}) collective-permute-start(bf16[2,256,16]{1,2,0:T(8,128)(2,1)} %param.15), channel_id=1, source_target_pairs={{0,12},{4,0},{8,4},{12,8},{1,13},{5,1},{9,5},{13,9},{2,14},{6,2},{... | collective-permute-start | bytes 49160 | tf_op jit(solution)/shard_map/ppermute | solution.py:110
  16.1 8.9 %copy-start.6 = (bf16[8192]{0:T(1024)(128)(2,1)S(1)}, bf16[8192]{0:T(1024)(128)(2,1)}, u32[]{:S(2)}) copy-start(bf16[8192]{0:T(1024)(128)(2,1)} %param.11) | copy-start | bytes 49156
  16.1 8.9 %copy-start.5 = (bf16[4,8,2048]{2,1,0:T(8,128)(2,1)S(1)}, bf16[4,8,2048]{2,1,0:T(8,128)(2,1)}, u32[]{:S(2)}) copy-start(bf16[4,8,2048]{2,1,0:T(8,128)(2,1)} %param.10) | copy-start | bytes 393220
  24.9 1.6 %copy-start.3 = (bf16[8,512,2,128]{3,2,1,0:T(2,128)(2,1)S(1)}, bf16[8,512,2,128]{3,2,1,0:T(2,128)(2,1)}, u32[]{:S(2)}) copy-start(bf16[8,512,2,128]{3,2,1,0:T(2,128)(2,1)} %reshape.115) | copy-start | bytes 6291460
  24.9 1.6 %copy-start.9 = (bf16[4,8,2048]{2,1,0:T(8,128)(2,1)S(1)}, bf16[4,8,2048]{2,1,0:T(8,128)(2,1)}, u32[]{:S(2)}) copy-start(bf16[4,8,2048]{2,1,0:T(8,128)(2,1)} %param.16) | copy-start | bytes 393220
  26.1 2.4 %copy-start.8 = (bf16[2,256]{1,0:T(2,128)(2,1)S(1)}, bf16[2,256]{1,0:T(2,128)(2,1)}, u32[]{:S(2)}) copy-start(bf16[2,256]{1,0:T(2,128)(2,1)} %param.13) | copy-start | bytes 3076
  32.9 13.6 %collective-permute-start.4 = (f32[4,8,2,64]{3,1,2,0:T(8,128)S(1)}, f32[4,8,2,64]{3,1,2,0:T(8,128)S(1)}, u32[]{:S(2)}, u32[]{:S(2)}) collective-permute-start(f32[4,8,2,64]{3,1,2,0:T(8,128)S(1)} %fusion.39), channel_id=1, source_target_pairs={{0,0},{6,1},{10,2},{12,3},{2,4},{4,5},{8,6},{14,7},{1,8},{7,9},{11... | collective-permute-start | bytes 49160 | tf_op jit(solution)/shard_map/ppermute | solution.py:99
  33.6 15.5 %collective-permute-start.5 = (f32[4,8,2,64]{3,1,2,0:T(8,128)S(1)}, f32[4,8,2,64]{3,1,2,0:T(8,128)S(1)}, u32[]{:S(2)}, u32[]{:S(2)}) collective-permute-start(f32[4,8,2,64]{3,1,2,0:T(8,128)S(1)} %fusion.39), channel_id=1, source_target_pairs={{0,1},{6,2},{10,3},{12,0},{2,5},{4,6},{8,7},{14,4},{1,9},{7,10},{1... | collective-permute-start | bytes 49160 | tf_op jit(solution)/shard_map/ppermute | solution.py:99
  36.6 8.7 %copy-start.1 = (bf16[2048,2,256]{2,1,0:T(2,128)(2,1)S(1)}, bf16[2048,2,256]{2,1,0:T(2,128)(2,1)}, u32[]{:S(2)}) copy-start(bf16[2048,2,256]{2,1,0:T(2,128)(2,1)} %get-tuple-element.6) | copy-start | bytes 6291460
  36.6 13.2 %collective-permute-start.6 = (f32[4,8,2,64]{3,1,2,0:T(8,128)S(1)}, f32[4,8,2,64]{3,1,2,0:T(8,128)S(1)}, u32[]{:S(2)}, u32[]{:S(2)}) collective-permute-start(f32[4,8,2,64]{3,1,2,0:T(8,128)S(1)} %fusion.39), channel_id=1, source_target_pairs={{0,2},{6,3},{10,0},{12,1},{2,6},{4,7},{8,4},{14,5},{1,10},{7,11},{... | collective-permute-start | bytes 49160 | tf_op jit(solution)/shard_map/ppermute | solution.py:99
  38.9 10.9 %collective-permute-start.7 = (f32[4,8,2,64]{3,1,2,0:T(8,128)S(1)}, f32[4,8,2,64]{3,1,2,0:T(8,128)S(1)}, u32[]{:S(2)}, u32[]{:S(2)}) collective-permute-start(f32[4,8,2,64]{3,1,2,0:T(8,128)S(1)} %fusion.39), channel_id=1, source_target_pairs={{0,3},{6,0},{10,1},{12,2},{2,7},{4,4},{8,5},{14,6},{1,11},{7,8},{1... | collective-permute-start | bytes 49160 | tf_op jit(solution)/shard_map/ppermute | solution.py:99
  45.2 0.9 %copy-start.10 = (f32[4,8,2,256]{3,1,2,0:T(8,128)S(1)}, f32[4,8,2,256]{3,1,2,0:T(8,128)}, u32[]{:S(2)}) copy-start(f32[4,8,2,256]{3,1,2,0:T(8,128)} %fusion.3) | copy-start | bytes 196612
  45.7 0.9 %copy-start.7 = (bf16[2,256,16]{1,2,0:T(8,128)(2,1)S(1)}, bf16[2,256,16]{1,2,0:T(8,128)(2,1)}, u32[]{:S(2)}) copy-start(bf16[2,256,16]{1,2,0:T(8,128)(2,1)} %param.15) | copy-start | bytes 49156
  46.1 11.3 %copy-start.4 = (f32[4,8,2,8,512]{4,3,0,2,1:T(8,128)S(1)}, f32[4,8,2,8,512]{4,3,0,2,1:T(8,128)}, u32[]{:S(2)}) copy-start(f32[4,8,2,8,512]{4,3,0,2,1:T(8,128)} %get-tuple-element.21) | copy-start | bytes 3145732
  46.6 4.9 %collective-permute-start.9 = (bf16[2,256,16]{1,2,0:T(8,128)(2,1)S(1)}, bf16[2,256,16]{1,2,0:T(8,128)(2,1)S(1)}, u32[]{:S(2)}, u32[]{:S(2)}) collective-permute-start(bf16[2,256,16]{1,2,0:T(8,128)(2,1)S(1)} %copy-done.7), channel_id=1, source_target_pairs={{0,8},{4,12},{8,0},{12,4},{1,9},{5,13},{9,1},{13,5},{2,10},{6,14},... | collective-permute-start | bytes 49160 | tf_op jit(solution)/shard_map/ppermute | solution.py:110
  49.1 5.5 %collective-permute-start.8 = (bf16[2,256,16]{1,2,0:T(8,128)(2,1)S(1)}, bf16[2,256,16]{1,2,0:T(8,128)(2,1)S(1)}, u32[]{:S(2)}, u32[]{:S(2)}) collective-permute-start(bf16[2,256,16]{1,2,0:T(8,128)(2,1)S(1)} %copy-done.7), channel_id=1, source_target_pairs={{0,4},{4,8},{8,12},{12,0},{1,5},{5,9},{9,13},{13,1},{2,6},{6,10},{... | collective-permute-start | bytes 49160 | tf_op jit(solution)/shard_map/ppermute | solution.py:110
  49.8 8.3 %copy-start.2 = (bf16[8,512,2,128]{3,2,1,0:T(2,128)(2,1)S(1)}, bf16[8,512,2,128]{3,2,1,0:T(2,128)(2,1)}, u32[]{:S(2)}) copy-start(bf16[8,512,2,128]{3,2,1,0:T(2,128)(2,1)} %reshape.117) | copy-start | bytes 6291460

commit v2 on v0

v2 whole, which is shorter than its diff:
```python
import functools
import math

import jax
import jax.numpy as jnp
from jax import lax
from jax.experimental import pallas as pl
from jax.experimental.pallas import tpu as pltpu
from jax.sharding import PartitionSpec as P

HD = 128


norm_eps = 1e-06
adapter_scale = 2.0
rope_base = 1000000.0
masked_score = -1e30
score_scale = 1.0 / math.sqrt(HD)

VMEM = pl.BlockSpec(memory_space=pltpu.VMEM)
SMEM = pl.BlockSpec(memory_space=pltpu.SMEM)
HBM = pl.BlockSpec(memory_space=pltpu.HBM)


def query_block(query_ref, group, per_group):
    steps = query_ref.shape[0]
    tiles = []
    for head in range(per_group):
        at = (group * per_group + head) * HD
        for step in range(steps):
            tiles.append(query_ref[step, :, at : at + HD].astype(jnp.float32))
    return jnp.concatenate(tiles, axis=0)


def cache_kernel(
    lengths_ref,
    query_ref,
    key_ref,
    value_ref,
    weight_ref,
    weight_out,
    acc_out,
    top_out,
    total_out,
    cos_out,
    sin_out,
    query_rows,
    key_buffer,
    value_buffer,
    sems,
    weight_sems,
):
    steps, rows, query_width = query_ref.shape
    cache_span = key_ref.shape[1]
    groups = key_ref.shape[2] // HD
    per_group = query_width // HD // groups
    copies = []
    for row in range(rows):
        pair = (
            pltpu.make_async_copy(key_ref.at[row], key_buffer.at[row], sems.at[0, row]),
            pltpu.make_async_copy(value_ref.at[row], value_buffer.at[row], sems.at[1, row]),
        )
        for copy in pair:
            copy.start()
        copies.append(pair)
    pieces = weight_sems.shape[0]
    piece = weight_ref.shape[0] // pieces
    weight_copies = []
    for i in range(pieces):
        at = pl.ds(i * piece, piece)
        copy = pltpu.make_async_copy(weight_ref.at[at], weight_out.at[at], weight_sems.at[i])
        copy.start()
        weight_copies.append(copy)

    for group in range(groups):
        query_rows[group] = query_block(query_ref, group, per_group)

    lane = lax.broadcasted_iota(jnp.int32, (rows, HD), 1)
    half = HD // 2
    second = lane >= half
    index = jnp.where(second, lane - half, lane).astype(jnp.float32)
    inv_freq = jnp.exp(index * (-2.0 * math.log(rope_base) / HD))
    row_index = lax.broadcasted_iota(jnp.int32, (rows, HD), 0)
    row_lengths = jnp.zeros((rows, HD), jnp.int32)
    for row in range(rows):
        row_lengths = jnp.where(row_index == row, lengths_ref[row], row_lengths)
    for step in range(steps):
        angles = (row_lengths + step).astype(jnp.float32) * inv_freq
        sine = jnp.sin(angles)
        cos_out[pl.ds(step * rows, rows)] = jnp.cos(angles)
        sin_out[pl.ds(step * rows, rows)] = jnp.where(second, sine, -sine)

    place = lax.broadcasted_iota(jnp.int32, (steps * per_group, cache_span), 1)
    for row in range(rows):
        for copy in copies[row]:
            copy.wait()
        live = place < lengths_ref[row]
        for group in range(groups):
            at = pl.ds(group * HD, HD)
            mine = pl.ds(row, steps * per_group, stride=rows)
            query = query_rows[group, mine, :].astype(jnp.bfloat16)
            scores = lax.dot_general(
                query,
                key_buffer[row, :, at],
                (((1,), (1,)), ((), ())),
                preferred_element_type=jnp.float32,
            )
            scores = jnp.where(live, scores * score_scale, masked_score)
            top = jnp.max(scores, axis=1, keepdims=True)
            exps = jnp.exp(scores - top)
            total = jnp.sum(exps, axis=1, keepdims=True)
            acc = jnp.dot(
                exps.astype(jnp.bfloat16),
                value_buffer[row, :, at],
                preferred_element_type=jnp.float32,
            )
            acc_out[group, mine, :] = acc
            top_out[group, mine, :] = jnp.broadcast_to(top, acc.shape)
            total_out[group, mine, :] = jnp.broadcast_to(total, acc.shape)
    for copy in weight_copies:
        copy.wait()


def cache_call(lengths, queries, keys, values, weight):
    steps, rows, query_width = queries.shape
    cache_span, key_width = keys.shape[1:]
    groups = key_width // HD
    block = (groups, steps * rows * (query_width // key_width), HD)
    table = (steps * rows, HD)
    pieces = 4
    return pl.pallas_call(
        cache_kernel,
        out_shape=(
            pltpu.VMEM(weight.shape, weight.dtype),
            pltpu.VMEM(block, jnp.float32),
            pltpu.VMEM(block, jnp.float32),
            pltpu.VMEM(block, jnp.float32),
            pltpu.VMEM(table, jnp.float32),
            pltpu.VMEM(table, jnp.float32),
        ),
        in_specs=[SMEM, VMEM, HBM, HBM, HBM],
        out_specs=(VMEM,) * 6,
        scratch_shapes=[
            pltpu.VMEM(block, jnp.float32),
            pltpu.VMEM(keys.shape, keys.dtype),
            pltpu.VMEM(values.shape, values.dtype),
            pltpu.SemaphoreType.DMA((2, rows)),
            pltpu.SemaphoreType.DMA((pieces,)),
        ],
        compiler_params=pltpu.CompilerParams(vmem_limit_bytes=24 << 20),
        cost_estimate=pl.CostEstimate(flops=2 * 67 << 20, bytes_accessed=13 << 20, transcendentals=0),
        name="cache_attention",
    )(lengths, queries, keys, values, weight)


def scaled_chunks(block, gain, start):
    chunks = []
    for i in range(block.shape[1] // HD):
        chunk = block[:, i * HD : (i + 1) * HD]
        chunks.append((chunk * gain[start + i : start + i + 1]).astype(jnp.bfloat16))
    return chunks


def rows_of(ref):
    steps = ref.shape[0]
    return jnp.concatenate([ref[s].astype(jnp.float32) for s in range(steps)], axis=0)


def inner_kernel(count, hidden_ref, gain_ref, down_ref, out_ref, gain_rows):
    width = hidden_ref.shape[2]
    gain_rows[...] = gain_ref[...].astype(jnp.float32)
    start = pl.multiple_of(lax.axis_index("wide") * (width // HD), width // HD)
    gain = gain_rows[pl.ds(start, width // HD)]
    scaled = jnp.concatenate(scaled_chunks(rows_of(hidden_ref), gain, 0), axis=1)
    ranks = down_ref.shape[1]
    for kind in range(down_ref.shape[0]):
        inner = lax.dot_general(
            scaled,
            down_ref[kind],
            (((1,), (1,)), ((), ())),
            preferred_element_type=jnp.float32,
        ).astype(jnp.bfloat16)
        for i in range(count):
            out_ref[i, :, kind * ranks : (kind + 1) * ranks] = inner


def inner_call(count, hidden, gain, down):
    steps, rows, _ = hidden.shape
    kinds, ranks, _ = down.shape
    return pl.pallas_call(
        functools.partial(inner_kernel, count),
        out_shape=jax.ShapeDtypeStruct((count, steps * rows, kinds * ranks), jnp.bfloat16),
        in_specs=[VMEM] * 3,
        out_specs=VMEM,
        scratch_shapes=[pltpu.VMEM(gain.shape, jnp.float32)],
        compiler_params=pltpu.CompilerParams(vmem_limit_bytes=8 << 20),
        name="rank_inner",
    )(hidden, gain, down)


def base_kernel(offsets, gain_ref, weight_ref, *rest):
    parts = rest[: len(offsets)]
    base_out, square_out, gain_rows = rest[len(offsets) :]
    steps, rows, width = parts[0].shape
    count = steps * rows
    kinds, columns = weight_ref.shape[1:]
    flat = weight_ref.reshape(weight_ref.shape[0] * kinds, columns)
    gain_rows[...] = gain_ref[...].astype(jnp.float32)
    me = lax.axis_index("tp")
    lane = lax.broadcasted_iota(jnp.int32, (count, HD), 1)
    low, high = lane // 2, lane // 2 + HD // 2
    even = lane % 2 == 0
    acc = jnp.zeros((kinds * count, columns), jnp.float32)
    squares = jnp.zeros((count, HD), jnp.float32)
    for offset, part in zip(offsets, parts):
        block = me ^ offset
        start = pl.multiple_of(block * (width // HD), width // HD)
        gain = gain_rows[pl.ds(start, width // HD)]
        values = rows_of(part)
        for i in range(width // HD):
            chunk = values[:, i * HD : (i + 1) * HD]
            squares += chunk * chunk
            chunk = chunk * gain[i : i + 1]
            halves = [
                jnp.take_along_axis(chunk, low, axis=1),
                jnp.take_along_axis(chunk, high, axis=1),
            ]
            spread = jnp.concatenate(
                [
                    jnp.concatenate([jnp.where(even, h, 0.0) for h in halves], axis=1),
                    jnp.concatenate([jnp.where(even, 0.0, h) for h in halves], axis=1),
                ],
                axis=0,
            ).astype(jnp.bfloat16)
            at = pl.multiple_of(block * (width * kinds) + i * HD * kinds, HD * kinds)
            acc += jnp.dot(
                spread, flat[pl.ds(at, HD * kinds), :], preferred_element_type=jnp.float32
            )
    base_out[...] = acc
    square_out[...] = jnp.broadcast_to(jnp.sum(squares, axis=1, keepdims=True), squares.shape)


def base_call(offsets, gain, weight, parts):
    steps, rows, _ = parts[0].shape
    kinds, columns = weight.shape[1:]
    return pl.pallas_call(
        functools.partial(base_kernel, offsets),
        out_shape=(
            pltpu.VMEM((kinds * steps * rows, columns), jnp.float32),
            pltpu.VMEM((steps * rows, HD), jnp.float32),
        ),
        in_specs=[VMEM] * (2 + len(parts)),
        out_specs=(VMEM, VMEM),
        scratch_shapes=[pltpu.VMEM(gain.shape, jnp.float32)],
        compiler_params=pltpu.CompilerParams(vmem_limit_bytes=8 << 20),
        cost_estimate=pl.CostEstimate(flops=4 * 134 << 20, bytes_accessed=9 << 20, transcendentals=0),
        name="base_projection",
    )(gain, weight, *parts)


def final_kernel(
    width,
    sources,
    base_ref,
    square_ref,
    inner_ref,
    up_ref,
    bias_ref,
    query_ref,
    acc_ref,
    top_ref,
    total_ref,
    cos_ref,
    sin_ref,
    keys_out,
    values_out,
    attended_out,
):
    steps, rows, query_width = query_ref.shape
    count = steps * rows
    blocks, kinds, rank_part, columns = up_ref.shape
    ranks = blocks * rank_part
    groups = columns // HD
    per_group = query_width // HD // groups
    row_scale = lax.rsqrt(square_ref[:, :1] * (1.0 / width) + norm_eps)
    inner = None
    for source in sources(lax.axis_index("wide")):
        part = inner_ref[source].astype(jnp.float32)
        inner = part if inner is None else inner + part
    high = inner.astype(jnp.bfloat16)
    low = (inner - high.astype(jnp.float32)).astype(jnp.bfloat16)
    bias = bias_ref[...].astype(jnp.float32)
    linear = []
    for kind in range(kinds):
        up = jnp.concatenate([up_ref[i, kind] for i in range(blocks)], axis=0)
        cols = slice(kind * ranks, (kind + 1) * ranks)
        lora = jnp.dot(high[:, cols], up, preferred_element_type=jnp.float32) + jnp.dot(
            low[:, cols], up, preferred_element_type=jnp.float32
        )
        base = base_ref[kind * count : (kind + 1) * count]
        linear.append((base + adapter_scale * lora) * row_scale + bias[kind : kind + 1])
    cosine, sine = cos_ref[...], sin_ref[...]
    size = count * per_group
    line = lax.broadcasted_iota(jnp.int32, (size, count), 0)
    other = lax.broadcasted_iota(jnp.int32, (size, count), 1)
    live = (line % rows == other % rows) & (other // rows <= line // rows % steps)
    for group in range(groups):
        at = slice(group * HD, (group + 1) * HD)
        key = linear[0][:, at]
        key = (key * cosine + pltpu.roll(key, HD // 2, 1) * sine).astype(jnp.bfloat16)
        value = linear[1][:, at].astype(jnp.bfloat16)
        for step in range(steps):
            keys_out[step, :, at] = key[step * rows : (step + 1) * rows]
            values_out[step, :, at] = value[step * rows : (step + 1) * rows]
        query = query_block(query_ref, group, per_group).astype(jnp.bfloat16)
        scores = lax.dot_general(
            query, key, (((1,), (1,)), ((), ())), preferred_element_type=jnp.float32
        )
        scores = jnp.where(live, scores * score_scale, masked_score)
        old_top = top_ref[group][:, :1]
        top = jnp.maximum(old_top, jnp.max(scores, axis=1, keepdims=True))
        exps = jnp.exp(scores - top)
        keep = jnp.exp(old_top - top)
        total = total_ref[group][:, :1] * keep + jnp.sum(exps, axis=1, keepdims=True)
        acc = acc_ref[group] * keep + jnp.dot(
            exps.astype(jnp.bfloat16), value, preferred_element_type=jnp.float32
        )
        attended = (acc / total).astype(jnp.bfloat16)
        for head in range(per_group):
            lanes = pl.ds((group * per_group + head) * HD, HD)
            for step in range(steps):
                tile = (head * steps + step) * rows
                attended_out[step, :, lanes] = attended[tile : tile + rows]


def final_call(width, sources, base, square, inner, up, bias, queries, cached):
    steps, rows, query_width = queries.shape
    columns = up.shape[3]
    small = jax.ShapeDtypeStruct((steps, rows, columns), jnp.bfloat16)
    return pl.pallas_call(
        functools.partial(final_kernel, width, sources),
        out_shape=(small, small, jax.ShapeDtypeStruct(queries.shape, jnp.bfloat16)),
        in_specs=[VMEM] * (6 + len(cached)),
        out_specs=(VMEM,) * 3,
        compiler_params=pltpu.CompilerParams(vmem_limit_bytes=8 << 20),
        name="fresh_attention",
    )(base, square, inner, up, bias, queries, *cached)


def swap(block, offset, count):
    return lax.ppermute(block, "tp", [(i, i ^ offset) for i in range(count)])


def meeting_core(wide_index, tp_index):
    return 2 * ((tp_index // 2) ^ ((wide_index + tp_index) & 1)) + wide_index // 2


def on_device(
    wide_count,
    tp_count,
    hidden,
    input_norm_gain,
    key_value_weight,
    key_value_bias,
    adapter_down_factor,
    adapter_up_factor,
    queries,
    stored_rotated_keys,
    stored_value_rows,
    lengths,
):
    steps, rows, part_width = hidden.shape
    width = part_width * tp_count
    kinds, ranks, down_width = adapter_down_factor.shape
    gain = input_norm_gain.reshape(width // HD, HD)
    up_part = jnp.transpose(adapter_up_factor, (0, 2, 1))
    both = ("wide", "tp")

    direct = wide_count == 4 and tp_count == 4
    if direct:
        there = [(w * 4 + t, t * 4 + meeting_core(w, t)) for w in range(4) for t in range(4)]
        moved = lax.ppermute(hidden, both, there)
    crossed = swap(hidden, 2, tp_count)
    beside = swap(hidden, 1, tp_count)
    weight, *cached = cache_call(
        lengths, queries, stored_rotated_keys, stored_value_rows, key_value_weight
    )
    relayed = swap(crossed, 1, tp_count)
    if direct:
        inner = inner_call(16, moved, gain, adapter_down_factor)
        inner = lax.all_to_all(inner, both, 0, 0)
        up = lax.all_to_all(jnp.broadcast_to(up_part[None], (4,) + up_part.shape), "wide", 0, 0)

        def sources(wide_index):
            return [f * 4 + 2 * ((f // 2) ^ ((wide_index + f) & 1)) + wide_index // 2 for f in range(4)]

    else:
        gathered = lax.all_gather(hidden, "tp", axis=2, tiled=True).astype(jnp.float32)
        scaled = (gathered * input_norm_gain.astype(jnp.float32)).astype(jnp.bfloat16)
        down = lax.all_gather(adapter_down_factor, "wide", axis=2, tiled=True)
        inner = jnp.einsum("srd,kad->srka", scaled, down, preferred_element_type=jnp.float32)
        inner = inner.reshape(1, steps * rows, kinds * ranks)
        up = lax.all_gather(up_part, "wide", axis=1, tiled=True)[None]

        def sources(wide_index):
            return [0]

    base, square = base_call(
        (0, 1, 2, 3), gain, weight, (hidden, beside, crossed, relayed)
    )
    return final_call(width, sources, base, square, inner, up, key_value_bias, queries, cached)


def solution(mesh):
    in_specs = (
        P(None, ("groups", "wide"), "tp"),
        P(),
        P(None, None, "tp"),
        P(None, "tp"),
        P("groups", None, "wide"),
        P("groups", "tp", "wide"),
        P(None, ("groups", "wide"), "tp"),
        P(("groups", "wide"), None, "tp"),
        P(("groups", "wide"), None, "tp"),
        P(("groups", "wide")),
    )
    out_specs = (
        P(None, ("groups", "wide"), "tp"),
        P(None, ("groups", "wide"), "tp"),
        P(None, ("groups", "wide"), "tp"),
    )
    body = functools.partial(on_device, mesh.shape["wide"], mesh.shape["tp"])
    return jax.shard_map(
        body, mesh=mesh, in_specs=in_specs, out_specs=out_specs, check_vma=False
    )
```

time: 80 us -> 42.8 us (0.53)
  blocking collectives: 22.4 us -> 0 us
  starting transfers between devices: 0.04 us -> 17 us
  waiting for transfers between devices: 17.2 us -> 1.01 us
  matrix products: 14.5 us -> 0 us
  between operations: 14.2 us -> 0.73 us
  Pallas kernels: 0 us -> 12.3 us
  other arithmetic: 2.66 us -> 0 us
  local copies, waits for them, and re-layouts: 8.59 us -> 11.2 us
    all_gather x2 -> x0, blocking collectives: 22.4 us -> none  [the longest x1 15.2 us: on_device(): lax.all_gather(adapter_up_factor, 'wide', axis=2, tiled=True)]
    all_gather x1 -> x0, waiting for transfers between devices: 16.6 us -> none  [on_device(): lax.all_gather(adapter_down_factor, 'wide', axis=2, tiled=True)]
    dot_general x7 -> x0, matrix products: 14.5 us -> none  [the longest x1 6.4 us: on_device(): jnp.einsum('kca,kad->dkc', rank_full, down_full, preferred_element_type=j...]
    all_to_all x0 -> x2, starting transfers between devices: none -> 12.8 us  [the longest x1 7.26 us: on_device(): lax.all_to_all(jnp.broadcast_to(up_part[None], (4,) + up_part.shape), 'wi...]
    pallas_call x0 -> x4, Pallas kernels: none -> 12.3 us  [the longest x1 6.58 us: cache_call(): pl.pallas_call(cache_kernel, out_shape=(pltpu.VMEM(weight.shape, weight.d...]
    unnamed x10 -> x22, local copies, waits for them, and re-layouts: 0.03 us -> 9.9 us
    reshape x3 -> x0, local copies, waits for them, and re-layouts: 7.24 us -> none  [the longest x1 3.98 us: attend(): stored_rotated_keys.reshape(row_count, cache_span, group_count, HD)]
    ppermute x0 -> x4, starting transfers between devices: none -> 4.25 us  [the longest x3 2.55 us: swap(): return lax.ppermute(block, 'tp', [(i, i ^ offset) for i in range(count)])]
  transfers between devices with their start and end apart: 1 -> 6, of which waited for: 1 -> 1; matrix products, arithmetic and copies ran while one was open for 15% -> 3% of each run, Pallas kernels for 0% -> 26%
where the time goes in v2:
time: 42.8 us; the launch traced here: 42.2 us
  starting transfers between devices  17 us (40%)
  Pallas kernels  12.3 us (29%)
  local copies, waits for them, and re-layouts  11.2 us (26%)
  waiting for transfers between devices  1.01 us (2%)
  between operations  0.73 us (2%)
    unnamed x22, local copies, waits for them, and re-layouts  9.9 us
    all_to_all x1, starting transfers between devices, on_device(): lax.all_to_all(jnp.broadcast_to(up_part[None], (4,) + up_part.shape), 'wi...  7.26 us
    pallas_call x1, Pallas kernels, cache_call(): pl.pallas_call(cache_kernel, out_shape=(pltpu.VMEM(weight.shape, weight.d...  6.58 us
    all_to_all x1, starting transfers between devices, on_device(): inner = lax.all_to_all(inner, both, 0, 0)  5.5 us
    pallas_call x1, Pallas kernels, base_call(): pl.pallas_call(functools.partial(base_kernel, offsets), out_shape=(pltpu....  3.19 us
    ppermute x3, starting transfers between devices, swap(): return lax.ppermute(block, 'tp', [(i, i ^ offset) for i in range(count)])  2.55 us
    ppermute x1, starting transfers between devices, on_device(): moved = lax.ppermute(hidden, both, there)  1.7 us
    pallas_call x1, Pallas kernels, final_call(): pl.pallas_call(functools.partial(final_kernel, width, sources), out_shape...  1.48 us
  transfers between devices with their start and end apart: 6, of which 1 were waited for; matrix products, arithmetic and copies ran while one was open for 3% of the time, Pallas kernels for 26%

profile of v2, /device:TPU:0, one launch (start us, length us, event | category | flops | bytes accessed | tf_op | source)
XLA Modules:
  0.0 42.2 jit_solution(7685617119865054985)
XLA Ops:
  0.6 0.0 copy-start.6
  0.6 0.0 copy-start.8
  0.7 1.7 %collective-permute-start.3 = (bf16[4,8,2048]{2,1,0:T(8,128)(2,1)}, bf16[4,8,2048]{2,1,0:T(8,128)(2,1)S(1)}, u32[]{:S(2)}, u32[]{:S(2)}) collective-permute-start(bf16[4,8,2048]{2,1,0:T(8,128)(2,1)} %rest_0_.1), channel_id=1, source_target_pairs={{0,0},{1,6},{2,10},{3,12},{4,2},{5,4},{6,8},{7,14},{8,1},{9,7},{10... | collective-permute-start | bytes 393224 | tf_op jit(solution)/shard_map/ppermute | solution.py:382
  2.4 1.3 %broadcast_in_dim.2 = bf16[4,2,16,256]{3,2,1,0:T(8,128)(2,1)} broadcast(bf16[2,16,256]{2,1,0:T(8,128)(2,1)} %bitcast.4), dimensions={1,2,3} | broadcast | bytes 81920 | tf_op jit(solution)/shard_map/broadcast_in_dim | solution.py:392
  3.7 7.3 %all-to-all-start.1 = ((bf16[4,2,16,256]{3,2,1,0:T(8,128)(2,1)}), bf16[4,2,16,256]{3,2,1,0:T(8,128)(2,1)S(1)}, u32[]{:S(2)}, u32[]{:S(2)}) async-start(bf16[4,2,16,256]{3,2,1,0:T(8,128)(2,1)} %broadcast_in_dim.2), calls=%async_computation.1 | async-start | bytes 131072 | tf_op jit(solution)/shard_map/all_to_all | solution.py:392
  10.9 2.0 %collective-permute-start.1 = (bf16[4,8,2048]{2,1,0:T(8,128)(2,1)}, bf16[4,8,2048]{2,1,0:T(8,128)(2,1)S(1)}, u32[]{:S(2)}, u32[]{:S(2)}) collective-permute-start(bf16[4,8,2048]{2,1,0:T(8,128)(2,1)} %rest_0_.1), channel_id=1, source_target_pairs={{0,2},{1,3},{2,0},{3,1},{4,6},{5,7},{6,4},{7,5},{8,10},{9,11},{10,... | collective-permute-start | bytes 393224 | tf_op jit(solution)/shard_map/ppermute | solution.py:351
  12.9 0.0 collective-permute-done.3.hidden_ref
  12.9 0.0 copy-start.5
  12.9 1.0 %copy-done.5 = bf16[2,64,2048]{2,1,0:T(8,128)(2,1)S(1)} copy-done((bf16[2,64,2048]{2,1,0:T(8,128)(2,1)S(1)}, bf16[2,64,2048]{2,1,0:T(8,128)(2,1)}, u32[]{:S(2)}) %copy-start.5) | copy-done | bytes 524312
  14.0 0.0 copy-start.7
  14.0 0.7 %copy-done.7 = bf16[8192]{0:T(1024)(128)(2,1)S(1)} copy-done((bf16[8192]{0:T(1024)(128)(2,1)S(1)}, bf16[8192]{0:T(1024)(128)(2,1)}, u32[]{:S(2)}) %copy-start.7) | copy-done | bytes 16408
  14.7 1.0 %rank_inner.1 = bf16[16,32,128]{2,1,0:T(8,128)(2,1)} custom-call(bf16[4,8,2048]{2,1,0:T(8,128)(2,1)S(1)} %collective-permute-done.3.hidden_ref, bf16[64,128]{1,0:T(8,128)(2,1)S(1)} %bitcast.2, bf16[2,64,2048]{2,1,0:T(8,128)(2,1)S(1)} %copy-done.5), custom_call_target="tpu_custom_call" | custom-call | tf_op jit(solution)/shard_map/rank_inner/pallas_call | solution.py:190
  15.7 1.0 %all-to-all-done.1.up_ref = bf16[4,2,16,256]{3,2,1,0:T(8,128)(2,1)S(1)} async-done(((bf16[4,2,16,256]{3,2,1,0:T(8,128)(2,1)}), bf16[4,2,16,256]{3,2,1,0:T(8,128)(2,1)S(1)}, u32[]{:S(2)}, u32[]{:S(2)}) %all-to-all-start.1) | async-done | bytes 65568 | tf_op jit(solution)/shard_map/all_to_all | solution.py:392
  16.7 0.0 copy-start.4
  16.7 0.0 copy-start.9
  16.7 5.5 %all-to-all-start = ((bf16[16,32,128]{2,1,0:T(8,128)(2,1)}), bf16[16,32,128]{2,1,0:T(8,128)(2,1)S(1)}, u32[]{:S(2)}, u32[]{:S(2)}) async-start(bf16[16,32,128]{2,1,0:T(8,128)(2,1)} %rank_inner.1), calls=%async_computation | async-start | bytes 262144 | tf_op jit(solution)/shard_map/all_to_all | solution.py:391
  22.2 0.4 collective-permute-start
  22.6 0.0 collective-permute-done.1.rest_2_
  22.6 0.2 collective-permute-start.2
  22.8 0.0 copy-start
  22.8 3.4 %copy-done = bf16[8192,2,256]{2,1,0:T(2,128)(2,1)S(1)} copy-done((bf16[8192,2,256]{2,1,0:T(2,128)(2,1)S(1)}, bf16[8192,2,256]{2,1,0:T(2,128)(2,1)}, u32[]{:S(2)}) %copy-start) | copy-done | bytes 8388632
  26.2 0.0 copy-start.1
  26.2 1.6 %copy-done.1 = bf16[8,512,256]{2,1,0:T(8,128)(2,1)S(1)} copy-done((bf16[8,512,256]{2,1,0:T(8,128)(2,1)S(1)}, bf16[8,512,256]{2,1,0:T(8,128)(2,1)}, u32[]{:S(2)}) %copy-start.1) | copy-done | bytes 2097176
  27.8 0.0 copy-start.2
  27.8 1.6 %copy-done.2 = bf16[8,512,256]{2,1,0:T(8,128)(2,1)S(1)} copy-done((bf16[8,512,256]{2,1,0:T(8,128)(2,1)S(1)}, bf16[8,512,256]{2,1,0:T(8,128)(2,1)}, u32[]{:S(2)}) %copy-start.2) | copy-done | bytes 2097176
  29.3 0.0 copy-start.3
  29.4 0.9 %copy-done.3 = bf16[4,8,2048]{2,1,0:T(8,128)(2,1)S(1)} copy-done((bf16[4,8,2048]{2,1,0:T(8,128)(2,1)S(1)}, bf16[4,8,2048]{2,1,0:T(8,128)(2,1)}, u32[]{:S(2)}) %copy-start.3) | copy-done | bytes 131096
  30.3 0.0 copy-start.10
  30.3 0.7 %copy-done.10 = s32[8]{0:T(128)S(1)} copy-done((s32[8]{0:T(128)S(1)}, s32[8]{0:T(128)}, u32[]{:S(2)}) %copy-start.10) | copy-done | bytes 56
  30.9 6.6 %cache_attention.1 = (bf16[8192,2,256]{2,1,0:T(2,128)(2,1)S(1)}, f32[2,256,128]{2,1,0:T(8,128)S(1)}, f32[2,256,128]{2,1,0:T(8,128)S(1)}, f32[2,256,128]{2,1,0:T(...) custom-call(s32[8]{0:T(128)S(1)} %copy-done.10, bf16[4,8,2048]{2,1,0:T(8,128)(2,1)S(1)} %copy-done.3, ...), custom_call_target="tpu_custom_call" | custom-call | flops 140509184 | bytes 13631488 | tf_op jit(solution)/shard_map/cache_attention/pallas_call | solution.py:131
  37.5 0.0 collective-permute-done.rest_1_
  37.5 0.0 collective-permute-done.2.rest_3_
  37.5 0.0 copy-done.6
  37.5 0.0 copy-done.8
  37.5 3.2 %base_projection.1 = (f32[64,256]{1,0:T(8,128)S(1)}, f32[32,128]{1,0:T(8,128)S(1)}) custom-call(bf16[64,128]{1,0:T(8,128)(2,1)S(1)} %bitcast.3, bf16[8192,2,256]{2,1,0:T(2,128)(2,1)S(1)} %get-tuple-element.11.weight_ref, bf16[4,8,2048]{2,1,0:T(8,128)(2,1)S(1)} %copy-done.6, bf16[4,8,2048]{2,1,0:T(8,128)(2,1)S(1)} %collective-permute-done.rest_1_, ...), custom_call_target="tpu_custom_call" | custom-call | flops 562036736 | bytes 9437184 | tf_op jit(solution)/shard_map/base_projection/pallas_call | solution.py:246
  40.7 0.0 all-to-all-done.inner_ref
  40.7 0.0 copy-done.4
  40.8 0.0 copy-done.9
  40.8 1.5 %fresh_attention.1 = (bf16[4,8,256]{2,1,0:T(8,128)(2,1)}, bf16[4,8,256]{2,1,0:T(8,128)(2,1)}, bf16[4,8,2048]{2,1,0:T(8,128)(2,1)}) custom-call(f32[64,256]{1,0:T(8,128)S(1)} %get-tuple-element.12.base_ref, f32[32,128]{1,0:T(8,128)S(1)} %get-tuple-element.13.square_ref, bf16[16,32,128]{2,1,0:T(8,128)(2,1)S(1)} %all-to-all-done.inner_ref, ...), custom_call_target="tpu_custom_call" | custom-call | tf_op jit(solution)/shard_map/fresh_attention/pallas_call | solution.py:340
Async XLA Ops:
  0.6 36.9 %copy-start.6 = (bf16[4,8,2048]{2,1,0:T(8,128)(2,1)S(1)}, bf16[4,8,2048]{2,1,0:T(8,128)(2,1)}, u32[]{:S(2)}) copy-start(bf16[4,8,2048]{2,1,0:T(8,128)(2,1)} %rest_0_.1) | copy-start | bytes 393220
  0.6 36.9 %copy-start.8 = (bf16[8192]{0:T(1024)(128)(2,1)S(1)}, bf16[8192]{0:T(1024)(128)(2,1)}, u32[]{:S(2)}) copy-start(bf16[8192]{0:T(1024)(128)(2,1)} %param.11) | copy-start | bytes 49156
  0.7 12.3 %collective-permute-start.3 = (bf16[4,8,2048]{2,1,0:T(8,128)(2,1)}, bf16[4,8,2048]{2,1,0:T(8,128)(2,1)S(1)}, u32[]{:S(2)}, u32[]{:S(2)}) collective-permute-start(bf16[4,8,2048]{2,1,0:T(8,128)(2,1)} %rest_0_.1), channel_id=1, source_target_pairs={{0,0},{1,6},{2,10},{3,12},{4,2},{5,4},{6,8},{7,14},{8,1},{9,7},{10... | collective-permute-start | bytes 393224 | tf_op jit(solution)/shard_map/ppermute | solution.py:382
  3.7 13.0 %all-to-all-start.1 = ((bf16[4,2,16,256]{3,2,1,0:T(8,128)(2,1)}), bf16[4,2,16,256]{3,2,1,0:T(8,128)(2,1)S(1)}, u32[]{:S(2)}, u32[]{:S(2)}) async-start(bf16[4,2,16,256]{3,2,1,0:T(8,128)(2,1)} %broadcast_in_dim.2), calls=%async_computation.1 | async-start | bytes 131072 | tf_op jit(solution)/shard_map/all_to_all | solution.py:392
  10.9 11.7 %collective-permute-start.1 = (bf16[4,8,2048]{2,1,0:T(8,128)(2,1)}, bf16[4,8,2048]{2,1,0:T(8,128)(2,1)S(1)}, u32[]{:S(2)}, u32[]{:S(2)}) collective-permute-start(bf16[4,8,2048]{2,1,0:T(8,128)(2,1)} %rest_0_.1), channel_id=1, source_target_pairs={{0,2},{1,3},{2,0},{3,1},{4,6},{5,7},{6,4},{7,5},{8,10},{9,11},{10,... | collective-permute-start | bytes 393224 | tf_op jit(solution)/shard_map/ppermute | solution.py:351
  12.9 1.0 %copy-start.5 = (bf16[2,64,2048]{2,1,0:T(8,128)(2,1)S(1)}, bf16[2,64,2048]{2,1,0:T(8,128)(2,1)}, u32[]{:S(2)}) copy-start(bf16[2,64,2048]{2,1,0:T(8,128)(2,1)} %down_ref.1) | copy-start | bytes 1572868
  14.0 0.7 %copy-start.7 = (bf16[8192]{0:T(1024)(128)(2,1)S(1)}, bf16[8192]{0:T(1024)(128)(2,1)}, u32[]{:S(2)}) copy-start(bf16[8192]{0:T(1024)(128)(2,1)} %param.11) | copy-start | bytes 49156
  16.7 24.1 %copy-start.4 = (bf16[4,8,2048]{2,1,0:T(8,128)(2,1)S(1)}, bf16[4,8,2048]{2,1,0:T(8,128)(2,1)}, u32[]{:S(2)}) copy-start(bf16[4,8,2048]{2,1,0:T(8,128)(2,1)} %query_ref.3) | copy-start | bytes 393220
  16.7 24.1 %copy-start.9 = (bf16[2,256]{1,0:T(2,128)(2,1)S(1)}, bf16[2,256]{1,0:T(2,128)(2,1)}, u32[]{:S(2)}) copy-start(bf16[2,256]{1,0:T(2,128)(2,1)} %bias_ref.1) | copy-start | bytes 3076
  16.7 24.0 %all-to-all-start = ((bf16[16,32,128]{2,1,0:T(8,128)(2,1)}), bf16[16,32,128]{2,1,0:T(8,128)(2,1)S(1)}, u32[]{:S(2)}, u32[]{:S(2)}) async-start(bf16[16,32,128]{2,1,0:T(8,128)(2,1)} %rank_inner.1), calls=%async_computation | async-start | bytes 262144 | tf_op jit(solution)/shard_map/all_to_all | solution.py:391
  22.2 15.3 %collective-permute-start = (bf16[4,8,2048]{2,1,0:T(8,128)(2,1)}, bf16[4,8,2048]{2,1,0:T(8,128)(2,1)S(1)}, u32[]{:S(2)}, u32[]{:S(2)}) collective-permute-start(bf16[4,8,2048]{2,1,0:T(8,128)(2,1)} %rest_0_.1), channel_id=1, source_target_pairs={{0,1},{1,0},{2,3},{3,2},{4,5},{5,4},{6,7},{7,6},{8,9},{9,8},{10,11... | collective-permute-start | bytes 393224 | tf_op jit(solution)/shard_map/ppermute | solution.py:351
  22.6 14.9 %collective-permute-start.2 = (bf16[4,8,2048]{2,1,0:T(8,128)(2,1)S(1)}, bf16[4,8,2048]{2,1,0:T(8,128)(2,1)S(1)}, u32[]{:S(2)}, u32[]{:S(2)}) collective-permute-start(bf16[4,8,2048]{2,1,0:T(8,128)(2,1)S(1)} %collective-permute-done.1.rest_2_), channel_id=1, source_target_pairs={{0,1},{1,0},{2,3},{3,2},{4,5},{5,4},{6,7},{7,6},{8,9},{9,8},{10,11... | collective-permute-start | bytes 393224 | tf_op jit(solution)/shard_map/ppermute | solution.py:351
  22.8 3.4 %copy-start = (bf16[8192,2,256]{2,1,0:T(2,128)(2,1)S(1)}, bf16[8192,2,256]{2,1,0:T(2,128)(2,1)}, u32[]{:S(2)}) copy-start(bf16[8192,2,256]{2,1,0:T(2,128)(2,1)} %weight_ref.1) | copy-start | bytes 25165828
  26.2 1.6 %copy-start.1 = (bf16[8,512,256]{2,1,0:T(8,128)(2,1)S(1)}, bf16[8,512,256]{2,1,0:T(8,128)(2,1)}, u32[]{:S(2)}) copy-start(bf16[8,512,256]{2,1,0:T(8,128)(2,1)} %key_ref.1) | copy-start | bytes 6291460
  27.8 1.6 %copy-start.2 = (bf16[8,512,256]{2,1,0:T(8,128)(2,1)S(1)}, bf16[8,512,256]{2,1,0:T(8,128)(2,1)}, u32[]{:S(2)}) copy-start(bf16[8,512,256]{2,1,0:T(8,128)(2,1)} %value_ref.1) | copy-start | bytes 6291460
  29.3 0.9 %copy-start.3 = (bf16[4,8,2048]{2,1,0:T(8,128)(2,1)S(1)}, bf16[4,8,2048]{2,1,0:T(8,128)(2,1)}, u32[]{:S(2)}) copy-start(bf16[4,8,2048]{2,1,0:T(8,128)(2,1)} %query_ref.3) | copy-start | bytes 393220
  30.3 0.7 %copy-start.10 = (s32[8]{0:T(128)S(1)}, s32[8]{0:T(128)}, u32[]{:S(2)}) copy-start(s32[8]{0:T(128)} %lengths_ref.1) | copy-start | bytes 100

commit v3 on v2

v3 whole, which is shorter than its diff:
```python
import functools
import math

import jax
import jax.numpy as jnp
from jax import lax
from jax.experimental import pallas as pl
from jax.experimental.pallas import tpu as pltpu
from jax.sharding import PartitionSpec as P

HD = 128


norm_eps = 1e-06
adapter_scale = 2.0
rope_base = 1000000.0
masked_score = -1e30
score_scale = 1.0 / math.sqrt(HD)

VMEM = pl.BlockSpec(memory_space=pltpu.VMEM)
HBM = pl.BlockSpec(memory_space=pltpu.HBM)


def query_block(query_ref, group, per_group):
    steps = query_ref.shape[0]
    tiles = []
    for head in range(per_group):
        at = (group * per_group + head) * HD
        for step in range(steps):
            tiles.append(query_ref[step, :, at : at + HD].astype(jnp.float32))
    return jnp.concatenate(tiles, axis=0)


def cache_kernel(
    lengths_ref,
    query_ref,
    key_ref,
    value_ref,
    weight_ref,
    down_ref,
    gain_ref,
    weight_out,
    down_out,
    gain_out,
    query_out,
    acc_out,
    top_out,
    total_out,
    cos_out,
    sin_out,
    lengths,
    queries,
    gain_buffer,
    key_buffer,
    value_buffer,
    small_sems,
    sems,
    weight_sems,
):
    steps, rows, query_width = query_ref.shape
    cache_span = key_ref.shape[1]
    groups = key_ref.shape[2] // HD
    per_group = query_width // HD // groups
    first = [
        pltpu.make_async_copy(lengths_ref, lengths, small_sems.at[0]),
        pltpu.make_async_copy(query_ref, queries, small_sems.at[1]),
    ]
    last = [
        pltpu.make_async_copy(gain_ref, gain_buffer, small_sems.at[2]),
        pltpu.make_async_copy(down_ref, down_out, small_sems.at[3]),
    ]
    copies = []
    for row in range(rows):
        copies.append(
            (
                pltpu.make_async_copy(key_ref.at[row], key_buffer.at[row], sems.at[0, row]),
                pltpu.make_async_copy(value_ref.at[row], value_buffer.at[row], sems.at[1, row]),
            )
        )
    pieces = weight_sems.shape[0]
    piece = weight_ref.shape[0] // pieces
    for i in range(pieces):
        at = pl.ds(i * piece, piece)
        last.append(
            pltpu.make_async_copy(weight_ref.at[at], weight_out.at[at], weight_sems.at[i])
        )
    for copy in first:
        copy.start()
    for pair in copies:
        for copy in pair:
            copy.start()
    for copy in last:
        copy.start()

    first[0].wait()
    lane = lax.broadcasted_iota(jnp.int32, (rows, HD), 1)
    half = HD // 2
    second = lane >= half
    index = jnp.where(second, lane - half, lane).astype(jnp.float32)
    inv_freq = jnp.exp(index * (-2.0 * math.log(rope_base) / HD))
    row_index = lax.broadcasted_iota(jnp.int32, (rows, HD), 0)
    row_lengths = jnp.zeros((rows, HD), jnp.int32)
    for row in range(rows):
        row_lengths = jnp.where(row_index == row, lengths[row], row_lengths)
    for step in range(steps):
        angles = (row_lengths + step).astype(jnp.float32) * inv_freq
        sine = jnp.sin(angles)
        cos_out[pl.ds(step * rows, rows)] = jnp.cos(angles)
        sin_out[pl.ds(step * rows, rows)] = jnp.where(second, sine, -sine)
    first[1].wait()
    for group in range(groups):
        query_out[group] = query_block(queries, group, per_group)

    place = lax.broadcasted_iota(jnp.int32, (steps * per_group, cache_span), 1)
    for row in range(rows):
        for copy in copies[row]:
            copy.wait()
        live = place < lengths[row]
        for group in range(groups):
            at = pl.ds(group * HD, HD)
            mine = pl.ds(row, steps * per_group, stride=rows)
            query = query_out[group, mine, :].astype(jnp.bfloat16)
            scores = lax.dot_general(
                query,
                key_buffer[row, :, at],
                (((1,), (1,)), ((), ())),
                preferred_element_type=jnp.float32,
            )
            scores = jnp.where(live, scores * score_scale, masked_score)
            top = jnp.max(scores, axis=1, keepdims=True)
            exps = jnp.exp(scores - top)
            total = jnp.sum(exps, axis=1, keepdims=True)
            acc = jnp.dot(
                exps.astype(jnp.bfloat16),
                value_buffer[row, :, at],
                preferred_element_type=jnp.float32,
            )
            acc_out[group, mine, :] = acc
            top_out[group, mine, :] = jnp.broadcast_to(top, acc.shape)
            total_out[group, mine, :] = jnp.broadcast_to(total, acc.shape)
    last[0].wait()
    gain_out[...] = gain_buffer[...].astype(jnp.float32)
    for copy in last[1:]:
        copy.wait()


def cache_call(lengths, queries, keys, values, weight, down, gain):
    steps, rows, query_width = queries.shape
    cache_span, key_width = keys.shape[1:]
    groups = key_width // HD
    block = (groups, steps * rows * (query_width // key_width), HD)
    table = (steps * rows, HD)
    pieces = 4
    return pl.pallas_call(
        cache_kernel,
        out_shape=(
            pltpu.VMEM(weight.shape, weight.dtype),
            pltpu.VMEM(down.shape, down.dtype),
            pltpu.VMEM(gain.shape, jnp.float32),
            pltpu.VMEM(block, jnp.float32),
            pltpu.VMEM(block, jnp.float32),
            pltpu.VMEM(block, jnp.float32),
            pltpu.VMEM(block, jnp.float32),
            pltpu.VMEM(table, jnp.float32),
            pltpu.VMEM(table, jnp.float32),
        ),
        in_specs=[HBM] * 7,
        out_specs=(VMEM,) * 9,
        scratch_shapes=[
            pltpu.SMEM(lengths.shape, jnp.int32),
            pltpu.VMEM(queries.shape, queries.dtype),
            pltpu.VMEM(gain.shape, gain.dtype),
            pltpu.VMEM(keys.shape, keys.dtype),
            pltpu.VMEM(values.shape, values.dtype),
            pltpu.SemaphoreType.DMA((4,)),
            pltpu.SemaphoreType.DMA((2, rows)),
            pltpu.SemaphoreType.DMA((pieces,)),
        ],
        compiler_params=pltpu.CompilerParams(vmem_limit_bytes=52 << 20),
        cost_estimate=pl.CostEstimate(flops=2 * 67 << 20, bytes_accessed=13 << 20, transcendentals=0),
        name="cache_attention",
    )(lengths, queries, keys, values, weight, down, gain)


def scaled_chunks(block, gain, start):
    chunks = []
    for i in range(block.shape[1] // HD):
        chunk = block[:, i * HD : (i + 1) * HD]
        chunks.append((chunk * gain[start + i : start + i + 1]).astype(jnp.bfloat16))
    return chunks


def rows_of(ref):
    steps = ref.shape[0]
    return jnp.concatenate([ref[s].astype(jnp.float32) for s in range(steps)], axis=0)


def inner_kernel(hidden_ref, gain_ref, down_ref, up_ref, beside_ref, out_ref, up_out):
    width = hidden_ref.shape[2]
    start = pl.multiple_of(lax.axis_index("wide") * (width // HD), width // HD)
    gain = gain_ref[pl.ds(start, width // HD)]
    scaled = jnp.concatenate(scaled_chunks(rows_of(hidden_ref), gain, 0), axis=1)
    ranks = down_ref.shape[1]
    for kind in range(down_ref.shape[0]):
        out_ref[:, kind * ranks : (kind + 1) * ranks] = lax.dot_general(
            scaled,
            down_ref[kind],
            (((1,), (1,)), ((), ())),
            preferred_element_type=jnp.float32,
        )
    up_out[0] = up_ref[...]
    up_out[1] = beside_ref[...]


def inner_call(hidden, gain, down, up_part, up_beside):
    steps, rows, _ = hidden.shape
    kinds, ranks, _ = down.shape
    return pl.pallas_call(
        inner_kernel,
        out_shape=(
            jax.ShapeDtypeStruct((steps * rows, kinds * ranks), jnp.float32),
            jax.ShapeDtypeStruct((2,) + up_part.shape, up_part.dtype),
        ),
        in_specs=[VMEM] * 5,
        out_specs=(VMEM, VMEM),
        compiler_params=pltpu.CompilerParams(vmem_limit_bytes=8 << 20),
        name="rank_inner",
    )(hidden, gain, down, up_part, up_beside)


def base_kernel(offsets, gain_ref, weight_ref, *rest):
    parts = rest[: len(offsets)]
    base_out, square_out = rest[len(offsets) :]
    steps, rows, width = parts[0].shape
    count = steps * rows
    kinds, columns = weight_ref.shape[1:]
    flat = weight_ref.reshape(weight_ref.shape[0] * kinds, columns)
    me = lax.axis_index("tp")
    lane = lax.broadcasted_iota(jnp.int32, (count, HD), 1)
    low, high = lane // 2, lane // 2 + HD // 2
    even = lane % 2 == 0
    acc = jnp.zeros((kinds * count, columns), jnp.float32)
    squares = jnp.zeros((count, HD), jnp.float32)
    for offset, part in zip(offsets, parts):
        block = me ^ offset
        start = pl.multiple_of(block * (width // HD), width // HD)
        gain = gain_ref[pl.ds(start, width // HD)]
        values = rows_of(part)
        for i in range(width // HD):
            chunk = values[:, i * HD : (i + 1) * HD]
            squares += chunk * chunk
            chunk = chunk * gain[i : i + 1]
            halves = [
                jnp.take_along_axis(chunk, low, axis=1),
                jnp.take_along_axis(chunk, high, axis=1),
            ]
            spread = jnp.concatenate(
                [
                    jnp.concatenate([jnp.where(even, h, 0.0) for h in halves], axis=1),
                    jnp.concatenate([jnp.where(even, 0.0, h) for h in halves], axis=1),
                ],
                axis=0,
            ).astype(jnp.bfloat16)
            at = pl.multiple_of(block * (width * kinds) + i * HD * kinds, HD * kinds)
            acc += jnp.dot(
                spread, flat[pl.ds(at, HD * kinds), :], preferred_element_type=jnp.float32
            )
    base_out[...] = acc
    square_out[...] = jnp.broadcast_to(jnp.sum(squares, axis=1, keepdims=True), squares.shape)


def base_call(offsets, gain, weight, parts):
    steps, rows, _ = parts[0].shape
    kinds, columns = weight.shape[1:]
    return pl.pallas_call(
        functools.partial(base_kernel, offsets),
        out_shape=(
            pltpu.VMEM((kinds * steps * rows, columns), jnp.float32),
            pltpu.VMEM((steps * rows, HD), jnp.float32),
        ),
        in_specs=[VMEM] * (2 + len(parts)),
        out_specs=(VMEM, VMEM),
        compiler_params=pltpu.CompilerParams(vmem_limit_bytes=8 << 20),
        cost_estimate=pl.CostEstimate(flops=4 * 134 << 20, bytes_accessed=9 << 20, transcendentals=0),
        name="base_projection",
    )(gain, weight, *parts)


def final_kernel(width, inner_count, up_count, base_ref, square_ref, bias_ref, *rest):
    query_ref, acc_ref, top_ref, total_ref, cos_ref, sin_ref = rest[:6]
    inner_refs = rest[6 : 6 + inner_count]
    up_refs = rest[6 + inner_count : 6 + inner_count + up_count]
    keys_out, values_out, attended_out = rest[6 + inner_count + up_count :]
    steps, rows, columns = keys_out.shape
    count = steps * rows
    groups, size, _ = query_ref.shape
    per_group = size // count
    kinds = bias_ref.shape[0]
    row_scale = lax.rsqrt(square_ref[:, :1] * (1.0 / width) + norm_eps)
    inner = inner_refs[0][...]
    for ref in inner_refs[1:]:
        inner = inner + ref[...]
    high = inner.astype(jnp.bfloat16)
    low = (inner - high.astype(jnp.float32)).astype(jnp.bfloat16)
    ranks = inner.shape[1] // kinds
    bias = bias_ref[...].astype(jnp.float32)
    linear = []
    for kind in range(kinds):
        if up_count == 1:
            up = up_refs[0][0, kind]
        else:
            me = lax.axis_index("wide")
            pieces = []
            for i in range(4):
                at = (me ^ i) & 1
                near = up_refs[0][at, kind].astype(jnp.float32)
                far = up_refs[1][at, kind].astype(jnp.float32)
                pieces.append(jnp.where(me // 2 == i // 2, near, far))
            up = jnp.concatenate(pieces, axis=0).astype(jnp.bfloat16)
        cols = slice(kind * ranks, (kind + 1) * ranks)
        lora = jnp.dot(high[:, cols], up, preferred_element_type=jnp.float32) + jnp.dot(
            low[:, cols], up, preferred_element_type=jnp.float32
        )
        base = base_ref[kind * count : (kind + 1) * count]
        linear.append((base + adapter_scale * lora) * row_scale + bias[kind : kind + 1])
    cosine, sine = cos_ref[...], sin_ref[...]
    line = lax.broadcasted_iota(jnp.int32, (size, count), 0)
    other = lax.broadcasted_iota(jnp.int32, (size, count), 1)
    live = (line % rows == other % rows) & (other // rows <= line // rows % steps)
    for group in range(groups):
        at = slice(group * HD, (group + 1) * HD)
        key = linear[0][:, at]
        key = (key * cosine + pltpu.roll(key, HD // 2, 1) * sine).astype(jnp.bfloat16)
        value = linear[1][:, at].astype(jnp.bfloat16)
        for step in range(steps):
            keys_out[step, :, at] = key[step * rows : (step + 1) * rows]
            values_out[step, :, at] = value[step * rows : (step + 1) * rows]
        scores = lax.dot_general(
            query_ref[group].astype(jnp.bfloat16),
            key,
            (((1,), (1,)), ((), ())),
            preferred_element_type=jnp.float32,
        )
        scores = jnp.where(live, scores * score_scale, masked_score)
        old_top = top_ref[group][:, :1]
        top = jnp.maximum(old_top, jnp.max(scores, axis=1, keepdims=True))
        exps = jnp.exp(scores - top)
        keep = jnp.exp(old_top - top)
        total = total_ref[group][:, :1] * keep + jnp.sum(exps, axis=1, keepdims=True)
        acc = acc_ref[group] * keep + jnp.dot(
            exps.astype(jnp.bfloat16), value, preferred_element_type=jnp.float32
        )
        attended = (acc / total).astype(jnp.bfloat16)
        for head in range(per_group):
            lanes = pl.ds((group * per_group + head) * HD, HD)
            for step in range(steps):
                tile = (head * steps + step) * rows
                attended_out[step, :, lanes] = attended[tile : tile + rows]


def final_call(shape, width, base, square, bias, cached, inner, up):
    steps, rows, query_width = shape
    small = jax.ShapeDtypeStruct((steps, rows, base.shape[1]), jnp.bfloat16)
    return pl.pallas_call(
        functools.partial(final_kernel, width, len(inner), len(up)),
        out_shape=(small, small, jax.ShapeDtypeStruct(shape, jnp.bfloat16)),
        in_specs=[VMEM] * (3 + len(cached) + len(inner) + len(up)),
        out_specs=(VMEM,) * 3,
        compiler_params=pltpu.CompilerParams(vmem_limit_bytes=8 << 20),
        name="fresh_attention",
    )(base, square, bias, *cached, *inner, *up)


def swap(block, axis, offset, count):
    return lax.ppermute(block, axis, [(i, i ^ offset) for i in range(count)])


def meeting_place():
    pairs = []
    for w in range(4):
        for t in range(4):
            pairs.append((w * 4 + t, t * 4 + 2 * ((t // 2) ^ ((w + t) & 1)) + w // 2))
    return pairs


def on_device(
    wide_count,
    tp_count,
    hidden,
    input_norm_gain,
    key_value_weight,
    key_value_bias,
    adapter_down_factor,
    adapter_up_factor,
    queries,
    stored_rotated_keys,
    stored_value_rows,
    lengths,
):
    steps, rows, part_width = hidden.shape
    width = part_width * tp_count
    kinds, ranks, down_width = adapter_down_factor.shape
    gain = input_norm_gain.reshape(width // HD, HD)
    up_part = jnp.transpose(adapter_up_factor, (0, 2, 1))
    both = ("wide", "tp")

    direct = wide_count == 4 and tp_count == 4
    if direct:
        there = meeting_place()
        moved = lax.ppermute(hidden, both, there)
        up_beside = swap(up_part, "wide", 1, 4)
    crossed = swap(hidden, "tp", 2, tp_count)
    beside = swap(hidden, "tp", 1, tp_count)
    weight, down, gain_rows, *cached = cache_call(
        lengths,
        queries,
        stored_rotated_keys,
        stored_value_rows,
        key_value_weight,
        adapter_down_factor,
        gain,
    )
    relayed, gain_rows = lax.optimization_barrier((crossed, gain_rows))
    relayed = swap(relayed, "tp", 1, tp_count)
    if direct:
        inner, up_pair = inner_call(moved, gain_rows, down, up_part, up_beside)
        inner = lax.ppermute(inner, both, [(b, a) for a, b in there])
        up = [up_pair, swap(up_pair, "wide", 2, 4)]
    else:
        gathered = lax.all_gather(hidden, "tp", axis=2, tiled=True).astype(jnp.float32)
        scaled = (gathered * input_norm_gain.astype(jnp.float32)).astype(jnp.bfloat16)
        all_down = lax.all_gather(adapter_down_factor, "wide", axis=2, tiled=True)
        inner = jnp.einsum("srd,kad->srka", scaled, all_down, preferred_element_type=jnp.float32)
        inner = [inner.reshape(steps * rows, kinds * ranks)]
        up = [lax.all_gather(up_part, "wide", axis=1, tiled=True)[None]]

    base, square = base_call(
        (0, 1, 2, 3), gain_rows, weight, (hidden, beside, crossed, relayed)
    )
    if direct:
        inner, square = lax.optimization_barrier((inner, square))
        inner = [inner] + [swap(inner, "tp", offset, 4) for offset in (2, 3, 1)]
    return final_call(queries.shape, width, base, square, key_value_bias, cached, inner, up)


def solution(mesh):
    in_specs = (
        P(None, ("groups", "wide"), "tp"),
        P(),
        P(None, None, "tp"),
        P(None, "tp"),
        P("groups", None, "wide"),
        P("groups", "tp", "wide"),
        P(None, ("groups", "wide"), "tp"),
        P(("groups", "wide"), None, "tp"),
        P(("groups", "wide"), None, "tp"),
        P(("groups", "wide")),
    )
    out_specs = (
        P(None, ("groups", "wide"), "tp"),
        P(None, ("groups", "wide"), "tp"),
        P(None, ("groups", "wide"), "tp"),
    )
    body = functools.partial(on_device, mesh.shape["wide"], mesh.shape["tp"])
    return jax.shard_map(
        body, mesh=mesh, in_specs=in_specs, out_specs=out_specs, check_vma=False
    )
```

time: 42.8 us -> 36.3 us (0.85)
  local copies, waits for them, and re-layouts: 11.2 us -> 0.01 us
  waiting for transfers between devices: 1.01 us -> 7.01 us
  starting transfers between devices: 17 us -> 15.7 us
    all_to_all x2 -> x0, starting transfers between devices: 12.8 us -> none  [the longest x1 7.26 us: on_device(): lax.all_to_all(jnp.broadcast_to(up_part[None], (4,) + up_part.shape), 'wi...]
    ppermute x3 -> x9, starting transfers between devices: 2.55 us -> 14.2 us  [the longest x8 13.5 us: swap(): return lax.ppermute(block, axis, [(i, i ^ offset) for i in range(count)])]
    unnamed x22 -> x6, local copies, waits for them, and re-layouts: 9.9 us -> 0.01 us
    ppermute x3 -> x9, waiting for transfers between devices: 0.01 us -> 7.01 us  [the longest x8 7.01 us: swap(): return lax.ppermute(block, axis, [(i, i ^ offset) for i in range(count)])]
    broadcast_in_dim x1 -> x0, local copies, waits for them, and re-layouts: 1.33 us -> none  [on_device(): jnp.broadcast_to(up_part[None], (4,) + up_part.shape)]
    pallas_call x1, Pallas kernels: 6.58 us -> 7.7 us  [cache_call(): pl.pallas_call(cache_kernel, out_shape=(pltpu.VMEM(weight.shape, weight.d...]
    all_to_all x2 -> x0, waiting for transfers between devices: 1 us -> none  [the longest x1 0.99 us: on_device(): lax.all_to_all(jnp.broadcast_to(up_part[None], (4,) + up_part.shape), 'wi...]
    pallas_call x2, Pallas kernels: 2.49 us -> 1.8 us  [the longest x1 1.48 us: final_call(): pl.pallas_call(functools.partial(final_kernel, width, len(inner), len(up)...]
  transfers between devices with their start and end apart: 6 -> 10, of which waited for: 1 -> 3; matrix products, arithmetic and copies ran while one was open for 3% -> 0% of each run, Pallas kernels for 26% -> 31%
where the time goes in v3:
time: 36.3 us; the launch traced here: 36.1 us
  starting transfers between devices  15.7 us (43%)
  Pallas kernels  12.7 us (35%)
  waiting for transfers between devices  7.01 us (19%)
  between operations  0.7 us (2%)
    ppermute x8, starting transfers between devices, swap(): return lax.ppermute(block, axis, [(i, i ^ offset) for i in range(count)])  13.5 us
    pallas_call x1, Pallas kernels, cache_call(): pl.pallas_call(cache_kernel, out_shape=(pltpu.VMEM(weight.shape, weight.d...  7.7 us
    ppermute x8, waiting for transfers between devices, swap(): return lax.ppermute(block, axis, [(i, i ^ offset) for i in range(count)])  7.01 us
    pallas_call x1, Pallas kernels, base_call(): pl.pallas_call(functools.partial(base_kernel, offsets), out_shape=(pltpu....  3.16 us
    ppermute x1, starting transfers between devices, on_device(): moved = lax.ppermute(hidden, both, there)  1.55 us
    pallas_call x1, Pallas kernels, final_call(): pl.pallas_call(functools.partial(final_kernel, width, len(inner), len(up)...  1.48 us
  transfers between devices with their start and end apart: 10, of which 3 were waited for; matrix products, arithmetic and copies ran while one was open for 0% of the time, Pallas kernels for 31%

profile of v3, /device:TPU:0, one launch (start us, length us, event | category | flops | bytes accessed | tf_op | source)
XLA Modules:
  0.0 36.1 jit_solution(14202819411795074867)
XLA Ops:
  0.6 0.0 copy-start
  0.6 0.0 copy-start.1
  0.7 3.0 %collective-permute-start = (bf16[4,8,2048]{2,1,0:T(8,128)(2,1)}, bf16[4,8,2048]{2,1,0:T(8,128)(2,1)S(1)}, u32[]{:S(2)}, u32[]{:S(2)}) collective-permute-start(bf16[4,8,2048]{2,1,0:T(8,128)(2,1)} %rest_0_.1), channel_id=1, source_target_pairs={{0,2},{1,3},{2,0},{3,1},{4,6},{5,7},{6,4},{7,5},{8,10},{9,11},{10,... | collective-permute-start | bytes 393224 | tf_op jit(solution)/shard_map/ppermute | solution.py:375
  3.7 0.0 collective-permute-start.1
  3.7 1.6 %collective-permute-start.3 = (bf16[4,8,2048]{2,1,0:T(8,128)(2,1)}, bf16[4,8,2048]{2,1,0:T(8,128)(2,1)S(1)}, u32[]{:S(2)}, u32[]{:S(2)}) collective-permute-start(bf16[4,8,2048]{2,1,0:T(8,128)(2,1)} %rest_0_.1), channel_id=1, source_target_pairs={{0,0},{1,6},{2,10},{3,12},{4,2},{5,4},{6,8},{7,14},{8,1},{9,7},{10... | collective-permute-start | bytes 393224 | tf_op jit(solution)/shard_map/ppermute | solution.py:410
  5.2 0.0 copy-start.2
  5.2 7.7 %cache_attention.1 = (bf16[8192,2,256]{2,1,0:T(2,128)(2,1)S(1)}, bf16[2,64,2048]{2,1,0:T(8,128)(2,1)S(1)}, f32[64,128]{1,0:T(8,128)S(1)}, f32[2,256,128]{2,1,0:T...) custom-call(s32[8]{0:T(128)} %lengths_ref.1, ...), custom_call_target="tpu_custom_call" | custom-call | flops 140509184 | bytes 13631488 | tf_op jit(solution)/shard_map/cache_attention/pallas_call | solution.py:154
  12.9 0.0 collective-permute-done.rest_2_
  12.9 2.1 %collective-permute-start.2 = (bf16[4,8,2048]{2,1,0:T(8,128)(2,1)S(1)}, bf16[4,8,2048]{2,1,0:T(8,128)(2,1)S(1)}, u32[]{:S(2)}, u32[]{:S(2)}) collective-permute-start(bf16[4,8,2048]{2,1,0:T(8,128)(2,1)S(1)} %collective-permute-done.rest_2_), channel_id=1, source_target_pairs={{0,1},{1,0},{2,3},{3,2},{4,5},{5,4},{6,7},{7,6},{8,9},{9,8},{10,11... | collective-permute-start | bytes 393224 | tf_op jit(solution)/shard_map/ppermute | solution.py:375
  15.0 0.0 copy-done.1
  15.0 0.4 %collective-permute-start.4 = (bf16[2,16,256]{2,1,0:T(8,128)(2,1)S(1)}, bf16[2,16,256]{2,1,0:T(8,128)(2,1)S(1)}, u32[]{:S(2)}, u32[]{:S(2)}) collective-permute-start(bf16[2,16,256]{2,1,0:T(8,128)(2,1)S(1)} %bitcast.2), channel_id=1, source_target_pairs={{0,4},{4,0},{8,12},{12,8},{1,5},{5,1},{9,13},{13,9},{2,6},{6,2},{1... | collective-permute-start | bytes 49160 | tf_op jit(solution)/shard_map/ppermute | solution.py:375
  15.5 3.3 %collective-permute-done.4.beside_ref = bf16[2,16,256]{2,1,0:T(8,128)(2,1)S(1)} collective-permute-done((bf16[2,16,256]{2,1,0:T(8,128)(2,1)S(1)}, bf16[2,16,256]{2,1,0:T(8,128)(2,1)S(1)}, u32[]{:S(2)}, u32[]{:S(2)}) %collective-permute-start.4) | collective-permute-done | bytes 16416 | tf_op jit(solution)/shard_map/ppermute | solution.py:375
  18.8 0.0 collective-permute-done.3.hidden_ref
  18.8 0.3 rank_inner.1
  19.1 0.7 %collective-permute-start.5 = (f32[32,128]{1,0:T(8,128)S(1)}, f32[32,128]{1,0:T(8,128)S(1)}, u32[]{:S(2)}, u32[]{:S(2)}) collective-permute-start(f32[32,128]{1,0:T(8,128)S(1)} %get-tuple-element.26), channel_id=1, source_target_pairs={{0,0},{6,1},{10,2},{12,3},{2,4},{4,5},{8,6},{14,7},{1,8},{7,9},{11... | collective-permute-start | bytes 49160 | tf_op jit(solution)/shard_map/ppermute | solution.py:427
  19.8 5.7 %collective-permute-start.9 = (bf16[2,2,16,256]{3,2,1,0:T(8,128)(2,1)S(1)}, bf16[2,2,16,256]{3,2,1,0:T(8,128)(2,1)S(1)}, u32[]{:S(2)}, u32[]{:S(2)}) collective-permute-start(bf16[2,2,16,256]{3,2,1,0:T(8,128)(2,1)S(1)} %get-tuple-element.36.rest_10_), channel_id=1, source_target_pairs={{0,8},{4,12},{8,0},{12,4},{1,9},{5,13},{9,1},{13,5},{2,10},{6,14},... | collective-permute-start | bytes 98312 | tf_op jit(solution)/shard_map/ppermute | solution.py:375
  25.5 0.0 collective-permute-done.1.rest_1_
  25.5 0.0 collective-permute-done.2.rest_3_
  25.5 0.0 copy-done
  25.5 3.2 %base_projection.1 = (f32[64,256]{1,0:T(8,128)S(1)}, f32[32,128]{1,0:T(8,128)S(1)}) custom-call(f32[64,128]{1,0:T(8,128)S(1)} %get-tuple-element.21.gain_ref, bf16[8192,2,256]{2,1,0:T(2,128)(2,1)S(1)} %get-tuple-element.22.weight_ref, bf16[4,8,2048]{2,1,0:T(8,128)(2,1)S(1)} %copy-done, bf16[4,8,2048]{2,1,0:T(8,128)(2,1)S(1)} %collective-permute-done.1.rest_1_, ...), custom_call_target="tpu_custom_call" | custom-call | flops 562036736 | bytes 9437184 | tf_op jit(solution)/shard_map/base_projection/pallas_call | solution.py:275
  28.7 0.0 collective-permute-done.5.rest_6_
  28.7 0.1 collective-permute-start.8
  28.8 2.1 %collective-permute-start.7 = (f32[32,128]{1,0:T(8,128)S(1)}, f32[32,128]{1,0:T(8,128)S(1)}, u32[]{:S(2)}, u32[]{:S(2)}) collective-permute-start(f32[32,128]{1,0:T(8,128)S(1)} %collective-permute-done.5.rest_6_), channel_id=1, source_target_pairs={{0,3},{1,2},{2,1},{3,0},{4,7},{5,6},{6,5},{7,4},{8,11},{9,10},{10,... | collective-permute-start | bytes 49160 | tf_op jit(solution)/shard_map/ppermute | solution.py:375
  30.9 0.0 collective-permute-start.6
  30.9 0.0 collective-permute-done.9.rest_11_
  30.9 0.0 collective-permute-done.8.rest_9_
  30.9 1.4 %collective-permute-done.7.rest_8_ = f32[32,128]{1,0:T(8,128)S(1)} collective-permute-done((f32[32,128]{1,0:T(8,128)S(1)}, f32[32,128]{1,0:T(8,128)S(1)}, u32[]{:S(2)}, u32[]{:S(2)}) %collective-permute-start.7) | collective-permute-done | bytes 16416 | tf_op jit(solution)/shard_map/ppermute | solution.py:375
  32.3 2.3 %collective-permute-done.6.rest_7_ = f32[32,128]{1,0:T(8,128)S(1)} collective-permute-done((f32[32,128]{1,0:T(8,128)S(1)}, f32[32,128]{1,0:T(8,128)S(1)}, u32[]{:S(2)}, u32[]{:S(2)}) %collective-permute-start.6) | collective-permute-done | bytes 16416 | tf_op jit(solution)/shard_map/ppermute | solution.py:375
  34.6 0.0 copy-done.2
  34.6 1.5 %fresh_attention.1 = (bf16[4,8,256]{2,1,0:T(8,128)(2,1)}, bf16[4,8,256]{2,1,0:T(8,128)(2,1)}, bf16[4,8,2048]{2,1,0:T(8,128)(2,1)}) custom-call(f32[64,256]{1,0:T(8,128)S(1)} %get-tuple-element.24.base_ref, f32[32,128]{1,0:T(8,128)S(1)} %get-tuple-element.28.square_ref, bf16[2,256]{1,0:T(2,128)(2,1)S(1)} %copy-done.2, ...), custom_call_target="tpu_custom_call" | custom-call | tf_op jit(solution)/shard_map/fresh_attention/pallas_call | solution.py:364
Async XLA Ops:
  0.6 24.9 %copy-start = (bf16[4,8,2048]{2,1,0:T(8,128)(2,1)S(1)}, bf16[4,8,2048]{2,1,0:T(8,128)(2,1)}, u32[]{:S(2)}) copy-start(bf16[4,8,2048]{2,1,0:T(8,128)(2,1)} %rest_0_.1) | copy-start | bytes 393220
  0.6 14.4 %copy-start.1 = (bf16[2,256,16]{1,2,0:T(8,128)(2,1)S(1)}, bf16[2,256,16]{1,2,0:T(8,128)(2,1)}, u32[]{:S(2)}) copy-start(bf16[2,256,16]{1,2,0:T(8,128)(2,1)} %param.15) | copy-start | bytes 49156
  0.7 12.3 %collective-permute-start = (bf16[4,8,2048]{2,1,0:T(8,128)(2,1)}, bf16[4,8,2048]{2,1,0:T(8,128)(2,1)S(1)}, u32[]{:S(2)}, u32[]{:S(2)}) collective-permute-start(bf16[4,8,2048]{2,1,0:T(8,128)(2,1)} %rest_0_.1), channel_id=1, source_target_pairs={{0,2},{1,3},{2,0},{3,1},{4,6},{5,7},{6,4},{7,5},{8,10},{9,11},{10,... | collective-permute-start | bytes 393224 | tf_op jit(solution)/shard_map/ppermute | solution.py:375
  3.7 21.8 %collective-permute-start.1 = (bf16[4,8,2048]{2,1,0:T(8,128)(2,1)}, bf16[4,8,2048]{2,1,0:T(8,128)(2,1)S(1)}, u32[]{:S(2)}, u32[]{:S(2)}) collective-permute-start(bf16[4,8,2048]{2,1,0:T(8,128)(2,1)} %rest_0_.1), channel_id=1, source_target_pairs={{0,1},{1,0},{2,3},{3,2},{4,5},{5,4},{6,7},{7,6},{8,9},{9,8},{10,11... | collective-permute-start | bytes 393224 | tf_op jit(solution)/shard_map/ppermute | solution.py:375
  3.7 15.1 %collective-permute-start.3 = (bf16[4,8,2048]{2,1,0:T(8,128)(2,1)}, bf16[4,8,2048]{2,1,0:T(8,128)(2,1)S(1)}, u32[]{:S(2)}, u32[]{:S(2)}) collective-permute-start(bf16[4,8,2048]{2,1,0:T(8,128)(2,1)} %rest_0_.1), channel_id=1, source_target_pairs={{0,0},{1,6},{2,10},{3,12},{4,2},{5,4},{6,8},{7,14},{8,1},{9,7},{10... | collective-permute-start | bytes 393224 | tf_op jit(solution)/shard_map/ppermute | solution.py:410
  5.2 29.4 %copy-start.2 = (bf16[2,256]{1,0:T(2,128)(2,1)S(1)}, bf16[2,256]{1,0:T(2,128)(2,1)}, u32[]{:S(2)}) copy-start(bf16[2,256]{1,0:T(2,128)(2,1)} %bias_ref.1) | copy-start | bytes 3076
  12.9 12.6 %collective-permute-start.2 = (bf16[4,8,2048]{2,1,0:T(8,128)(2,1)S(1)}, bf16[4,8,2048]{2,1,0:T(8,128)(2,1)S(1)}, u32[]{:S(2)}, u32[]{:S(2)}) collective-permute-start(bf16[4,8,2048]{2,1,0:T(8,128)(2,1)S(1)} %collective-permute-done.rest_2_), channel_id=1, source_target_pairs={{0,1},{1,0},{2,3},{3,2},{4,5},{5,4},{6,7},{7,6},{8,9},{9,8},{10,11... | collective-permute-start | bytes 393224 | tf_op jit(solution)/shard_map/ppermute | solution.py:375
  15.0 3.7 %collective-permute-start.4 = (bf16[2,16,256]{2,1,0:T(8,128)(2,1)S(1)}, bf16[2,16,256]{2,1,0:T(8,128)(2,1)S(1)}, u32[]{:S(2)}, u32[]{:S(2)}) collective-permute-start(bf16[2,16,256]{2,1,0:T(8,128)(2,1)S(1)} %bitcast.2), channel_id=1, source_target_pairs={{0,4},{4,0},{8,12},{12,8},{1,5},{5,1},{9,13},{13,9},{2,6},{6,2},{1... | collective-permute-start | bytes 49160 | tf_op jit(solution)/shard_map/ppermute | solution.py:375
  19.1 9.6 %collective-permute-start.5 = (f32[32,128]{1,0:T(8,128)S(1)}, f32[32,128]{1,0:T(8,128)S(1)}, u32[]{:S(2)}, u32[]{:S(2)}) collective-permute-start(f32[32,128]{1,0:T(8,128)S(1)} %get-tuple-element.26), channel_id=1, source_target_pairs={{0,0},{6,1},{10,2},{12,3},{2,4},{4,5},{8,6},{14,7},{1,8},{7,9},{11... | collective-permute-start | bytes 49160 | tf_op jit(solution)/shard_map/ppermute | solution.py:427
  19.8 11.2 %collective-permute-start.9 = (bf16[2,2,16,256]{3,2,1,0:T(8,128)(2,1)S(1)}, bf16[2,2,16,256]{3,2,1,0:T(8,128)(2,1)S(1)}, u32[]{:S(2)}, u32[]{:S(2)}) collective-permute-start(bf16[2,2,16,256]{3,2,1,0:T(8,128)(2,1)S(1)} %get-tuple-element.36.rest_10_), channel_id=1, source_target_pairs={{0,8},{4,12},{8,0},{12,4},{1,9},{5,13},{9,1},{13,5},{2,10},{6,14},... | collective-permute-start | bytes 98312 | tf_op jit(solution)/shard_map/ppermute | solution.py:375
  28.7 2.3 %collective-permute-start.8 = (f32[32,128]{1,0:T(8,128)S(1)}, f32[32,128]{1,0:T(8,128)S(1)}, u32[]{:S(2)}, u32[]{:S(2)}) collective-permute-start(f32[32,128]{1,0:T(8,128)S(1)} %collective-permute-done.5.rest_6_), channel_id=1, source_target_pairs={{0,1},{1,0},{2,3},{3,2},{4,5},{5,4},{6,7},{7,6},{8,9},{9,8},{10,11... | collective-permute-start | bytes 49160 | tf_op jit(solution)/shard_map/ppermute | solution.py:375
  28.8 3.6 %collective-permute-start.7 = (f32[32,128]{1,0:T(8,128)S(1)}, f32[32,128]{1,0:T(8,128)S(1)}, u32[]{:S(2)}, u32[]{:S(2)}) collective-permute-start(f32[32,128]{1,0:T(8,128)S(1)} %collective-permute-done.5.rest_6_), channel_id=1, source_target_pairs={{0,3},{1,2},{2,1},{3,0},{4,7},{5,6},{6,5},{7,4},{8,11},{9,10},{10,... | collective-permute-start | bytes 49160 | tf_op jit(solution)/shard_map/ppermute | solution.py:375
  30.9 3.7 %collective-permute-start.6 = (f32[32,128]{1,0:T(8,128)S(1)}, f32[32,128]{1,0:T(8,128)S(1)}, u32[]{:S(2)}, u32[]{:S(2)}) collective-permute-start(f32[32,128]{1,0:T(8,128)S(1)} %collective-permute-done.5.rest_6_), channel_id=1, source_target_pairs={{0,2},{1,3},{2,0},{3,1},{4,6},{5,7},{6,4},{7,5},{8,10},{9,11},{10,... | collective-permute-start | bytes 49160 | tf_op jit(solution)/shard_map/ppermute | solution.py:375

commit v4 on v3

v4 whole, which is shorter than its diff:
```python
import functools
import math

import jax
import jax.numpy as jnp
from jax import lax
from jax.experimental import pallas as pl
from jax.experimental.pallas import tpu as pltpu
from jax.sharding import PartitionSpec as P

HD = 128


norm_eps = 1e-06
adapter_scale = 2.0
rope_base = 1000000.0
masked_score = -1e30
score_scale = 1.0 / math.sqrt(HD)

VMEM = pl.BlockSpec(memory_space=pltpu.VMEM)
HBM = pl.BlockSpec(memory_space=pltpu.HBM)


def query_block(query_ref, group, per_group):
    steps = query_ref.shape[0]
    tiles = []
    for head in range(per_group):
        at = (group * per_group + head) * HD
        for step in range(steps):
            tiles.append(query_ref[step, :, at : at + HD].astype(jnp.float32))
    return jnp.concatenate(tiles, axis=0)


def weight_block(weight_ref, block, width):
    return weight_ref.at[pl.ds(pl.multiple_of(block * width, width), width)]


def cache_kernel(
    staged,
    lengths_ref,
    query_ref,
    key_ref,
    value_ref,
    down_ref,
    gain_ref,
    up_ref,
    bias_ref,
    weight_ref,
    weight_out,
    down_out,
    gain_out,
    up_out,
    bias_out,
    query_out,
    acc_out,
    top_out,
    total_out,
    cos_out,
    sin_out,
    lengths,
    queries,
    gain_buffer,
    key_buffer,
    value_buffer,
    score_buffer,
    sems,
):
    steps, rows, query_width = query_ref.shape
    cache_span = key_ref.shape[1]
    groups = key_ref.shape[2] // HD
    per_group = query_width // HD // groups
    lines = steps * per_group
    half_rows = rows // 2
    halves = [pl.ds(0, half_rows), pl.ds(half_rows, half_rows)]
    copies = [
        (lengths_ref, lengths),
        (query_ref, queries),
        (key_ref.at[halves[0]], key_buffer.at[halves[0]]),
        (key_ref.at[halves[1]], key_buffer.at[halves[1]]),
        (value_ref.at[halves[0]], value_buffer.at[halves[0]]),
        (value_ref.at[halves[1]], value_buffer.at[halves[1]]),
        (gain_ref, gain_buffer),
        (down_ref, down_out),
        (up_ref, up_out),
        (bias_ref, bias_out),
    ]
    me = lax.axis_index("tp")
    for i, offset in enumerate(staged):
        copies.append((weight_block(weight_ref, me ^ offset, weight_out.shape[1]), weight_out.at[i]))
    copies = [pltpu.make_async_copy(*pair, sems.at[i]) for i, pair in enumerate(copies)]
    for copy in copies:
        copy.start()

    copies[0].wait()
    lane = lax.broadcasted_iota(jnp.int32, (rows, HD), 1)
    half = HD // 2
    second = lane >= half
    index = jnp.where(second, lane - half, lane).astype(jnp.float32)
    inv_freq = jnp.exp(index * (-2.0 * math.log(rope_base) / HD))
    row_index = lax.broadcasted_iota(jnp.int32, (rows, HD), 0)
    row_lengths = jnp.zeros((rows, HD), jnp.int32)
    for row in range(rows):
        row_lengths = jnp.where(row_index == row, lengths[row], row_lengths)
    for step in range(steps):
        angles = (row_lengths + step).astype(jnp.float32) * inv_freq
        sine = jnp.sin(angles)
        cos_out[pl.ds(step * rows, rows)] = jnp.cos(angles)
        sin_out[pl.ds(step * rows, rows)] = jnp.where(second, sine, -sine)
    copies[1].wait()
    for group in range(groups):
        query_out[group] = query_block(queries, group, per_group)

    place = lax.broadcasted_iota(jnp.int32, (lines, cache_span), 1)
    for i in range(2):
        copies[2 + i].wait()
        for row in range(i * half_rows, (i + 1) * half_rows):
            for group in range(groups):
                query = query_out[group, pl.ds(row, lines, stride=rows), :].astype(jnp.bfloat16)
                score_buffer[row * groups + group] = lax.dot_general(
                    query,
                    key_buffer[row, :, pl.ds(group * HD, HD)],
                    (((1,), (1,)), ((), ())),
                    preferred_element_type=jnp.float32,
                )
    for i in range(2):
        copies[4 + i].wait()
        for row in range(i * half_rows, (i + 1) * half_rows):
            live = place < lengths[row]
            for group in range(groups):
                mine = pl.ds(row, lines, stride=rows)
                scores = score_buffer[row * groups + group]
                scores = jnp.where(live, scores * score_scale, masked_score)
                top = jnp.max(scores, axis=1, keepdims=True)
                exps = jnp.exp(scores - top)
                total = jnp.sum(exps, axis=1, keepdims=True)
                acc = jnp.dot(
                    exps.astype(jnp.bfloat16),
                    value_buffer[row, :, pl.ds(group * HD, HD)],
                    preferred_element_type=jnp.float32,
                )
                acc_out[group, mine, :] = acc
                top_out[group, mine, :] = jnp.broadcast_to(top, acc.shape)
                total_out[group, mine, :] = jnp.broadcast_to(total, acc.shape)
    copies[6].wait()
    gain_out[...] = gain_buffer[...].astype(jnp.float32)
    for copy in copies[7:]:
        copy.wait()


def cache_call(staged, part_width, lengths, queries, keys, values, down, gain, up, bias, weight):
    steps, rows, query_width = queries.shape
    cache_span, key_width = keys.shape[1:]
    groups = key_width // HD
    lines = steps * (query_width // key_width)
    block = (groups, lines * rows, HD)
    table = (steps * rows, HD)
    operands = (lengths, queries, keys, values, down, gain, up, bias, weight)
    return pl.pallas_call(
        functools.partial(cache_kernel, staged),
        out_shape=(
            pltpu.VMEM((len(staged), part_width) + weight.shape[1:], weight.dtype),
            pltpu.VMEM(down.shape, down.dtype),
            pltpu.VMEM(gain.shape, jnp.float32),
            pltpu.VMEM(up.shape, up.dtype),
            pltpu.VMEM(bias.shape, bias.dtype),
            pltpu.VMEM(block, jnp.float32),
            pltpu.VMEM(block, jnp.float32),
            pltpu.VMEM(block, jnp.float32),
            pltpu.VMEM(block, jnp.float32),
            pltpu.VMEM(table, jnp.float32),
            pltpu.VMEM(table, jnp.float32),
        ),
        in_specs=[HBM] * len(operands),
        out_specs=(VMEM,) * 11,
        scratch_shapes=[
            pltpu.SMEM(lengths.shape, jnp.int32),
            pltpu.VMEM(queries.shape, queries.dtype),
            pltpu.VMEM(gain.shape, gain.dtype),
            pltpu.VMEM(keys.shape, keys.dtype),
            pltpu.VMEM(values.shape, values.dtype),
            pltpu.VMEM((rows * groups, lines, cache_span), jnp.float32),
            pltpu.SemaphoreType.DMA((10 + len(staged),)),
        ],
        compiler_params=pltpu.CompilerParams(vmem_limit_bytes=16 << 20),
        cost_estimate=pl.CostEstimate(flops=2 * 67 << 20, bytes_accessed=9 << 20, transcendentals=0),
        name="cache_attention",
    )(*[pltpu.with_memory_space_constraint(x, pltpu.HBM) for x in operands])


def scaled_chunks(block, gain, start):
    chunks = []
    for i in range(block.shape[1] // HD):
        chunk = block[:, i * HD : (i + 1) * HD]
        chunks.append((chunk * gain[start + i : start + i + 1]).astype(jnp.bfloat16))
    return chunks


def rows_of(ref):
    steps = ref.shape[0]
    return jnp.concatenate([ref[s].astype(jnp.float32) for s in range(steps)], axis=0)


def inner_kernel(hidden_ref, gain_ref, down_ref, out_ref):
    width = hidden_ref.shape[2]
    start = pl.multiple_of(lax.axis_index("wide") * (width // HD), width // HD)
    gain = gain_ref[pl.ds(start, width // HD)]
    scaled = jnp.concatenate(scaled_chunks(rows_of(hidden_ref), gain, 0), axis=1)
    ranks = down_ref.shape[1]
    for kind in range(down_ref.shape[0]):
        out_ref[:, kind * ranks : (kind + 1) * ranks] = lax.dot_general(
            scaled,
            down_ref[kind],
            (((1,), (1,)), ((), ())),
            preferred_element_type=jnp.float32,
        )


def inner_call(hidden, gain, down):
    steps, rows, _ = hidden.shape
    kinds, ranks, _ = down.shape
    return pl.pallas_call(
        inner_kernel,
        out_shape=jax.ShapeDtypeStruct((steps * rows, kinds * ranks), jnp.float32),
        in_specs=[VMEM] * 3,
        out_specs=VMEM,
        compiler_params=pltpu.CompilerParams(vmem_limit_bytes=8 << 20),
        name="rank_inner",
    )(hidden, gain, down)


def base_kernel(staged, streamed, gain_ref, staged_ref, weight_ref, *rest):
    offsets = staged + streamed
    parts = rest[: len(offsets)]
    base_out, square_out, spread, buffer, sems = rest[len(offsets) :]
    steps, rows, width = parts[0].shape
    count = steps * rows
    kinds, columns = weight_ref.shape[1:]
    me = lax.axis_index("tp")
    copies = []
    for i, offset in enumerate(streamed):
        copy = pltpu.make_async_copy(
            weight_block(weight_ref, me ^ offset, width), buffer.at[i], sems.at[i]
        )
        copy.start()
        copies.append(copy)
    lane = lax.broadcasted_iota(jnp.int32, (count, HD), 1)
    low, high = lane // 2, lane // 2 + HD // 2
    even = lane % 2 == 0
    squares = jnp.zeros((count, HD), jnp.float32)
    acc = None
    for k, (offset, part) in enumerate(zip(offsets, parts)):
        start = pl.multiple_of((me ^ offset) * (width // HD), width // HD)
        gain = gain_ref[pl.ds(start, width // HD)]
        values = rows_of(part)
        for i in range(width // HD):
            chunk = values[:, i * HD : (i + 1) * HD]
            squares += chunk * chunk
            chunk = chunk * gain[i : i + 1]
            for j, index in enumerate((low, high)):
                wide = jnp.take_along_axis(chunk, index, axis=1)
                at = pl.ds((2 * i + j) * HD, HD)
                spread[k, :count, at] = jnp.where(even, wide, 0.0).astype(jnp.bfloat16)
                spread[k, count:, at] = jnp.where(even, 0.0, wide).astype(jnp.bfloat16)
        if k < len(staged):
            block = staged_ref.at[k]
        else:
            copies[k - len(staged)].wait()
            block = buffer.at[k - len(staged)]
        product = jnp.dot(
            spread[k],
            block.reshape(width * kinds, columns)[...],
            preferred_element_type=jnp.float32,
        )
        acc = product if acc is None else acc + product
    base_out[...] = acc
    square_out[...] = jnp.broadcast_to(jnp.sum(squares, axis=1, keepdims=True), squares.shape)


def base_call(staged, streamed, gain, staged_weight, weight, parts):
    steps, rows, width = parts[0].shape
    kinds, columns = weight.shape[1:]
    return pl.pallas_call(
        functools.partial(base_kernel, staged, streamed),
        out_shape=(
            pltpu.VMEM((kinds * steps * rows, columns), jnp.float32),
            pltpu.VMEM((steps * rows, HD), jnp.float32),
        ),
        in_specs=[VMEM, VMEM, HBM] + [VMEM] * len(parts),
        out_specs=(VMEM, VMEM),
        scratch_shapes=[
            pltpu.VMEM((len(parts), kinds * steps * rows, kinds * width), jnp.bfloat16),
            pltpu.VMEM((len(streamed), width, kinds, columns), weight.dtype),
            pltpu.SemaphoreType.DMA((len(streamed),)),
        ],
        compiler_params=pltpu.CompilerParams(vmem_limit_bytes=16 << 20),
        cost_estimate=pl.CostEstimate(flops=4 * 134 << 20, bytes_accessed=9 << 20, transcendentals=0),
        name="base_projection",
    )(gain, staged_weight, pltpu.with_memory_space_constraint(weight, pltpu.HBM), *parts)


def final_kernel(width, inner_count, up_count, base_ref, square_ref, bias_ref, *rest):
    query_ref, acc_ref, top_ref, total_ref, cos_ref, sin_ref = rest[:6]
    inner_refs = rest[6 : 6 + inner_count]
    up_refs = rest[6 + inner_count : 6 + inner_count + up_count]
    keys_out, values_out, attended_out, up_buffer = rest[6 + inner_count + up_count :]
    steps, rows, columns = keys_out.shape
    count = steps * rows
    groups, size, _ = query_ref.shape
    per_group = size // count
    kinds = bias_ref.shape[0]
    row_scale = lax.rsqrt(square_ref[:, :1] * (1.0 / width) + norm_eps)
    inner = inner_refs[0][...]
    for ref in inner_refs[1:]:
        inner = inner + ref[...]
    high = inner.astype(jnp.bfloat16)
    low = (inner - high.astype(jnp.float32)).astype(jnp.bfloat16)
    ranks = inner.shape[1] // kinds
    bias = bias_ref[...].astype(jnp.float32)
    linear = []
    for i, ref in enumerate(up_refs):
        up_buffer[i] = ref[...]
    me = lax.axis_index("wide") if up_count > 1 else 0
    for kind in range(kinds):
        up = jnp.concatenate([up_buffer[me ^ i, kind] for i in range(up_count)], axis=0)
        cols = slice(kind * ranks, (kind + 1) * ranks)
        lora = jnp.dot(high[:, cols], up, preferred_element_type=jnp.float32) + jnp.dot(
            low[:, cols], up, preferred_element_type=jnp.float32
        )
        base = base_ref[kind * count : (kind + 1) * count]
        linear.append((base + adapter_scale * lora) * row_scale + bias[kind : kind + 1])
    cosine, sine = cos_ref[...], sin_ref[...]
    line = lax.broadcasted_iota(jnp.int32, (size, count), 0)
    other = lax.broadcasted_iota(jnp.int32, (size, count), 1)
    live = (line % rows == other % rows) & (other // rows <= line // rows % steps)
    for group in range(groups):
        at = slice(group * HD, (group + 1) * HD)
        key = linear[0][:, at]
        key = (key * cosine + pltpu.roll(key, HD // 2, 1) * sine).astype(jnp.bfloat16)
        value = linear[1][:, at].astype(jnp.bfloat16)
        for step in range(steps):
            keys_out[step, :, at] = key[step * rows : (step + 1) * rows]
            values_out[step, :, at] = value[step * rows : (step + 1) * rows]
        scores = lax.dot_general(
            query_ref[group].astype(jnp.bfloat16),
            key,
            (((1,), (1,)), ((), ())),
            preferred_element_type=jnp.float32,
        )
        scores = jnp.where(live, scores * score_scale, masked_score)
        old_top = top_ref[group][:, :1]
        top = jnp.maximum(old_top, jnp.max(scores, axis=1, keepdims=True))
        exps = jnp.exp(scores - top)
        keep = jnp.exp(old_top - top)
        total = total_ref[group][:, :1] * keep + jnp.sum(exps, axis=1, keepdims=True)
        acc = acc_ref[group] * keep + jnp.dot(
            exps.astype(jnp.bfloat16), value, preferred_element_type=jnp.float32
        )
        attended = (acc / total).astype(jnp.bfloat16)
        for head in range(per_group):
            lanes = pl.ds((group * per_group + head) * HD, HD)
            for step in range(steps):
                tile = (head * steps + step) * rows
                attended_out[step, :, lanes] = attended[tile : tile + rows]


def final_call(shape, width, base, square, bias, cached, inner, up):
    steps, rows, query_width = shape
    small = jax.ShapeDtypeStruct((steps, rows, base.shape[1]), jnp.bfloat16)
    return pl.pallas_call(
        functools.partial(final_kernel, width, len(inner), len(up)),
        out_shape=(small, small, jax.ShapeDtypeStruct(shape, jnp.bfloat16)),
        in_specs=[VMEM] * (3 + len(cached) + len(inner) + len(up)),
        out_specs=(VMEM,) * 3,
        scratch_shapes=[pltpu.VMEM((len(up),) + up[0].shape, up[0].dtype)],
        compiler_params=pltpu.CompilerParams(vmem_limit_bytes=8 << 20),
        name="fresh_attention",
    )(base, square, bias, *cached, *inner, *up)


def swap(block, axis, offset, count):
    return lax.ppermute(block, axis, [(i, i ^ offset) for i in range(count)])


def meeting_place():
    pairs = []
    for w in range(4):
        for t in range(4):
            pairs.append((w * 4 + t, t * 4 + 2 * ((t // 2) ^ ((w + t) & 1)) + w // 2))
    return pairs


def on_device(
    wide_count,
    tp_count,
    hidden,
    input_norm_gain,
    key_value_weight,
    key_value_bias,
    adapter_down_factor,
    adapter_up_factor,
    queries,
    stored_rotated_keys,
    stored_value_rows,
    lengths,
):
    steps, rows, part_width = hidden.shape
    width = part_width * tp_count
    kinds, ranks, down_width = adapter_down_factor.shape
    gain = input_norm_gain.reshape(width // HD, HD)
    up_part = jnp.transpose(adapter_up_factor, (0, 2, 1))
    both = ("wide", "tp")

    direct = wide_count == 4 and tp_count == 4
    parts = [hidden] + [swap(hidden, "tp", offset, tp_count) for offset in (1, 2, 3)]
    if direct:
        there = meeting_place()
        moved = lax.ppermute(hidden, both, there)
        up = [swap(up_part, "wide", offset, 4) for offset in (1, 2, 3)]
    staged, streamed = (0, 1), (2, 3)
    staged_weight, down, gain_rows, my_up, bias, *cached = cache_call(
        staged,
        part_width,
        lengths,
        queries,
        stored_rotated_keys,
        stored_value_rows,
        adapter_down_factor,
        gain,
        up_part,
        key_value_bias,
        key_value_weight,
    )
    if direct:
        inner = inner_call(moved, gain_rows, down)
        inner = lax.ppermute(inner, both, [(b, a) for a, b in there])
        up = [my_up] + up
    else:
        gathered = lax.all_gather(hidden, "tp", axis=2, tiled=True).astype(jnp.float32)
        scaled = (gathered * input_norm_gain.astype(jnp.float32)).astype(jnp.bfloat16)
        all_down = lax.all_gather(adapter_down_factor, "wide", axis=2, tiled=True)
        inner = jnp.einsum("srd,kad->srka", scaled, all_down, preferred_element_type=jnp.float32)
        inner = [inner.reshape(steps * rows, kinds * ranks)]
        up = [lax.all_gather(up_part, "wide", axis=1, tiled=True)]

    base, square = base_call(staged, streamed, gain_rows, staged_weight, key_value_weight, parts)
    if direct:
        inner, square = lax.optimization_barrier((inner, square))
        inner = [inner] + [swap(inner, "tp", offset, 4) for offset in (2, 3, 1)]
    return final_call(queries.shape, width, base, square, bias, cached, inner, up)


def solution(mesh):
    in_specs = (
        P(None, ("groups", "wide"), "tp"),
        P(),
        P(None, None, "tp"),
        P(None, "tp"),
        P("groups", None, "wide"),
        P("groups", "tp", "wide"),
        P(None, ("groups", "wide"), "tp"),
        P(("groups", "wide"), None, "tp"),
        P(("groups", "wide"), None, "tp"),
        P(("groups", "wide")),
    )
    out_specs = (
        P(None, ("groups", "wide"), "tp"),
        P(None, ("groups", "wide"), "tp"),
        P(None, ("groups", "wide"), "tp"),
    )
    body = functools.partial(on_device, mesh.shape["wide"], mesh.shape["tp"])
    return jax.shard_map(
        body, mesh=mesh, in_specs=in_specs, out_specs=out_specs, check_vma=False
    )
```

time: 36.3 us -> 32.3 us (0.89)
  waiting for transfers between devices: 7.01 us -> 2.98 us
  starting transfers between devices: 15.7 us -> 18 us
  Pallas kernels: 12.7 us -> 10.5 us
    ppermute x8 -> x9, waiting for transfers between devices: 7.01 us -> 2.98 us  [swap(): return lax.ppermute(block, axis, [(i, i ^ offset) for i in range(count)])]
    ppermute x8 -> x9, starting transfers between devices: 13.5 us -> 15.8 us  [swap(): return lax.ppermute(block, axis, [(i, i ^ offset) for i in range(count)])]
    pallas_call x3, Pallas kernels: 11.2 us -> 9.02 us  [the longest x1 4.84 us: base_call(): pl.pallas_call(functools.partial(base_kernel, staged, streamed), out_shap...]
  transfers between devices with their start and end apart: 10 -> 11, of which waited for: 3 -> 2; matrix products, arithmetic and copies ran while one was open for 0% -> 0% of each run, Pallas kernels for 31% -> 28%
where the time goes in v4:
time: 32.3 us; the launch traced here: 32.2 us
  starting transfers between devices  18 us (56%)
  Pallas kernels  10.5 us (33%)
  waiting for transfers between devices  2.98 us (9%)
  between operations  0.71 us (2%)
    ppermute x9, starting transfers between devices, swap(): return lax.ppermute(block, axis, [(i, i ^ offset) for i in range(count)])  15.8 us
    pallas_call x1, Pallas kernels, base_call(): pl.pallas_call(functools.partial(base_kernel, staged, streamed), out_shap...  4.84 us
    pallas_call x1, Pallas kernels, cache_call(): pl.pallas_call(functools.partial(cache_kernel, staged), out_shape=(pltpu....  3.85 us
    ppermute x9, waiting for transfers between devices, swap(): return lax.ppermute(block, axis, [(i, i ^ offset) for i in range(count)])  2.98 us
    ppermute x1, starting transfers between devices, on_device(): moved = lax.ppermute(hidden, both, there)  1.56 us
    pallas_call x1, Pallas kernels, final_call(): pl.pallas_call(functools.partial(final_kernel, width, len(inner), len(up)...  1.46 us
    ppermute x1, starting transfers between devices, on_device(): inner = lax.ppermute(inner, both, [(b, a) for a, b in there])  0.65 us
  transfers between devices with their start and end apart: 11, of which 2 were waited for; matrix products, arithmetic and copies ran while one was open for 0% of the time, Pallas kernels for 28%

profile of v4, /device:TPU:0, one launch (start us, length us, event | category | flops | bytes accessed | tf_op | source)
XLA Modules:
  0.0 32.2 jit_solution(3256844876935668600)
XLA Ops:
  0.6 1.6 %collective-permute-start.3 = (bf16[4,8,2048]{2,1,0:T(8,128)(2,1)}, bf16[4,8,2048]{2,1,0:T(8,128)(2,1)S(1)}, u32[]{:S(2)}, u32[]{:S(2)}) collective-permute-start(bf16[4,8,2048]{2,1,0:T(8,128)(2,1)} %rest_0_.1), channel_id=1, source_target_pairs={{0,0},{1,6},{2,10},{3,12},{4,2},{5,4},{6,8},{7,14},{8,1},{9,7},{10... | collective-permute-start | bytes 393224 | tf_op jit(solution)/shard_map/ppermute | solution.py:417
  2.2 4.5 %collective-permute-start = (bf16[4,8,2048]{2,1,0:T(8,128)(2,1)}, bf16[4,8,2048]{2,1,0:T(8,128)(2,1)S(1)}, u32[]{:S(2)}, u32[]{:S(2)}) collective-permute-start(bf16[4,8,2048]{2,1,0:T(8,128)(2,1)} %rest_0_.1), channel_id=1, source_target_pairs={{0,1},{1,0},{2,3},{3,2},{4,5},{5,4},{6,7},{7,6},{8,9},{9,8},{10,11... | collective-permute-start | bytes 393224 | tf_op jit(solution)/shard_map/ppermute | solution.py:381
  6.7 2.6 %collective-permute-start.1 = (bf16[4,8,2048]{2,1,0:T(8,128)(2,1)}, bf16[4,8,2048]{2,1,0:T(8,128)(2,1)S(1)}, u32[]{:S(2)}, u32[]{:S(2)}) collective-permute-start(bf16[4,8,2048]{2,1,0:T(8,128)(2,1)} %rest_0_.1), channel_id=1, source_target_pairs={{0,2},{1,3},{2,0},{3,1},{4,6},{5,7},{6,4},{7,5},{8,10},{9,11},{10,... | collective-permute-start | bytes 393224 | tf_op jit(solution)/shard_map/ppermute | solution.py:381
  9.2 0.0 collective-permute-start.2
  9.2 0.9 %collective-permute-start.10 = (bf16[2,16,256]{2,1,0:T(8,128)(2,1)}, bf16[2,16,256]{2,1,0:T(8,128)(2,1)S(1)}, u32[]{:S(2)}, u32[]{:S(2)}) collective-permute-start(bf16[2,16,256]{2,1,0:T(8,128)(2,1)} %bitcast.3), channel_id=1, source_target_pairs={{0,12},{4,8},{8,4},{12,0},{1,13},{5,9},{9,5},{13,1},{2,14},{6,10},... | collective-permute-start | bytes 49160 | tf_op jit(solution)/shard_map/ppermute | solution.py:381
  10.1 0.0 copy-start.1
  10.1 0.0 copy-start
  10.1 3.8 %cache_attention.1 = (bf16[2,2048,2,256]{3,2,1,0:T(2,128)(2,1)S(1)}, bf16[2,64,2048]{2,1,0:T(8,128)(2,1)S(1)}, f32[64,128]{1,0:T(8,128)S(1)}, bf16[2,16,256]{2,1...) custom-call(s32[8]{0:T(128)} %lengths_ref.1, ...), custom_call_target="tpu_custom_call" | custom-call | flops 140509184 | bytes 9437184 | tf_op jit(solution)/shard_map/cache_attention/pallas_call | solution.py:158
  14.0 0.0 collective-permute-done.3.hidden_ref
  14.0 0.0 copy-done.1
  14.0 0.1 collective-permute-start.8
  14.1 0.3 %rank_inner.1 = f32[32,128]{1,0:T(8,128)S(1)} custom-call(bf16[4,8,2048]{2,1,0:T(8,128)(2,1)S(1)} %collective-permute-done.3.hidden_ref, f32[64,128]{1,0:T(8,128)S(1)} %get-tuple-element.18.gain_ref, bf16[2,64,2048]{2,1,0:T(8,128)(2,1)S(1)} %get-tuple-element.21.down_ref), custom_call_target="tpu_custom_call" | custom-call | tf_op jit(solution)/shard_map/rank_inner/pallas_call | solution.py:221
  14.4 0.0 collective-permute-done.rest_1_
  14.4 3.5 %collective-permute-start.9 = (bf16[2,16,256]{2,1,0:T(8,128)(2,1)S(1)}, bf16[2,16,256]{2,1,0:T(8,128)(2,1)S(1)}, u32[]{:S(2)}, u32[]{:S(2)}) collective-permute-start(bf16[2,16,256]{2,1,0:T(8,128)(2,1)S(1)} %bitcast.6), channel_id=1, source_target_pairs={{0,8},{4,12},{8,0},{12,4},{1,9},{5,13},{9,1},{13,5},{2,10},{6,14},... | collective-permute-start | bytes 49160 | tf_op jit(solution)/shard_map/ppermute | solution.py:381
  17.9 0.0 collective-permute-done.1.rest_2_
  17.9 0.7 %collective-permute-start.4 = (f32[32,128]{1,0:T(8,128)S(1)}, f32[32,128]{1,0:T(8,128)S(1)}, u32[]{:S(2)}, u32[]{:S(2)}) collective-permute-start(f32[32,128]{1,0:T(8,128)S(1)} %rank_inner.1), channel_id=1, source_target_pairs={{0,0},{6,1},{10,2},{12,3},{2,4},{4,5},{8,6},{14,7},{1,8},{7,9},{11... | collective-permute-start | bytes 49160 | tf_op jit(solution)/shard_map/ppermute | solution.py:435
  18.6 0.0 collective-permute-done.2.rest_3_
  18.6 0.0 copy-done
  18.6 4.8 %base_projection.1 = (f32[64,256]{1,0:T(8,128)S(1)}, f32[32,128]{1,0:T(8,128)S(1)}) custom-call(f32[64,128]{1,0:T(8,128)S(1)} %get-tuple-element.18.gain_ref, bf16[2,2048,2,256]{3,2,1,0:T(2,128)(2,1)S(1)} %get-tuple-element.19.staged_ref, bf16[8192,2,256]{2,1,0:T(2,128)(2,1)} %weight_ref.3, bf16[4,8,2048]{2,1,0:T(8,128)(2,1)S(1)} %copy-done, ...), custom_call_target="tpu_custom_call" | custom-call | flops 562036736 | bytes 9437184 | tf_op jit(solution)/shard_map/base_projection/pallas_call | solution.py:282
  23.5 0.0 collective-permute-done.4.rest_6_
  23.5 4.0 %collective-permute-start.5 = (f32[32,128]{1,0:T(8,128)S(1)}, f32[32,128]{1,0:T(8,128)S(1)}, u32[]{:S(2)}, u32[]{:S(2)}) collective-permute-start(f32[32,128]{1,0:T(8,128)S(1)} %collective-permute-done.4.rest_6_), channel_id=1, source_target_pairs={{0,2},{1,3},{2,0},{3,1},{4,6},{5,7},{6,4},{7,5},{8,10},{9,11},{10,... | collective-permute-start | bytes 49160 | tf_op jit(solution)/shard_map/ppermute | solution.py:381
  27.5 0.0 collective-permute-start.6
  27.5 0.0 collective-permute-done.10.rest_13_
  27.5 0.2 collective-permute-start.7
  27.7 0.0 collective-permute-done.8.rest_11_
  27.7 0.0 collective-permute-done.9.rest_12_
  27.7 1.5 %collective-permute-done.5.rest_7_ = f32[32,128]{1,0:T(8,128)S(1)} collective-permute-done((f32[32,128]{1,0:T(8,128)S(1)}, f32[32,128]{1,0:T(8,128)S(1)}, u32[]{:S(2)}, u32[]{:S(2)}) %collective-permute-start.5) | collective-permute-done | bytes 16416 | tf_op jit(solution)/shard_map/ppermute | solution.py:381
  29.2 1.4 %collective-permute-done.6.rest_8_ = f32[32,128]{1,0:T(8,128)S(1)} collective-permute-done((f32[32,128]{1,0:T(8,128)S(1)}, f32[32,128]{1,0:T(8,128)S(1)}, u32[]{:S(2)}, u32[]{:S(2)}) %collective-permute-start.6) | collective-permute-done | bytes 16416 | tf_op jit(solution)/shard_map/ppermute | solution.py:381
  30.7 0.0 collective-permute-done.7.rest_9_
  30.7 1.5 %fresh_attention.1 = (bf16[4,8,256]{2,1,0:T(8,128)(2,1)}, bf16[4,8,256]{2,1,0:T(8,128)(2,1)}, bf16[4,8,2048]{2,1,0:T(8,128)(2,1)}) custom-call(f32[64,256]{1,0:T(8,128)S(1)} %get-tuple-element.20.base_ref, f32[32,128]{1,0:T(8,128)S(1)} %get-tuple-element.23.square_ref, bf16[2,256]{1,0:T(2,128)(2,1)S(1)} %get-tuple-element.24.bias_ref, ...), custom_call_target="tpu_custom_call" | custom-call | tf_op jit(solution)/shard_map/fresh_attention/pallas_call | solution.py:369
Async XLA Ops:
  0.6 13.4 %collective-permute-start.3 = (bf16[4,8,2048]{2,1,0:T(8,128)(2,1)}, bf16[4,8,2048]{2,1,0:T(8,128)(2,1)S(1)}, u32[]{:S(2)}, u32[]{:S(2)}) collective-permute-start(bf16[4,8,2048]{2,1,0:T(8,128)(2,1)} %rest_0_.1), channel_id=1, source_target_pairs={{0,0},{1,6},{2,10},{3,12},{4,2},{5,4},{6,8},{7,14},{8,1},{9,7},{10... | collective-permute-start | bytes 393224 | tf_op jit(solution)/shard_map/ppermute | solution.py:417
  2.2 12.2 %collective-permute-start = (bf16[4,8,2048]{2,1,0:T(8,128)(2,1)}, bf16[4,8,2048]{2,1,0:T(8,128)(2,1)S(1)}, u32[]{:S(2)}, u32[]{:S(2)}) collective-permute-start(bf16[4,8,2048]{2,1,0:T(8,128)(2,1)} %rest_0_.1), channel_id=1, source_target_pairs={{0,1},{1,0},{2,3},{3,2},{4,5},{5,4},{6,7},{7,6},{8,9},{9,8},{10,11... | collective-permute-start | bytes 393224 | tf_op jit(solution)/shard_map/ppermute | solution.py:381
  6.7 11.3 %collective-permute-start.1 = (bf16[4,8,2048]{2,1,0:T(8,128)(2,1)}, bf16[4,8,2048]{2,1,0:T(8,128)(2,1)S(1)}, u32[]{:S(2)}, u32[]{:S(2)}) collective-permute-start(bf16[4,8,2048]{2,1,0:T(8,128)(2,1)} %rest_0_.1), channel_id=1, source_target_pairs={{0,2},{1,3},{2,0},{3,1},{4,6},{5,7},{6,4},{7,5},{8,10},{9,11},{10,... | collective-permute-start | bytes 393224 | tf_op jit(solution)/shard_map/ppermute | solution.py:381
  9.2 9.4 %collective-permute-start.2 = (bf16[4,8,2048]{2,1,0:T(8,128)(2,1)}, bf16[4,8,2048]{2,1,0:T(8,128)(2,1)S(1)}, u32[]{:S(2)}, u32[]{:S(2)}) collective-permute-start(bf16[4,8,2048]{2,1,0:T(8,128)(2,1)} %rest_0_.1), channel_id=1, source_target_pairs={{0,3},{1,2},{2,1},{3,0},{4,7},{5,6},{6,5},{7,4},{8,11},{9,10},{10,... | collective-permute-start | bytes 393224 | tf_op jit(solution)/shard_map/ppermute | solution.py:381
  9.2 18.3 %collective-permute-start.10 = (bf16[2,16,256]{2,1,0:T(8,128)(2,1)}, bf16[2,16,256]{2,1,0:T(8,128)(2,1)S(1)}, u32[]{:S(2)}, u32[]{:S(2)}) collective-permute-start(bf16[2,16,256]{2,1,0:T(8,128)(2,1)} %bitcast.3), channel_id=1, source_target_pairs={{0,12},{4,8},{8,4},{12,0},{1,13},{5,9},{9,5},{13,1},{2,14},{6,10},... | collective-permute-start | bytes 49160 | tf_op jit(solution)/shard_map/ppermute | solution.py:381
  10.1 3.9 %copy-start.1 = (bf16[2,256,16]{1,2,0:T(8,128)(2,1)S(1)}, bf16[2,256,16]{1,2,0:T(8,128)(2,1)}, u32[]{:S(2)}) copy-start(bf16[2,256,16]{1,2,0:T(8,128)(2,1)} %param.15) | copy-start | bytes 49156
  10.1 8.5 %copy-start = (bf16[4,8,2048]{2,1,0:T(8,128)(2,1)S(1)}, bf16[4,8,2048]{2,1,0:T(8,128)(2,1)}, u32[]{:S(2)}) copy-start(bf16[4,8,2048]{2,1,0:T(8,128)(2,1)} %rest_0_.1) | copy-start | bytes 393220
  14.0 13.7 %collective-permute-start.8 = (bf16[2,16,256]{2,1,0:T(8,128)(2,1)S(1)}, bf16[2,16,256]{2,1,0:T(8,128)(2,1)S(1)}, u32[]{:S(2)}, u32[]{:S(2)}) collective-permute-start(bf16[2,16,256]{2,1,0:T(8,128)(2,1)S(1)} %bitcast.5), channel_id=1, source_target_pairs={{0,4},{4,0},{8,12},{12,8},{1,5},{5,1},{9,13},{13,9},{2,6},{6,2},{1... | collective-permute-start | bytes 49160 | tf_op jit(solution)/shard_map/ppermute | solution.py:381
  14.4 13.3 %collective-permute-start.9 = (bf16[2,16,256]{2,1,0:T(8,128)(2,1)S(1)}, bf16[2,16,256]{2,1,0:T(8,128)(2,1)S(1)}, u32[]{:S(2)}, u32[]{:S(2)}) collective-permute-start(bf16[2,16,256]{2,1,0:T(8,128)(2,1)S(1)} %bitcast.6), channel_id=1, source_target_pairs={{0,8},{4,12},{8,0},{12,4},{1,9},{5,13},{9,1},{13,5},{2,10},{6,14},... | collective-permute-start | bytes 49160 | tf_op jit(solution)/shard_map/ppermute | solution.py:381
  17.9 5.5 %collective-permute-start.4 = (f32[32,128]{1,0:T(8,128)S(1)}, f32[32,128]{1,0:T(8,128)S(1)}, u32[]{:S(2)}, u32[]{:S(2)}) collective-permute-start(f32[32,128]{1,0:T(8,128)S(1)} %rank_inner.1), channel_id=1, source_target_pairs={{0,0},{6,1},{10,2},{12,3},{2,4},{4,5},{8,6},{14,7},{1,8},{7,9},{11... | collective-permute-start | bytes 49160 | tf_op jit(solution)/shard_map/ppermute | solution.py:435
  23.5 5.8 %collective-permute-start.5 = (f32[32,128]{1,0:T(8,128)S(1)}, f32[32,128]{1,0:T(8,128)S(1)}, u32[]{:S(2)}, u32[]{:S(2)}) collective-permute-start(f32[32,128]{1,0:T(8,128)S(1)} %collective-permute-done.4.rest_6_), channel_id=1, source_target_pairs={{0,2},{1,3},{2,0},{3,1},{4,6},{5,7},{6,4},{7,5},{8,10},{9,11},{10,... | collective-permute-start | bytes 49160 | tf_op jit(solution)/shard_map/ppermute | solution.py:381
  27.5 3.2 %collective-permute-start.6 = (f32[32,128]{1,0:T(8,128)S(1)}, f32[32,128]{1,0:T(8,128)S(1)}, u32[]{:S(2)}, u32[]{:S(2)}) collective-permute-start(f32[32,128]{1,0:T(8,128)S(1)} %collective-permute-done.4.rest_6_), channel_id=1, source_target_pairs={{0,3},{1,2},{2,1},{3,0},{4,7},{5,6},{6,5},{7,4},{8,11},{9,10},{10,... | collective-permute-start | bytes 49160 | tf_op jit(solution)/shard_map/ppermute | solution.py:381
  27.5 3.2 %collective-permute-start.7 = (f32[32,128]{1,0:T(8,128)S(1)}, f32[32,128]{1,0:T(8,128)S(1)}, u32[]{:S(2)}, u32[]{:S(2)}) collective-permute-start(f32[32,128]{1,0:T(8,128)S(1)} %collective-permute-done.4.rest_6_), channel_id=1, source_target_pairs={{0,1},{1,0},{2,3},{3,2},{4,5},{5,4},{6,7},{7,6},{8,9},{9,8},{10,11... | collective-permute-start | bytes 49160 | tf_op jit(solution)/shard_map/ppermute | solution.py:381

commit v5 on v4

--- a/solution.py
+++ b/solution.py
@@ -41,15 +41,11 @@
     query_ref,
     key_ref,
     value_ref,
-    down_ref,
     gain_ref,
-    up_ref,
     bias_ref,
     weight_ref,
     weight_out,
-    down_out,
     gain_out,
-    up_out,
     bias_out,
     query_out,
     acc_out,
@@ -80,8 +76,6 @@
         (value_ref.at[halves[0]], value_buffer.at[halves[0]]),
         (value_ref.at[halves[1]], value_buffer.at[halves[1]]),
         (gain_ref, gain_buffer),
-        (down_ref, down_out),
-        (up_ref, up_out),
         (bias_ref, bias_out),
     ]
     me = lax.axis_index("tp")
@@ -147,21 +141,19 @@
         copy.wait()
 
 
-def cache_call(staged, part_width, lengths, queries, keys, values, down, gain, up, bias, weight):
+def cache_call(staged, part_width, lengths, queries, keys, values, gain, bias, weight):
     steps, rows, query_width = queries.shape
     cache_span, key_width = keys.shape[1:]
     groups = key_width // HD
     lines = steps * (query_width // key_width)
     block = (groups, lines * rows, HD)
     table = (steps * rows, HD)
-    operands = (lengths, queries, keys, values, down, gain, up, bias, weight)
+    operands = (lengths, queries, keys, values, gain, bias, weight)
     return pl.pallas_call(
         functools.partial(cache_kernel, staged),
         out_shape=(
             pltpu.VMEM((len(staged), part_width) + weight.shape[1:], weight.dtype),
-            pltpu.VMEM(down.shape, down.dtype),
             pltpu.VMEM(gain.shape, jnp.float32),
-            pltpu.VMEM(up.shape, up.dtype),
             pltpu.VMEM(bias.shape, bias.dtype),
             pltpu.VMEM(block, jnp.float32),
             pltpu.VMEM(block, jnp.float32),
@@ -171,7 +163,7 @@
             pltpu.VMEM(table, jnp.float32),
         ),
         in_specs=[HBM] * len(operands),
-        out_specs=(VMEM,) * 11,
+        out_specs=(VMEM,) * 9,
         scratch_shapes=[
             pltpu.SMEM(lengths.shape, jnp.int32),
             pltpu.VMEM(queries.shape, queries.dtype),
@@ -179,7 +171,7 @@
             pltpu.VMEM(keys.shape, keys.dtype),
             pltpu.VMEM(values.shape, values.dtype),
             pltpu.VMEM((rows * groups, lines, cache_span), jnp.float32),
-            pltpu.SemaphoreType.DMA((10 + len(staged),)),
+            pltpu.SemaphoreType.DMA((8 + len(staged),)),
         ],
         compiler_params=pltpu.CompilerParams(vmem_limit_bytes=16 << 20),
         cost_estimate=pl.CostEstimate(flops=2 * 67 << 20, bytes_accessed=9 << 20, transcendentals=0),
@@ -187,54 +179,74 @@
     )(*[pltpu.with_memory_space_constraint(x, pltpu.HBM) for x in operands])
 
 
-def scaled_chunks(block, gain, start):
-    chunks = []
-    for i in range(block.shape[1] // HD):
-        chunk = block[:, i * HD : (i + 1) * HD]
-        chunks.append((chunk * gain[start + i : start + i + 1]).astype(jnp.bfloat16))
-    return chunks
-
-
 def rows_of(ref):
-    steps = ref.shape[0]
-    return jnp.concatenate([ref[s].astype(jnp.float32) for s in range(steps)], axis=0)
-
-
-def inner_kernel(hidden_ref, gain_ref, down_ref, out_ref):
-    width = hidden_ref.shape[2]
-    start = pl.multiple_of(lax.axis_index("wide") * (width // HD), width // HD)
-    gain = gain_ref[pl.ds(start, width // HD)]
-    scaled = jnp.concatenate(scaled_chunks(rows_of(hidden_ref), gain, 0), axis=1)
-    ranks = down_ref.shape[1]
-    for kind in range(down_ref.shape[0]):
-        out_ref[:, kind * ranks : (kind + 1) * ranks] = lax.dot_general(
-            scaled,
-            down_ref[kind],
+    return jnp.concatenate([ref[s].astype(jnp.float32) for s in range(ref.shape[0])], axis=0)
+
+
+def pack_kernel(down_ref, up_ref, out_ref, sems):
+    share = out_ref.shape[1]
+    width = down_ref.shape[2]
+    at = pl.ds(pl.multiple_of(lax.axis_index("tp") * share, share), share)
+    down = pltpu.make_async_copy(
+        down_ref.at[:, at, :], out_ref.at[:, :, pl.ds(0, width)], sems.at[0]
+    )
+    up = pltpu.make_async_copy(
+        up_ref, out_ref.at[:, :, pl.ds(width, up_ref.shape[2])], sems.at[1]
+    )
+    down.start()
+    up.start()
+    down.wait()
+    up.wait()
+
+
+def pack_call(down, up):
+    kinds, share, columns = up.shape
+    return pl.pallas_call(
+        pack_kernel,
+        out_shape=pltpu.VMEM((kinds, share, down.shape[2] + columns), down.dtype),
+        in_specs=[HBM] * 2,
+        out_specs=VMEM,
+        scratch_shapes=[pltpu.SemaphoreType.DMA((2,))],
+        name="pack_factors",
+    )(*[pltpu.with_memory_space_constraint(x, pltpu.HBM) for x in (down, up)])
+
+
+def inner_kernel(scaled_ref, *rest):
+    packs, out_ref = rest[:-1], rest[-1]
+    me = lax.axis_index("wide")
+    width = scaled_ref.shape[2]
+    total = None
+    for offset, pack in enumerate(packs):
+        part = lax.dot_general(
+            scaled_ref[me ^ offset],
+            pack[:, :, :width].reshape(out_ref.shape[1], width),
             (((1,), (1,)), ((), ())),
             preferred_element_type=jnp.float32,
         )
-
-
-def inner_call(hidden, gain, down):
-    steps, rows, _ = hidden.shape
-    kinds, ranks, _ = down.shape
+        total = part if total is None else total + part
+    out_ref[...] = total
+
+
+def inner_call(scaled, packs):
+    kinds, share, _ = packs[0].shape
     return pl.pallas_call(
         inner_kernel,
-        out_shape=jax.ShapeDtypeStruct((steps * rows, kinds * ranks), jnp.float32),
-        in_specs=[VMEM] * 3,
+        out_shape=jax.ShapeDtypeStruct((scaled.shape[1], kinds * share), jnp.float32),
+        in_specs=[VMEM] * (1 + len(packs)),
         out_specs=VMEM,
         compiler_params=pltpu.CompilerParams(vmem_limit_bytes=8 << 20),
         name="rank_inner",
-    )(hidden, gain, down)
+    )(scaled, *packs)
 
 
 def base_kernel(staged, streamed, gain_ref, staged_ref, weight_ref, *rest):
     offsets = staged + streamed
     parts = rest[: len(offsets)]
-    base_out, square_out, spread, buffer, sems = rest[len(offsets) :]
+    base_out, square_out, scaled_out, buffer, sems = rest[len(offsets) :]
     steps, rows, width = parts[0].shape
     count = steps * rows
     kinds, columns = weight_ref.shape[1:]
+    chunks = width // HD
     me = lax.axis_index("tp")
     copies = []
     for i, offset in enumerate(streamed):
@@ -243,35 +255,39 @@
         )
         copy.start()
         copies.append(copy)
-    lane = lax.broadcasted_iota(jnp.int32, (count, HD), 1)
-    low, high = lane // 2, lane // 2 + HD // 2
-    even = lane % 2 == 0
+    feature = lax.broadcasted_iota(jnp.int32, (HD, kinds * kinds * HD), 0)
+    place = lax.broadcasted_iota(jnp.int32, (HD, kinds * kinds * HD), 1)
+    kind = place // (kinds * HD)
+    spreader = jnp.where(feature * kinds + kind == place % (kinds * HD), 1.0, 0.0).astype(jnp.bfloat16)
     squares = jnp.zeros((count, HD), jnp.float32)
-    acc = None
+    acc = jnp.zeros((kinds * count, columns), jnp.float32)
     for k, (offset, part) in enumerate(zip(offsets, parts)):
-        start = pl.multiple_of((me ^ offset) * (width // HD), width // HD)
-        gain = gain_ref[pl.ds(start, width // HD)]
+        start = pl.multiple_of((me ^ offset) * chunks, chunks)
+        gain = gain_ref[pl.ds(start, chunks)]
         values = rows_of(part)
-        for i in range(width // HD):
+        scaled = []
+        for i in range(chunks):
             chunk = values[:, i * HD : (i + 1) * HD]
             squares += chunk * chunk
-            chunk = chunk * gain[i : i + 1]
-            for j, index in enumerate((low, high)):
-                wide = jnp.take_along_axis(chunk, index, axis=1)
-                at = pl.ds((2 * i + j) * HD, HD)
-                spread[k, :count, at] = jnp.where(even, wide, 0.0).astype(jnp.bfloat16)
-                spread[k, count:, at] = jnp.where(even, 0.0, wide).astype(jnp.bfloat16)
+            scaled.append((chunk * gain[i : i + 1]).astype(jnp.bfloat16))
+            scaled_out[me ^ offset, :, i * HD : (i + 1) * HD] = scaled[i]
+        spread = jnp.dot(
+            jnp.concatenate(scaled, axis=0), spreader, preferred_element_type=jnp.float32
+        ).astype(jnp.bfloat16)
         if k < len(staged):
             block = staged_ref.at[k]
         else:
             copies[k - len(staged)].wait()
             block = buffer.at[k - len(staged)]
-        product = jnp.dot(
-            spread[k],
-            block.reshape(width * kinds, columns)[...],
-            preferred_element_type=jnp.float32,
-        )
-        acc = product if acc is None else acc + product
+        flat = block.reshape(width * kinds, columns)
+        for i in range(chunks):
+            lines = spread[i * count : (i + 1) * count]
+            lines = jnp.concatenate(
+                [lines[:, j * kinds * HD : (j + 1) * kinds * HD] for j in range(kinds)], axis=0
+            )
+            acc += jnp.dot(
+                lines, flat[pl.ds(i * HD * kinds, HD * kinds), :], preferred_element_type=jnp.float32
+            )
     base_out[...] = acc
     square_out[...] = jnp.broadcast_to(jnp.sum(squares, axis=1, keepdims=True), squares.shape)
 
@@ -284,11 +300,11 @@
         out_shape=(
             pltpu.VMEM((kinds * steps * rows, columns), jnp.float32),
             pltpu.VMEM((steps * rows, HD), jnp.float32),
+            pltpu.VMEM((len(parts), steps * rows, width), jnp.bfloat16),
         ),
         in_specs=[VMEM, VMEM, HBM] + [VMEM] * len(parts),
-        out_specs=(VMEM, VMEM),
+        out_specs=(VMEM,) * 3,
         scratch_shapes=[
-            pltpu.VMEM((len(parts), kinds * steps * rows, kinds * width), jnp.bfloat16),
             pltpu.VMEM((len(streamed), width, kinds, columns), weight.dtype),
             pltpu.SemaphoreType.DMA((len(streamed),)),
         ],
@@ -298,34 +314,32 @@
     )(gain, staged_weight, pltpu.with_memory_space_constraint(weight, pltpu.HBM), *parts)
 
 
-def final_kernel(width, inner_count, up_count, base_ref, square_ref, bias_ref, *rest):
+def final_kernel(width, blocks, base_ref, square_ref, bias_ref, *rest):
     query_ref, acc_ref, top_ref, total_ref, cos_ref, sin_ref = rest[:6]
-    inner_refs = rest[6 : 6 + inner_count]
-    up_refs = rest[6 + inner_count : 6 + inner_count + up_count]
-    keys_out, values_out, attended_out, up_buffer = rest[6 + inner_count + up_count :]
+    inner_refs = rest[6 : 6 + blocks]
+    up_refs = rest[6 + blocks : 6 + 2 * blocks]
+    keys_out, values_out, attended_out, inner_buffer, up_buffer = rest[6 + 2 * blocks :]
     steps, rows, columns = keys_out.shape
     count = steps * rows
     groups, size, _ = query_ref.shape
     per_group = size // count
-    kinds = bias_ref.shape[0]
+    kinds, share, pack_width = up_refs[0].shape
     row_scale = lax.rsqrt(square_ref[:, :1] * (1.0 / width) + norm_eps)
-    inner = inner_refs[0][...]
-    for ref in inner_refs[1:]:
-        inner = inner + ref[...]
-    high = inner.astype(jnp.bfloat16)
-    low = (inner - high.astype(jnp.float32)).astype(jnp.bfloat16)
-    ranks = inner.shape[1] // kinds
+    my_tp, my_wide = (lax.axis_index("tp"), lax.axis_index("wide")) if blocks > 1 else (0, 0)
+    for i in range(blocks):
+        inner_buffer[my_tp ^ i] = inner_refs[i][...]
+        up_buffer[my_wide ^ i] = up_refs[i][:, :, pack_width - columns :]
     bias = bias_ref[...].astype(jnp.float32)
     linear = []
-    for i, ref in enumerate(up_refs):
-        up_buffer[i] = ref[...]
-    me = lax.axis_index("wide") if up_count > 1 else 0
     for kind in range(kinds):
-        up = jnp.concatenate([up_buffer[me ^ i, kind] for i in range(up_count)], axis=0)
-        cols = slice(kind * ranks, (kind + 1) * ranks)
-        lora = jnp.dot(high[:, cols], up, preferred_element_type=jnp.float32) + jnp.dot(
-            low[:, cols], up, preferred_element_type=jnp.float32
-        )
+        lora = jnp.zeros((count, columns), jnp.float32)
+        for i in range(blocks):
+            inner = inner_buffer[i, :, kind * share : (kind + 1) * share]
+            high = inner.astype(jnp.bfloat16)
+            low = (inner - high.astype(jnp.float32)).astype(jnp.bfloat16)
+            up = up_buffer[i, kind]
+            lora += jnp.dot(high, up, preferred_element_type=jnp.float32)
+            lora += jnp.dot(low, up, preferred_element_type=jnp.float32)
         base = base_ref[kind * count : (kind + 1) * count]
         linear.append((base + adapter_scale * lora) * row_scale + bias[kind : kind + 1])
     cosine, sine = cos_ref[...], sin_ref[...]
@@ -365,13 +379,17 @@
 
 def final_call(shape, width, base, square, bias, cached, inner, up):
     steps, rows, query_width = shape
-    small = jax.ShapeDtypeStruct((steps, rows, base.shape[1]), jnp.bfloat16)
+    columns = base.shape[1]
+    small = jax.ShapeDtypeStruct((steps, rows, columns), jnp.bfloat16)
     return pl.pallas_call(
-        functools.partial(final_kernel, width, len(inner), len(up)),
+        functools.partial(final_kernel, width, len(inner)),
         out_shape=(small, small, jax.ShapeDtypeStruct(shape, jnp.bfloat16)),
         in_specs=[VMEM] * (3 + len(cached) + len(inner) + len(up)),
         out_specs=(VMEM,) * 3,
-        scratch_shapes=[pltpu.VMEM((len(up),) + up[0].shape, up[0].dtype)],
+        scratch_shapes=[
+            pltpu.VMEM((len(inner),) + inner[0].shape, jnp.float32),
+            pltpu.VMEM((len(up),) + up[0].shape[:2] + (columns,), up[0].dtype),
+        ],
         compiler_params=pltpu.CompilerParams(vmem_limit_bytes=8 << 20),
         name="fresh_attention",
     )(base, square, bias, *cached, *inner, *up)
@@ -379,14 +397,6 @@
 
 def swap(block, axis, offset, count):
     return lax.ppermute(block, axis, [(i, i ^ offset) for i in range(count)])
-
-
-def meeting_place():
-    pairs = []
-    for w in range(4):
-        for t in range(4):
-            pairs.append((w * 4 + t, t * 4 + 2 * ((t // 2) ^ ((w + t) & 1)) + w // 2))
-    return pairs
 
 
 def on_device(
@@ -408,44 +418,38 @@
     kinds, ranks, down_width = adapter_down_factor.shape
     gain = input_norm_gain.reshape(width // HD, HD)
     up_part = jnp.transpose(adapter_up_factor, (0, 2, 1))
-    both = ("wide", "tp")
-
-    direct = wide_count == 4 and tp_count == 4
+    direct = wide_count == tp_count == 4
     parts = [hidden] + [swap(hidden, "tp", offset, tp_count) for offset in (1, 2, 3)]
     if direct:
-        there = meeting_place()
-        moved = lax.ppermute(hidden, both, there)
-        up = [swap(up_part, "wide", offset, 4) for offset in (1, 2, 3)]
+        pack = pack_call(adapter_down_factor, up_part)
+        packs = [pack] + [swap(pack, "wide", offset, wide_count) for offset in (1, 2, 3)]
     staged, streamed = (0, 1), (2, 3)
-    staged_weight, down, gain_rows, my_up, bias, *cached = cache_call(
+    staged_weight, gain_rows, bias, *cached = cache_call(
         staged,
         part_width,
         lengths,
         queries,
         stored_rotated_keys,
         stored_value_rows,
-        adapter_down_factor,
         gain,
-        up_part,
         key_value_bias,
         key_value_weight,
     )
+    base, square, scaled = base_call(
+        staged, streamed, gain_rows, staged_weight, key_value_weight, parts
+    )
     if direct:
-        inner = inner_call(moved, gain_rows, down)
-        inner = lax.ppermute(inner, both, [(b, a) for a, b in there])
-        up = [my_up] + up
+        inner = inner_call(scaled, packs)
+        inner = [inner] + [swap(inner, "tp", offset, tp_count) for offset in (2, 3, 1)]
+        inner = [inner[i] for i in (0, 3, 1, 2)]
+        up = packs
     else:
-        gathered = lax.all_gather(hidden, "tp", axis=2, tiled=True).astype(jnp.float32)
-        scaled = (gathered * input_norm_gain.astype(jnp.float32)).astype(jnp.bfloat16)
-        all_down = lax.all_gather(adapter_down_factor, "wide", axis=2, tiled=True)
-        inner = jnp.einsum("srd,kad->srka", scaled, all_down, preferred_element_type=jnp.float32)
-        inner = [inner.reshape(steps * rows, kinds * ranks)]
+        down = lax.all_gather(adapter_down_factor, "wide", axis=2, tiled=True)
+        down = down.reshape(kinds * ranks, tp_count, part_width)
+        inner = [
+            jnp.einsum("brd,kbd->rk", scaled, down, preferred_element_type=jnp.float32)
+        ]
         up = [lax.all_gather(up_part, "wide", axis=1, tiled=True)]
-
-    base, square = base_call(staged, streamed, gain_rows, staged_weight, key_value_weight, parts)
-    if direct:
-        inner, square = lax.optimization_barrier((inner, square))
-        inner = [inner] + [swap(inner, "tp", offset, 4) for offset in (2, 3, 1)]
     return final_call(queries.shape, width, base, square, bias, cached, inner, up)
 
 

time: 32.3 us -> 27.4 us (0.85)
  starting transfers between devices: 18 us -> 9.49 us
  waiting for transfers between devices: 2.98 us -> 6.93 us
  Pallas kernels: 10.5 us -> 9.98 us
    ppermute x9, starting transfers between devices: 15.8 us -> 9.49 us  [swap(): return lax.ppermute(block, axis, [(i, i ^ offset) for i in range(count)])]
    ppermute x9, waiting for transfers between devices: 2.98 us -> 6.93 us  [swap(): return lax.ppermute(block, axis, [(i, i ^ offset) for i in range(count)])]
    ppermute x2 -> x0, starting transfers between devices: 2.21 us -> none  [the longest x1 1.56 us: on_device(): moved = lax.ppermute(hidden, both, there)]
    pallas_call x1, Pallas kernels: 4.84 us -> 3.56 us  [base_call(): pl.pallas_call(functools.partial(base_kernel, staged, streamed), out_shap...]
    pallas_call x2 -> x3, Pallas kernels: 1.79 us -> 2.72 us  [the longest x1 1.54 us: final_call(): pl.pallas_call(functools.partial(final_kernel, width, len(inner)), out_sh...]
  transfers between devices with their start and end apart: 11 -> 9, of which waited for: 2 -> 3; matrix products, arithmetic and copies ran while one was open for 0% -> 0% of each run, Pallas kernels for 28% -> 30%
where the time goes in v5:
time: 27.4 us; the launch traced here: 27.1 us
  Pallas kernels  9.98 us (36%)
  starting transfers between devices  9.49 us (35%)
  waiting for transfers between devices  6.93 us (25%)
  between operations  0.7 us (3%)
    ppermute x9, starting transfers between devices, swap(): return lax.ppermute(block, axis, [(i, i ^ offset) for i in range(count)])  9.49 us
    ppermute x9, waiting for transfers between devices, swap(): return lax.ppermute(block, axis, [(i, i ^ offset) for i in range(count)])  6.93 us
    pallas_call x1, Pallas kernels, cache_call(): pl.pallas_call(functools.partial(cache_kernel, staged), out_shape=(pltpu....  3.7 us
    pallas_call x1, Pallas kernels, base_call(): pl.pallas_call(functools.partial(base_kernel, staged, streamed), out_shap...  3.56 us
    pallas_call x1, Pallas kernels, final_call(): pl.pallas_call(functools.partial(final_kernel, width, len(inner)), out_sh...  1.54 us
    pallas_call x1, Pallas kernels, pack_call(): pl.pallas_call(pack_kernel, out_shape=pltpu.VMEM((kinds, share, down.shap...  0.92 us
  transfers between devices with their start and end apart: 9, of which 3 were waited for; matrix products, arithmetic and copies ran while one was open for 0% of the time, Pallas kernels for 30%

profile of v5, /device:TPU:0, one launch (start us, length us, event | category | flops | bytes accessed | tf_op | source)
XLA Modules:
  0.0 27.1 jit_solution(4437636692550188664)
XLA Ops:
  0.6 0.5 %collective-permute-start = (bf16[4,8,2048]{2,1,0:T(8,128)(2,1)}, bf16[4,8,2048]{2,1,0:T(8,128)(2,1)S(1)}, u32[]{:S(2)}, u32[]{:S(2)}) collective-permute-start(bf16[4,8,2048]{2,1,0:T(8,128)(2,1)} %rest_0_.1), channel_id=1, source_target_pairs={{0,1},{1,0},{2,3},{3,2},{4,5},{5,4},{6,7},{7,6},{8,9},{9,8},{10,11... | collective-permute-start | bytes 393224 | tf_op jit(solution)/shard_map/ppermute | solution.py:399
  1.1 2.6 %collective-permute-start.1 = (bf16[4,8,2048]{2,1,0:T(8,128)(2,1)}, bf16[4,8,2048]{2,1,0:T(8,128)(2,1)S(1)}, u32[]{:S(2)}, u32[]{:S(2)}) collective-permute-start(bf16[4,8,2048]{2,1,0:T(8,128)(2,1)} %rest_0_.1), channel_id=1, source_target_pairs={{0,2},{1,3},{2,0},{3,1},{4,6},{5,7},{6,4},{7,5},{8,10},{9,11},{10,... | collective-permute-start | bytes 393224 | tf_op jit(solution)/shard_map/ppermute | solution.py:399
  3.7 0.1 collective-permute-start.2
  3.8 0.9 %pack_factors.1.rest_0_.rest_10_ = bf16[2,16,2304]{2,1,0:T(8,128)(2,1)S(1)} custom-call(bf16[2,64,2048]{2,1,0:T(8,128)(2,1)} %down_ref.1, bf16[2,16,256]{2,1,0:T(8,128)(2,1)} %bitcast.3), custom_call_target="tpu_custom_call" | custom-call | tf_op jit(solution)/shard_map/pack_factors/pallas_call | solution.py:204
  4.7 1.9 %collective-permute-start.3 = (bf16[2,16,2304]{2,1,0:T(8,128)(2,1)S(1)}, bf16[2,16,2304]{2,1,0:T(8,128)(2,1)S(1)}, u32[]{:S(2)}, u32[]{:S(2)}) collective-permute-start(bf16[2,16,2304]{2,1,0:T(8,128)(2,1)S(1)} %pack_factors.1.rest_0_.rest_10_), channel_id=1, source_target_pairs={{0,4},{4,0},{8,12},{12,8},{1,5},{5,1},{9,13},{13,9},{2,6},{6,2},{1... | collective-permute-start | bytes 442376 | tf_op jit(solution)/shard_map/ppermute | solution.py:399
  6.6 2.6 %collective-permute-start.4 = (bf16[2,16,2304]{2,1,0:T(8,128)(2,1)S(1)}, bf16[2,16,2304]{2,1,0:T(8,128)(2,1)S(1)}, u32[]{:S(2)}, u32[]{:S(2)}) collective-permute-start(bf16[2,16,2304]{2,1,0:T(8,128)(2,1)S(1)} %pack_factors.1.rest_0_.rest_10_), channel_id=1, source_target_pairs={{0,8},{4,12},{8,0},{12,4},{1,9},{5,13},{9,1},{13,5},{2,10},{6,14},... | collective-permute-start | bytes 442376 | tf_op jit(solution)/shard_map/ppermute | solution.py:399
  9.2 0.0 collective-permute-done.rest_1_
  9.2 0.0 collective-permute-start.5
  9.2 0.0 copy-start
  9.2 3.7 %cache_attention.1 = (bf16[2,2048,2,256]{3,2,1,0:T(2,128)(2,1)S(1)}, f32[64,128]{1,0:T(8,128)S(1)}, bf16[2,256]{1,0:T(2,128)(2,1)S(1)}, f32[2,256,128]{2,1,0:T(8...) custom-call(s32[8]{0:T(128)} %lengths_ref.1, ...), custom_call_target="tpu_custom_call" | custom-call | flops 140509184 | bytes 9437184 | tf_op jit(solution)/shard_map/cache_attention/pallas_call | solution.py:152
  12.9 0.0 collective-permute-done.1.rest_2_
  12.9 0.0 collective-permute-done.2.rest_3_
  12.9 0.0 copy-done
  12.9 3.6 %base_projection.1 = (f32[64,256]{1,0:T(8,128)S(1)}, f32[32,128]{1,0:T(8,128)S(1)}, bf16[4,32,2048]{2,1,0:T(8,128)(2,1)S(1)}) custom-call(f32[64,128]{1,0:T(8,128)S(1)} %get-tuple-element.15.gain_ref, bf16[2,2048,2,256]{3,2,1,0:T(2,128)(2,1)S(1)} %get-tuple-element.16.staged_ref, bf16[8192,2,256]{2,1,0:T(2,128)(2,1)} %weight_ref.3, ...), custom_call_target="tpu_custom_call" | custom-call | flops 562036736 | bytes 9437184 | tf_op jit(solution)/shard_map/base_projection/pallas_call | solution.py:298
  16.5 0.0 collective-permute-done.3.rest_1_.rest_11_
  16.5 4.1 %collective-permute-done.4.rest_2_.rest_12_ = bf16[2,16,2304]{2,1,0:T(8,128)(2,1)S(1)} collective-permute-done((bf16[2,16,2304]{2,1,0:T(8,128)(2,1)S(1)}, bf16[2,16,2304]{2,1,0:T(8,128)(2,1)S(1)}, u32[]{:S(2)}, u32[]{:S(2)}) %collective-permute-start.4) | collective-permute-done | bytes 147488 | tf_op jit(solution)/shard_map/ppermute | solution.py:399
  20.6 0.0 collective-permute-done.5.rest_3_.rest_13_
  20.6 0.3 rank_inner.1.rest_6_
  20.8 0.0 collective-permute-start.6
  20.8 1.6 %collective-permute-start.7 = (f32[32,32]{1,0:T(8,128)S(1)}, f32[32,32]{1,0:T(8,128)S(1)}, u32[]{:S(2)}, u32[]{:S(2)}) collective-permute-start(f32[32,32]{1,0:T(8,128)S(1)} %rank_inner.1.rest_6_), channel_id=1, source_target_pairs={{0,2},{1,3},{2,0},{3,1},{4,6},{5,7},{6,4},{7,5},{8,10},{9,11},{10,... | collective-permute-start | bytes 12296 | tf_op jit(solution)/shard_map/ppermute | solution.py:399
  22.4 0.3 %collective-permute-start.8 = (f32[32,32]{1,0:T(8,128)S(1)}, f32[32,32]{1,0:T(8,128)S(1)}, u32[]{:S(2)}, u32[]{:S(2)}) collective-permute-start(f32[32,32]{1,0:T(8,128)S(1)} %rank_inner.1.rest_6_), channel_id=1, source_target_pairs={{0,3},{1,2},{2,1},{3,0},{4,7},{5,6},{6,5},{7,4},{8,11},{9,10},{10,... | collective-permute-start | bytes 12296 | tf_op jit(solution)/shard_map/ppermute | solution.py:399
  22.7 0.0 collective-permute-done.6.rest_7_
  22.7 1.9 %collective-permute-done.7.rest_8_ = f32[32,32]{1,0:T(8,128)S(1)} collective-permute-done((f32[32,32]{1,0:T(8,128)S(1)}, f32[32,32]{1,0:T(8,128)S(1)}, u32[]{:S(2)}, u32[]{:S(2)}) %collective-permute-start.7) | collective-permute-done | bytes 4128 | tf_op jit(solution)/shard_map/ppermute | solution.py:399
  24.7 0.9 %collective-permute-done.8.rest_9_ = f32[32,32]{1,0:T(8,128)S(1)} collective-permute-done((f32[32,32]{1,0:T(8,128)S(1)}, f32[32,32]{1,0:T(8,128)S(1)}, u32[]{:S(2)}, u32[]{:S(2)}) %collective-permute-start.8) | collective-permute-done | bytes 4128 | tf_op jit(solution)/shard_map/ppermute | solution.py:399
  25.6 1.5 %fresh_attention.1 = (bf16[4,8,256]{2,1,0:T(8,128)(2,1)}, bf16[4,8,256]{2,1,0:T(8,128)(2,1)}, bf16[4,8,2048]{2,1,0:T(8,128)(2,1)}) custom-call(f32[64,256]{1,0:T(8,128)S(1)} %get-tuple-element.17.base_ref, f32[32,128]{1,0:T(8,128)S(1)} %get-tuple-element.18.square_ref, bf16[2,256]{1,0:T(2,128)(2,1)S(1)} %get-tuple-element.19.bias_ref, ...), custom_call_target="tpu_custom_call" | custom-call | tf_op jit(solution)/shard_map/fresh_attention/pallas_call | solution.py:384
Async XLA Ops:
  0.6 8.6 %collective-permute-start = (bf16[4,8,2048]{2,1,0:T(8,128)(2,1)}, bf16[4,8,2048]{2,1,0:T(8,128)(2,1)S(1)}, u32[]{:S(2)}, u32[]{:S(2)}) collective-permute-start(bf16[4,8,2048]{2,1,0:T(8,128)(2,1)} %rest_0_.1), channel_id=1, source_target_pairs={{0,1},{1,0},{2,3},{3,2},{4,5},{5,4},{6,7},{7,6},{8,9},{9,8},{10,11... | collective-permute-start | bytes 393224 | tf_op jit(solution)/shard_map/ppermute | solution.py:399
  1.1 11.8 %collective-permute-start.1 = (bf16[4,8,2048]{2,1,0:T(8,128)(2,1)}, bf16[4,8,2048]{2,1,0:T(8,128)(2,1)S(1)}, u32[]{:S(2)}, u32[]{:S(2)}) collective-permute-start(bf16[4,8,2048]{2,1,0:T(8,128)(2,1)} %rest_0_.1), channel_id=1, source_target_pairs={{0,2},{1,3},{2,0},{3,1},{4,6},{5,7},{6,4},{7,5},{8,10},{9,11},{10,... | collective-permute-start | bytes 393224 | tf_op jit(solution)/shard_map/ppermute | solution.py:399
  3.7 9.2 %collective-permute-start.2 = (bf16[4,8,2048]{2,1,0:T(8,128)(2,1)}, bf16[4,8,2048]{2,1,0:T(8,128)(2,1)S(1)}, u32[]{:S(2)}, u32[]{:S(2)}) collective-permute-start(bf16[4,8,2048]{2,1,0:T(8,128)(2,1)} %rest_0_.1), channel_id=1, source_target_pairs={{0,3},{1,2},{2,1},{3,0},{4,7},{5,6},{6,5},{7,4},{8,11},{9,10},{10,... | collective-permute-start | bytes 393224 | tf_op jit(solution)/shard_map/ppermute | solution.py:399
  4.7 11.8 %collective-permute-start.3 = (bf16[2,16,2304]{2,1,0:T(8,128)(2,1)S(1)}, bf16[2,16,2304]{2,1,0:T(8,128)(2,1)S(1)}, u32[]{:S(2)}, u32[]{:S(2)}) collective-permute-start(bf16[2,16,2304]{2,1,0:T(8,128)(2,1)S(1)} %pack_factors.1.rest_0_.rest_10_), channel_id=1, source_target_pairs={{0,4},{4,0},{8,12},{12,8},{1,5},{5,1},{9,13},{13,9},{2,6},{6,2},{1... | collective-permute-start | bytes 442376 | tf_op jit(solution)/shard_map/ppermute | solution.py:399
  6.6 14.0 %collective-permute-start.4 = (bf16[2,16,2304]{2,1,0:T(8,128)(2,1)S(1)}, bf16[2,16,2304]{2,1,0:T(8,128)(2,1)S(1)}, u32[]{:S(2)}, u32[]{:S(2)}) collective-permute-start(bf16[2,16,2304]{2,1,0:T(8,128)(2,1)S(1)} %pack_factors.1.rest_0_.rest_10_), channel_id=1, source_target_pairs={{0,8},{4,12},{8,0},{12,4},{1,9},{5,13},{9,1},{13,5},{2,10},{6,14},... | collective-permute-start | bytes 442376 | tf_op jit(solution)/shard_map/ppermute | solution.py:399
  9.2 11.4 %collective-permute-start.5 = (bf16[2,16,2304]{2,1,0:T(8,128)(2,1)S(1)}, bf16[2,16,2304]{2,1,0:T(8,128)(2,1)S(1)}, u32[]{:S(2)}, u32[]{:S(2)}) collective-permute-start(bf16[2,16,2304]{2,1,0:T(8,128)(2,1)S(1)} %pack_factors.1.rest_0_.rest_10_), channel_id=1, source_target_pairs={{0,12},{4,8},{8,4},{12,0},{1,13},{5,9},{9,5},{13,1},{2,14},{6,10},... | collective-permute-start | bytes 442376 | tf_op jit(solution)/shard_map/ppermute | solution.py:399
  9.2 3.7 %copy-start = (bf16[4,8,2048]{2,1,0:T(8,128)(2,1)S(1)}, bf16[4,8,2048]{2,1,0:T(8,128)(2,1)}, u32[]{:S(2)}) copy-start(bf16[4,8,2048]{2,1,0:T(8,128)(2,1)} %rest_0_.1) | copy-start | bytes 393220
  20.8 1.9 %collective-permute-start.6 = (f32[32,32]{1,0:T(8,128)S(1)}, f32[32,32]{1,0:T(8,128)S(1)}, u32[]{:S(2)}, u32[]{:S(2)}) collective-permute-start(f32[32,32]{1,0:T(8,128)S(1)} %rank_inner.1.rest_6_), channel_id=1, source_target_pairs={{0,1},{1,0},{2,3},{3,2},{4,5},{5,4},{6,7},{7,6},{8,9},{9,8},{10,11... | collective-permute-start | bytes 12296 | tf_op jit(solution)/shard_map/ppermute | solution.py:399
  20.8 3.8 %collective-permute-start.7 = (f32[32,32]{1,0:T(8,128)S(1)}, f32[32,32]{1,0:T(8,128)S(1)}, u32[]{:S(2)}, u32[]{:S(2)}) collective-permute-start(f32[32,32]{1,0:T(8,128)S(1)} %rank_inner.1.rest_6_), channel_id=1, source_target_pairs={{0,2},{1,3},{2,0},{3,1},{4,6},{5,7},{6,4},{7,5},{8,10},{9,11},{10,... | collective-permute-start | bytes 12296 | tf_op jit(solution)/shard_map/ppermute | solution.py:399
  22.4 3.2 %collective-permute-start.8 = (f32[32,32]{1,0:T(8,128)S(1)}, f32[32,32]{1,0:T(8,128)S(1)}, u32[]{:S(2)}, u32[]{:S(2)}) collective-permute-start(f32[32,32]{1,0:T(8,128)S(1)} %rank_inner.1.rest_6_), channel_id=1, source_target_pairs={{0,3},{1,2},{2,1},{3,0},{4,7},{5,6},{6,5},{7,4},{8,11},{9,10},{10,... | collective-permute-start | bytes 12296 | tf_op jit(solution)/shard_map/ppermute | solution.py:399

commit v6 on v5

--- a/solution.py
+++ b/solution.py
@@ -215,16 +215,17 @@
     packs, out_ref = rest[:-1], rest[-1]
     me = lax.axis_index("wide")
     width = scaled_ref.shape[2]
-    total = None
+    total = []
     for offset, pack in enumerate(packs):
-        part = lax.dot_general(
-            scaled_ref[me ^ offset],
-            pack[:, :, :width].reshape(out_ref.shape[1], width),
-            (((1,), (1,)), ((), ())),
-            preferred_element_type=jnp.float32,
+        total.append(
+            lax.dot_general(
+                scaled_ref[me ^ offset],
+                pack[:, :, :width].reshape(out_ref.shape[1], width),
+                (((1,), (1,)), ((), ())),
+                preferred_element_type=jnp.float32,
+            )
         )
-        total = part if total is None else total + part
-    out_ref[...] = total
+    out_ref[...] = sum(total[1:], total[0])
 
 
 def inner_call(scaled, packs):
@@ -239,109 +240,152 @@
     )(scaled, *packs)
 
 
-def base_kernel(staged, streamed, gain_ref, staged_ref, weight_ref, *rest):
-    offsets = staged + streamed
-    parts = rest[: len(offsets)]
-    base_out, square_out, scaled_out, buffer, sems = rest[len(offsets) :]
-    steps, rows, width = parts[0].shape
-    count = steps * rows
-    kinds, columns = weight_ref.shape[1:]
+def project(scaled, block, kinds):
+    count, width = scaled.shape
+    columns = block.shape[2]
     chunks = width // HD
-    me = lax.axis_index("tp")
-    copies = []
-    for i, offset in enumerate(streamed):
-        copy = pltpu.make_async_copy(
-            weight_block(weight_ref, me ^ offset, width), buffer.at[i], sems.at[i]
-        )
-        copy.start()
-        copies.append(copy)
+    group = 4
     feature = lax.broadcasted_iota(jnp.int32, (HD, kinds * kinds * HD), 0)
     place = lax.broadcasted_iota(jnp.int32, (HD, kinds * kinds * HD), 1)
     kind = place // (kinds * HD)
     spreader = jnp.where(feature * kinds + kind == place % (kinds * HD), 1.0, 0.0).astype(jnp.bfloat16)
+    stacked = jnp.concatenate([scaled[:, i * HD : (i + 1) * HD] for i in range(chunks)], axis=0)
+    spread = jnp.dot(stacked, spreader, preferred_element_type=jnp.float32).astype(jnp.bfloat16)
+    flat = block.reshape(width * kinds, columns)
+    products = []
+    for first in range(0, chunks, group):
+        lines = []
+        for i in range(first, first + group):
+            chunk = spread[i * count : (i + 1) * count]
+            lines.append(
+                jnp.concatenate(
+                    [chunk[:, j * kinds * HD : (j + 1) * kinds * HD] for j in range(kinds)], axis=0
+                )
+            )
+        at = pl.ds(first * HD * kinds, group * HD * kinds)
+        products.append(
+            jnp.dot(jnp.concatenate(lines, axis=1), flat[at, :], preferred_element_type=jnp.float32)
+        )
+    return sum(products[1:], products[0])
+
+
+def near_kernel(near, far, gain_ref, near_ref, weight_ref, *rest):
+    offsets = near + far
+    parts = rest[: len(offsets)]
+    base_out, square_out, scaled_out, weight_out, sems = rest[len(offsets) :]
+    steps, rows, width = parts[0].shape
+    count = steps * rows
+    kinds = weight_ref.shape[1]
+    chunks = width // HD
+    me = lax.axis_index("tp")
+    copies = []
+    for i, offset in enumerate(far):
+        copy = pltpu.make_async_copy(
+            weight_block(weight_ref, me ^ offset, width), weight_out.at[i], sems.at[i]
+        )
+        copy.start()
+        copies.append(copy)
     squares = jnp.zeros((count, HD), jnp.float32)
-    acc = jnp.zeros((kinds * count, columns), jnp.float32)
-    for k, (offset, part) in enumerate(zip(offsets, parts)):
+    for offset, part in zip(offsets, parts):
         start = pl.multiple_of((me ^ offset) * chunks, chunks)
         gain = gain_ref[pl.ds(start, chunks)]
         values = rows_of(part)
-        scaled = []
         for i in range(chunks):
             chunk = values[:, i * HD : (i + 1) * HD]
             squares += chunk * chunk
-            scaled.append((chunk * gain[i : i + 1]).astype(jnp.bfloat16))
-            scaled_out[me ^ offset, :, i * HD : (i + 1) * HD] = scaled[i]
-        spread = jnp.dot(
-            jnp.concatenate(scaled, axis=0), spreader, preferred_element_type=jnp.float32
-        ).astype(jnp.bfloat16)
-        if k < len(staged):
-            block = staged_ref.at[k]
-        else:
-            copies[k - len(staged)].wait()
-            block = buffer.at[k - len(staged)]
-        flat = block.reshape(width * kinds, columns)
-        for i in range(chunks):
-            lines = spread[i * count : (i + 1) * count]
-            lines = jnp.concatenate(
-                [lines[:, j * kinds * HD : (j + 1) * kinds * HD] for j in range(kinds)], axis=0
-            )
-            acc += jnp.dot(
-                lines, flat[pl.ds(i * HD * kinds, HD * kinds), :], preferred_element_type=jnp.float32
-            )
+            scaled_out[me ^ offset, :, i * HD : (i + 1) * HD] = (chunk * gain[i : i + 1]).astype(jnp.bfloat16)
+    square_out[...] = jnp.broadcast_to(jnp.sum(squares, axis=1, keepdims=True), squares.shape)
+    acc = None
+    for k, offset in enumerate(near):
+        product = project(scaled_out[me ^ offset], near_ref.at[k], kinds)
+        acc = product if acc is None else acc + product
     base_out[...] = acc
-    square_out[...] = jnp.broadcast_to(jnp.sum(squares, axis=1, keepdims=True), squares.shape)
-
-
-def base_call(staged, streamed, gain, staged_weight, weight, parts):
+    for copy in copies:
+        copy.wait()
+
+
+def near_call(near, far, gain, near_weight, weight, parts):
     steps, rows, width = parts[0].shape
     kinds, columns = weight.shape[1:]
     return pl.pallas_call(
-        functools.partial(base_kernel, staged, streamed),
+        functools.partial(near_kernel, near, far),
         out_shape=(
             pltpu.VMEM((kinds * steps * rows, columns), jnp.float32),
             pltpu.VMEM((steps * rows, HD), jnp.float32),
             pltpu.VMEM((len(parts), steps * rows, width), jnp.bfloat16),
+            pltpu.VMEM((len(far), width, kinds, columns), weight.dtype),
         ),
         in_specs=[VMEM, VMEM, HBM] + [VMEM] * len(parts),
-        out_specs=(VMEM,) * 3,
-        scratch_shapes=[
-            pltpu.VMEM((len(streamed), width, kinds, columns), weight.dtype),
-            pltpu.SemaphoreType.DMA((len(streamed),)),
-        ],
+        out_specs=(VMEM,) * 4,
+        scratch_shapes=[pltpu.SemaphoreType.DMA((len(far),))],
         compiler_params=pltpu.CompilerParams(vmem_limit_bytes=16 << 20),
-        cost_estimate=pl.CostEstimate(flops=4 * 134 << 20, bytes_accessed=9 << 20, transcendentals=0),
-        name="base_projection",
-    )(gain, staged_weight, pltpu.with_memory_space_constraint(weight, pltpu.HBM), *parts)
-
-
-def final_kernel(width, blocks, base_ref, square_ref, bias_ref, *rest):
+        cost_estimate=pl.CostEstimate(flops=2 * 134 << 20, bytes_accessed=5 << 20, transcendentals=0),
+        name="near_projection",
+    )(gain, near_weight, pltpu.with_memory_space_constraint(weight, pltpu.HBM), *parts)
+
+
+def far_kernel(far, base_ref, scaled_ref, weight_ref, *rest):
+    packs = rest[:-2]
+    base_out, up_out = rest[-2:]
+    kinds, share, pack_width = packs[0].shape
+    columns = base_out.shape[1]
+    me = lax.axis_index("wide") if len(packs) > 1 else 0
+    up_out[...] = jnp.zeros_like(up_out)
+    for offset, pack in enumerate(packs):
+        for kind in range(kinds):
+            at = pl.multiple_of(((me ^ offset) * kinds + kind) * share, share)
+            up_out[pl.ds(at, share), kind * columns : (kind + 1) * columns] = pack[
+                kind, :, pack_width - columns :
+            ]
+    acc = base_ref[...]
+    tp = lax.axis_index("tp")
+    for k, offset in enumerate(far):
+        acc = acc + project(scaled_ref[tp ^ offset], weight_ref.at[k], kinds)
+    base_out[...] = acc
+
+
+def far_call(far, base, scaled, weight, packs):
+    kinds, share, _ = packs[0].shape
+    return pl.pallas_call(
+        functools.partial(far_kernel, far),
+        out_shape=(
+            pltpu.VMEM(base.shape, base.dtype),
+            pltpu.VMEM((len(packs) * kinds * share, kinds * base.shape[1]), jnp.bfloat16),
+        ),
+        in_specs=[VMEM] * (3 + len(packs)),
+        out_specs=(VMEM,) * 2,
+        compiler_params=pltpu.CompilerParams(vmem_limit_bytes=16 << 20),
+        cost_estimate=pl.CostEstimate(flops=2 * 134 << 20, bytes_accessed=5 << 20, transcendentals=0),
+        name="far_projection",
+    )(base, scaled, weight, *packs)
+
+
+def final_kernel(width, blocks, base_ref, square_ref, up_ref, bias_ref, *rest):
     query_ref, acc_ref, top_ref, total_ref, cos_ref, sin_ref = rest[:6]
     inner_refs = rest[6 : 6 + blocks]
-    up_refs = rest[6 + blocks : 6 + 2 * blocks]
-    keys_out, values_out, attended_out, inner_buffer, up_buffer = rest[6 + 2 * blocks :]
+    keys_out, values_out, attended_out, inner_buffer = rest[6 + blocks :]
     steps, rows, columns = keys_out.shape
     count = steps * rows
     groups, size, _ = query_ref.shape
     per_group = size // count
-    kinds, share, pack_width = up_refs[0].shape
+    kinds = bias_ref.shape[0]
     row_scale = lax.rsqrt(square_ref[:, :1] * (1.0 / width) + norm_eps)
-    my_tp, my_wide = (lax.axis_index("tp"), lax.axis_index("wide")) if blocks > 1 else (0, 0)
+    me = lax.axis_index("tp") if blocks > 1 else 0
     for i in range(blocks):
-        inner_buffer[my_tp ^ i] = inner_refs[i][...]
-        up_buffer[my_wide ^ i] = up_refs[i][:, :, pack_width - columns :]
+        inner_buffer[me ^ i] = inner_refs[i][...]
+    inner = jnp.concatenate([inner_buffer[i] for i in range(blocks)], axis=1)
+    high = inner.astype(jnp.bfloat16)
+    low = (inner - high.astype(jnp.float32)).astype(jnp.bfloat16)
+    lora = jnp.dot(
+        jnp.concatenate([high, low], axis=0), up_ref[...], preferred_element_type=jnp.float32
+    )
+    lora = lora[:count] + lora[count:]
     bias = bias_ref[...].astype(jnp.float32)
     linear = []
     for kind in range(kinds):
-        lora = jnp.zeros((count, columns), jnp.float32)
-        for i in range(blocks):
-            inner = inner_buffer[i, :, kind * share : (kind + 1) * share]
-            high = inner.astype(jnp.bfloat16)
-            low = (inner - high.astype(jnp.float32)).astype(jnp.bfloat16)
-            up = up_buffer[i, kind]
-            lora += jnp.dot(high, up, preferred_element_type=jnp.float32)
-            lora += jnp.dot(low, up, preferred_element_type=jnp.float32)
         base = base_ref[kind * count : (kind + 1) * count]
-        linear.append((base + adapter_scale * lora) * row_scale + bias[kind : kind + 1])
+        part = lora[:, kind * columns : (kind + 1) * columns]
+        linear.append((base + adapter_scale * part) * row_scale + bias[kind : kind + 1])
     cosine, sine = cos_ref[...], sin_ref[...]
     line = lax.broadcasted_iota(jnp.int32, (size, count), 0)
     other = lax.broadcasted_iota(jnp.int32, (size, count), 1)
@@ -377,22 +421,19 @@
                 attended_out[step, :, lanes] = attended[tile : tile + rows]
 
 
-def final_call(shape, width, base, square, bias, cached, inner, up):
+def final_call(shape, width, base, square, up, bias, cached, inner):
     steps, rows, query_width = shape
     columns = base.shape[1]
     small = jax.ShapeDtypeStruct((steps, rows, columns), jnp.bfloat16)
     return pl.pallas_call(
         functools.partial(final_kernel, width, len(inner)),
         out_shape=(small, small, jax.ShapeDtypeStruct(shape, jnp.bfloat16)),
-        in_specs=[VMEM] * (3 + len(cached) + len(inner) + len(up)),
+        in_specs=[VMEM] * (4 + len(cached) + len(inner)),
         out_specs=(VMEM,) * 3,
-        scratch_shapes=[
-            pltpu.VMEM((len(inner),) + inner[0].shape, jnp.float32),
-            pltpu.VMEM((len(up),) + up[0].shape[:2] + (columns,), up[0].dtype),
-        ],
+        scratch_shapes=[pltpu.VMEM((len(inner),) + inner[0].shape, jnp.float32)],
         compiler_params=pltpu.CompilerParams(vmem_limit_bytes=8 << 20),
         name="fresh_attention",
-    )(base, square, bias, *cached, *inner, *up)
+    )(base, square, up, bias, *cached, *inner)
 
 
 def swap(block, axis, offset, count):
@@ -422,10 +463,11 @@
     parts = [hidden] + [swap(hidden, "tp", offset, tp_count) for offset in (1, 2, 3)]
     if direct:
         pack = pack_call(adapter_down_factor, up_part)
-        packs = [pack] + [swap(pack, "wide", offset, wide_count) for offset in (1, 2, 3)]
-    staged, streamed = (0, 1), (2, 3)
-    staged_weight, gain_rows, bias, *cached = cache_call(
-        staged,
+        second = swap(pack, "wide", 2, wide_count)
+        first = swap(pack, "wide", 1, wide_count)
+    near, far = (0, 1), (2, 3)
+    near_weight, gain_rows, bias, *cached = cache_call(
+        near,
         part_width,
         lengths,
         queries,
@@ -435,22 +477,25 @@
         key_value_bias,
         key_value_weight,
     )
-    base, square, scaled = base_call(
-        staged, streamed, gain_rows, staged_weight, key_value_weight, parts
+    if direct:
+        relayed, gain_rows = lax.optimization_barrier((second, gain_rows))
+        packs = [pack, first, second, swap(relayed, "wide", 1, wide_count)]
+    base, square, scaled, far_weight = near_call(
+        near, far, gain_rows, near_weight, key_value_weight, parts
     )
     if direct:
         inner = inner_call(scaled, packs)
-        inner = [inner] + [swap(inner, "tp", offset, tp_count) for offset in (2, 3, 1)]
-        inner = [inner[i] for i in (0, 3, 1, 2)]
-        up = packs
+        inner, scaled = lax.optimization_barrier((inner, scaled))
+        inner = [inner] + [swap(inner, "tp", offset, tp_count) for offset in (1, 2, 3)]
     else:
         down = lax.all_gather(adapter_down_factor, "wide", axis=2, tiled=True)
         down = down.reshape(kinds * ranks, tp_count, part_width)
         inner = [
             jnp.einsum("brd,kbd->rk", scaled, down, preferred_element_type=jnp.float32)
         ]
-        up = [lax.all_gather(up_part, "wide", axis=1, tiled=True)]
-    return final_call(queries.shape, width, base, square, bias, cached, inner, up)
+        packs = [lax.all_gather(up_part, "wide", axis=1, tiled=True)]
+    base, up = far_call(far, base, scaled, far_weight, packs)
+    return final_call(queries.shape, width, base, square, up, bias, cached, inner)
 
 
 def solution(mesh):

time: 27.4 us -> 25.5 us (0.931)
  waiting for transfers between devices: 6.93 us -> 2.37 us
  Pallas kernels: 9.98 us -> 12.2 us
  starting transfers between devices: 9.49 us -> 10.1 us
    ppermute x9, waiting for transfers between devices: 6.93 us -> 2.37 us  [swap(): return lax.ppermute(block, axis, [(i, i ^ offset) for i in range(count)])]
    pallas_call x1 -> x2, Pallas kernels: 3.56 us -> 5.75 us  [the longest x1 3.99 us: near_call(): pl.pallas_call(functools.partial(near_kernel, near, far), out_shape=(pltp...]
    ppermute x9, starting transfers between devices: 9.49 us -> 10.1 us  [swap(): return lax.ppermute(block, axis, [(i, i ^ offset) for i in range(count)])]
  transfers between devices with their start and end apart: 9 -> 9, of which waited for: 3 -> 4; matrix products, arithmetic and copies ran while one was open for 0% -> 0% of each run, Pallas kernels for 30% -> 37%
where the time goes in v6:
time: 25.5 us; the launch traced here: 25.3 us
  Pallas kernels  12.2 us (48%)
  starting transfers between devices  10.1 us (40%)
  waiting for transfers between devices  2.37 us (9%)
  between operations  0.69 us (3%)
    ppermute x9, starting transfers between devices, swap(): return lax.ppermute(block, axis, [(i, i ^ offset) for i in range(count)])  10.1 us
    pallas_call x1, Pallas kernels, near_call(): pl.pallas_call(functools.partial(near_kernel, near, far), out_shape=(pltp...  3.99 us
    pallas_call x1, Pallas kernels, cache_call(): pl.pallas_call(functools.partial(cache_kernel, staged), out_shape=(pltpu....  3.69 us
    ppermute x9, waiting for transfers between devices, swap(): return lax.ppermute(block, axis, [(i, i ^ offset) for i in range(count)])  2.37 us
    pallas_call x1, Pallas kernels, far_call(): pl.pallas_call(functools.partial(far_kernel, far), out_shape=(pltpu.VMEM(...  1.75 us
    pallas_call x1, Pallas kernels, final_call(): pl.pallas_call(functools.partial(final_kernel, width, len(inner)), out_sh...  1.54 us
    pallas_call x1, Pallas kernels, pack_call(): pl.pallas_call(pack_kernel, out_shape=pltpu.VMEM((kinds, share, down.shap...  0.93 us
  transfers between devices with their start and end apart: 9, of which 4 were waited for; matrix products, arithmetic and copies ran while one was open for 0% of the time, Pallas kernels for 37%

profile of v6, /device:TPU:0, one launch (start us, length us, event | category | flops | bytes accessed | tf_op | source)
XLA Modules:
  0.0 25.3 jit_solution(14652785242464049353)
XLA Ops:
  0.6 0.9 %pack_factors.1.rest_0_ = bf16[2,16,2304]{2,1,0:T(8,128)(2,1)S(1)} custom-call(bf16[2,64,2048]{2,1,0:T(8,128)(2,1)} %down_ref.1, bf16[2,16,256]{2,1,0:T(8,128)(2,1)} %bitcast.3), custom_call_target="tpu_custom_call" | custom-call | tf_op jit(solution)/shard_map/pack_factors/pallas_call | solution.py:204
  1.6 4.1 %collective-permute-start = (bf16[2,16,2304]{2,1,0:T(8,128)(2,1)S(1)}, bf16[2,16,2304]{2,1,0:T(8,128)(2,1)S(1)}, u32[]{:S(2)}, u32[]{:S(2)}) collective-permute-start(bf16[2,16,2304]{2,1,0:T(8,128)(2,1)S(1)} %pack_factors.1.rest_0_), channel_id=1, source_target_pairs={{0,8},{4,12},{8,0},{12,4},{1,9},{5,13},{9,1},{13,5},{2,10},{6,14},... | collective-permute-start | bytes 442376 | tf_op jit(solution)/shard_map/ppermute | solution.py:440
  5.7 0.0 collective-permute-start.1
  5.7 1.5 %collective-permute-start.2 = (bf16[4,8,2048]{2,1,0:T(8,128)(2,1)}, bf16[4,8,2048]{2,1,0:T(8,128)(2,1)S(1)}, u32[]{:S(2)}, u32[]{:S(2)}) collective-permute-start(bf16[4,8,2048]{2,1,0:T(8,128)(2,1)} %rest_0_.1), channel_id=1, source_target_pairs={{0,2},{1,3},{2,0},{3,1},{4,6},{5,7},{6,4},{7,5},{8,10},{9,11},{10,... | collective-permute-start | bytes 393224 | tf_op jit(solution)/shard_map/ppermute | solution.py:440
  7.2 0.4 %collective-permute-start.3 = (bf16[4,8,2048]{2,1,0:T(8,128)(2,1)}, bf16[4,8,2048]{2,1,0:T(8,128)(2,1)S(1)}, u32[]{:S(2)}, u32[]{:S(2)}) collective-permute-start(bf16[4,8,2048]{2,1,0:T(8,128)(2,1)} %rest_0_.1), channel_id=1, source_target_pairs={{0,3},{1,2},{2,1},{3,0},{4,7},{5,6},{6,5},{7,4},{8,11},{9,10},{10,... | collective-permute-start | bytes 393224 | tf_op jit(solution)/shard_map/ppermute | solution.py:440
  7.5 1.6 %collective-permute-start.4 = (bf16[2,16,2304]{2,1,0:T(8,128)(2,1)S(1)}, bf16[2,16,2304]{2,1,0:T(8,128)(2,1)S(1)}, u32[]{:S(2)}, u32[]{:S(2)}) collective-permute-start(bf16[2,16,2304]{2,1,0:T(8,128)(2,1)S(1)} %pack_factors.1.rest_0_), channel_id=1, source_target_pairs={{0,4},{4,0},{8,12},{12,8},{1,5},{5,1},{9,13},{13,9},{2,6},{6,2},{1... | collective-permute-start | bytes 442376 | tf_op jit(solution)/shard_map/ppermute | solution.py:440
  9.1 0.0 copy-start
  9.1 3.7 %cache_attention.1 = (bf16[2,2048,2,256]{3,2,1,0:T(2,128)(2,1)S(1)}, f32[64,128]{1,0:T(8,128)S(1)}, bf16[2,256]{1,0:T(2,128)(2,1)S(1)}, f32[2,256,128]{2,1,0:T(8...) custom-call(s32[8]{0:T(128)} %lengths_ref.1, ...), custom_call_target="tpu_custom_call" | custom-call | flops 140509184 | bytes 9437184 | tf_op jit(solution)/shard_map/cache_attention/pallas_call | solution.py:152
  12.8 0.0 collective-permute-done.rest_2_
  12.8 0.6 %collective-permute-start.5 = (bf16[2,16,2304]{2,1,0:T(8,128)(2,1)S(1)}, bf16[2,16,2304]{2,1,0:T(8,128)(2,1)S(1)}, u32[]{:S(2)}, u32[]{:S(2)}) collective-permute-start(bf16[2,16,2304]{2,1,0:T(8,128)(2,1)S(1)} %collective-permute-done.rest_2_), channel_id=1, source_target_pairs={{0,4},{4,0},{8,12},{12,8},{1,5},{5,1},{9,13},{13,9},{2,6},{6,2},{1... | collective-permute-start | bytes 442376 | tf_op jit(solution)/shard_map/ppermute | solution.py:440
  13.4 0.0 collective-permute-done.1.rest_1_
  13.5 0.0 collective-permute-done.2.rest_2_
  13.5 0.8 %collective-permute-done.3.rest_3_ = bf16[4,8,2048]{2,1,0:T(8,128)(2,1)S(1)} collective-permute-done((bf16[4,8,2048]{2,1,0:T(8,128)(2,1)}, bf16[4,8,2048]{2,1,0:T(8,128)(2,1)S(1)}, u32[]{:S(2)}, u32[]{:S(2)}) %collective-permute-start.3) | collective-permute-done | bytes 131104 | tf_op jit(solution)/shard_map/ppermute | solution.py:440
  14.2 0.0 copy-done
  14.2 4.0 %near_projection.1 = (f32[64,256]{1,0:T(8,128)S(1)}, f32[32,128]{1,0:T(8,128)S(1)}, bf16[4,32,2048]{2,1,0:T(8,128)(2,1)S(1)}, bf16[2,2048,2,256]{3,2,1,0:T(2,128)(2,1)S(1)}) custom-call(f32[64,128]{1,0:T(8,128)S(1)} %get-tuple-element.23.gain_ref, bf16[2,2048,2,256]{3,2,1,0:T(2,128)(2,1)S(1)} %get-tuple-element.24.near_ref, ...), custom_call_target="tpu_custom_call" | custom-call | flops 281018368 | bytes 5242880 | tf_op jit(solution)/shard_map/near_projection/pallas_call | solution.py:310
  18.2 0.0 collective-permute-done.4.rest_1_
  18.2 0.4 %collective-permute-done.5.rest_3_ = bf16[2,16,2304]{2,1,0:T(8,128)(2,1)S(1)} collective-permute-done((bf16[2,16,2304]{2,1,0:T(8,128)(2,1)S(1)}, bf16[2,16,2304]{2,1,0:T(8,128)(2,1)S(1)}, u32[]{:S(2)}, u32[]{:S(2)}) %collective-permute-start.5) | collective-permute-done | bytes 147488 | tf_op jit(solution)/shard_map/ppermute | solution.py:440
  18.6 0.3 %rank_inner.1.rest_6_ = f32[32,32]{1,0:T(8,128)S(1)} custom-call(bf16[4,32,2048]{2,1,0:T(8,128)(2,1)S(1)} %get-tuple-element.28.scaled_ref, bf16[2,16,2304]{2,1,0:T(8,128)(2,1)S(1)} %pack_factors.1.rest_0_, bf16[2,16,2304]{2,1,0:T(8,128)(2,1)S(1)} %collective-permute-done.4.rest_1_, bf16[2,16,2304]{2,1,0:T(8,128)(2,1)S(1)} %collective-permute-done.rest_2_, ...), custom_call_target="tpu_custom_call" | custom-call | tf_op jit(solution)/shard_map/rank_inner/pallas_call | solution.py:233
  18.9 0.1 collective-permute-start.6
  19.0 1.6 %collective-permute-start.7 = (f32[32,32]{1,0:T(8,128)S(1)}, f32[32,32]{1,0:T(8,128)S(1)}, u32[]{:S(2)}, u32[]{:S(2)}) collective-permute-start(f32[32,32]{1,0:T(8,128)S(1)} %rank_inner.1.rest_6_), channel_id=1, source_target_pairs={{0,2},{1,3},{2,0},{3,1},{4,6},{5,7},{6,4},{7,5},{8,10},{9,11},{10,... | collective-permute-start | bytes 12296 | tf_op jit(solution)/shard_map/ppermute | solution.py:440
  20.6 0.2 collective-permute-start.8
  20.8 1.8 %far_projection.1 = (f32[64,256]{1,0:T(8,128)S(1)}, bf16[128,512]{1,0:T(8,128)(2,1)S(1)}) custom-call(f32[64,256]{1,0:T(8,128)S(1)} %get-tuple-element.25.base_ref, bf16[4,32,2048]{2,1,0:T(8,128)(2,1)S(1)} %get-tuple-element.28.scaled_ref, bf16[2,2048,2,256]{3,2,1,0:T(2,128)(2,1)S(1)} %get-tuple-element.29.weight_ref, ...), custom_call_target="tpu_custom_call" | custom-call | flops 281018368 | bytes 5242880 | tf_op jit(solution)/shard_map/far_projection/pallas_call | solution.py:349
  22.6 0.0 collective-permute-done.6.rest_7_
  22.6 0.2 collective-permute-done.7.rest_8_
  22.8 1.0 %collective-permute-done.8.rest_9_ = f32[32,32]{1,0:T(8,128)S(1)} collective-permute-done((f32[32,32]{1,0:T(8,128)S(1)}, f32[32,32]{1,0:T(8,128)S(1)}, u32[]{:S(2)}, u32[]{:S(2)}) %collective-permute-start.8) | collective-permute-done | bytes 4128 | tf_op jit(solution)/shard_map/ppermute | solution.py:440
  23.8 1.5 %fresh_attention.1 = (bf16[4,8,256]{2,1,0:T(8,128)(2,1)}, bf16[4,8,256]{2,1,0:T(8,128)(2,1)}, bf16[4,8,2048]{2,1,0:T(8,128)(2,1)}) custom-call(f32[64,256]{1,0:T(8,128)S(1)} %get-tuple-element.30.base_ref, f32[32,128]{1,0:T(8,128)S(1)} %get-tuple-element.31.square_ref, bf16[128,512]{1,0:T(8,128)(2,1)S(1)} %get-tuple-element.32.up_ref, ...), custom_call_target="tpu_custom_call" | custom-call | tf_op jit(solution)/shard_map/fresh_attention/pallas_call | solution.py:428
Async XLA Ops:
  1.6 11.2 %collective-permute-start = (bf16[2,16,2304]{2,1,0:T(8,128)(2,1)S(1)}, bf16[2,16,2304]{2,1,0:T(8,128)(2,1)S(1)}, u32[]{:S(2)}, u32[]{:S(2)}) collective-permute-start(bf16[2,16,2304]{2,1,0:T(8,128)(2,1)S(1)} %pack_factors.1.rest_0_), channel_id=1, source_target_pairs={{0,8},{4,12},{8,0},{12,4},{1,9},{5,13},{9,1},{13,5},{2,10},{6,14},... | collective-permute-start | bytes 442376 | tf_op jit(solution)/shard_map/ppermute | solution.py:440
  5.7 7.8 %collective-permute-start.1 = (bf16[4,8,2048]{2,1,0:T(8,128)(2,1)}, bf16[4,8,2048]{2,1,0:T(8,128)(2,1)S(1)}, u32[]{:S(2)}, u32[]{:S(2)}) collective-permute-start(bf16[4,8,2048]{2,1,0:T(8,128)(2,1)} %rest_0_.1), channel_id=1, source_target_pairs={{0,1},{1,0},{2,3},{3,2},{4,5},{5,4},{6,7},{7,6},{8,9},{9,8},{10,11... | collective-permute-start | bytes 393224 | tf_op jit(solution)/shard_map/ppermute | solution.py:440
  5.7 7.8 %collective-permute-start.2 = (bf16[4,8,2048]{2,1,0:T(8,128)(2,1)}, bf16[4,8,2048]{2,1,0:T(8,128)(2,1)S(1)}, u32[]{:S(2)}, u32[]{:S(2)}) collective-permute-start(bf16[4,8,2048]{2,1,0:T(8,128)(2,1)} %rest_0_.1), channel_id=1, source_target_pairs={{0,2},{1,3},{2,0},{3,1},{4,6},{5,7},{6,4},{7,5},{8,10},{9,11},{10,... | collective-permute-start | bytes 393224 | tf_op jit(solution)/shard_map/ppermute | solution.py:440
  7.2 7.0 %collective-permute-start.3 = (bf16[4,8,2048]{2,1,0:T(8,128)(2,1)}, bf16[4,8,2048]{2,1,0:T(8,128)(2,1)S(1)}, u32[]{:S(2)}, u32[]{:S(2)}) collective-permute-start(bf16[4,8,2048]{2,1,0:T(8,128)(2,1)} %rest_0_.1), channel_id=1, source_target_pairs={{0,3},{1,2},{2,1},{3,0},{4,7},{5,6},{6,5},{7,4},{8,11},{9,10},{10,... | collective-permute-start | bytes 393224 | tf_op jit(solution)/shard_map/ppermute | solution.py:440
  7.5 10.7 %collective-permute-start.4 = (bf16[2,16,2304]{2,1,0:T(8,128)(2,1)S(1)}, bf16[2,16,2304]{2,1,0:T(8,128)(2,1)S(1)}, u32[]{:S(2)}, u32[]{:S(2)}) collective-permute-start(bf16[2,16,2304]{2,1,0:T(8,128)(2,1)S(1)} %pack_factors.1.rest_0_), channel_id=1, source_target_pairs={{0,4},{4,0},{8,12},{12,8},{1,5},{5,1},{9,13},{13,9},{2,6},{6,2},{1... | collective-permute-start | bytes 442376 | tf_op jit(solution)/shard_map/ppermute | solution.py:440
  9.1 5.1 %copy-start = (bf16[4,8,2048]{2,1,0:T(8,128)(2,1)S(1)}, bf16[4,8,2048]{2,1,0:T(8,128)(2,1)}, u32[]{:S(2)}) copy-start(bf16[4,8,2048]{2,1,0:T(8,128)(2,1)} %rest_0_.1) | copy-start | bytes 393220
  12.8 5.8 %collective-permute-start.5 = (bf16[2,16,2304]{2,1,0:T(8,128)(2,1)S(1)}, bf16[2,16,2304]{2,1,0:T(8,128)(2,1)S(1)}, u32[]{:S(2)}, u32[]{:S(2)}) collective-permute-start(bf16[2,16,2304]{2,1,0:T(8,128)(2,1)S(1)} %collective-permute-done.rest_2_), channel_id=1, source_target_pairs={{0,4},{4,0},{8,12},{12,8},{1,5},{5,1},{9,13},{13,9},{2,6},{6,2},{1... | collective-permute-start | bytes 442376 | tf_op jit(solution)/shard_map/ppermute | solution.py:440
  18.9 3.7 %collective-permute-start.6 = (f32[32,32]{1,0:T(8,128)S(1)}, f32[32,32]{1,0:T(8,128)S(1)}, u32[]{:S(2)}, u32[]{:S(2)}) collective-permute-start(f32[32,32]{1,0:T(8,128)S(1)} %rank_inner.1.rest_6_), channel_id=1, source_target_pairs={{0,1},{1,0},{2,3},{3,2},{4,5},{5,4},{6,7},{7,6},{8,9},{9,8},{10,11... | collective-permute-start | bytes 12296 | tf_op jit(solution)/shard_map/ppermute | solution.py:440
  19.0 3.7 %collective-permute-start.7 = (f32[32,32]{1,0:T(8,128)S(1)}, f32[32,32]{1,0:T(8,128)S(1)}, u32[]{:S(2)}, u32[]{:S(2)}) collective-permute-start(f32[32,32]{1,0:T(8,128)S(1)} %rank_inner.1.rest_6_), channel_id=1, source_target_pairs={{0,2},{1,3},{2,0},{3,1},{4,6},{5,7},{6,4},{7,5},{8,10},{9,11},{10,... | collective-permute-start | bytes 12296 | tf_op jit(solution)/shard_map/ppermute | solution.py:440
  20.6 3.2 %collective-permute-start.8 = (f32[32,32]{1,0:T(8,128)S(1)}, f32[32,32]{1,0:T(8,128)S(1)}, u32[]{:S(2)}, u32[]{:S(2)}) collective-permute-start(f32[32,32]{1,0:T(8,128)S(1)} %rank_inner.1.rest_6_), channel_id=1, source_target_pairs={{0,3},{1,2},{2,1},{3,0},{4,7},{5,6},{6,5},{7,4},{8,11},{9,10},{10,... | collective-permute-start | bytes 12296 | tf_op jit(solution)/shard_map/ppermute | solution.py:440

commit v7 on v6

--- a/solution.py
+++ b/solution.py
@@ -31,22 +31,17 @@
     return jnp.concatenate(tiles, axis=0)
 
 
-def weight_block(weight_ref, block, width):
-    return weight_ref.at[pl.ds(pl.multiple_of(block * width, width), width)]
-
-
 def cache_kernel(
-    staged,
     lengths_ref,
     query_ref,
     key_ref,
     value_ref,
     gain_ref,
     bias_ref,
-    weight_ref,
-    weight_out,
+    hidden_ref,
     gain_out,
     bias_out,
+    hidden_out,
     query_out,
     acc_out,
     top_out,
@@ -77,10 +72,8 @@
         (value_ref.at[halves[1]], value_buffer.at[halves[1]]),
         (gain_ref, gain_buffer),
         (bias_ref, bias_out),
+        (hidden_ref, hidden_out),
     ]
-    me = lax.axis_index("tp")
-    for i, offset in enumerate(staged):
-        copies.append((weight_block(weight_ref, me ^ offset, weight_out.shape[1]), weight_out.at[i]))
     copies = [pltpu.make_async_copy(*pair, sems.at[i]) for i, pair in enumerate(copies)]
     for copy in copies:
         copy.start()
@@ -141,20 +134,20 @@
         copy.wait()
 
 
-def cache_call(staged, part_width, lengths, queries, keys, values, gain, bias, weight):
+def cache_call(lengths, queries, keys, values, gain, bias, hidden):
     steps, rows, query_width = queries.shape
     cache_span, key_width = keys.shape[1:]
     groups = key_width // HD
     lines = steps * (query_width // key_width)
     block = (groups, lines * rows, HD)
     table = (steps * rows, HD)
-    operands = (lengths, queries, keys, values, gain, bias, weight)
+    operands = (lengths, queries, keys, values, gain, bias, hidden)
     return pl.pallas_call(
-        functools.partial(cache_kernel, staged),
+        cache_kernel,
         out_shape=(
-            pltpu.VMEM((len(staged), part_width) + weight.shape[1:], weight.dtype),
             pltpu.VMEM(gain.shape, jnp.float32),
             pltpu.VMEM(bias.shape, bias.dtype),
+            pltpu.VMEM(hidden.shape, hidden.dtype),
             pltpu.VMEM(block, jnp.float32),
             pltpu.VMEM(block, jnp.float32),
             pltpu.VMEM(block, jnp.float32),
@@ -171,10 +164,10 @@
             pltpu.VMEM(keys.shape, keys.dtype),
             pltpu.VMEM(values.shape, values.dtype),
             pltpu.VMEM((rows * groups, lines, cache_span), jnp.float32),
-            pltpu.SemaphoreType.DMA((8 + len(staged),)),
+            pltpu.SemaphoreType.DMA((9,)),
         ],
         compiler_params=pltpu.CompilerParams(vmem_limit_bytes=16 << 20),
-        cost_estimate=pl.CostEstimate(flops=2 * 67 << 20, bytes_accessed=9 << 20, transcendentals=0),
+        cost_estimate=pl.CostEstimate(flops=2 * 67 << 20, bytes_accessed=5 << 20, transcendentals=0),
         name="cache_attention",
     )(*[pltpu.with_memory_space_constraint(x, pltpu.HBM) for x in operands])
 
@@ -214,12 +207,12 @@
 def inner_kernel(scaled_ref, *rest):
     packs, out_ref = rest[:-1], rest[-1]
     me = lax.axis_index("wide")
-    width = scaled_ref.shape[2]
+    width = scaled_ref.shape[1] // len(packs)
     total = []
     for offset, pack in enumerate(packs):
         total.append(
             lax.dot_general(
-                scaled_ref[me ^ offset],
+                scaled_ref[:, pl.ds(pl.multiple_of((me ^ offset) * width, width), width)],
                 pack[:, :, :width].reshape(out_ref.shape[1], width),
                 (((1,), (1,)), ((), ())),
                 preferred_element_type=jnp.float32,
@@ -232,7 +225,7 @@
     kinds, share, _ = packs[0].shape
     return pl.pallas_call(
         inner_kernel,
-        out_shape=jax.ShapeDtypeStruct((scaled.shape[1], kinds * share), jnp.float32),
+        out_shape=jax.ShapeDtypeStruct((scaled.shape[0], kinds * share), jnp.float32),
         in_specs=[VMEM] * (1 + len(packs)),
         out_specs=VMEM,
         compiler_params=pltpu.CompilerParams(vmem_limit_bytes=8 << 20),
@@ -240,95 +233,46 @@
     )(scaled, *packs)
 
 
-def project(scaled, block, kinds):
-    count, width = scaled.shape
-    columns = block.shape[2]
-    chunks = width // HD
-    group = 4
-    feature = lax.broadcasted_iota(jnp.int32, (HD, kinds * kinds * HD), 0)
-    place = lax.broadcasted_iota(jnp.int32, (HD, kinds * kinds * HD), 1)
-    kind = place // (kinds * HD)
-    spreader = jnp.where(feature * kinds + kind == place % (kinds * HD), 1.0, 0.0).astype(jnp.bfloat16)
-    stacked = jnp.concatenate([scaled[:, i * HD : (i + 1) * HD] for i in range(chunks)], axis=0)
-    spread = jnp.dot(stacked, spreader, preferred_element_type=jnp.float32).astype(jnp.bfloat16)
-    flat = block.reshape(width * kinds, columns)
-    products = []
-    for first in range(0, chunks, group):
-        lines = []
-        for i in range(first, first + group):
-            chunk = spread[i * count : (i + 1) * count]
-            lines.append(
-                jnp.concatenate(
-                    [chunk[:, j * kinds * HD : (j + 1) * kinds * HD] for j in range(kinds)], axis=0
-                )
-            )
-        at = pl.ds(first * HD * kinds, group * HD * kinds)
-        products.append(
-            jnp.dot(jnp.concatenate(lines, axis=1), flat[at, :], preferred_element_type=jnp.float32)
-        )
-    return sum(products[1:], products[0])
-
-
-def near_kernel(near, far, gain_ref, near_ref, weight_ref, *rest):
-    offsets = near + far
-    parts = rest[: len(offsets)]
-    base_out, square_out, scaled_out, weight_out, sems = rest[len(offsets) :]
+def scale_kernel(gain_ref, *rest):
+    parts = rest[:-2]
+    scaled_out, square_out = rest[-2:]
     steps, rows, width = parts[0].shape
-    count = steps * rows
-    kinds = weight_ref.shape[1]
     chunks = width // HD
     me = lax.axis_index("tp")
-    copies = []
-    for i, offset in enumerate(far):
-        copy = pltpu.make_async_copy(
-            weight_block(weight_ref, me ^ offset, width), weight_out.at[i], sems.at[i]
-        )
-        copy.start()
-        copies.append(copy)
-    squares = jnp.zeros((count, HD), jnp.float32)
-    for offset, part in zip(offsets, parts):
-        start = pl.multiple_of((me ^ offset) * chunks, chunks)
-        gain = gain_ref[pl.ds(start, chunks)]
+    squares = jnp.zeros(square_out.shape, jnp.float32)
+    for offset, part in enumerate(parts):
+        block = me ^ offset
+        gain = gain_ref[pl.ds(pl.multiple_of(block * chunks, chunks), chunks)]
         values = rows_of(part)
+        scaled = []
         for i in range(chunks):
             chunk = values[:, i * HD : (i + 1) * HD]
             squares += chunk * chunk
-            scaled_out[me ^ offset, :, i * HD : (i + 1) * HD] = (chunk * gain[i : i + 1]).astype(jnp.bfloat16)
+            scaled.append((chunk * gain[i : i + 1]).astype(jnp.bfloat16))
+        at = pl.ds(pl.multiple_of(block * width, width), width)
+        scaled_out[:, at] = jnp.concatenate(scaled, axis=1)
     square_out[...] = jnp.broadcast_to(jnp.sum(squares, axis=1, keepdims=True), squares.shape)
-    acc = None
-    for k, offset in enumerate(near):
-        product = project(scaled_out[me ^ offset], near_ref.at[k], kinds)
-        acc = product if acc is None else acc + product
-    base_out[...] = acc
-    for copy in copies:
-        copy.wait()
-
-
-def near_call(near, far, gain, near_weight, weight, parts):
+
+
+def scale_call(gain, parts):
     steps, rows, width = parts[0].shape
-    kinds, columns = weight.shape[1:]
     return pl.pallas_call(
-        functools.partial(near_kernel, near, far),
+        scale_kernel,
         out_shape=(
-            pltpu.VMEM((kinds * steps * rows, columns), jnp.float32),
+            pltpu.VMEM((steps * rows, len(parts) * width), jnp.bfloat16),
             pltpu.VMEM((steps * rows, HD), jnp.float32),
-            pltpu.VMEM((len(parts), steps * rows, width), jnp.bfloat16),
-            pltpu.VMEM((len(far), width, kinds, columns), weight.dtype),
         ),
-        in_specs=[VMEM, VMEM, HBM] + [VMEM] * len(parts),
-        out_specs=(VMEM,) * 4,
-        scratch_shapes=[pltpu.SemaphoreType.DMA((len(far),))],
-        compiler_params=pltpu.CompilerParams(vmem_limit_bytes=16 << 20),
-        cost_estimate=pl.CostEstimate(flops=2 * 134 << 20, bytes_accessed=5 << 20, transcendentals=0),
-        name="near_projection",
-    )(gain, near_weight, pltpu.with_memory_space_constraint(weight, pltpu.HBM), *parts)
-
-
-def far_kernel(far, base_ref, scaled_ref, weight_ref, *rest):
-    packs = rest[:-2]
-    base_out, up_out = rest[-2:]
+        in_specs=[VMEM] * (1 + len(parts)),
+        out_specs=(VMEM,) * 2,
+        compiler_params=pltpu.CompilerParams(vmem_limit_bytes=8 << 20),
+        name="scale_features",
+    )(gain, *parts)
+
+
+def up_kernel(*refs):
+    packs, up_out = refs[:-1], refs[-1]
     kinds, share, pack_width = packs[0].shape
-    columns = base_out.shape[1]
+    columns = up_out.shape[1] // kinds
     me = lax.axis_index("wide") if len(packs) > 1 else 0
     up_out[...] = jnp.zeros_like(up_out)
     for offset, pack in enumerate(packs):
@@ -337,33 +281,14 @@
             up_out[pl.ds(at, share), kind * columns : (kind + 1) * columns] = pack[
                 kind, :, pack_width - columns :
             ]
-    acc = base_ref[...]
-    tp = lax.axis_index("tp")
-    for k, offset in enumerate(far):
-        acc = acc + project(scaled_ref[tp ^ offset], weight_ref.at[k], kinds)
-    base_out[...] = acc
-
-
-def far_call(far, base, scaled, weight, packs):
-    kinds, share, _ = packs[0].shape
-    return pl.pallas_call(
-        functools.partial(far_kernel, far),
-        out_shape=(
-            pltpu.VMEM(base.shape, base.dtype),
-            pltpu.VMEM((len(packs) * kinds * share, kinds * base.shape[1]), jnp.bfloat16),
-        ),
-        in_specs=[VMEM] * (3 + len(packs)),
-        out_specs=(VMEM,) * 2,
-        compiler_params=pltpu.CompilerParams(vmem_limit_bytes=16 << 20),
-        cost_estimate=pl.CostEstimate(flops=2 * 134 << 20, bytes_accessed=5 << 20, transcendentals=0),
-        name="far_projection",
-    )(base, scaled, weight, *packs)
-
-
-def final_kernel(width, blocks, base_ref, square_ref, up_ref, bias_ref, *rest):
+
+
+def final_kernel(width, blocks, base_ref, square_ref, bias_ref, *rest):
     query_ref, acc_ref, top_ref, total_ref, cos_ref, sin_ref = rest[:6]
     inner_refs = rest[6 : 6 + blocks]
-    keys_out, values_out, attended_out, inner_buffer = rest[6 + blocks :]
+    packs = rest[6 + blocks : 6 + 2 * blocks]
+    keys_out, values_out, attended_out, inner_buffer, up_ref = rest[6 + 2 * blocks :]
+    up_kernel(*packs, up_ref)
     steps, rows, columns = keys_out.shape
     count = steps * rows
     groups, size, _ = query_ref.shape
@@ -383,7 +308,7 @@
     bias = bias_ref[...].astype(jnp.float32)
     linear = []
     for kind in range(kinds):
-        base = base_ref[kind * count : (kind + 1) * count]
+        base = base_ref[kind]
         part = lora[:, kind * columns : (kind + 1) * columns]
         linear.append((base + adapter_scale * part) * row_scale + bias[kind : kind + 1])
     cosine, sine = cos_ref[...], sin_ref[...]
@@ -421,19 +346,23 @@
                 attended_out[step, :, lanes] = attended[tile : tile + rows]
 
 
-def final_call(shape, width, base, square, up, bias, cached, inner):
+def final_call(shape, width, base, square, bias, cached, inner, packs):
     steps, rows, query_width = shape
-    columns = base.shape[1]
+    kinds, share, _ = packs[0].shape
+    columns = base.shape[2]
     small = jax.ShapeDtypeStruct((steps, rows, columns), jnp.bfloat16)
     return pl.pallas_call(
         functools.partial(final_kernel, width, len(inner)),
         out_shape=(small, small, jax.ShapeDtypeStruct(shape, jnp.bfloat16)),
-        in_specs=[VMEM] * (4 + len(cached) + len(inner)),
+        in_specs=[VMEM] * (3 + len(cached) + len(inner) + len(packs)),
         out_specs=(VMEM,) * 3,
-        scratch_shapes=[pltpu.VMEM((len(inner),) + inner[0].shape, jnp.float32)],
+        scratch_shapes=[
+            pltpu.VMEM((len(inner),) + inner[0].shape, jnp.float32),
+            pltpu.VMEM((len(packs) * kinds * share, kinds * columns), jnp.bfloat16),
+        ],
         compiler_params=pltpu.CompilerParams(vmem_limit_bytes=8 << 20),
         name="fresh_attention",
-    )(base, square, up, bias, *cached, *inner)
+    )(base, square, bias, *cached, *inner, *packs)
 
 
 def swap(block, axis, offset, count):
@@ -460,42 +389,27 @@
     gain = input_norm_gain.reshape(width // HD, HD)
     up_part = jnp.transpose(adapter_up_factor, (0, 2, 1))
     direct = wide_count == tp_count == 4
-    parts = [hidden] + [swap(hidden, "tp", offset, tp_count) for offset in (1, 2, 3)]
+    beside = swap(hidden, "tp", 1, tp_count)
+    crossed = swap(hidden, "tp", 2, tp_count)
     if direct:
         pack = pack_call(adapter_down_factor, up_part)
-        second = swap(pack, "wide", 2, wide_count)
-        first = swap(pack, "wide", 1, wide_count)
-    near, far = (0, 1), (2, 3)
-    near_weight, gain_rows, bias, *cached = cache_call(
-        near,
-        part_width,
-        lengths,
-        queries,
-        stored_rotated_keys,
-        stored_value_rows,
-        gain,
-        key_value_bias,
-        key_value_weight,
-    )
-    if direct:
-        relayed, gain_rows = lax.optimization_barrier((second, gain_rows))
-        packs = [pack, first, second, swap(relayed, "wide", 1, wide_count)]
-    base, square, scaled, far_weight = near_call(
-        near, far, gain_rows, near_weight, key_value_weight, parts
-    )
+        packs = [pack] + [swap(pack, "wide", offset, wide_count) for offset in (1, 2, 3)]
+    gain_rows, bias, near, *cached = cache_call(
+        lengths, queries, stored_rotated_keys, stored_value_rows, gain, key_value_bias, hidden
+    )
+    relayed, gain_rows = lax.optimization_barrier((crossed, gain_rows))
+    relayed = swap(relayed, "tp", 1, tp_count)
+    scaled, square = scale_call(gain_rows, (near, beside, crossed, relayed))
+    base = jnp.einsum("md,dkc->kmc", scaled, key_value_weight, preferred_element_type=jnp.float32)
     if direct:
         inner = inner_call(scaled, packs)
-        inner, scaled = lax.optimization_barrier((inner, scaled))
         inner = [inner] + [swap(inner, "tp", offset, tp_count) for offset in (1, 2, 3)]
     else:
         down = lax.all_gather(adapter_down_factor, "wide", axis=2, tiled=True)
-        down = down.reshape(kinds * ranks, tp_count, part_width)
-        inner = [
-            jnp.einsum("brd,kbd->rk", scaled, down, preferred_element_type=jnp.float32)
-        ]
+        down = down.reshape(kinds * ranks, width)
+        inner = [jnp.einsum("rd,kd->rk", scaled, down, preferred_element_type=jnp.float32)]
         packs = [lax.all_gather(up_part, "wide", axis=1, tiled=True)]
-    base, up = far_call(far, base, scaled, far_weight, packs)
-    return final_call(queries.shape, width, base, square, up, bias, cached, inner)
+    return final_call(queries.shape, width, base, square, bias, cached, inner, packs)
 
 
 def solution(mesh):

time: 25.5 us -> 28.9 us (1.13)
  Pallas kernels: 12.2 us -> 6 us
  matrix products: 0 us -> 4.94 us
  waiting for transfers between devices: 2.37 us -> 7.21 us
    pallas_call x3 -> x2, Pallas kernels: 9.43 us -> 3.26 us  [the longest x1 3.04 us: cache_call(): pl.pallas_call(cache_kernel, out_shape=(pltpu.VMEM(gain.shape, jnp.float3...]
    dot_general x0 -> x1, matrix products: none -> 4.94 us  [on_device(): jnp.einsum('md,dkc->kmc', scaled, key_value_weight, preferred_element_typ...]
    ppermute x9, waiting for transfers between devices: 2.37 us -> 7.21 us  [swap(): return lax.ppermute(block, axis, [(i, i ^ offset) for i in range(count)])]
  transfers between devices with their start and end apart: 9 -> 9, of which waited for: 4 -> 2; matrix products, arithmetic and copies ran while one was open for 0% -> 17% of each run, Pallas kernels for 37% -> 15%
where the time goes in v7:
time: 28.9 us; the launch traced here: 28.8 us
  starting transfers between devices  9.9 us (34%)
  waiting for transfers between devices  7.21 us (25%)
  Pallas kernels  6 us (21%)
  matrix products  4.94 us (17%)
  between operations  0.7 us (2%)
    ppermute x9, starting transfers between devices, swap(): return lax.ppermute(block, axis, [(i, i ^ offset) for i in range(count)])  9.9 us
    ppermute x9, waiting for transfers between devices, swap(): return lax.ppermute(block, axis, [(i, i ^ offset) for i in range(count)])  7.21 us
    dot_general x1, matrix products, on_device(): jnp.einsum('md,dkc->kmc', scaled, key_value_weight, preferred_element_typ...  4.94 us
    pallas_call x1, Pallas kernels, cache_call(): pl.pallas_call(cache_kernel, out_shape=(pltpu.VMEM(gain.shape, jnp.float3...  3.04 us
    pallas_call x1, Pallas kernels, final_call(): pl.pallas_call(functools.partial(final_kernel, width, len(inner)), out_sh...  1.55 us
    pallas_call x1, Pallas kernels, pack_call(): pl.pallas_call(pack_kernel, out_shape=pltpu.VMEM((kinds, share, down.shap...  0.92 us
  transfers between devices with their start and end apart: 9, of which 2 were waited for; matrix products, arithmetic and copies ran while one was open for 17% of the time, Pallas kernels for 15%

profile of v7, /device:TPU:0, one launch (start us, length us, event | category | flops | bytes accessed | tf_op | source)
XLA Modules:
  0.0 28.8 jit_solution(5713048906957081455)
XLA Ops:
  0.6 3.0 %collective-permute-start = (bf16[4,8,2048]{2,1,0:T(8,128)(2,1)}, bf16[4,8,2048]{2,1,0:T(8,128)(2,1)S(1)}, u32[]{:S(2)}, u32[]{:S(2)}) collective-permute-start(bf16[4,8,2048]{2,1,0:T(8,128)(2,1)} %hidden_ref.1), channel_id=1, source_target_pairs={{0,2},{1,3},{2,0},{3,1},{4,6},{5,7},{6,4},{7,5},{8,10},{9,11},{10,... | collective-permute-start | bytes 393224 | tf_op jit(solution)/shard_map/ppermute | solution.py:369
  3.6 0.9 %pack_factors.1.rest_0_.rest_10_ = bf16[2,16,2304]{2,1,0:T(8,128)(2,1)S(1)} custom-call(bf16[2,64,2048]{2,1,0:T(8,128)(2,1)} %down_ref.1, bf16[2,16,256]{2,1,0:T(8,128)(2,1)} %bitcast.8), custom_call_target="tpu_custom_call" | custom-call | tf_op jit(solution)/shard_map/pack_factors/pallas_call | solution.py:197
  4.6 1.6 %collective-permute-start.3 = (bf16[2,16,2304]{2,1,0:T(8,128)(2,1)S(1)}, bf16[2,16,2304]{2,1,0:T(8,128)(2,1)S(1)}, u32[]{:S(2)}, u32[]{:S(2)}) collective-permute-start(bf16[2,16,2304]{2,1,0:T(8,128)(2,1)S(1)} %pack_factors.1.rest_0_.rest_10_), channel_id=1, source_target_pairs={{0,4},{4,0},{8,12},{12,8},{1,5},{5,1},{9,13},{13,9},{2,6},{6,2},{1... | collective-permute-start | bytes 442376 | tf_op jit(solution)/shard_map/ppermute | solution.py:369
  6.2 2.6 %collective-permute-start.4 = (bf16[2,16,2304]{2,1,0:T(8,128)(2,1)S(1)}, bf16[2,16,2304]{2,1,0:T(8,128)(2,1)S(1)}, u32[]{:S(2)}, u32[]{:S(2)}) collective-permute-start(bf16[2,16,2304]{2,1,0:T(8,128)(2,1)S(1)} %pack_factors.1.rest_0_.rest_10_), channel_id=1, source_target_pairs={{0,8},{4,12},{8,0},{12,4},{1,9},{5,13},{9,1},{13,5},{2,10},{6,14},... | collective-permute-start | bytes 442376 | tf_op jit(solution)/shard_map/ppermute | solution.py:369
  8.8 0.2 collective-permute-start.5
  9.0 0.0 collective-permute-start.1
  9.0 3.0 %cache_attention.1 = (f32[64,128]{1,0:T(8,128)S(1)}, bf16[2,256]{1,0:T(2,128)(2,1)S(1)}, bf16[4,8,2048]{2,1,0:T(8,128)(2,1)S(1)}, f32[2,256,128]{2,1,0:T(8,128)S...) custom-call(s32[8]{0:T(128)} %lengths_ref.1, ...), custom_call_target="tpu_custom_call" | custom-call | flops 140509184 | bytes 5242880 | tf_op jit(solution)/shard_map/cache_attention/pallas_call | solution.py:145
  12.1 0.0 collective-permute-done.rest_2_
  12.1 0.6 %collective-permute-start.2 = (bf16[4,8,2048]{2,1,0:T(8,128)(2,1)S(1)}, bf16[4,8,2048]{2,1,0:T(8,128)(2,1)S(1)}, u32[]{:S(2)}, u32[]{:S(2)}) collective-permute-start(bf16[4,8,2048]{2,1,0:T(8,128)(2,1)S(1)} %collective-permute-done.rest_2_), channel_id=1, source_target_pairs={{0,1},{1,0},{2,3},{3,2},{4,5},{5,4},{6,7},{7,6},{8,9},{9,8},{10,11... | collective-permute-start | bytes 393224 | tf_op jit(solution)/shard_map/ppermute | solution.py:369
  12.7 0.0 collective-permute-done.1.rest_1_
  12.7 1.0 %collective-permute-done.2.rest_3_ = bf16[4,8,2048]{2,1,0:T(8,128)(2,1)S(1)} collective-permute-done((bf16[4,8,2048]{2,1,0:T(8,128)(2,1)S(1)}, bf16[4,8,2048]{2,1,0:T(8,128)(2,1)S(1)}, u32[]{:S(2)}, u32[]{:S(2)}) %collective-permute-start.2) | collective-permute-done | bytes 131104 | tf_op jit(solution)/shard_map/ppermute | solution.py:369
  13.6 0.2 scale_features.1
  13.9 0.0 collective-permute-done.3.rest_1_.rest_11_
  13.9 6.2 %collective-permute-done.4.rest_2_.rest_12_ = bf16[2,16,2304]{2,1,0:T(8,128)(2,1)S(1)} collective-permute-done((bf16[2,16,2304]{2,1,0:T(8,128)(2,1)S(1)}, bf16[2,16,2304]{2,1,0:T(8,128)(2,1)S(1)}, u32[]{:S(2)}, u32[]{:S(2)}) %collective-permute-start.4) | collective-permute-done | bytes 147488 | tf_op jit(solution)/shard_map/ppermute | solution.py:369
  20.1 0.0 collective-permute-done.5.rest_3_.rest_13_
  20.1 0.3 rank_inner.1.rest_6_
  20.4 0.0 collective-permute-start.6
  20.4 0.6 %collective-permute-start.7 = (f32[32,32]{1,0:T(8,128)S(1)}, f32[32,32]{1,0:T(8,128)S(1)}, u32[]{:S(2)}, u32[]{:S(2)}) collective-permute-start(f32[32,32]{1,0:T(8,128)S(1)} %rank_inner.1.rest_6_), channel_id=1, source_target_pairs={{0,2},{1,3},{2,0},{3,1},{4,6},{5,7},{6,4},{7,5},{8,10},{9,11},{10,... | collective-permute-start | bytes 12296 | tf_op jit(solution)/shard_map/ppermute | solution.py:369
  21.0 1.3 %collective-permute-start.8 = (f32[32,32]{1,0:T(8,128)S(1)}, f32[32,32]{1,0:T(8,128)S(1)}, u32[]{:S(2)}, u32[]{:S(2)}) collective-permute-start(f32[32,32]{1,0:T(8,128)S(1)} %rank_inner.1.rest_6_), channel_id=1, source_target_pairs={{0,3},{1,2},{2,1},{3,0},{4,7},{5,6},{6,5},{7,4},{8,11},{9,10},{10,... | collective-permute-start | bytes 12296 | tf_op jit(solution)/shard_map/ppermute | solution.py:369
  22.2 4.9 %fusion.2.base_ref = f32[2,32,256]{2,1,0:T(8,128)S(1)} fusion(bf16[8192,2,256]{2,1,0:T(2,128)(2,1)} %param.12, bf16[32,8192]{1,0:T(8,128)(2,1)S(1)} %get-tuple-element.20.scaled_ref), kind=kOutput, calls=%fused_computation.2 | convolution fusion | flops 268435456 | bytes 8978432 | tf_op jit(solution)/shard_map/md,dkc->kmc/dot_general | solution.py:403
  27.2 0.0 collective-permute-done.6.rest_7_
  27.2 0.0 collective-permute-done.7.rest_8_
  27.2 0.0 collective-permute-done.8.rest_9_
  27.2 1.5 %fresh_attention.1 = (bf16[4,8,256]{2,1,0:T(8,128)(2,1)}, bf16[4,8,256]{2,1,0:T(8,128)(2,1)}, bf16[4,8,2048]{2,1,0:T(8,128)(2,1)}) custom-call(f32[2,32,256]{2,1,0:T(8,128)S(1)} %fusion.2.base_ref, f32[32,128]{1,0:T(8,128)S(1)} %get-tuple-element.21.square_ref, bf16[2,256]{1,0:T(2,128)(2,1)S(1)} %get-tuple-element.22.bias_ref, ...), custom_call_target="tpu_custom_call" | custom-call | tf_op jit(solution)/shard_map/fresh_attention/pallas_call | solution.py:354
Async XLA Ops:
  0.6 11.4 %collective-permute-start = (bf16[4,8,2048]{2,1,0:T(8,128)(2,1)}, bf16[4,8,2048]{2,1,0:T(8,128)(2,1)S(1)}, u32[]{:S(2)}, u32[]{:S(2)}) collective-permute-start(bf16[4,8,2048]{2,1,0:T(8,128)(2,1)} %hidden_ref.1), channel_id=1, source_target_pairs={{0,2},{1,3},{2,0},{3,1},{4,6},{5,7},{6,4},{7,5},{8,10},{9,11},{10,... | collective-permute-start | bytes 393224 | tf_op jit(solution)/shard_map/ppermute | solution.py:369
  4.6 9.3 %collective-permute-start.3 = (bf16[2,16,2304]{2,1,0:T(8,128)(2,1)S(1)}, bf16[2,16,2304]{2,1,0:T(8,128)(2,1)S(1)}, u32[]{:S(2)}, u32[]{:S(2)}) collective-permute-start(bf16[2,16,2304]{2,1,0:T(8,128)(2,1)S(1)} %pack_factors.1.rest_0_.rest_10_), channel_id=1, source_target_pairs={{0,4},{4,0},{8,12},{12,8},{1,5},{5,1},{9,13},{13,9},{2,6},{6,2},{1... | collective-permute-start | bytes 442376 | tf_op jit(solution)/shard_map/ppermute | solution.py:369
  6.2 13.9 %collective-permute-start.4 = (bf16[2,16,2304]{2,1,0:T(8,128)(2,1)S(1)}, bf16[2,16,2304]{2,1,0:T(8,128)(2,1)S(1)}, u32[]{:S(2)}, u32[]{:S(2)}) collective-permute-start(bf16[2,16,2304]{2,1,0:T(8,128)(2,1)S(1)} %pack_factors.1.rest_0_.rest_10_), channel_id=1, source_target_pairs={{0,8},{4,12},{8,0},{12,4},{1,9},{5,13},{9,1},{13,5},{2,10},{6,14},... | collective-permute-start | bytes 442376 | tf_op jit(solution)/shard_map/ppermute | solution.py:369
  8.8 11.3 %collective-permute-start.5 = (bf16[2,16,2304]{2,1,0:T(8,128)(2,1)S(1)}, bf16[2,16,2304]{2,1,0:T(8,128)(2,1)S(1)}, u32[]{:S(2)}, u32[]{:S(2)}) collective-permute-start(bf16[2,16,2304]{2,1,0:T(8,128)(2,1)S(1)} %pack_factors.1.rest_0_.rest_10_), channel_id=1, source_target_pairs={{0,12},{4,8},{8,4},{12,0},{1,13},{5,9},{9,5},{13,1},{2,14},{6,10},... | collective-permute-start | bytes 442376 | tf_op jit(solution)/shard_map/ppermute | solution.py:369
  9.0 3.6 %collective-permute-start.1 = (bf16[4,8,2048]{2,1,0:T(8,128)(2,1)}, bf16[4,8,2048]{2,1,0:T(8,128)(2,1)S(1)}, u32[]{:S(2)}, u32[]{:S(2)}) collective-permute-start(bf16[4,8,2048]{2,1,0:T(8,128)(2,1)} %hidden_ref.1), channel_id=1, source_target_pairs={{0,1},{1,0},{2,3},{3,2},{4,5},{5,4},{6,7},{7,6},{8,9},{9,8},{10,11... | collective-permute-start | bytes 393224 | tf_op jit(solution)/shard_map/ppermute | solution.py:369
  12.1 1.6 %collective-permute-start.2 = (bf16[4,8,2048]{2,1,0:T(8,128)(2,1)S(1)}, bf16[4,8,2048]{2,1,0:T(8,128)(2,1)S(1)}, u32[]{:S(2)}, u32[]{:S(2)}) collective-permute-start(bf16[4,8,2048]{2,1,0:T(8,128)(2,1)S(1)} %collective-permute-done.rest_2_), channel_id=1, source_target_pairs={{0,1},{1,0},{2,3},{3,2},{4,5},{5,4},{6,7},{7,6},{8,9},{9,8},{10,11... | collective-permute-start | bytes 393224 | tf_op jit(solution)/shard_map/ppermute | solution.py:369
  20.4 6.8 %collective-permute-start.6 = (f32[32,32]{1,0:T(8,128)S(1)}, f32[32,32]{1,0:T(8,128)S(1)}, u32[]{:S(2)}, u32[]{:S(2)}) collective-permute-start(f32[32,32]{1,0:T(8,128)S(1)} %rank_inner.1.rest_6_), channel_id=1, source_target_pairs={{0,1},{1,0},{2,3},{3,2},{4,5},{5,4},{6,7},{7,6},{8,9},{9,8},{10,11... | collective-permute-start | bytes 12296 | tf_op jit(solution)/shard_map/ppermute | solution.py:369
  20.4 6.8 %collective-permute-start.7 = (f32[32,32]{1,0:T(8,128)S(1)}, f32[32,32]{1,0:T(8,128)S(1)}, u32[]{:S(2)}, u32[]{:S(2)}) collective-permute-start(f32[32,32]{1,0:T(8,128)S(1)} %rank_inner.1.rest_6_), channel_id=1, source_target_pairs={{0,2},{1,3},{2,0},{3,1},{4,6},{5,7},{6,4},{7,5},{8,10},{9,11},{10,... | collective-permute-start | bytes 12296 | tf_op jit(solution)/shard_map/ppermute | solution.py:369
  21.0 6.2 %collective-permute-start.8 = (f32[32,32]{1,0:T(8,128)S(1)}, f32[32,32]{1,0:T(8,128)S(1)}, u32[]{:S(2)}, u32[]{:S(2)}) collective-permute-start(f32[32,32]{1,0:T(8,128)S(1)} %rank_inner.1.rest_6_), channel_id=1, source_target_pairs={{0,3},{1,2},{2,1},{3,0},{4,7},{5,6},{6,5},{7,4},{8,11},{9,10},{10,... | collective-permute-start | bytes 12296 | tf_op jit(solution)/shard_map/ppermute | solution.py:369

commit v8 on v7

--- a/solution.py
+++ b/solution.py
@@ -32,6 +32,8 @@
 
 
 def cache_kernel(
+    near,
+    far,
     lengths_ref,
     query_ref,
     key_ref,
@@ -39,6 +41,9 @@
     gain_ref,
     bias_ref,
     hidden_ref,
+    weight_ref,
+    near_out,
+    far_out,
     gain_out,
     bias_out,
     hidden_out,
@@ -74,6 +79,12 @@
         (bias_ref, bias_out),
         (hidden_ref, hidden_out),
     ]
+    me = lax.axis_index("tp")
+    width = hidden_ref.shape[2]
+    for offsets, out in ((near, near_out), (far, far_out)):
+        for i, offset in enumerate(offsets):
+            block = pl.ds(pl.multiple_of((me ^ offset) * width, width), width)
+            copies.append((weight_ref.at[block], out.at[pl.ds(i * width, width)]))
     copies = [pltpu.make_async_copy(*pair, sems.at[i]) for i, pair in enumerate(copies)]
     for copy in copies:
         copy.start()
@@ -134,17 +145,20 @@
         copy.wait()
 
 
-def cache_call(lengths, queries, keys, values, gain, bias, hidden):
+def cache_call(near, far, lengths, queries, keys, values, gain, bias, hidden, weight):
     steps, rows, query_width = queries.shape
     cache_span, key_width = keys.shape[1:]
     groups = key_width // HD
     lines = steps * (query_width // key_width)
     block = (groups, lines * rows, HD)
     table = (steps * rows, HD)
-    operands = (lengths, queries, keys, values, gain, bias, hidden)
+    operands = (lengths, queries, keys, values, gain, bias, hidden, weight)
+    part = hidden.shape[2]
     return pl.pallas_call(
-        cache_kernel,
+        functools.partial(cache_kernel, near, far),
         out_shape=(
+            pltpu.VMEM((len(near) * part,) + weight.shape[1:], weight.dtype),
+            pltpu.VMEM((len(far) * part,) + weight.shape[1:], weight.dtype),
             pltpu.VMEM(gain.shape, jnp.float32),
             pltpu.VMEM(bias.shape, bias.dtype),
             pltpu.VMEM(hidden.shape, hidden.dtype),
@@ -156,7 +170,7 @@
             pltpu.VMEM(table, jnp.float32),
         ),
         in_specs=[HBM] * len(operands),
-        out_specs=(VMEM,) * 9,
+        out_specs=(VMEM,) * 11,
         scratch_shapes=[
             pltpu.SMEM(lengths.shape, jnp.int32),
             pltpu.VMEM(queries.shape, queries.dtype),
@@ -164,10 +178,10 @@
             pltpu.VMEM(keys.shape, keys.dtype),
             pltpu.VMEM(values.shape, values.dtype),
             pltpu.VMEM((rows * groups, lines, cache_span), jnp.float32),
-            pltpu.SemaphoreType.DMA((9,)),
+            pltpu.SemaphoreType.DMA((9 + len(near) + len(far),)),
         ],
         compiler_params=pltpu.CompilerParams(vmem_limit_bytes=16 << 20),
-        cost_estimate=pl.CostEstimate(flops=2 * 67 << 20, bytes_accessed=5 << 20, transcendentals=0),
+        cost_estimate=pl.CostEstimate(flops=2 * 67 << 20, bytes_accessed=13 << 20, transcendentals=0),
         name="cache_attention",
     )(*[pltpu.with_memory_space_constraint(x, pltpu.HBM) for x in operands])
 
@@ -233,9 +247,9 @@
     )(scaled, *packs)
 
 
-def scale_kernel(gain_ref, *rest):
-    parts = rest[:-2]
-    scaled_out, square_out = rest[-2:]
+def scale_kernel(near_count, gain_ref, *rest):
+    parts = rest[:-4]
+    scaled_out, near_out, far_out, square_out = rest[-4:]
     steps, rows, width = parts[0].shape
     chunks = width // HD
     me = lax.axis_index("tp")
@@ -250,20 +264,25 @@
             squares += chunk * chunk
             scaled.append((chunk * gain[i : i + 1]).astype(jnp.bfloat16))
         at = pl.ds(pl.multiple_of(block * width, width), width)
-        scaled_out[:, at] = jnp.concatenate(scaled, axis=1)
+        scaled = jnp.concatenate(scaled, axis=1)
+        scaled_out[:, at] = scaled
+        out, i = (near_out, offset) if offset < near_count else (far_out, offset - near_count)
+        out[:, i * width : (i + 1) * width] = scaled
     square_out[...] = jnp.broadcast_to(jnp.sum(squares, axis=1, keepdims=True), squares.shape)
 
 
-def scale_call(gain, parts):
+def scale_call(near_count, gain, parts):
     steps, rows, width = parts[0].shape
     return pl.pallas_call(
-        scale_kernel,
+        functools.partial(scale_kernel, near_count),
         out_shape=(
             pltpu.VMEM((steps * rows, len(parts) * width), jnp.bfloat16),
+            pltpu.VMEM((steps * rows, near_count * width), jnp.bfloat16),
+            pltpu.VMEM((steps * rows, (len(parts) - near_count) * width), jnp.bfloat16),
             pltpu.VMEM((steps * rows, HD), jnp.float32),
         ),
         in_specs=[VMEM] * (1 + len(parts)),
-        out_specs=(VMEM,) * 2,
+        out_specs=(VMEM,) * 4,
         compiler_params=pltpu.CompilerParams(vmem_limit_bytes=8 << 20),
         name="scale_features",
     )(gain, *parts)
@@ -283,7 +302,7 @@
             ]
 
 
-def final_kernel(width, blocks, base_ref, square_ref, bias_ref, *rest):
+def final_kernel(width, blocks, near_ref, far_ref, square_ref, bias_ref, *rest):
     query_ref, acc_ref, top_ref, total_ref, cos_ref, sin_ref = rest[:6]
     inner_refs = rest[6 : 6 + blocks]
     packs = rest[6 + blocks : 6 + 2 * blocks]
@@ -308,7 +327,7 @@
     bias = bias_ref[...].astype(jnp.float32)
     linear = []
     for kind in range(kinds):
-        base = base_ref[kind]
+        base = near_ref[kind] + far_ref[kind]
         part = lora[:, kind * columns : (kind + 1) * columns]
         linear.append((base + adapter_scale * part) * row_scale + bias[kind : kind + 1])
     cosine, sine = cos_ref[...], sin_ref[...]
@@ -346,15 +365,15 @@
                 attended_out[step, :, lanes] = attended[tile : tile + rows]
 
 
-def final_call(shape, width, base, square, bias, cached, inner, packs):
+def final_call(shape, width, near, far, square, bias, cached, inner, packs):
     steps, rows, query_width = shape
     kinds, share, _ = packs[0].shape
-    columns = base.shape[2]
+    columns = near.shape[2]
     small = jax.ShapeDtypeStruct((steps, rows, columns), jnp.bfloat16)
     return pl.pallas_call(
         functools.partial(final_kernel, width, len(inner)),
         out_shape=(small, small, jax.ShapeDtypeStruct(shape, jnp.bfloat16)),
-        in_specs=[VMEM] * (3 + len(cached) + len(inner) + len(packs)),
+        in_specs=[VMEM] * (4 + len(cached) + len(inner) + len(packs)),
         out_specs=(VMEM,) * 3,
         scratch_shapes=[
             pltpu.VMEM((len(inner),) + inner[0].shape, jnp.float32),
@@ -362,7 +381,7 @@
         ],
         compiler_params=pltpu.CompilerParams(vmem_limit_bytes=8 << 20),
         name="fresh_attention",
-    )(base, square, bias, *cached, *inner, *packs)
+    )(near, far, square, bias, *cached, *inner, *packs)
 
 
 def swap(block, axis, offset, count):
@@ -393,23 +412,46 @@
     crossed = swap(hidden, "tp", 2, tp_count)
     if direct:
         pack = pack_call(adapter_down_factor, up_part)
-        packs = [pack] + [swap(pack, "wide", offset, wide_count) for offset in (1, 2, 3)]
-    gain_rows, bias, near, *cached = cache_call(
-        lengths, queries, stored_rotated_keys, stored_value_rows, gain, key_value_bias, hidden
+        second = swap(pack, "wide", 2, wide_count)
+        first = swap(pack, "wide", 1, wide_count)
+    near, far = (0, 1), (2, 3)
+    near_weight, far_weight, gain_rows, bias, mine, *cached = cache_call(
+        near,
+        far,
+        lengths,
+        queries,
+        stored_rotated_keys,
+        stored_value_rows,
+        gain,
+        key_value_bias,
+        hidden,
+        key_value_weight,
     )
     relayed, gain_rows = lax.optimization_barrier((crossed, gain_rows))
     relayed = swap(relayed, "tp", 1, tp_count)
-    scaled, square = scale_call(gain_rows, (near, beside, crossed, relayed))
-    base = jnp.einsum("md,dkc->kmc", scaled, key_value_weight, preferred_element_type=jnp.float32)
+    if direct:
+        third, gain_rows = lax.optimization_barrier((second, gain_rows))
+        relayed, first = lax.optimization_barrier((relayed, first))
+        packs = [pack, first, second, swap(third, "wide", 1, wide_count)]
+    scaled, near_scaled, far_scaled, square = scale_call(
+        len(near), gain_rows, (mine, beside, crossed, relayed)
+    )
     if direct:
         inner = inner_call(scaled, packs)
+        inner, far_scaled = lax.optimization_barrier((inner, far_scaled))
         inner = [inner] + [swap(inner, "tp", offset, tp_count) for offset in (1, 2, 3)]
     else:
         down = lax.all_gather(adapter_down_factor, "wide", axis=2, tiled=True)
         down = down.reshape(kinds * ranks, width)
         inner = [jnp.einsum("rd,kd->rk", scaled, down, preferred_element_type=jnp.float32)]
         packs = [lax.all_gather(up_part, "wide", axis=1, tiled=True)]
-    return final_call(queries.shape, width, base, square, bias, cached, inner, packs)
+    near_base, far_base = [
+        jnp.einsum("md,dkc->kmc", x, y, preferred_element_type=jnp.float32)
+        for x, y in ((near_scaled, near_weight), (far_scaled, far_weight))
+    ]
+    return final_call(
+        queries.shape, width, near_base, far_base, square, bias, cached, inner, packs
+    )
 
 
 def solution(mesh):

time: 28.9 us -> 26.1 us (0.903)
  matrix products: 4.94 us -> 1.66 us
  Pallas kernels: 6 us -> 7.93 us
  waiting for transfers between devices: 7.21 us -> 5.56 us
    dot_general x1 -> x2, matrix products: 4.94 us -> 1.66 us  [on_device(): jnp.einsum('md,dkc->kmc', x, y, preferred_element_type=jnp.float32)]
    pallas_call x2, Pallas kernels: 3.26 us -> 5.19 us  [the longest x1 4.94 us: cache_call(): pl.pallas_call(functools.partial(cache_kernel, near, far), out_shape=(plt...]
    ppermute x9, waiting for transfers between devices: 7.21 us -> 5.56 us  [swap(): return lax.ppermute(block, axis, [(i, i ^ offset) for i in range(count)])]
  transfers between devices with their start and end apart: 9 -> 9, of which waited for: 2 -> 4; matrix products, arithmetic and copies ran while one was open for 17% -> 6% of each run, Pallas kernels for 15% -> 24%
where the time goes in v8:
time: 26.1 us; the launch traced here: 26 us
  starting transfers between devices  10.1 us (39%)
  Pallas kernels  7.93 us (30%)
  waiting for transfers between devices  5.56 us (21%)
  matrix products  1.66 us (6%)
  between operations  0.69 us (3%)
    ppermute x9, starting transfers between devices, swap(): return lax.ppermute(block, axis, [(i, i ^ offset) for i in range(count)])  10.1 us
    ppermute x9, waiting for transfers between devices, swap(): return lax.ppermute(block, axis, [(i, i ^ offset) for i in range(count)])  5.56 us
    pallas_call x1, Pallas kernels, cache_call(): pl.pallas_call(functools.partial(cache_kernel, near, far), out_shape=(plt...  4.94 us
    dot_general x2, matrix products, on_device(): jnp.einsum('md,dkc->kmc', x, y, preferred_element_type=jnp.float32)  1.66 us
    pallas_call x1, Pallas kernels, final_call(): pl.pallas_call(functools.partial(final_kernel, width, len(inner)), out_sh...  1.55 us
    pallas_call x1, Pallas kernels, pack_call(): pl.pallas_call(pack_kernel, out_shape=pltpu.VMEM((kinds, share, down.shap...  0.92 us
  transfers between devices with their start and end apart: 9, of which 4 were waited for; matrix products, arithmetic and copies ran while one was open for 6% of the time, Pallas kernels for 24%

profile of v8, /device:TPU:0, one launch (start us, length us, event | category | flops | bytes accessed | tf_op | source)
XLA Modules:
  0.0 26.0 jit_solution(5937244191801339515)
XLA Ops:
  0.6 3.0 %collective-permute-start.1 = (bf16[4,8,2048]{2,1,0:T(8,128)(2,1)}, bf16[4,8,2048]{2,1,0:T(8,128)(2,1)S(1)}, u32[]{:S(2)}, u32[]{:S(2)}) collective-permute-start(bf16[4,8,2048]{2,1,0:T(8,128)(2,1)} %hidden_ref.1), channel_id=1, source_target_pairs={{0,2},{1,3},{2,0},{3,1},{4,6},{5,7},{6,4},{7,5},{8,10},{9,11},{10,... | collective-permute-start | bytes 393224 | tf_op jit(solution)/shard_map/ppermute | solution.py:388
  3.6 0.9 %pack_factors.1.rest_0_.rest_10_ = bf16[2,16,2304]{2,1,0:T(8,128)(2,1)S(1)} custom-call(bf16[2,64,2048]{2,1,0:T(8,128)(2,1)} %down_ref.1, bf16[2,16,256]{2,1,0:T(8,128)(2,1)} %bitcast.13), custom_call_target="tpu_custom_call" | custom-call | tf_op jit(solution)/shard_map/pack_factors/pallas_call | solution.py:211
  4.6 2.7 %collective-permute-start = (bf16[2,16,2304]{2,1,0:T(8,128)(2,1)S(1)}, bf16[2,16,2304]{2,1,0:T(8,128)(2,1)S(1)}, u32[]{:S(2)}, u32[]{:S(2)}) collective-permute-start(bf16[2,16,2304]{2,1,0:T(8,128)(2,1)S(1)} %pack_factors.1.rest_0_.rest_10_), channel_id=1, source_target_pairs={{0,8},{4,12},{8,0},{12,4},{1,9},{5,13},{9,1},{13,5},{2,10},{6,14},... | collective-permute-start | bytes 442376 | tf_op jit(solution)/shard_map/ppermute | solution.py:388
  7.2 1.6 %collective-permute-start.4 = (bf16[2,16,2304]{2,1,0:T(8,128)(2,1)S(1)}, bf16[2,16,2304]{2,1,0:T(8,128)(2,1)S(1)}, u32[]{:S(2)}, u32[]{:S(2)}) collective-permute-start(bf16[2,16,2304]{2,1,0:T(8,128)(2,1)S(1)} %pack_factors.1.rest_0_.rest_10_), channel_id=1, source_target_pairs={{0,4},{4,0},{8,12},{12,8},{1,5},{5,1},{9,13},{13,9},{2,6},{6,2},{1... | collective-permute-start | bytes 442376 | tf_op jit(solution)/shard_map/ppermute | solution.py:388
  8.8 0.0 copy-start
  8.8 4.9 %cache_attention.1 = (bf16[4096,2,256]{2,1,0:T(2,128)(2,1)S(1)}, bf16[4096,2,256]{2,1,0:T(2,128)(2,1)S(1)}, f32[64,128]{1,0:T(8,128)S(1)}, bf16[2,256]{1,0:T(2,1...) custom-call(s32[8]{0:T(128)} %lengths_ref.1, ...), custom_call_target="tpu_custom_call" | custom-call | flops 140509184 | bytes 13631488 | tf_op jit(solution)/shard_map/cache_attention/pallas_call | solution.py:157
  13.8 0.0 collective-permute-done.1.rest_2_
  13.8 0.1 collective-permute-start.3
  13.8 0.0 copy-done
  13.8 0.5 %collective-permute-start.2 = (bf16[4,8,2048]{2,1,0:T(8,128)(2,1)S(1)}, bf16[4,8,2048]{2,1,0:T(8,128)(2,1)S(1)}, u32[]{:S(2)}, u32[]{:S(2)}) collective-permute-start(bf16[4,8,2048]{2,1,0:T(8,128)(2,1)S(1)} %copy-done), channel_id=1, source_target_pairs={{0,1},{1,0},{2,3},{3,2},{4,5},{5,4},{6,7},{7,6},{8,9},{9,8},{10,11... | collective-permute-start | bytes 393224 | tf_op jit(solution)/shard_map/ppermute | solution.py:388
  14.3 0.0 collective-permute-done.rest_2_.rest_12_
  14.3 0.5 %collective-permute-start.5 = (bf16[2,16,2304]{2,1,0:T(8,128)(2,1)S(1)}, bf16[2,16,2304]{2,1,0:T(8,128)(2,1)S(1)}, u32[]{:S(2)}, u32[]{:S(2)}) collective-permute-start(bf16[2,16,2304]{2,1,0:T(8,128)(2,1)S(1)} %collective-permute-done.rest_2_.rest_12_), channel_id=1, source_target_pairs={{0,4},{4,0},{8,12},{12,8},{1,5},{5,1},{9,13},{13,9},{2,6},{6,2},{1... | collective-permute-start | bytes 442376 | tf_op jit(solution)/shard_map/ppermute | solution.py:388
  14.8 0.0 collective-permute-done.4.rest_1_.rest_11_
  14.8 0.4 %collective-permute-done.3.rest_3_ = bf16[4,8,2048]{2,1,0:T(8,128)(2,1)S(1)} collective-permute-done((bf16[4,8,2048]{2,1,0:T(8,128)(2,1)S(1)}, bf16[4,8,2048]{2,1,0:T(8,128)(2,1)S(1)}, u32[]{:S(2)}, u32[]{:S(2)}) %collective-permute-start.3) | collective-permute-done | bytes 131104 | tf_op jit(solution)/shard_map/ppermute | solution.py:388
  15.2 0.2 collective-permute-done.2.rest_1_
  15.4 0.2 scale_features.1
  15.6 0.8 %fusion.4.near_ref = f32[2,32,256]{2,1,0:T(8,128)S(1)} fusion(bf16[4096,2,256]{2,1,0:T(2,128)(2,1)S(1)} %get-tuple-element.26, bf16[32,4096]{1,0:T(8,128)(2,1)S(1)} %get-tuple-element.33), kind=kOutput, calls=%fused_computation.4 | convolution fusion | flops 134217728 | bytes 4521984 | tf_op jit(solution)/shard_map/md,dkc->kmc/dot_general | solution.py:449
  16.4 3.7 %collective-permute-done.5.rest_3_.rest_13_ = bf16[2,16,2304]{2,1,0:T(8,128)(2,1)S(1)} collective-permute-done((bf16[2,16,2304]{2,1,0:T(8,128)(2,1)S(1)}, bf16[2,16,2304]{2,1,0:T(8,128)(2,1)S(1)}, u32[]{:S(2)}, u32[]{:S(2)}) %collective-permute-start.5) | collective-permute-done | bytes 147488 | tf_op jit(solution)/shard_map/ppermute | solution.py:388
  20.2 0.3 %rank_inner.1.rest_6_ = f32[32,32]{1,0:T(8,128)S(1)} custom-call(bf16[32,8192]{1,0:T(8,128)(2,1)S(1)} %get-tuple-element.35.scaled_ref, bf16[2,16,2304]{2,1,0:T(8,128)(2,1)S(1)} %pack_factors.1.rest_0_.rest_10_, bf16[2,16,2304]{2,1,0:T(8,128)(2,1)S(1)} %collective-permute-done.4.rest_1_.rest_11_, ...), custom_call_target="tpu_custom_call" | custom-call | tf_op jit(solution)/shard_map/rank_inner/pallas_call | solution.py:240
  20.5 0.0 collective-permute-start.6
  20.5 0.6 %collective-permute-start.7 = (f32[32,32]{1,0:T(8,128)S(1)}, f32[32,32]{1,0:T(8,128)S(1)}, u32[]{:S(2)}, u32[]{:S(2)}) collective-permute-start(f32[32,32]{1,0:T(8,128)S(1)} %rank_inner.1.rest_6_), channel_id=1, source_target_pairs={{0,2},{1,3},{2,0},{3,1},{4,6},{5,7},{6,4},{7,5},{8,10},{9,11},{10,... | collective-permute-start | bytes 12296 | tf_op jit(solution)/shard_map/ppermute | solution.py:388
  21.1 1.3 %collective-permute-start.8 = (f32[32,32]{1,0:T(8,128)S(1)}, f32[32,32]{1,0:T(8,128)S(1)}, u32[]{:S(2)}, u32[]{:S(2)}) collective-permute-start(f32[32,32]{1,0:T(8,128)S(1)} %rank_inner.1.rest_6_), channel_id=1, source_target_pairs={{0,3},{1,2},{2,1},{3,0},{4,7},{5,6},{6,5},{7,4},{8,11},{9,10},{10,... | collective-permute-start | bytes 12296 | tf_op jit(solution)/shard_map/ppermute | solution.py:388
  22.3 0.8 %fusion.7.far_ref = f32[2,32,256]{2,1,0:T(8,128)S(1)} fusion(bf16[4096,2,256]{2,1,0:T(2,128)(2,1)S(1)} %get-tuple-element.34, bf16[32,4096]{1,0:T(8,128)(2,1)S(1)} %get-tuple-element.39), kind=kOutput, calls=%fused_computation.5 | convolution fusion | flops 134217728 | bytes 4521984 | tf_op jit(solution)/shard_map/md,dkc->kmc/dot_general | solution.py:449
  23.2 0.0 collective-permute-done.6.rest_7_
  23.2 1.3 %collective-permute-done.7.rest_8_ = f32[32,32]{1,0:T(8,128)S(1)} collective-permute-done((f32[32,32]{1,0:T(8,128)S(1)}, f32[32,32]{1,0:T(8,128)S(1)}, u32[]{:S(2)}, u32[]{:S(2)}) %collective-permute-start.7) | collective-permute-done | bytes 4128 | tf_op jit(solution)/shard_map/ppermute | solution.py:388
  24.4 0.0 collective-permute-done.8.rest_9_
  24.4 1.5 %fresh_attention.1 = (bf16[4,8,256]{2,1,0:T(8,128)(2,1)}, bf16[4,8,256]{2,1,0:T(8,128)(2,1)}, bf16[4,8,2048]{2,1,0:T(8,128)(2,1)}) custom-call(f32[2,32,256]{2,1,0:T(8,128)S(1)} %fusion.4.near_ref, f32[2,32,256]{2,1,0:T(8,128)S(1)} %fusion.7.far_ref, f32[32,128]{1,0:T(8,128)S(1)} %get-tuple-element.40.square_ref, ...), custom_call_target="tpu_custom_call" | custom-call | tf_op jit(solution)/shard_map/fresh_attention/pallas_call | solution.py:373
Async XLA Ops:
  0.6 13.1 %collective-permute-start.1 = (bf16[4,8,2048]{2,1,0:T(8,128)(2,1)}, bf16[4,8,2048]{2,1,0:T(8,128)(2,1)S(1)}, u32[]{:S(2)}, u32[]{:S(2)}) collective-permute-start(bf16[4,8,2048]{2,1,0:T(8,128)(2,1)} %hidden_ref.1), channel_id=1, source_target_pairs={{0,2},{1,3},{2,0},{3,1},{4,6},{5,7},{6,4},{7,5},{8,10},{9,11},{10,... | collective-permute-start | bytes 393224 | tf_op jit(solution)/shard_map/ppermute | solution.py:388
  4.6 9.8 %collective-permute-start = (bf16[2,16,2304]{2,1,0:T(8,128)(2,1)S(1)}, bf16[2,16,2304]{2,1,0:T(8,128)(2,1)S(1)}, u32[]{:S(2)}, u32[]{:S(2)}) collective-permute-start(bf16[2,16,2304]{2,1,0:T(8,128)(2,1)S(1)} %pack_factors.1.rest_0_.rest_10_), channel_id=1, source_target_pairs={{0,8},{4,12},{8,0},{12,4},{1,9},{5,13},{9,1},{13,5},{2,10},{6,14},... | collective-permute-start | bytes 442376 | tf_op jit(solution)/shard_map/ppermute | solution.py:388
  7.2 7.6 %collective-permute-start.4 = (bf16[2,16,2304]{2,1,0:T(8,128)(2,1)S(1)}, bf16[2,16,2304]{2,1,0:T(8,128)(2,1)S(1)}, u32[]{:S(2)}, u32[]{:S(2)}) collective-permute-start(bf16[2,16,2304]{2,1,0:T(8,128)(2,1)S(1)} %pack_factors.1.rest_0_.rest_10_), channel_id=1, source_target_pairs={{0,4},{4,0},{8,12},{12,8},{1,5},{5,1},{9,13},{13,9},{2,6},{6,2},{1... | collective-permute-start | bytes 442376 | tf_op jit(solution)/shard_map/ppermute | solution.py:388
  8.8 5.0 %copy-start = (bf16[4,8,2048]{2,1,0:T(8,128)(2,1)S(1)}, bf16[4,8,2048]{2,1,0:T(8,128)(2,1)}, u32[]{:S(2)}) copy-start(bf16[4,8,2048]{2,1,0:T(8,128)(2,1)} %hidden_ref.1) | copy-start | bytes 393220
  13.8 1.4 %collective-permute-start.3 = (bf16[4,8,2048]{2,1,0:T(8,128)(2,1)S(1)}, bf16[4,8,2048]{2,1,0:T(8,128)(2,1)S(1)}, u32[]{:S(2)}, u32[]{:S(2)}) collective-permute-start(bf16[4,8,2048]{2,1,0:T(8,128)(2,1)S(1)} %collective-permute-done.1.rest_2_), channel_id=1, source_target_pairs={{0,1},{1,0},{2,3},{3,2},{4,5},{5,4},{6,7},{7,6},{8,9},{9,8},{10,11... | collective-permute-start | bytes 393224 | tf_op jit(solution)/shard_map/ppermute | solution.py:388
  13.8 1.5 %collective-permute-start.2 = (bf16[4,8,2048]{2,1,0:T(8,128)(2,1)S(1)}, bf16[4,8,2048]{2,1,0:T(8,128)(2,1)S(1)}, u32[]{:S(2)}, u32[]{:S(2)}) collective-permute-start(bf16[4,8,2048]{2,1,0:T(8,128)(2,1)S(1)} %copy-done), channel_id=1, source_target_pairs={{0,1},{1,0},{2,3},{3,2},{4,5},{5,4},{6,7},{7,6},{8,9},{9,8},{10,11... | collective-permute-start | bytes 393224 | tf_op jit(solution)/shard_map/ppermute | solution.py:388
  14.3 5.8 %collective-permute-start.5 = (bf16[2,16,2304]{2,1,0:T(8,128)(2,1)S(1)}, bf16[2,16,2304]{2,1,0:T(8,128)(2,1)S(1)}, u32[]{:S(2)}, u32[]{:S(2)}) collective-permute-start(bf16[2,16,2304]{2,1,0:T(8,128)(2,1)S(1)} %collective-permute-done.rest_2_.rest_12_), channel_id=1, source_target_pairs={{0,4},{4,0},{8,12},{12,8},{1,5},{5,1},{9,13},{13,9},{2,6},{6,2},{1... | collective-permute-start | bytes 442376 | tf_op jit(solution)/shard_map/ppermute | solution.py:388
  20.5 2.7 %collective-permute-start.6 = (f32[32,32]{1,0:T(8,128)S(1)}, f32[32,32]{1,0:T(8,128)S(1)}, u32[]{:S(2)}, u32[]{:S(2)}) collective-permute-start(f32[32,32]{1,0:T(8,128)S(1)} %rank_inner.1.rest_6_), channel_id=1, source_target_pairs={{0,1},{1,0},{2,3},{3,2},{4,5},{5,4},{6,7},{7,6},{8,9},{9,8},{10,11... | collective-permute-start | bytes 12296 | tf_op jit(solution)/shard_map/ppermute | solution.py:388
  20.5 3.9 %collective-permute-start.7 = (f32[32,32]{1,0:T(8,128)S(1)}, f32[32,32]{1,0:T(8,128)S(1)}, u32[]{:S(2)}, u32[]{:S(2)}) collective-permute-start(f32[32,32]{1,0:T(8,128)S(1)} %rank_inner.1.rest_6_), channel_id=1, source_target_pairs={{0,2},{1,3},{2,0},{3,1},{4,6},{5,7},{6,4},{7,5},{8,10},{9,11},{10,... | collective-permute-start | bytes 12296 | tf_op jit(solution)/shard_map/ppermute | solution.py:388
  21.1 3.3 %collective-permute-start.8 = (f32[32,32]{1,0:T(8,128)S(1)}, f32[32,32]{1,0:T(8,128)S(1)}, u32[]{:S(2)}, u32[]{:S(2)}) collective-permute-start(f32[32,32]{1,0:T(8,128)S(1)} %rank_inner.1.rest_6_), channel_id=1, source_target_pairs={{0,3},{1,2},{2,1},{3,0},{4,7},{5,6},{6,5},{7,4},{8,11},{9,10},{10,... | collective-permute-start | bytes 12296 | tf_op jit(solution)/shard_map/ppermute | solution.py:388

commit v9 on v8

--- a/solution.py
+++ b/solution.py
@@ -227,19 +227,21 @@
         total.append(
             lax.dot_general(
                 scaled_ref[:, pl.ds(pl.multiple_of((me ^ offset) * width, width), width)],
-                pack[:, :, :width].reshape(out_ref.shape[1], width),
+                pack[:, :, :width].reshape(out_ref.shape[2], width),
                 (((1,), (1,)), ((), ())),
                 preferred_element_type=jnp.float32,
             )
         )
-    out_ref[...] = sum(total[1:], total[0])
+    total = sum(total[1:], total[0])
+    for i in range(out_ref.shape[0]):
+        out_ref[i] = total
 
 
 def inner_call(scaled, packs):
     kinds, share, _ = packs[0].shape
     return pl.pallas_call(
         inner_kernel,
-        out_shape=jax.ShapeDtypeStruct((scaled.shape[0], kinds * share), jnp.float32),
+        out_shape=jax.ShapeDtypeStruct((len(packs), scaled.shape[0], kinds * share), jnp.float32),
         in_specs=[VMEM] * (1 + len(packs)),
         out_specs=VMEM,
         compiler_params=pltpu.CompilerParams(vmem_limit_bytes=8 << 20),
@@ -304,9 +306,9 @@
 
 def final_kernel(width, blocks, near_ref, far_ref, square_ref, bias_ref, *rest):
     query_ref, acc_ref, top_ref, total_ref, cos_ref, sin_ref = rest[:6]
-    inner_refs = rest[6 : 6 + blocks]
-    packs = rest[6 + blocks : 6 + 2 * blocks]
-    keys_out, values_out, attended_out, inner_buffer, up_ref = rest[6 + 2 * blocks :]
+    inner_ref = rest[6]
+    packs = rest[7 : 7 + blocks]
+    keys_out, values_out, attended_out, up_ref = rest[7 + blocks :]
     up_kernel(*packs, up_ref)
     steps, rows, columns = keys_out.shape
     count = steps * rows
@@ -314,10 +316,7 @@
     per_group = size // count
     kinds = bias_ref.shape[0]
     row_scale = lax.rsqrt(square_ref[:, :1] * (1.0 / width) + norm_eps)
-    me = lax.axis_index("tp") if blocks > 1 else 0
-    for i in range(blocks):
-        inner_buffer[me ^ i] = inner_refs[i][...]
-    inner = jnp.concatenate([inner_buffer[i] for i in range(blocks)], axis=1)
+    inner = jnp.concatenate([inner_ref[i] for i in range(blocks)], axis=1)
     high = inner.astype(jnp.bfloat16)
     low = (inner - high.astype(jnp.float32)).astype(jnp.bfloat16)
     lora = jnp.dot(
@@ -371,17 +370,16 @@
     columns = near.shape[2]
     small = jax.ShapeDtypeStruct((steps, rows, columns), jnp.bfloat16)
     return pl.pallas_call(
-        functools.partial(final_kernel, width, len(inner)),
+        functools.partial(final_kernel, width, len(packs)),
         out_shape=(small, small, jax.ShapeDtypeStruct(shape, jnp.bfloat16)),
-        in_specs=[VMEM] * (4 + len(cached) + len(inner) + len(packs)),
+        in_specs=[VMEM] * (5 + len(cached) + len(packs)),
         out_specs=(VMEM,) * 3,
         scratch_shapes=[
-            pltpu.VMEM((len(inner),) + inner[0].shape, jnp.float32),
             pltpu.VMEM((len(packs) * kinds * share, kinds * columns), jnp.bfloat16),
         ],
         compiler_params=pltpu.CompilerParams(vmem_limit_bytes=8 << 20),
         name="fresh_attention",
-    )(near, far, square, bias, *cached, *inner, *packs)
+    )(near, far, square, bias, *cached, inner, *packs)
 
 
 def swap(block, axis, offset, count):
@@ -410,6 +408,7 @@
     direct = wide_count == tp_count == 4
     beside = swap(hidden, "tp", 1, tp_count)
     crossed = swap(hidden, "tp", 2, tp_count)
+    across = swap(hidden, "tp", 3, tp_count)
     if direct:
         pack = pack_call(adapter_down_factor, up_part)
         second = swap(pack, "wide", 2, wide_count)
@@ -427,23 +426,20 @@
         hidden,
         key_value_weight,
     )
-    relayed, gain_rows = lax.optimization_barrier((crossed, gain_rows))
-    relayed = swap(relayed, "tp", 1, tp_count)
     if direct:
         third, gain_rows = lax.optimization_barrier((second, gain_rows))
-        relayed, first = lax.optimization_barrier((relayed, first))
+        across, first = lax.optimization_barrier((across, first))
         packs = [pack, first, second, swap(third, "wide", 1, wide_count)]
     scaled, near_scaled, far_scaled, square = scale_call(
-        len(near), gain_rows, (mine, beside, crossed, relayed)
+        len(near), gain_rows, (mine, beside, crossed, across)
     )
     if direct:
         inner = inner_call(scaled, packs)
-        inner, far_scaled = lax.optimization_barrier((inner, far_scaled))
-        inner = [inner] + [swap(inner, "tp", offset, tp_count) for offset in (1, 2, 3)]
+        inner = lax.all_to_all(inner, "tp", 0, 0)
     else:
         down = lax.all_gather(adapter_down_factor, "wide", axis=2, tiled=True)
         down = down.reshape(kinds * ranks, width)
-        inner = [jnp.einsum("rd,kd->rk", scaled, down, preferred_element_type=jnp.float32)]
+        inner = jnp.einsum("rd,kd->rk", scaled, down, preferred_element_type=jnp.float32)[None]
         packs = [lax.all_gather(up_part, "wide", axis=1, tiled=True)]
     near_base, far_base = [
         jnp.einsum("md,dkc->kmc", x, y, preferred_element_type=jnp.float32)

time: 26.1 us -> 31 us (1.19)
  matrix products: 1.66 us -> 3.85 us
  starting transfers between devices: 10.1 us -> 11.6 us
  local copies, waits for them, and re-layouts: 0.01 us -> 1.32 us
  waiting for transfers between devices: 5.56 us -> 4.76 us
  other arithmetic: 0 us -> 0.69 us
    all_to_all x0 -> x1, starting transfers between devices: none -> 3.25 us  [on_device(): inner = lax.all_to_all(inner, 'tp', 0, 0)]
    dot_general x2, matrix products: 1.66 us -> 3.85 us  [on_device(): jnp.einsum('md,dkc->kmc', x, y, preferred_element_type=jnp.float32)]
    ppermute x9 -> x6, starting transfers between devices: 10.1 us -> 8.33 us  [swap(): return lax.ppermute(block, axis, [(i, i ^ offset) for i in range(count)])]
    ppermute x9 -> x6, waiting for transfers between devices: 5.56 us -> 3.95 us  [swap(): return lax.ppermute(block, axis, [(i, i ^ offset) for i in range(count)])]
    all_to_all x0 -> x1, waiting for transfers between devices: none -> 0.81 us  [on_device(): inner = lax.all_to_all(inner, 'tp', 0, 0)]
    unnamed x2 -> x4, local copies, waits for them, and re-layouts: 0.01 us -> 0.81 us
    all_to_all x0 -> x1, other arithmetic: none -> 0.69 us  [on_device(): inner = lax.all_to_all(inner, 'tp', 0, 0)]
    all_to_all x0 -> x1, local copies, waits for them, and re-layouts: none -> 0.51 us  [on_device(): inner = lax.all_to_all(inner, 'tp', 0, 0)]
  transfers between devices with their start and end apart: 9 -> 7, of which waited for: 4 -> 3; matrix products, arithmetic and copies ran while one was open for 6% -> 12% of each run, Pallas kernels for 24% -> 17%
where the time goes in v9:
time: 31 us; the launch traced here: 30.8 us
  starting transfers between devices  11.6 us (37%)
  Pallas kernels  7.88 us (25%)
  waiting for transfers between devices  4.76 us (15%)
  matrix products  3.85 us (12%)
  local copies, waits for them, and re-layouts  1.32 us (4%)
  between operations  0.7 us (2%)
  other arithmetic  0.69 us (2%)
    ppermute x6, starting transfers between devices, swap(): return lax.ppermute(block, axis, [(i, i ^ offset) for i in range(count)])  8.33 us
    pallas_call x1, Pallas kernels, cache_call(): pl.pallas_call(functools.partial(cache_kernel, near, far), out_shape=(plt...  4.91 us
    ppermute x6, waiting for transfers between devices, swap(): return lax.ppermute(block, axis, [(i, i ^ offset) for i in range(count)])  3.95 us
    dot_general x2, matrix products, on_device(): jnp.einsum('md,dkc->kmc', x, y, preferred_element_type=jnp.float32)  3.85 us
    all_to_all x1, starting transfers between devices, on_device(): inner = lax.all_to_all(inner, 'tp', 0, 0)  3.25 us
    pallas_call x1, Pallas kernels, final_call(): pl.pallas_call(functools.partial(final_kernel, width, len(packs)), out_sh...  1.52 us
    pallas_call x1, Pallas kernels, pack_call(): pl.pallas_call(pack_kernel, out_shape=pltpu.VMEM((kinds, share, down.shap...  0.93 us
    unnamed x4, local copies, waits for them, and re-layouts  0.81 us
  transfers between devices with their start and end apart: 7, of which 3 were waited for; matrix products, arithmetic and copies ran while one was open for 12% of the time, Pallas kernels for 17%

profile of v9, /device:TPU:0, one launch (start us, length us, event | category | flops | bytes accessed | tf_op | source)
XLA Modules:
  0.0 30.8 jit_solution(5020767163604716288)
XLA Ops:
  0.6 0.9 %pack_factors.1.rest_0_.rest_7_ = bf16[2,16,2304]{2,1,0:T(8,128)(2,1)S(1)} custom-call(bf16[2,64,2048]{2,1,0:T(8,128)(2,1)} %down_ref.1, bf16[2,16,256]{2,1,0:T(8,128)(2,1)} %bitcast.13), custom_call_target="tpu_custom_call" | custom-call | tf_op jit(solution)/shard_map/pack_factors/pallas_call | solution.py:211
  1.6 4.1 %collective-permute-start = (bf16[2,16,2304]{2,1,0:T(8,128)(2,1)S(1)}, bf16[2,16,2304]{2,1,0:T(8,128)(2,1)S(1)}, u32[]{:S(2)}, u32[]{:S(2)}) collective-permute-start(bf16[2,16,2304]{2,1,0:T(8,128)(2,1)S(1)} %pack_factors.1.rest_0_.rest_7_), channel_id=1, source_target_pairs={{0,8},{4,12},{8,0},{12,4},{1,9},{5,13},{9,1},{13,5},{2,10},{6,14},... | collective-permute-start | bytes 442376 | tf_op jit(solution)/shard_map/ppermute | solution.py:386
  5.7 1.6 %collective-permute-start.4 = (bf16[2,16,2304]{2,1,0:T(8,128)(2,1)S(1)}, bf16[2,16,2304]{2,1,0:T(8,128)(2,1)S(1)}, u32[]{:S(2)}, u32[]{:S(2)}) collective-permute-start(bf16[2,16,2304]{2,1,0:T(8,128)(2,1)S(1)} %pack_factors.1.rest_0_.rest_7_), channel_id=1, source_target_pairs={{0,4},{4,0},{8,12},{12,8},{1,5},{5,1},{9,13},{13,9},{2,6},{6,2},{1... | collective-permute-start | bytes 442376 | tf_op jit(solution)/shard_map/ppermute | solution.py:386
  7.2 0.4 %collective-permute-start.3 = (bf16[4,8,2048]{2,1,0:T(8,128)(2,1)}, bf16[4,8,2048]{2,1,0:T(8,128)(2,1)S(1)}, u32[]{:S(2)}, u32[]{:S(2)}) collective-permute-start(bf16[4,8,2048]{2,1,0:T(8,128)(2,1)} %hidden_ref.1), channel_id=1, source_target_pairs={{0,3},{1,2},{2,1},{3,0},{4,7},{5,6},{6,5},{7,4},{8,11},{9,10},{10,... | collective-permute-start | bytes 393224 | tf_op jit(solution)/shard_map/ppermute | solution.py:386
  7.6 1.2 %collective-permute-start.1 = (bf16[4,8,2048]{2,1,0:T(8,128)(2,1)}, bf16[4,8,2048]{2,1,0:T(8,128)(2,1)S(1)}, u32[]{:S(2)}, u32[]{:S(2)}) collective-permute-start(bf16[4,8,2048]{2,1,0:T(8,128)(2,1)} %hidden_ref.1), channel_id=1, source_target_pairs={{0,1},{1,0},{2,3},{3,2},{4,5},{5,4},{6,7},{7,6},{8,9},{9,8},{10,11... | collective-permute-start | bytes 393224 | tf_op jit(solution)/shard_map/ppermute | solution.py:386
  8.9 0.5 %collective-permute-start.2 = (bf16[4,8,2048]{2,1,0:T(8,128)(2,1)}, bf16[4,8,2048]{2,1,0:T(8,128)(2,1)S(1)}, u32[]{:S(2)}, u32[]{:S(2)}) collective-permute-start(bf16[4,8,2048]{2,1,0:T(8,128)(2,1)} %hidden_ref.1), channel_id=1, source_target_pairs={{0,2},{1,3},{2,0},{3,1},{4,6},{5,7},{6,4},{7,5},{8,10},{9,11},{10,... | collective-permute-start | bytes 393224 | tf_op jit(solution)/shard_map/ppermute | solution.py:386
  9.4 4.9 %cache_attention.1 = (bf16[4096,2,256]{2,1,0:T(2,128)(2,1)S(1)}, bf16[4096,2,256]{2,1,0:T(2,128)(2,1)S(1)}, f32[64,128]{1,0:T(8,128)S(1)}, bf16[2,256]{1,0:T(2,1...) custom-call(s32[8]{0:T(128)} %lengths_ref.1, ...), custom_call_target="tpu_custom_call" | custom-call | flops 140509184 | bytes 13631488 | tf_op jit(solution)/shard_map/cache_attention/pallas_call | solution.py:157
  14.3 0.0 copy-start
  14.3 0.0 collective-permute-done.rest_2_.rest_9_
  14.3 0.0 collective-permute-done.3.rest_3_
  14.3 0.0 collective-permute-done.4.rest_1_.rest_8_
  14.4 0.5 %collective-permute-start.5 = (bf16[2,16,2304]{2,1,0:T(8,128)(2,1)S(1)}, bf16[2,16,2304]{2,1,0:T(8,128)(2,1)S(1)}, u32[]{:S(2)}, u32[]{:S(2)}) collective-permute-start(bf16[2,16,2304]{2,1,0:T(8,128)(2,1)S(1)} %collective-permute-done.rest_2_.rest_9_), channel_id=1, source_target_pairs={{0,4},{4,0},{8,12},{12,8},{1,5},{5,1},{9,13},{13,9},{2,6},{6,2},{1... | collective-permute-start | bytes 442376 | tf_op jit(solution)/shard_map/ppermute | solution.py:386
  14.9 0.0 collective-permute-done.1.rest_1_
  14.9 1.2 %collective-permute-done.2.rest_2_ = bf16[4,8,2048]{2,1,0:T(8,128)(2,1)S(1)} collective-permute-done((bf16[4,8,2048]{2,1,0:T(8,128)(2,1)}, bf16[4,8,2048]{2,1,0:T(8,128)(2,1)S(1)}, u32[]{:S(2)}, u32[]{:S(2)}) %collective-permute-start.2) | collective-permute-done | bytes 131104 | tf_op jit(solution)/shard_map/ppermute | solution.py:386
  16.1 0.2 scale_features.1
  16.3 0.8 %fusion.7.far_ref = f32[2,32,256]{2,1,0:T(8,128)S(1)} fusion(bf16[4096,2,256]{2,1,0:T(2,128)(2,1)S(1)} %get-tuple-element.28, bf16[32,4096]{1,0:T(8,128)(2,1)S(1)} %get-tuple-element.29), kind=kOutput, calls=%fused_computation.5 | convolution fusion | flops 134217728 | bytes 4521984 | tf_op jit(solution)/shard_map/md,dkc->kmc/dot_general | solution.py:445
  17.1 2.7 %collective-permute-done.5.rest_3_.rest_10_ = bf16[2,16,2304]{2,1,0:T(8,128)(2,1)S(1)} collective-permute-done((bf16[2,16,2304]{2,1,0:T(8,128)(2,1)S(1)}, bf16[2,16,2304]{2,1,0:T(8,128)(2,1)S(1)}, u32[]{:S(2)}, u32[]{:S(2)}) %collective-permute-start.5) | collective-permute-done | bytes 147488 | tf_op jit(solution)/shard_map/ppermute | solution.py:386
  19.9 0.0 copy-done
  19.9 0.3 rank_inner.1
  20.2 0.7 %reshape.12 = f32[4,1,1024]{2,1,0:T(1,128)} reshape(f32[4,32,32]{2,1,0:T(8,128)S(1)} %rank_inner.1) | data formatting | bytes 32768
  20.9 3.3 %all-to-all-start = ((f32[4,1,1024]{2,1,0:T(1,128)}), f32[4,1,1024]{2,1,0:T(1,128)S(1)}, u32[]{:S(2)}, u32[]{:S(2)}) async-start(f32[4,1,1024]{2,1,0:T(1,128)} %reshape.12), calls=%async_computation | async-start | bytes 32768 | tf_op jit(solution)/shard_map/all_to_all | solution.py:438
  24.1 3.0 %fusion.4.near_ref = f32[2,32,256]{2,1,0:T(8,128)S(1)} fusion(bf16[4096,2,256]{2,1,0:T(2,128)(2,1)} %copy-done, bf16[32,4096]{1,0:T(8,128)(2,1)S(1)} %get-tuple-element.27), kind=kOutput, calls=%fused_computation.4 | convolution fusion | flops 134217728 | bytes 4521984 | tf_op jit(solution)/shard_map/md,dkc->kmc/dot_general | solution.py:445
  27.2 0.8 %all-to-all-done = f32[4,1,1024]{2,1,0:T(1,128)S(1)} async-done(((f32[4,1,1024]{2,1,0:T(1,128)}), f32[4,1,1024]{2,1,0:T(1,128)S(1)}, u32[]{:S(2)}, u32[]{:S(2)}) %all-to-all-start) | async-done | bytes 16416 | tf_op jit(solution)/shard_map/all_to_all | solution.py:438
  28.0 0.5 %broadcast = f32[]{:T(128)} broadcast(f32[]{:T(128)} %constant.2), dimensions={} | broadcast | bytes 8 | tf_op jit(solution)/shard_map/all_to_all | solution.py:438
  28.5 0.7 %reduce = f32[4,1024]{1,0:T(4,128)S(1)} reduce(f32[4,1,1024]{2,1,0:T(1,128)S(1)} %all-to-all-done, f32[]{:T(128)} %broadcast), dimensions={1}, to_apply=%all_to_all.3.reduce_sub_computation | reduce | bytes 32772 | tf_op jit(solution)/shard_map/all_to_all | solution.py:438
  29.2 0.1 reshape.13.rest_6_
  29.3 1.5 %fresh_attention.1 = (bf16[4,8,256]{2,1,0:T(8,128)(2,1)}, bf16[4,8,256]{2,1,0:T(8,128)(2,1)}, bf16[4,8,2048]{2,1,0:T(8,128)(2,1)}) custom-call(f32[2,32,256]{2,1,0:T(8,128)S(1)} %fusion.4.near_ref, f32[2,32,256]{2,1,0:T(8,128)S(1)} %fusion.7.far_ref, f32[32,128]{1,0:T(8,128)S(1)} %get-tuple-element.30.square_ref, ...), custom_call_target="tpu_custom_call" | custom-call | tf_op jit(solution)/shard_map/fresh_attention/pallas_call | solution.py:372
Async XLA Ops:
  1.6 12.8 %collective-permute-start = (bf16[2,16,2304]{2,1,0:T(8,128)(2,1)S(1)}, bf16[2,16,2304]{2,1,0:T(8,128)(2,1)S(1)}, u32[]{:S(2)}, u32[]{:S(2)}) collective-permute-start(bf16[2,16,2304]{2,1,0:T(8,128)(2,1)S(1)} %pack_factors.1.rest_0_.rest_7_), channel_id=1, source_target_pairs={{0,8},{4,12},{8,0},{12,4},{1,9},{5,13},{9,1},{13,5},{2,10},{6,14},... | collective-permute-start | bytes 442376 | tf_op jit(solution)/shard_map/ppermute | solution.py:386
  5.7 8.7 %collective-permute-start.4 = (bf16[2,16,2304]{2,1,0:T(8,128)(2,1)S(1)}, bf16[2,16,2304]{2,1,0:T(8,128)(2,1)S(1)}, u32[]{:S(2)}, u32[]{:S(2)}) collective-permute-start(bf16[2,16,2304]{2,1,0:T(8,128)(2,1)S(1)} %pack_factors.1.rest_0_.rest_7_), channel_id=1, source_target_pairs={{0,4},{4,0},{8,12},{12,8},{1,5},{5,1},{9,13},{13,9},{2,6},{6,2},{1... | collective-permute-start | bytes 442376 | tf_op jit(solution)/shard_map/ppermute | solution.py:386
  7.2 7.1 %collective-permute-start.3 = (bf16[4,8,2048]{2,1,0:T(8,128)(2,1)}, bf16[4,8,2048]{2,1,0:T(8,128)(2,1)S(1)}, u32[]{:S(2)}, u32[]{:S(2)}) collective-permute-start(bf16[4,8,2048]{2,1,0:T(8,128)(2,1)} %hidden_ref.1), channel_id=1, source_target_pairs={{0,3},{1,2},{2,1},{3,0},{4,7},{5,6},{6,5},{7,4},{8,11},{9,10},{10,... | collective-permute-start | bytes 393224 | tf_op jit(solution)/shard_map/ppermute | solution.py:386
  7.6 7.3 %collective-permute-start.1 = (bf16[4,8,2048]{2,1,0:T(8,128)(2,1)}, bf16[4,8,2048]{2,1,0:T(8,128)(2,1)S(1)}, u32[]{:S(2)}, u32[]{:S(2)}) collective-permute-start(bf16[4,8,2048]{2,1,0:T(8,128)(2,1)} %hidden_ref.1), channel_id=1, source_target_pairs={{0,1},{1,0},{2,3},{3,2},{4,5},{5,4},{6,7},{7,6},{8,9},{9,8},{10,11... | collective-permute-start | bytes 393224 | tf_op jit(solution)/shard_map/ppermute | solution.py:386
  8.9 7.2 %collective-permute-start.2 = (bf16[4,8,2048]{2,1,0:T(8,128)(2,1)}, bf16[4,8,2048]{2,1,0:T(8,128)(2,1)S(1)}, u32[]{:S(2)}, u32[]{:S(2)}) collective-permute-start(bf16[4,8,2048]{2,1,0:T(8,128)(2,1)} %hidden_ref.1), channel_id=1, source_target_pairs={{0,2},{1,3},{2,0},{3,1},{4,6},{5,7},{6,4},{7,5},{8,10},{9,11},{10,... | collective-permute-start | bytes 393224 | tf_op jit(solution)/shard_map/ppermute | solution.py:386
  14.3 5.6 %copy-start = (bf16[4096,2,256]{2,1,0:T(2,128)(2,1)}, bf16[4096,2,256]{2,1,0:T(2,128)(2,1)S(1)}, u32[]{:S(2)}) copy-start(bf16[4096,2,256]{2,1,0:T(2,128)(2,1)S(1)} %get-tuple-element.22) | copy-start | bytes 12582916
  14.4 5.5 %collective-permute-start.5 = (bf16[2,16,2304]{2,1,0:T(8,128)(2,1)S(1)}, bf16[2,16,2304]{2,1,0:T(8,128)(2,1)S(1)}, u32[]{:S(2)}, u32[]{:S(2)}) collective-permute-start(bf16[2,16,2304]{2,1,0:T(8,128)(2,1)S(1)} %collective-permute-done.rest_2_.rest_9_), channel_id=1, source_target_pairs={{0,4},{4,0},{8,12},{12,8},{1,5},{5,1},{9,13},{13,9},{2,6},{6,2},{1... | collective-permute-start | bytes 442376 | tf_op jit(solution)/shard_map/ppermute | solution.py:386
  20.9 7.1 %all-to-all-start = ((f32[4,1,1024]{2,1,0:T(1,128)}), f32[4,1,1024]{2,1,0:T(1,128)S(1)}, u32[]{:S(2)}, u32[]{:S(2)}) async-start(f32[4,1,1024]{2,1,0:T(1,128)} %reshape.12), calls=%async_computation | async-start | bytes 32768 | tf_op jit(solution)/shard_map/all_to_all | solution.py:438

commit v10 on v8

--- a/solution.py
+++ b/solution.py
@@ -31,9 +31,22 @@
     return jnp.concatenate(tiles, axis=0)
 
 
+def copy_blocks(offsets, width, weight_ref, out_ref, sems):
+    me = lax.axis_index("tp")
+    copies = []
+    for i, offset in enumerate(offsets):
+        block = pl.ds(pl.multiple_of((me ^ offset) * width, width), width)
+        copies.append(
+            pltpu.make_async_copy(
+                weight_ref.at[block], out_ref.at[pl.ds(i * width, width)], sems.at[i]
+            )
+        )
+        copies[-1].start()
+    return copies
+
+
 def cache_kernel(
     near,
-    far,
     lengths_ref,
     query_ref,
     key_ref,
@@ -43,7 +56,6 @@
     hidden_ref,
     weight_ref,
     near_out,
-    far_out,
     gain_out,
     bias_out,
     hidden_out,
@@ -60,6 +72,7 @@
     value_buffer,
     score_buffer,
     sems,
+    weight_sems,
 ):
     steps, rows, query_width = query_ref.shape
     cache_span = key_ref.shape[1]
@@ -79,15 +92,10 @@
         (bias_ref, bias_out),
         (hidden_ref, hidden_out),
     ]
-    me = lax.axis_index("tp")
-    width = hidden_ref.shape[2]
-    for offsets, out in ((near, near_out), (far, far_out)):
-        for i, offset in enumerate(offsets):
-            block = pl.ds(pl.multiple_of((me ^ offset) * width, width), width)
-            copies.append((weight_ref.at[block], out.at[pl.ds(i * width, width)]))
     copies = [pltpu.make_async_copy(*pair, sems.at[i]) for i, pair in enumerate(copies)]
     for copy in copies:
         copy.start()
+    copies += copy_blocks(near, hidden_ref.shape[2], weight_ref, near_out, weight_sems)
 
     copies[0].wait()
     lane = lax.broadcasted_iota(jnp.int32, (rows, HD), 1)
@@ -145,7 +153,7 @@
         copy.wait()
 
 
-def cache_call(near, far, lengths, queries, keys, values, gain, bias, hidden, weight):
+def cache_call(near, lengths, queries, keys, values, gain, bias, hidden, weight):
     steps, rows, query_width = queries.shape
     cache_span, key_width = keys.shape[1:]
     groups = key_width // HD
@@ -155,10 +163,9 @@
     operands = (lengths, queries, keys, values, gain, bias, hidden, weight)
     part = hidden.shape[2]
     return pl.pallas_call(
-        functools.partial(cache_kernel, near, far),
+        functools.partial(cache_kernel, near),
         out_shape=(
             pltpu.VMEM((len(near) * part,) + weight.shape[1:], weight.dtype),
-            pltpu.VMEM((len(far) * part,) + weight.shape[1:], weight.dtype),
             pltpu.VMEM(gain.shape, jnp.float32),
             pltpu.VMEM(bias.shape, bias.dtype),
             pltpu.VMEM(hidden.shape, hidden.dtype),
@@ -170,7 +177,7 @@
             pltpu.VMEM(table, jnp.float32),
         ),
         in_specs=[HBM] * len(operands),
-        out_specs=(VMEM,) * 11,
+        out_specs=(VMEM,) * 10,
         scratch_shapes=[
             pltpu.SMEM(lengths.shape, jnp.int32),
             pltpu.VMEM(queries.shape, queries.dtype),
@@ -178,10 +185,11 @@
             pltpu.VMEM(keys.shape, keys.dtype),
             pltpu.VMEM(values.shape, values.dtype),
             pltpu.VMEM((rows * groups, lines, cache_span), jnp.float32),
-            pltpu.SemaphoreType.DMA((9 + len(near) + len(far),)),
+            pltpu.SemaphoreType.DMA((9,)),
+            pltpu.SemaphoreType.DMA((len(near),)),
         ],
         compiler_params=pltpu.CompilerParams(vmem_limit_bytes=16 << 20),
-        cost_estimate=pl.CostEstimate(flops=2 * 67 << 20, bytes_accessed=13 << 20, transcendentals=0),
+        cost_estimate=pl.CostEstimate(flops=2 * 67 << 20, bytes_accessed=9 << 20, transcendentals=0),
         name="cache_attention",
     )(*[pltpu.with_memory_space_constraint(x, pltpu.HBM) for x in operands])
 
@@ -247,14 +255,15 @@
     )(scaled, *packs)
 
 
-def scale_kernel(near_count, gain_ref, *rest):
-    parts = rest[:-4]
-    scaled_out, near_out, far_out, square_out = rest[-4:]
+def scale_kernel(near, far, weight_ref, gain_ref, *rest):
+    parts = rest[:-6]
+    scaled_out, near_out, far_out, square_out, weight_out, sems = rest[-6:]
     steps, rows, width = parts[0].shape
     chunks = width // HD
+    copies = copy_blocks(far, width, weight_ref, weight_out, sems)
     me = lax.axis_index("tp")
     squares = jnp.zeros(square_out.shape, jnp.float32)
-    for offset, part in enumerate(parts):
+    for k, (offset, part) in enumerate(zip(near + far, parts)):
         block = me ^ offset
         gain = gain_ref[pl.ds(pl.multiple_of(block * chunks, chunks), chunks)]
         values = rows_of(part)
@@ -266,26 +275,31 @@
         at = pl.ds(pl.multiple_of(block * width, width), width)
         scaled = jnp.concatenate(scaled, axis=1)
         scaled_out[:, at] = scaled
-        out, i = (near_out, offset) if offset < near_count else (far_out, offset - near_count)
+        out, i = (near_out, k) if k < len(near) else (far_out, k - len(near))
         out[:, i * width : (i + 1) * width] = scaled
     square_out[...] = jnp.broadcast_to(jnp.sum(squares, axis=1, keepdims=True), squares.shape)
-
-
-def scale_call(near_count, gain, parts):
+    for copy in copies:
+        copy.wait()
+
+
+def scale_call(near, far, weight, gain, parts):
     steps, rows, width = parts[0].shape
     return pl.pallas_call(
-        functools.partial(scale_kernel, near_count),
+        functools.partial(scale_kernel, near, far),
         out_shape=(
             pltpu.VMEM((steps * rows, len(parts) * width), jnp.bfloat16),
-            pltpu.VMEM((steps * rows, near_count * width), jnp.bfloat16),
-            pltpu.VMEM((steps * rows, (len(parts) - near_count) * width), jnp.bfloat16),
+            pltpu.VMEM((steps * rows, len(near) * width), jnp.bfloat16),
+            pltpu.VMEM((steps * rows, len(far) * width), jnp.bfloat16),
             pltpu.VMEM((steps * rows, HD), jnp.float32),
+            pltpu.VMEM((len(far) * width,) + weight.shape[1:], weight.dtype),
         ),
-        in_specs=[VMEM] * (1 + len(parts)),
-        out_specs=(VMEM,) * 4,
+        in_specs=[HBM] + [VMEM] * (1 + len(parts)),
+        out_specs=(VMEM,) * 5,
+        scratch_shapes=[pltpu.SemaphoreType.DMA((len(far),))],
         compiler_params=pltpu.CompilerParams(vmem_limit_bytes=8 << 20),
+        cost_estimate=pl.CostEstimate(flops=0, bytes_accessed=5 << 20, transcendentals=0),
         name="scale_features",
-    )(gain, *parts)
+    )(pltpu.with_memory_space_constraint(weight, pltpu.HBM), gain, *parts)
 
 
 def up_kernel(*refs):
@@ -408,16 +422,14 @@
     gain = input_norm_gain.reshape(width // HD, HD)
     up_part = jnp.transpose(adapter_up_factor, (0, 2, 1))
     direct = wide_count == tp_count == 4
-    beside = swap(hidden, "tp", 1, tp_count)
-    crossed = swap(hidden, "tp", 2, tp_count)
+    tp_parts = [swap(hidden, "tp", offset, tp_count) for offset in (1, 2, 3)]
     if direct:
         pack = pack_call(adapter_down_factor, up_part)
         second = swap(pack, "wide", 2, wide_count)
         first = swap(pack, "wide", 1, wide_count)
     near, far = (0, 1), (2, 3)
-    near_weight, far_weight, gain_rows, bias, mine, *cached = cache_call(
+    near_weight, gain_rows, bias, mine, *cached = cache_call(
         near,
-        far,
         lengths,
         queries,
         stored_rotated_keys,
@@ -427,14 +439,11 @@
         hidden,
         key_value_weight,
     )
-    relayed, gain_rows = lax.optimization_barrier((crossed, gain_rows))
-    relayed = swap(relayed, "tp", 1, tp_count)
     if direct:
         third, gain_rows = lax.optimization_barrier((second, gain_rows))
-        relayed, first = lax.optimization_barrier((relayed, first))
         packs = [pack, first, second, swap(third, "wide", 1, wide_count)]
-    scaled, near_scaled, far_scaled, square = scale_call(
-        len(near), gain_rows, (mine, beside, crossed, relayed)
+    scaled, near_scaled, far_scaled, square, far_weight = scale_call(
+        near, far, key_value_weight, gain_rows, [mine] + tp_parts
     )
     if direct:
         inner = inner_call(scaled, packs)

time: 26.1 us -> 25.5 us (0.977)
  waiting for transfers between devices: 5.56 us -> 4.12 us
  Pallas kernels: 7.93 us -> 8.82 us
    ppermute x9, waiting for transfers between devices: 5.56 us -> 4.12 us  [swap(): return lax.ppermute(block, axis, [(i, i ^ offset) for i in range(count)])]
    pallas_call x2, Pallas kernels: 5.19 us -> 6.07 us  [the longest x1 3.7 us: cache_call(): pl.pallas_call(functools.partial(cache_kernel, near), out_shape=(pltpu.VM...]
  transfers between devices with their start and end apart: 9 -> 9, of which waited for: 4 -> 4; matrix products, arithmetic and copies ran while one was open for 6% -> 7% of each run, Pallas kernels for 24% -> 24%
where the time goes in v10:
time: 25.5 us; the launch traced here: 25.3 us
  starting transfers between devices  10 us (39%)
  Pallas kernels  8.82 us (35%)
  waiting for transfers between devices  4.12 us (16%)
  matrix products  1.67 us (7%)
  between operations  0.68 us (3%)
    ppermute x9, starting transfers between devices, swap(): return lax.ppermute(block, axis, [(i, i ^ offset) for i in range(count)])  10 us
    ppermute x9, waiting for transfers between devices, swap(): return lax.ppermute(block, axis, [(i, i ^ offset) for i in range(count)])  4.12 us
    pallas_call x1, Pallas kernels, cache_call(): pl.pallas_call(functools.partial(cache_kernel, near), out_shape=(pltpu.VM...  3.7 us
    pallas_call x1, Pallas kernels, scale_call(): pl.pallas_call(functools.partial(scale_kernel, near, far), out_shape=(plt...  2.37 us
    dot_general x2, matrix products, on_device(): jnp.einsum('md,dkc->kmc', x, y, preferred_element_type=jnp.float32)  1.67 us
    pallas_call x1, Pallas kernels, final_call(): pl.pallas_call(functools.partial(final_kernel, width, len(inner)), out_sh...  1.55 us
    pallas_call x1, Pallas kernels, pack_call(): pl.pallas_call(pack_kernel, out_shape=pltpu.VMEM((kinds, share, down.shap...  0.93 us
  transfers between devices with their start and end apart: 9, of which 4 were waited for; matrix products, arithmetic and copies ran while one was open for 7% of the time, Pallas kernels for 24%

profile of v10, /device:TPU:0, one launch (start us, length us, event | category | flops | bytes accessed | tf_op | source)
XLA Modules:
  0.0 25.3 jit_solution(2491222209417449502)
XLA Ops:
  0.6 0.9 %pack_factors.1.rest_0_.rest_10_ = bf16[2,16,2304]{2,1,0:T(8,128)(2,1)S(1)} custom-call(bf16[2,64,2048]{2,1,0:T(8,128)(2,1)} %down_ref.1, bf16[2,16,256]{2,1,0:T(8,128)(2,1)} %bitcast.13), custom_call_target="tpu_custom_call" | custom-call | tf_op jit(solution)/shard_map/pack_factors/pallas_call | solution.py:219
  1.6 4.1 %collective-permute-start = (bf16[2,16,2304]{2,1,0:T(8,128)(2,1)S(1)}, bf16[2,16,2304]{2,1,0:T(8,128)(2,1)S(1)}, u32[]{:S(2)}, u32[]{:S(2)}) collective-permute-start(bf16[2,16,2304]{2,1,0:T(8,128)(2,1)S(1)} %pack_factors.1.rest_0_.rest_10_), channel_id=1, source_target_pairs={{0,8},{4,12},{8,0},{12,4},{1,9},{5,13},{9,1},{13,5},{2,10},{6,14},... | collective-permute-start | bytes 442376 | tf_op jit(solution)/shard_map/ppermute | solution.py:402
  5.7 0.0 collective-permute-start.1
  5.7 1.5 %collective-permute-start.2 = (bf16[4,8,2048]{2,1,0:T(8,128)(2,1)}, bf16[4,8,2048]{2,1,0:T(8,128)(2,1)S(1)}, u32[]{:S(2)}, u32[]{:S(2)}) collective-permute-start(bf16[4,8,2048]{2,1,0:T(8,128)(2,1)} %hidden_ref.1), channel_id=1, source_target_pairs={{0,2},{1,3},{2,0},{3,1},{4,6},{5,7},{6,4},{7,5},{8,10},{9,11},{10,... | collective-permute-start | bytes 393224 | tf_op jit(solution)/shard_map/ppermute | solution.py:402
  7.2 0.4 %collective-permute-start.3 = (bf16[4,8,2048]{2,1,0:T(8,128)(2,1)}, bf16[4,8,2048]{2,1,0:T(8,128)(2,1)S(1)}, u32[]{:S(2)}, u32[]{:S(2)}) collective-permute-start(bf16[4,8,2048]{2,1,0:T(8,128)(2,1)} %hidden_ref.1), channel_id=1, source_target_pairs={{0,3},{1,2},{2,1},{3,0},{4,7},{5,6},{6,5},{7,4},{8,11},{9,10},{10,... | collective-permute-start | bytes 393224 | tf_op jit(solution)/shard_map/ppermute | solution.py:402
  7.5 1.6 %collective-permute-start.4 = (bf16[2,16,2304]{2,1,0:T(8,128)(2,1)S(1)}, bf16[2,16,2304]{2,1,0:T(8,128)(2,1)S(1)}, u32[]{:S(2)}, u32[]{:S(2)}) collective-permute-start(bf16[2,16,2304]{2,1,0:T(8,128)(2,1)S(1)} %pack_factors.1.rest_0_.rest_10_), channel_id=1, source_target_pairs={{0,4},{4,0},{8,12},{12,8},{1,5},{5,1},{9,13},{13,9},{2,6},{6,2},{1... | collective-permute-start | bytes 442376 | tf_op jit(solution)/shard_map/ppermute | solution.py:402
  9.1 3.7 %cache_attention.1 = (bf16[4096,2,256]{2,1,0:T(2,128)(2,1)S(1)}, f32[64,128]{1,0:T(8,128)S(1)}, bf16[2,256]{1,0:T(2,128)(2,1)S(1)}, bf16[4,8,2048]{2,1,0:T(8,128...) custom-call(s32[8]{0:T(128)} %lengths_ref.1, ...), custom_call_target="tpu_custom_call" | custom-call | flops 140509184 | bytes 9437184 | tf_op jit(solution)/shard_map/cache_attention/pallas_call | solution.py:165
  12.8 0.0 collective-permute-done.rest_2_.rest_12_
  12.8 0.6 %collective-permute-start.5 = (bf16[2,16,2304]{2,1,0:T(8,128)(2,1)S(1)}, bf16[2,16,2304]{2,1,0:T(8,128)(2,1)S(1)}, u32[]{:S(2)}, u32[]{:S(2)}) collective-permute-start(bf16[2,16,2304]{2,1,0:T(8,128)(2,1)S(1)} %collective-permute-done.rest_2_.rest_12_), channel_id=1, source_target_pairs={{0,4},{4,0},{8,12},{12,8},{1,5},{5,1},{9,13},{13,9},{2,6},{6,2},{1... | collective-permute-start | bytes 442376 | tf_op jit(solution)/shard_map/ppermute | solution.py:402
  13.4 0.0 collective-permute-done.1.rest_1_
  13.5 0.0 collective-permute-done.2.rest_2_
  13.5 0.8 %collective-permute-done.3.rest_3_ = bf16[4,8,2048]{2,1,0:T(8,128)(2,1)S(1)} collective-permute-done((bf16[4,8,2048]{2,1,0:T(8,128)(2,1)}, bf16[4,8,2048]{2,1,0:T(8,128)(2,1)S(1)}, u32[]{:S(2)}, u32[]{:S(2)}) %collective-permute-start.3) | collective-permute-done | bytes 131104 | tf_op jit(solution)/shard_map/ppermute | solution.py:402
  14.2 2.4 %scale_features.1 = (bf16[32,8192]{1,0:T(8,128)(2,1)S(1)}, bf16[32,4096]{1,0:T(8,128)(2,1)S(1)}, bf16[32,4096]{1,0:T(8,128)(2,1)S(1)}, f32[32,128]{1,0:T(8,128)S(1)}, bf16[4096,2,256]{2,1,0:T(2,128)(2,1)S(1)}) custom-call(bf16[8192,2,256]{2,1,0:T(2,128)(2,1)} %weight_ref.3, f32[64,128]{1,0:T(8,128)S(1)} %get-tuple-element.24.gain_ref, ...), custom_call_target="tpu_custom_call" | custom-call | bytes 5242880 | tf_op jit(solution)/shard_map/scale_features/pallas_call | solution.py:287
  16.6 0.8 %fusion.4.near_ref = f32[2,32,256]{2,1,0:T(8,128)S(1)} fusion(bf16[4096,2,256]{2,1,0:T(2,128)(2,1)S(1)} %get-tuple-element.22, bf16[32,4096]{1,0:T(8,128)(2,1)S(1)} %get-tuple-element.26), kind=kOutput, calls=%fused_computation.4 | convolution fusion | flops 134217728 | bytes 4521984 | tf_op jit(solution)/shard_map/md,dkc->kmc/dot_general | solution.py:458
  17.4 0.0 collective-permute-done.4.rest_1_.rest_11_
  17.4 1.2 %collective-permute-done.5.rest_3_.rest_13_ = bf16[2,16,2304]{2,1,0:T(8,128)(2,1)S(1)} collective-permute-done((bf16[2,16,2304]{2,1,0:T(8,128)(2,1)S(1)}, bf16[2,16,2304]{2,1,0:T(8,128)(2,1)S(1)}, u32[]{:S(2)}, u32[]{:S(2)}) %collective-permute-start.5) | collective-permute-done | bytes 147488 | tf_op jit(solution)/shard_map/ppermute | solution.py:402
  18.7 0.3 %rank_inner.1.rest_6_ = f32[32,32]{1,0:T(8,128)S(1)} custom-call(bf16[32,8192]{1,0:T(8,128)(2,1)S(1)} %get-tuple-element.28.scaled_ref, bf16[2,16,2304]{2,1,0:T(8,128)(2,1)S(1)} %pack_factors.1.rest_0_.rest_10_, bf16[2,16,2304]{2,1,0:T(8,128)(2,1)S(1)} %collective-permute-done.4.rest_1_.rest_11_, ...), custom_call_target="tpu_custom_call" | custom-call | tf_op jit(solution)/shard_map/rank_inner/pallas_call | solution.py:248
  18.9 0.0 collective-permute-start.6
  18.9 1.7 %collective-permute-start.7 = (f32[32,32]{1,0:T(8,128)S(1)}, f32[32,32]{1,0:T(8,128)S(1)}, u32[]{:S(2)}, u32[]{:S(2)}) collective-permute-start(f32[32,32]{1,0:T(8,128)S(1)} %rank_inner.1.rest_6_), channel_id=1, source_target_pairs={{0,2},{1,3},{2,0},{3,1},{4,6},{5,7},{6,4},{7,5},{8,10},{9,11},{10,... | collective-permute-start | bytes 12296 | tf_op jit(solution)/shard_map/ppermute | solution.py:402
  20.6 0.2 collective-permute-start.8
  20.8 0.8 %fusion.7.far_ref = f32[2,32,256]{2,1,0:T(8,128)S(1)} fusion(bf16[4096,2,256]{2,1,0:T(2,128)(2,1)S(1)} %get-tuple-element.27, bf16[32,4096]{1,0:T(8,128)(2,1)S(1)} %get-tuple-element.31), kind=kOutput, calls=%fused_computation.5 | convolution fusion | flops 134217728 | bytes 4521984 | tf_op jit(solution)/shard_map/md,dkc->kmc/dot_general | solution.py:458
  21.6 0.0 collective-permute-done.6.rest_7_
  21.6 1.1 %collective-permute-done.7.rest_8_ = f32[32,32]{1,0:T(8,128)S(1)} collective-permute-done((f32[32,32]{1,0:T(8,128)S(1)}, f32[32,32]{1,0:T(8,128)S(1)}, u32[]{:S(2)}, u32[]{:S(2)}) %collective-permute-start.7) | collective-permute-done | bytes 4128 | tf_op jit(solution)/shard_map/ppermute | solution.py:402
  22.7 1.0 %collective-permute-done.8.rest_9_ = f32[32,32]{1,0:T(8,128)S(1)} collective-permute-done((f32[32,32]{1,0:T(8,128)S(1)}, f32[32,32]{1,0:T(8,128)S(1)}, u32[]{:S(2)}, u32[]{:S(2)}) %collective-permute-start.8) | collective-permute-done | bytes 4128 | tf_op jit(solution)/shard_map/ppermute | solution.py:402
  23.8 1.5 %fresh_attention.1 = (bf16[4,8,256]{2,1,0:T(8,128)(2,1)}, bf16[4,8,256]{2,1,0:T(8,128)(2,1)}, bf16[4,8,2048]{2,1,0:T(8,128)(2,1)}) custom-call(f32[2,32,256]{2,1,0:T(8,128)S(1)} %fusion.4.near_ref, f32[2,32,256]{2,1,0:T(8,128)S(1)} %fusion.7.far_ref, f32[32,128]{1,0:T(8,128)S(1)} %get-tuple-element.32.square_ref, ...), custom_call_target="tpu_custom_call" | custom-call | tf_op jit(solution)/shard_map/fresh_attention/pallas_call | solution.py:387
Async XLA Ops:
  1.6 11.3 %collective-permute-start = (bf16[2,16,2304]{2,1,0:T(8,128)(2,1)S(1)}, bf16[2,16,2304]{2,1,0:T(8,128)(2,1)S(1)}, u32[]{:S(2)}, u32[]{:S(2)}) collective-permute-start(bf16[2,16,2304]{2,1,0:T(8,128)(2,1)S(1)} %pack_factors.1.rest_0_.rest_10_), channel_id=1, source_target_pairs={{0,8},{4,12},{8,0},{12,4},{1,9},{5,13},{9,1},{13,5},{2,10},{6,14},... | collective-permute-start | bytes 442376 | tf_op jit(solution)/shard_map/ppermute | solution.py:402
  5.7 7.8 %collective-permute-start.1 = (bf16[4,8,2048]{2,1,0:T(8,128)(2,1)}, bf16[4,8,2048]{2,1,0:T(8,128)(2,1)S(1)}, u32[]{:S(2)}, u32[]{:S(2)}) collective-permute-start(bf16[4,8,2048]{2,1,0:T(8,128)(2,1)} %hidden_ref.1), channel_id=1, source_target_pairs={{0,1},{1,0},{2,3},{3,2},{4,5},{5,4},{6,7},{7,6},{8,9},{9,8},{10,11... | collective-permute-start | bytes 393224 | tf_op jit(solution)/shard_map/ppermute | solution.py:402
  5.7 7.8 %collective-permute-start.2 = (bf16[4,8,2048]{2,1,0:T(8,128)(2,1)}, bf16[4,8,2048]{2,1,0:T(8,128)(2,1)S(1)}, u32[]{:S(2)}, u32[]{:S(2)}) collective-permute-start(bf16[4,8,2048]{2,1,0:T(8,128)(2,1)} %hidden_ref.1), channel_id=1, source_target_pairs={{0,2},{1,3},{2,0},{3,1},{4,6},{5,7},{6,4},{7,5},{8,10},{9,11},{10,... | collective-permute-start | bytes 393224 | tf_op jit(solution)/shard_map/ppermute | solution.py:402
  7.2 7.0 %collective-permute-start.3 = (bf16[4,8,2048]{2,1,0:T(8,128)(2,1)}, bf16[4,8,2048]{2,1,0:T(8,128)(2,1)S(1)}, u32[]{:S(2)}, u32[]{:S(2)}) collective-permute-start(bf16[4,8,2048]{2,1,0:T(8,128)(2,1)} %hidden_ref.1), channel_id=1, source_target_pairs={{0,3},{1,2},{2,1},{3,0},{4,7},{5,6},{6,5},{7,4},{8,11},{9,10},{10,... | collective-permute-start | bytes 393224 | tf_op jit(solution)/shard_map/ppermute | solution.py:402
  7.5 9.9 %collective-permute-start.4 = (bf16[2,16,2304]{2,1,0:T(8,128)(2,1)S(1)}, bf16[2,16,2304]{2,1,0:T(8,128)(2,1)S(1)}, u32[]{:S(2)}, u32[]{:S(2)}) collective-permute-start(bf16[2,16,2304]{2,1,0:T(8,128)(2,1)S(1)} %pack_factors.1.rest_0_.rest_10_), channel_id=1, source_target_pairs={{0,4},{4,0},{8,12},{12,8},{1,5},{5,1},{9,13},{13,9},{2,6},{6,2},{1... | collective-permute-start | bytes 442376 | tf_op jit(solution)/shard_map/ppermute | solution.py:402
  12.8 5.8 %collective-permute-start.5 = (bf16[2,16,2304]{2,1,0:T(8,128)(2,1)S(1)}, bf16[2,16,2304]{2,1,0:T(8,128)(2,1)S(1)}, u32[]{:S(2)}, u32[]{:S(2)}) collective-permute-start(bf16[2,16,2304]{2,1,0:T(8,128)(2,1)S(1)} %collective-permute-done.rest_2_.rest_12_), channel_id=1, source_target_pairs={{0,4},{4,0},{8,12},{12,8},{1,5},{5,1},{9,13},{13,9},{2,6},{6,2},{1... | collective-permute-start | bytes 442376 | tf_op jit(solution)/shard_map/ppermute | solution.py:402
  18.9 2.7 %collective-permute-start.6 = (f32[32,32]{1,0:T(8,128)S(1)}, f32[32,32]{1,0:T(8,128)S(1)}, u32[]{:S(2)}, u32[]{:S(2)}) collective-permute-start(f32[32,32]{1,0:T(8,128)S(1)} %rank_inner.1.rest_6_), channel_id=1, source_target_pairs={{0,1},{1,0},{2,3},{3,2},{4,5},{5,4},{6,7},{7,6},{8,9},{9,8},{10,11... | collective-permute-start | bytes 12296 | tf_op jit(solution)/shard_map/ppermute | solution.py:402
  18.9 3.8 %collective-permute-start.7 = (f32[32,32]{1,0:T(8,128)S(1)}, f32[32,32]{1,0:T(8,128)S(1)}, u32[]{:S(2)}, u32[]{:S(2)}) collective-permute-start(f32[32,32]{1,0:T(8,128)S(1)} %rank_inner.1.rest_6_), channel_id=1, source_target_pairs={{0,2},{1,3},{2,0},{3,1},{4,6},{5,7},{6,4},{7,5},{8,10},{9,11},{10,... | collective-permute-start | bytes 12296 | tf_op jit(solution)/shard_map/ppermute | solution.py:402
  20.6 3.2 %collective-permute-start.8 = (f32[32,32]{1,0:T(8,128)S(1)}, f32[32,32]{1,0:T(8,128)S(1)}, u32[]{:S(2)}, u32[]{:S(2)}) collective-permute-start(f32[32,32]{1,0:T(8,128)S(1)} %rank_inner.1.rest_6_), channel_id=1, source_target_pairs={{0,3},{1,2},{2,1},{3,0},{4,7},{5,6},{6,5},{7,4},{8,11},{9,10},{10,... | collective-permute-start | bytes 12296 | tf_op jit(solution)/shard_map/ppermute | solution.py:402

commit v11 on v10

--- a/solution.py
+++ b/solution.py
@@ -54,11 +54,15 @@
     gain_ref,
     bias_ref,
     hidden_ref,
+    down_ref,
+    up_ref,
     weight_ref,
     near_out,
     gain_out,
     bias_out,
     hidden_out,
+    down_out,
+    up_out,
     query_out,
     acc_out,
     top_out,
@@ -91,6 +95,8 @@
         (gain_ref, gain_buffer),
         (bias_ref, bias_out),
         (hidden_ref, hidden_out),
+        (down_ref, down_out),
+        (up_ref, up_out),
     ]
     copies = [pltpu.make_async_copy(*pair, sems.at[i]) for i, pair in enumerate(copies)]
     for copy in copies:
@@ -153,14 +159,14 @@
         copy.wait()
 
 
-def cache_call(near, lengths, queries, keys, values, gain, bias, hidden, weight):
+def cache_call(near, lengths, queries, keys, values, gain, bias, hidden, down, up, weight):
     steps, rows, query_width = queries.shape
     cache_span, key_width = keys.shape[1:]
     groups = key_width // HD
     lines = steps * (query_width // key_width)
     block = (groups, lines * rows, HD)
     table = (steps * rows, HD)
-    operands = (lengths, queries, keys, values, gain, bias, hidden, weight)
+    operands = (lengths, queries, keys, values, gain, bias, hidden, down, up, weight)
     part = hidden.shape[2]
     return pl.pallas_call(
         functools.partial(cache_kernel, near),
@@ -169,6 +175,8 @@
             pltpu.VMEM(gain.shape, jnp.float32),
             pltpu.VMEM(bias.shape, bias.dtype),
             pltpu.VMEM(hidden.shape, hidden.dtype),
+            pltpu.VMEM(down.shape, down.dtype),
+            pltpu.VMEM(up.shape, up.dtype),
             pltpu.VMEM(block, jnp.float32),
             pltpu.VMEM(block, jnp.float32),
             pltpu.VMEM(block, jnp.float32),
@@ -177,7 +185,7 @@
             pltpu.VMEM(table, jnp.float32),
         ),
         in_specs=[HBM] * len(operands),
-        out_specs=(VMEM,) * 10,
+        out_specs=(VMEM,) * 12,
         scratch_shapes=[
             pltpu.SMEM(lengths.shape, jnp.int32),
             pltpu.VMEM(queries.shape, queries.dtype),
@@ -185,7 +193,7 @@
             pltpu.VMEM(keys.shape, keys.dtype),
             pltpu.VMEM(values.shape, values.dtype),
             pltpu.VMEM((rows * groups, lines, cache_span), jnp.float32),
-            pltpu.SemaphoreType.DMA((9,)),
+            pltpu.SemaphoreType.DMA((11,)),
             pltpu.SemaphoreType.DMA((len(near),)),
         ],
         compiler_params=pltpu.CompilerParams(vmem_limit_bytes=16 << 20),
@@ -198,66 +206,48 @@
     return jnp.concatenate([ref[s].astype(jnp.float32) for s in range(ref.shape[0])], axis=0)
 
 
-def pack_kernel(down_ref, up_ref, out_ref, sems):
-    share = out_ref.shape[1]
-    width = down_ref.shape[2]
-    at = pl.ds(pl.multiple_of(lax.axis_index("tp") * share, share), share)
-    down = pltpu.make_async_copy(
-        down_ref.at[:, at, :], out_ref.at[:, :, pl.ds(0, width)], sems.at[0]
-    )
-    up = pltpu.make_async_copy(
-        up_ref, out_ref.at[:, :, pl.ds(width, up_ref.shape[2])], sems.at[1]
-    )
-    down.start()
-    up.start()
-    down.wait()
-    up.wait()
-
-
-def pack_call(down, up):
-    kinds, share, columns = up.shape
-    return pl.pallas_call(
-        pack_kernel,
-        out_shape=pltpu.VMEM((kinds, share, down.shape[2] + columns), down.dtype),
-        in_specs=[HBM] * 2,
-        out_specs=VMEM,
-        scratch_shapes=[pltpu.SemaphoreType.DMA((2,))],
-        name="pack_factors",
-    )(*[pltpu.with_memory_space_constraint(x, pltpu.HBM) for x in (down, up)])
-
-
-def inner_kernel(scaled_ref, *rest):
-    packs, out_ref = rest[:-1], rest[-1]
-    me = lax.axis_index("wide")
-    width = scaled_ref.shape[1] // len(packs)
-    total = []
-    for offset, pack in enumerate(packs):
-        total.append(
-            lax.dot_general(
-                scaled_ref[:, pl.ds(pl.multiple_of((me ^ offset) * width, width), width)],
-                pack[:, :, :width].reshape(out_ref.shape[1], width),
-                (((1,), (1,)), ((), ())),
-                preferred_element_type=jnp.float32,
-            )
+def inner_kernel(hidden_ref, gain_ref, down_ref, up_ref, beside_ref, out_ref, up_out):
+    width = hidden_ref.shape[2]
+    chunks = width // HD
+    start = pl.multiple_of(lax.axis_index("wide") * chunks, chunks)
+    gain = gain_ref[pl.ds(start, chunks)]
+    values = rows_of(hidden_ref)
+    scaled = [
+        (values[:, i * HD : (i + 1) * HD] * gain[i : i + 1]).astype(jnp.bfloat16)
+        for i in range(chunks)
+    ]
+    scaled = jnp.concatenate(scaled, axis=1)
+    kinds, ranks, _ = down_ref.shape
+    for kind in range(kinds):
+        out_ref[:, kind * ranks : (kind + 1) * ranks] = lax.dot_general(
+            scaled,
+            down_ref[kind],
+            (((1,), (1,)), ((), ())),
+            preferred_element_type=jnp.float32,
         )
-    out_ref[...] = sum(total[1:], total[0])
-
-
-def inner_call(scaled, packs):
-    kinds, share, _ = packs[0].shape
+    up_out[0] = up_ref[...]
+    up_out[1] = beside_ref[...]
+
+
+def inner_call(hidden, gain, down, up, beside):
+    steps, rows, _ = hidden.shape
+    kinds, ranks, _ = down.shape
     return pl.pallas_call(
         inner_kernel,
-        out_shape=jax.ShapeDtypeStruct((scaled.shape[0], kinds * share), jnp.float32),
-        in_specs=[VMEM] * (1 + len(packs)),
-        out_specs=VMEM,
+        out_shape=(
+            pltpu.VMEM((steps * rows, kinds * ranks), jnp.float32),
+            pltpu.VMEM((2,) + up.shape, up.dtype),
+        ),
+        in_specs=[VMEM] * 5,
+        out_specs=(VMEM,) * 2,
         compiler_params=pltpu.CompilerParams(vmem_limit_bytes=8 << 20),
         name="rank_inner",
-    )(scaled, *packs)
+    )(hidden, gain, down, up, beside)
 
 
 def scale_kernel(near, far, weight_ref, gain_ref, *rest):
-    parts = rest[:-6]
-    scaled_out, near_out, far_out, square_out, weight_out, sems = rest[-6:]
+    parts = rest[:-5]
+    near_out, far_out, square_out, weight_out, sems = rest[-5:]
     steps, rows, width = parts[0].shape
     chunks = width // HD
     copies = copy_blocks(far, width, weight_ref, weight_out, sems)
@@ -272,9 +262,7 @@
             chunk = values[:, i * HD : (i + 1) * HD]
             squares += chunk * chunk
             scaled.append((chunk * gain[i : i + 1]).astype(jnp.bfloat16))
-        at = pl.ds(pl.multiple_of(block * width, width), width)
         scaled = jnp.concatenate(scaled, axis=1)
-        scaled_out[:, at] = scaled
         out, i = (near_out, k) if k < len(near) else (far_out, k - len(near))
         out[:, i * width : (i + 1) * width] = scaled
     square_out[...] = jnp.broadcast_to(jnp.sum(squares, axis=1, keepdims=True), squares.shape)
@@ -287,14 +275,13 @@
     return pl.pallas_call(
         functools.partial(scale_kernel, near, far),
         out_shape=(
-            pltpu.VMEM((steps * rows, len(parts) * width), jnp.bfloat16),
             pltpu.VMEM((steps * rows, len(near) * width), jnp.bfloat16),
             pltpu.VMEM((steps * rows, len(far) * width), jnp.bfloat16),
             pltpu.VMEM((steps * rows, HD), jnp.float32),
             pltpu.VMEM((len(far) * width,) + weight.shape[1:], weight.dtype),
         ),
         in_specs=[HBM] + [VMEM] * (1 + len(parts)),
-        out_specs=(VMEM,) * 5,
+        out_specs=(VMEM,) * 4,
         scratch_shapes=[pltpu.SemaphoreType.DMA((len(far),))],
         compiler_params=pltpu.CompilerParams(vmem_limit_bytes=8 << 20),
         cost_estimate=pl.CostEstimate(flops=0, bytes_accessed=5 << 20, transcendentals=0),
@@ -302,36 +289,31 @@
     )(pltpu.with_memory_space_constraint(weight, pltpu.HBM), gain, *parts)
 
 
-def up_kernel(*refs):
-    packs, up_out = refs[:-1], refs[-1]
-    kinds, share, pack_width = packs[0].shape
-    columns = up_out.shape[1] // kinds
-    me = lax.axis_index("wide") if len(packs) > 1 else 0
-    up_out[...] = jnp.zeros_like(up_out)
-    for offset, pack in enumerate(packs):
+def lay_out(ups, out_ref):
+    kinds, share, columns = ups[0].shape
+    me = lax.axis_index("wide") if len(ups) > 1 else 0
+    out_ref[...] = jnp.zeros_like(out_ref)
+    for offset, up in enumerate(ups):
         for kind in range(kinds):
-            at = pl.multiple_of(((me ^ offset) * kinds + kind) * share, share)
-            up_out[pl.ds(at, share), kind * columns : (kind + 1) * columns] = pack[
-                kind, :, pack_width - columns :
-            ]
-
-
-def final_kernel(width, blocks, near_ref, far_ref, square_ref, bias_ref, *rest):
+            at = pl.multiple_of((kind * len(ups) + (me ^ offset)) * share, share)
+            out_ref[pl.ds(at, share), kind * columns : (kind + 1) * columns] = up[kind]
+
+
+def final_kernel(width, inner_count, up_count, near_ref, far_ref, square_ref, bias_ref, *rest):
     query_ref, acc_ref, top_ref, total_ref, cos_ref, sin_ref = rest[:6]
-    inner_refs = rest[6 : 6 + blocks]
-    packs = rest[6 + blocks : 6 + 2 * blocks]
-    keys_out, values_out, attended_out, inner_buffer, up_ref = rest[6 + 2 * blocks :]
-    up_kernel(*packs, up_ref)
+    inner_refs = rest[6 : 6 + inner_count]
+    up_refs = rest[6 + inner_count : 6 + inner_count + up_count]
+    keys_out, values_out, attended_out, up_ref = rest[6 + inner_count + up_count :]
+    lay_out([ref.at[i] for ref in up_refs for i in range(ref.shape[0])], up_ref)
     steps, rows, columns = keys_out.shape
     count = steps * rows
     groups, size, _ = query_ref.shape
     per_group = size // count
     kinds = bias_ref.shape[0]
     row_scale = lax.rsqrt(square_ref[:, :1] * (1.0 / width) + norm_eps)
-    me = lax.axis_index("tp") if blocks > 1 else 0
-    for i in range(blocks):
-        inner_buffer[me ^ i] = inner_refs[i][...]
-    inner = jnp.concatenate([inner_buffer[i] for i in range(blocks)], axis=1)
+    inner = inner_refs[0][...]
+    for ref in inner_refs[1:]:
+        inner = inner + ref[...]
     high = inner.astype(jnp.bfloat16)
     low = (inner - high.astype(jnp.float32)).astype(jnp.bfloat16)
     lora = jnp.dot(
@@ -379,27 +361,31 @@
                 attended_out[step, :, lanes] = attended[tile : tile + rows]
 
 
-def final_call(shape, width, near, far, square, bias, cached, inner, packs):
+def final_call(shape, width, near, far, square, bias, cached, inner, ups):
     steps, rows, query_width = shape
-    kinds, share, _ = packs[0].shape
-    columns = near.shape[2]
+    kinds, _, columns = near.shape
     small = jax.ShapeDtypeStruct((steps, rows, columns), jnp.bfloat16)
     return pl.pallas_call(
-        functools.partial(final_kernel, width, len(inner)),
+        functools.partial(final_kernel, width, len(inner), len(ups)),
         out_shape=(small, small, jax.ShapeDtypeStruct(shape, jnp.bfloat16)),
-        in_specs=[VMEM] * (4 + len(cached) + len(inner) + len(packs)),
+        in_specs=[VMEM] * (4 + len(cached) + len(inner) + len(ups)),
         out_specs=(VMEM,) * 3,
-        scratch_shapes=[
-            pltpu.VMEM((len(inner),) + inner[0].shape, jnp.float32),
-            pltpu.VMEM((len(packs) * kinds * share, kinds * columns), jnp.bfloat16),
-        ],
+        scratch_shapes=[pltpu.VMEM((inner[0].shape[1], kinds * columns), jnp.bfloat16)],
         compiler_params=pltpu.CompilerParams(vmem_limit_bytes=8 << 20),
         name="fresh_attention",
-    )(near, far, square, bias, *cached, *inner, *packs)
+    )(near, far, square, bias, *cached, *inner, *ups)
 
 
 def swap(block, axis, offset, count):
     return lax.ppermute(block, axis, [(i, i ^ offset) for i in range(count)])
+
+
+def meeting_place():
+    pairs = []
+    for w in range(4):
+        for t in range(4):
+            pairs.append((w * 4 + t, t * 4 + 2 * ((t // 2) ^ ((w + t) & 1)) + w // 2))
+    return pairs
 
 
 def on_device(
@@ -422,13 +408,14 @@
     gain = input_norm_gain.reshape(width // HD, HD)
     up_part = jnp.transpose(adapter_up_factor, (0, 2, 1))
     direct = wide_count == tp_count == 4
+    both = ("wide", "tp")
+    if direct:
+        there = meeting_place()
+        moved = lax.ppermute(hidden, both, there)
+        up_beside = swap(up_part, "wide", 1, wide_count)
     tp_parts = [swap(hidden, "tp", offset, tp_count) for offset in (1, 2, 3)]
-    if direct:
-        pack = pack_call(adapter_down_factor, up_part)
-        second = swap(pack, "wide", 2, wide_count)
-        first = swap(pack, "wide", 1, wide_count)
     near, far = (0, 1), (2, 3)
-    near_weight, gain_rows, bias, mine, *cached = cache_call(
+    near_weight, gain_rows, bias, mine, my_down, my_up, *cached = cache_call(
         near,
         lengths,
         queries,
@@ -437,30 +424,35 @@
         gain,
         key_value_bias,
         hidden,
+        adapter_down_factor,
+        up_part,
         key_value_weight,
     )
     if direct:
-        third, gain_rows = lax.optimization_barrier((second, gain_rows))
-        packs = [pack, first, second, swap(third, "wide", 1, wide_count)]
-    scaled, near_scaled, far_scaled, square, far_weight = scale_call(
+        inner, up_pair = inner_call(moved, gain_rows, my_down, my_up, up_beside)
+        inner = lax.ppermute(inner, both, [(b, a) for a, b in there])
+        gain_rows, up_pair = lax.optimization_barrier((gain_rows, up_pair))
+        ups = [up_pair, swap(up_pair, "wide", 2, wide_count)]
+    near_scaled, far_scaled, square, far_weight = scale_call(
         near, far, key_value_weight, gain_rows, [mine] + tp_parts
     )
     if direct:
-        inner = inner_call(scaled, packs)
-        inner, far_scaled = lax.optimization_barrier((inner, far_scaled))
+        inner, far_scaled, near_scaled = lax.optimization_barrier(
+            (inner, far_scaled, near_scaled)
+        )
         inner = [inner] + [swap(inner, "tp", offset, tp_count) for offset in (1, 2, 3)]
     else:
+        rows_full = lax.all_gather(hidden, "tp", axis=2, tiled=True).astype(jnp.float32)
+        rows_full = (rows_full * input_norm_gain.astype(jnp.float32)).astype(jnp.bfloat16)
         down = lax.all_gather(adapter_down_factor, "wide", axis=2, tiled=True)
-        down = down.reshape(kinds * ranks, width)
-        inner = [jnp.einsum("rd,kd->rk", scaled, down, preferred_element_type=jnp.float32)]
-        packs = [lax.all_gather(up_part, "wide", axis=1, tiled=True)]
+        inner = jnp.einsum("srd,kad->srka", rows_full, down, preferred_element_type=jnp.float32)
+        inner = [inner.reshape(steps * rows, kinds * ranks)]
+        ups = [lax.all_gather(up_part, "wide", axis=1, tiled=True)[None]]
     near_base, far_base = [
         jnp.einsum("md,dkc->kmc", x, y, preferred_element_type=jnp.float32)
         for x, y in ((near_scaled, near_weight), (far_scaled, far_weight))
     ]
-    return final_call(
-        queries.shape, width, near_base, far_base, square, bias, cached, inner, packs
-    )
+    return final_call(queries.shape, width, near_base, far_base, square, bias, cached, inner, ups)
 
 
 def solution(mesh):

time: 25.5 us -> 28.7 us (1.13)
  starting transfers between devices: 10 us -> 17.1 us
  waiting for transfers between devices: 4.12 us -> 1.01 us
  Pallas kernels: 8.82 us -> 8.08 us
    ppermute x9 -> x8, starting transfers between devices: 10 us -> 14.9 us  [swap(): return lax.ppermute(block, axis, [(i, i ^ offset) for i in range(count)])]
    ppermute x9 -> x8, waiting for transfers between devices: 4.12 us -> 1 us  [swap(): return lax.ppermute(block, axis, [(i, i ^ offset) for i in range(count)])]
    ppermute x0 -> x2, starting transfers between devices: none -> 2.23 us  [the longest x1 1.56 us: on_device(): moved = lax.ppermute(hidden, both, there)]
    pallas_call x3 -> x2, Pallas kernels: 2.74 us -> 1.83 us  [the longest x1 1.5 us: final_call(): pl.pallas_call(functools.partial(final_kernel, width, len(inner), len(ups...]
  transfers between devices with their start and end apart: 9 -> 10, of which waited for: 4 -> 2; matrix products, arithmetic and copies ran while one was open for 7% -> 6% of each run, Pallas kernels for 24% -> 23%
where the time goes in v11:
time: 28.7 us; the launch traced here: 28.5 us
  starting transfers between devices  17.1 us (60%)
  Pallas kernels  8.08 us (28%)
  matrix products  1.67 us (6%)
  waiting for transfers between devices  1.01 us (4%)
  between operations  0.69 us (2%)
    ppermute x8, starting transfers between devices, swap(): return lax.ppermute(block, axis, [(i, i ^ offset) for i in range(count)])  14.9 us
    pallas_call x1, Pallas kernels, cache_call(): pl.pallas_call(functools.partial(cache_kernel, near), out_shape=(pltpu.VM...  3.88 us
    pallas_call x1, Pallas kernels, scale_call(): pl.pallas_call(functools.partial(scale_kernel, near, far), out_shape=(plt...  2.38 us
    dot_general x2, matrix products, on_device(): jnp.einsum('md,dkc->kmc', x, y, preferred_element_type=jnp.float32)  1.67 us
    ppermute x1, starting transfers between devices, on_device(): moved = lax.ppermute(hidden, both, there)  1.56 us
    pallas_call x1, Pallas kernels, final_call(): pl.pallas_call(functools.partial(final_kernel, width, len(inner), len(ups...  1.5 us
    ppermute x8, waiting for transfers between devices, swap(): return lax.ppermute(block, axis, [(i, i ^ offset) for i in range(count)])  1 us
    ppermute x1, starting transfers between devices, on_device(): inner = lax.ppermute(inner, both, [(b, a) for a, b in there])  0.67 us
  transfers between devices with their start and end apart: 10, of which 2 were waited for; matrix products, arithmetic and copies ran while one was open for 6% of the time, Pallas kernels for 23%

profile of v11, /device:TPU:0, one launch (start us, length us, event | category | flops | bytes accessed | tf_op | source)
XLA Modules:
  0.0 28.5 jit_solution(1968910783220815402)
XLA Ops:
  0.6 1.6 %collective-permute-start = (bf16[4,8,2048]{2,1,0:T(8,128)(2,1)}, bf16[4,8,2048]{2,1,0:T(8,128)(2,1)S(1)}, u32[]{:S(2)}, u32[]{:S(2)}) collective-permute-start(bf16[4,8,2048]{2,1,0:T(8,128)(2,1)} %hidden_ref.1), channel_id=1, source_target_pairs={{0,0},{1,6},{2,10},{3,12},{4,2},{5,4},{6,8},{7,14},{8,1},{9,7},{10... | collective-permute-start | bytes 393224 | tf_op jit(solution)/shard_map/ppermute | solution.py:414
  2.2 4.5 %collective-permute-start.3 = (bf16[4,8,2048]{2,1,0:T(8,128)(2,1)}, bf16[4,8,2048]{2,1,0:T(8,128)(2,1)S(1)}, u32[]{:S(2)}, u32[]{:S(2)}) collective-permute-start(bf16[4,8,2048]{2,1,0:T(8,128)(2,1)} %hidden_ref.1), channel_id=1, source_target_pairs={{0,1},{1,0},{2,3},{3,2},{4,5},{5,4},{6,7},{7,6},{8,9},{9,8},{10,11... | collective-permute-start | bytes 393224 | tf_op jit(solution)/shard_map/ppermute | solution.py:380
  6.7 2.6 %collective-permute-start.4 = (bf16[4,8,2048]{2,1,0:T(8,128)(2,1)}, bf16[4,8,2048]{2,1,0:T(8,128)(2,1)S(1)}, u32[]{:S(2)}, u32[]{:S(2)}) collective-permute-start(bf16[4,8,2048]{2,1,0:T(8,128)(2,1)} %hidden_ref.1), channel_id=1, source_target_pairs={{0,2},{1,3},{2,0},{3,1},{4,6},{5,7},{6,4},{7,5},{8,10},{9,11},{10,... | collective-permute-start | bytes 393224 | tf_op jit(solution)/shard_map/ppermute | solution.py:380
  9.2 0.0 collective-permute-start.5
  9.2 0.6 %collective-permute-start.1 = (bf16[2,16,256]{2,1,0:T(8,128)(2,1)}, bf16[2,16,256]{2,1,0:T(8,128)(2,1)S(1)}, u32[]{:S(2)}, u32[]{:S(2)}) collective-permute-start(bf16[2,16,256]{2,1,0:T(8,128)(2,1)} %bitcast.13), channel_id=1, source_target_pairs={{0,4},{4,0},{8,12},{12,8},{1,5},{5,1},{9,13},{13,9},{2,6},{6,2},{1... | collective-permute-start | bytes 49160 | tf_op jit(solution)/shard_map/ppermute | solution.py:380
  9.8 3.9 %cache_attention.1 = (bf16[4096,2,256]{2,1,0:T(2,128)(2,1)S(1)}, f32[64,128]{1,0:T(8,128)S(1)}, bf16[2,256]{1,0:T(2,128)(2,1)S(1)}, bf16[4,8,2048]{2,1,0:T(8,128...) custom-call(s32[8]{0:T(128)} %lengths_ref.1, ...), custom_call_target="tpu_custom_call" | custom-call | flops 140509184 | bytes 9437184 | tf_op jit(solution)/shard_map/cache_attention/pallas_call | solution.py:171
  13.7 0.0 collective-permute-done.1.beside_ref
  13.7 0.0 collective-permute-done.hidden_ref
  13.7 0.3 %rank_inner.1 = (f32[32,128]{1,0:T(8,128)S(1)}, bf16[2,2,16,256]{3,2,1,0:T(8,128)(2,1)S(1)}) custom-call(bf16[4,8,2048]{2,1,0:T(8,128)(2,1)S(1)} %collective-permute-done.hidden_ref, f32[64,128]{1,0:T(8,128)S(1)} %get-tuple-element.32.gain_ref, bf16[2,64,2048]{2,1,0:T(8,128)(2,1)S(1)} %get-tuple-element.28.down_ref, ...), custom_call_target="tpu_custom_call" | custom-call | tf_op jit(solution)/shard_map/rank_inner/pallas_call | solution.py:235
  14.1 0.7 %collective-permute-start.2 = (f32[32,128]{1,0:T(8,128)S(1)}, f32[32,128]{1,0:T(8,128)S(1)}, u32[]{:S(2)}, u32[]{:S(2)}) collective-permute-start(f32[32,128]{1,0:T(8,128)S(1)} %get-tuple-element.30), channel_id=1, source_target_pairs={{0,0},{6,1},{10,2},{12,3},{2,4},{4,5},{8,6},{14,7},{1,8},{7,9},{11... | collective-permute-start | bytes 49160 | tf_op jit(solution)/shard_map/ppermute | solution.py:433
  14.7 5.1 %collective-permute-start.9 = (bf16[2,2,16,256]{3,2,1,0:T(8,128)(2,1)S(1)}, bf16[2,2,16,256]{3,2,1,0:T(8,128)(2,1)S(1)}, u32[]{:S(2)}, u32[]{:S(2)}) collective-permute-start(bf16[2,2,16,256]{3,2,1,0:T(8,128)(2,1)S(1)} %get-tuple-element.48.rest_10_), channel_id=1, source_target_pairs={{0,8},{4,12},{8,0},{12,4},{1,9},{5,13},{9,1},{13,5},{2,10},{6,14},... | collective-permute-start | bytes 98312 | tf_op jit(solution)/shard_map/ppermute | solution.py:380
  19.8 0.0 collective-permute-done.3.rest_1_
  19.8 0.0 collective-permute-done.4.rest_2_
  19.8 0.0 collective-permute-done.5.rest_3_
  19.8 2.4 %scale_features.1 = (bf16[32,4096]{1,0:T(8,128)(2,1)S(1)}, bf16[32,4096]{1,0:T(8,128)(2,1)S(1)}, f32[32,128]{1,0:T(8,128)S(1)}, bf16[4096,2,256]{2,1,0:T(2,128)(2,1)S(1)}) custom-call(bf16[8192,2,256]{2,1,0:T(2,128)(2,1)} %weight_ref.3, f32[64,128]{1,0:T(8,128)S(1)} %get-tuple-element.32.gain_ref, bf16[4,8,2048]{2,1,0:T(8,128)(2,1)S(1)} %get-tuple-element.33.rest_0_, ...), custom_call_target="tpu_custom_call" | custom-call | bytes 5242880 | tf_op jit(solution)/shard_map/scale_features/pallas_call | solution.py:275
  22.2 0.0 collective-permute-done.2.rest_6_
  22.2 0.7 %collective-permute-start.6 = (f32[32,128]{1,0:T(8,128)S(1)}, f32[32,128]{1,0:T(8,128)S(1)}, u32[]{:S(2)}, u32[]{:S(2)}) collective-permute-start(f32[32,128]{1,0:T(8,128)S(1)} %collective-permute-done.2.rest_6_), channel_id=1, source_target_pairs={{0,1},{1,0},{2,3},{3,2},{4,5},{5,4},{6,7},{7,6},{8,9},{9,8},{10,11... | collective-permute-start | bytes 49160 | tf_op jit(solution)/shard_map/ppermute | solution.py:380
  22.9 0.8 %collective-permute-start.7 = (f32[32,128]{1,0:T(8,128)S(1)}, f32[32,128]{1,0:T(8,128)S(1)}, u32[]{:S(2)}, u32[]{:S(2)}) collective-permute-start(f32[32,128]{1,0:T(8,128)S(1)} %collective-permute-done.2.rest_6_), channel_id=1, source_target_pairs={{0,2},{1,3},{2,0},{3,1},{4,6},{5,7},{6,4},{7,5},{8,10},{9,11},{10,... | collective-permute-start | bytes 49160 | tf_op jit(solution)/shard_map/ppermute | solution.py:380
  23.7 0.7 %collective-permute-start.8 = (f32[32,128]{1,0:T(8,128)S(1)}, f32[32,128]{1,0:T(8,128)S(1)}, u32[]{:S(2)}, u32[]{:S(2)}) collective-permute-start(f32[32,128]{1,0:T(8,128)S(1)} %collective-permute-done.2.rest_6_), channel_id=1, source_target_pairs={{0,3},{1,2},{2,1},{3,0},{4,7},{5,6},{6,5},{7,4},{8,11},{9,10},{10,... | collective-permute-start | bytes 49160 | tf_op jit(solution)/shard_map/ppermute | solution.py:380
  24.4 0.8 %fusion.4.near_ref = f32[2,32,256]{2,1,0:T(8,128)S(1)} fusion(bf16[4096,2,256]{2,1,0:T(2,128)(2,1)S(1)} %get-tuple-element.26, bf16[32,4096]{1,0:T(8,128)(2,1)S(1)} %get-tuple-element.36), kind=kOutput, calls=%fused_computation.4 | convolution fusion | flops 134217728 | bytes 4521984 | tf_op jit(solution)/shard_map/md,dkc->kmc/dot_general | solution.py:452
  25.2 0.8 %fusion.7.far_ref = f32[2,32,256]{2,1,0:T(8,128)S(1)} fusion(bf16[4096,2,256]{2,1,0:T(2,128)(2,1)S(1)} %get-tuple-element.37, bf16[32,4096]{1,0:T(8,128)(2,1)S(1)} %get-tuple-element.38), kind=kOutput, calls=%fused_computation.5 | convolution fusion | flops 134217728 | bytes 4521984 | tf_op jit(solution)/shard_map/md,dkc->kmc/dot_general | solution.py:452
  26.0 0.0 collective-permute-done.6.rest_7_
  26.0 0.6 %collective-permute-done.7.rest_8_ = f32[32,128]{1,0:T(8,128)S(1)} collective-permute-done((f32[32,128]{1,0:T(8,128)S(1)}, f32[32,128]{1,0:T(8,128)S(1)}, u32[]{:S(2)}, u32[]{:S(2)}) %collective-permute-start.7) | collective-permute-done | bytes 16416 | tf_op jit(solution)/shard_map/ppermute | solution.py:380
  26.7 0.4 %collective-permute-done.8.rest_9_ = f32[32,128]{1,0:T(8,128)S(1)} collective-permute-done((f32[32,128]{1,0:T(8,128)S(1)}, f32[32,128]{1,0:T(8,128)S(1)}, u32[]{:S(2)}, u32[]{:S(2)}) %collective-permute-start.8) | collective-permute-done | bytes 16416 | tf_op jit(solution)/shard_map/ppermute | solution.py:380
  27.0 0.0 collective-permute-done.9.rest_11_
  27.0 1.5 %fresh_attention.1 = (bf16[4,8,256]{2,1,0:T(8,128)(2,1)}, bf16[4,8,256]{2,1,0:T(8,128)(2,1)}, bf16[4,8,2048]{2,1,0:T(8,128)(2,1)}) custom-call(f32[2,32,256]{2,1,0:T(8,128)S(1)} %fusion.4.near_ref, f32[2,32,256]{2,1,0:T(8,128)S(1)} %fusion.7.far_ref, f32[32,128]{1,0:T(8,128)S(1)} %get-tuple-element.39.square_ref, ...), custom_call_target="tpu_custom_call" | custom-call | tf_op jit(solution)/shard_map/fresh_attention/pallas_call | solution.py:368
Async XLA Ops:
  0.6 13.1 %collective-permute-start = (bf16[4,8,2048]{2,1,0:T(8,128)(2,1)}, bf16[4,8,2048]{2,1,0:T(8,128)(2,1)S(1)}, u32[]{:S(2)}, u32[]{:S(2)}) collective-permute-start(bf16[4,8,2048]{2,1,0:T(8,128)(2,1)} %hidden_ref.1), channel_id=1, source_target_pairs={{0,0},{1,6},{2,10},{3,12},{4,2},{5,4},{6,8},{7,14},{8,1},{9,7},{10... | collective-permute-start | bytes 393224 | tf_op jit(solution)/shard_map/ppermute | solution.py:414
  2.2 17.6 %collective-permute-start.3 = (bf16[4,8,2048]{2,1,0:T(8,128)(2,1)}, bf16[4,8,2048]{2,1,0:T(8,128)(2,1)S(1)}, u32[]{:S(2)}, u32[]{:S(2)}) collective-permute-start(bf16[4,8,2048]{2,1,0:T(8,128)(2,1)} %hidden_ref.1), channel_id=1, source_target_pairs={{0,1},{1,0},{2,3},{3,2},{4,5},{5,4},{6,7},{7,6},{8,9},{9,8},{10,11... | collective-permute-start | bytes 393224 | tf_op jit(solution)/shard_map/ppermute | solution.py:380
  6.7 13.1 %collective-permute-start.4 = (bf16[4,8,2048]{2,1,0:T(8,128)(2,1)}, bf16[4,8,2048]{2,1,0:T(8,128)(2,1)S(1)}, u32[]{:S(2)}, u32[]{:S(2)}) collective-permute-start(bf16[4,8,2048]{2,1,0:T(8,128)(2,1)} %hidden_ref.1), channel_id=1, source_target_pairs={{0,2},{1,3},{2,0},{3,1},{4,6},{5,7},{6,4},{7,5},{8,10},{9,11},{10,... | collective-permute-start | bytes 393224 | tf_op jit(solution)/shard_map/ppermute | solution.py:380
  9.2 10.6 %collective-permute-start.5 = (bf16[4,8,2048]{2,1,0:T(8,128)(2,1)}, bf16[4,8,2048]{2,1,0:T(8,128)(2,1)S(1)}, u32[]{:S(2)}, u32[]{:S(2)}) collective-permute-start(bf16[4,8,2048]{2,1,0:T(8,128)(2,1)} %hidden_ref.1), channel_id=1, source_target_pairs={{0,3},{1,2},{2,1},{3,0},{4,7},{5,6},{6,5},{7,4},{8,11},{9,10},{10,... | collective-permute-start | bytes 393224 | tf_op jit(solution)/shard_map/ppermute | solution.py:380
  9.2 4.5 %collective-permute-start.1 = (bf16[2,16,256]{2,1,0:T(8,128)(2,1)}, bf16[2,16,256]{2,1,0:T(8,128)(2,1)S(1)}, u32[]{:S(2)}, u32[]{:S(2)}) collective-permute-start(bf16[2,16,256]{2,1,0:T(8,128)(2,1)} %bitcast.13), channel_id=1, source_target_pairs={{0,4},{4,0},{8,12},{12,8},{1,5},{5,1},{9,13},{13,9},{2,6},{6,2},{1... | collective-permute-start | bytes 49160 | tf_op jit(solution)/shard_map/ppermute | solution.py:380
  14.1 8.1 %collective-permute-start.2 = (f32[32,128]{1,0:T(8,128)S(1)}, f32[32,128]{1,0:T(8,128)S(1)}, u32[]{:S(2)}, u32[]{:S(2)}) collective-permute-start(f32[32,128]{1,0:T(8,128)S(1)} %get-tuple-element.30), channel_id=1, source_target_pairs={{0,0},{6,1},{10,2},{12,3},{2,4},{4,5},{8,6},{14,7},{1,8},{7,9},{11... | collective-permute-start | bytes 49160 | tf_op jit(solution)/shard_map/ppermute | solution.py:433
  14.7 12.3 %collective-permute-start.9 = (bf16[2,2,16,256]{3,2,1,0:T(8,128)(2,1)S(1)}, bf16[2,2,16,256]{3,2,1,0:T(8,128)(2,1)S(1)}, u32[]{:S(2)}, u32[]{:S(2)}) collective-permute-start(bf16[2,2,16,256]{3,2,1,0:T(8,128)(2,1)S(1)} %get-tuple-element.48.rest_10_), channel_id=1, source_target_pairs={{0,8},{4,12},{8,0},{12,4},{1,9},{5,13},{9,1},{13,5},{2,10},{6,14},... | collective-permute-start | bytes 98312 | tf_op jit(solution)/shard_map/ppermute | solution.py:380
  22.2 3.8 %collective-permute-start.6 = (f32[32,128]{1,0:T(8,128)S(1)}, f32[32,128]{1,0:T(8,128)S(1)}, u32[]{:S(2)}, u32[]{:S(2)}) collective-permute-start(f32[32,128]{1,0:T(8,128)S(1)} %collective-permute-done.2.rest_6_), channel_id=1, source_target_pairs={{0,1},{1,0},{2,3},{3,2},{4,5},{5,4},{6,7},{7,6},{8,9},{9,8},{10,11... | collective-permute-start | bytes 49160 | tf_op jit(solution)/shard_map/ppermute | solution.py:380
  22.9 3.7 %collective-permute-start.7 = (f32[32,128]{1,0:T(8,128)S(1)}, f32[32,128]{1,0:T(8,128)S(1)}, u32[]{:S(2)}, u32[]{:S(2)}) collective-permute-start(f32[32,128]{1,0:T(8,128)S(1)} %collective-permute-done.2.rest_6_), channel_id=1, source_target_pairs={{0,2},{1,3},{2,0},{3,1},{4,6},{5,7},{6,4},{7,5},{8,10},{9,11},{10,... | collective-permute-start | bytes 49160 | tf_op jit(solution)/shard_map/ppermute | solution.py:380
  23.7 3.3 %collective-permute-start.8 = (f32[32,128]{1,0:T(8,128)S(1)}, f32[32,128]{1,0:T(8,128)S(1)}, u32[]{:S(2)}, u32[]{:S(2)}) collective-permute-start(f32[32,128]{1,0:T(8,128)S(1)} %collective-permute-done.2.rest_6_), channel_id=1, source_target_pairs={{0,3},{1,2},{2,1},{3,0},{4,7},{5,6},{6,5},{7,4},{8,11},{9,10},{10,... | collective-permute-start | bytes 49160 | tf_op jit(solution)/shard_map/ppermute | solution.py:380

commit v12 on v10

--- a/solution.py
+++ b/solution.py
@@ -54,11 +54,13 @@
     gain_ref,
     bias_ref,
     hidden_ref,
+    down_ref,
     weight_ref,
     near_out,
     gain_out,
     bias_out,
     hidden_out,
+    down_out,
     query_out,
     acc_out,
     top_out,
@@ -91,6 +93,7 @@
         (gain_ref, gain_buffer),
         (bias_ref, bias_out),
         (hidden_ref, hidden_out),
+        (down_ref, down_out),
     ]
     copies = [pltpu.make_async_copy(*pair, sems.at[i]) for i, pair in enumerate(copies)]
     for copy in copies:
@@ -153,14 +156,14 @@
         copy.wait()
 
 
-def cache_call(near, lengths, queries, keys, values, gain, bias, hidden, weight):
+def cache_call(near, lengths, queries, keys, values, gain, bias, hidden, down, weight):
     steps, rows, query_width = queries.shape
     cache_span, key_width = keys.shape[1:]
     groups = key_width // HD
     lines = steps * (query_width // key_width)
     block = (groups, lines * rows, HD)
     table = (steps * rows, HD)
-    operands = (lengths, queries, keys, values, gain, bias, hidden, weight)
+    operands = (lengths, queries, keys, values, gain, bias, hidden, down, weight)
     part = hidden.shape[2]
     return pl.pallas_call(
         functools.partial(cache_kernel, near),
@@ -169,6 +172,7 @@
             pltpu.VMEM(gain.shape, jnp.float32),
             pltpu.VMEM(bias.shape, bias.dtype),
             pltpu.VMEM(hidden.shape, hidden.dtype),
+            pltpu.VMEM(down.shape, down.dtype),
             pltpu.VMEM(block, jnp.float32),
             pltpu.VMEM(block, jnp.float32),
             pltpu.VMEM(block, jnp.float32),
@@ -177,7 +181,7 @@
             pltpu.VMEM(table, jnp.float32),
         ),
         in_specs=[HBM] * len(operands),
-        out_specs=(VMEM,) * 10,
+        out_specs=(VMEM,) * 11,
         scratch_shapes=[
             pltpu.SMEM(lengths.shape, jnp.int32),
             pltpu.VMEM(queries.shape, queries.dtype),
@@ -185,7 +189,7 @@
             pltpu.VMEM(keys.shape, keys.dtype),
             pltpu.VMEM(values.shape, values.dtype),
             pltpu.VMEM((rows * groups, lines, cache_span), jnp.float32),
-            pltpu.SemaphoreType.DMA((9,)),
+            pltpu.SemaphoreType.DMA((10,)),
             pltpu.SemaphoreType.DMA((len(near),)),
         ],
         compiler_params=pltpu.CompilerParams(vmem_limit_bytes=16 << 20),
@@ -226,33 +230,71 @@
     )(*[pltpu.with_memory_space_constraint(x, pltpu.HBM) for x in (down, up)])
 
 
-def inner_kernel(scaled_ref, *rest):
+def visiting_kernel(shares, hidden_ref, gain_ref, down_ref, out_ref):
+    chunks = hidden_ref.shape[2] // HD
+    start = pl.multiple_of(lax.axis_index("wide") * chunks, chunks)
+    gain = gain_ref[pl.ds(start, chunks)]
+    values = rows_of(hidden_ref)
+    scaled = [
+        (values[:, i * HD : (i + 1) * HD] * gain[i : i + 1]).astype(jnp.bfloat16)
+        for i in range(chunks)
+    ]
+    kinds, ranks, _ = down_ref.shape
+    share = ranks // shares
+    down = [
+        down_ref[kind, i * share : (i + 1) * share] for i in range(shares) for kind in range(kinds)
+    ]
+    out_ref[...] = lax.dot_general(
+        jnp.concatenate(scaled, axis=1),
+        jnp.concatenate(down, axis=0),
+        (((1,), (1,)), ((), ())),
+        preferred_element_type=jnp.float32,
+    )
+
+
+def visiting_call(shares, hidden, gain, down):
+    steps, rows, _ = hidden.shape
+    kinds, ranks, _ = down.shape
+    return pl.pallas_call(
+        functools.partial(visiting_kernel, shares),
+        out_shape=pltpu.VMEM((steps * rows, kinds * ranks), jnp.float32),
+        in_specs=[VMEM] * 3,
+        out_specs=VMEM,
+        compiler_params=pltpu.CompilerParams(vmem_limit_bytes=8 << 20),
+        name="visiting_rows",
+    )(hidden, gain, down)
+
+
+def inner_kernel(shares, scaled_ref, far_ref, *rest):
     packs, out_ref = rest[:-1], rest[-1]
     me = lax.axis_index("wide")
-    width = scaled_ref.shape[1] // len(packs)
+    kinds, share, pack_width = packs[0].shape
+    width = scaled_ref.shape[1] // shares
     total = []
     for offset, pack in enumerate(packs):
         total.append(
             lax.dot_general(
                 scaled_ref[:, pl.ds(pl.multiple_of((me ^ offset) * width, width), width)],
-                pack[:, :, :width].reshape(out_ref.shape[1], width),
+                pack[:, :, :width].reshape(kinds * share, width),
                 (((1,), (1,)), ((), ())),
                 preferred_element_type=jnp.float32,
             )
         )
-    out_ref[...] = sum(total[1:], total[0])
-
-
-def inner_call(scaled, packs):
-    kinds, share, _ = packs[0].shape
+    total = jnp.concatenate([sum(total[1:], total[0])] * shares, axis=1)
+    lane = lax.broadcasted_iota(jnp.int32, total.shape, 1)
+    mine = lane // (kinds * share) == lax.axis_index("tp")
+    out_ref[...] = jnp.where(mine, total, 0.0) + far_ref[...]
+
+
+def inner_call(scaled, far, packs):
     return pl.pallas_call(
-        inner_kernel,
-        out_shape=jax.ShapeDtypeStruct((scaled.shape[0], kinds * share), jnp.float32),
-        in_specs=[VMEM] * (1 + len(packs)),
+        functools.partial(inner_kernel, len(packs) + 1),
+        out_shape=pltpu.VMEM(far.shape, jnp.float32),
+        in_specs=[VMEM] * (2 + len(packs)),
         out_specs=VMEM,
         compiler_params=pltpu.CompilerParams(vmem_limit_bytes=8 << 20),
         name="rank_inner",
-    )(scaled, *packs)
+    )(scaled, far, *packs)
 
 
 def scale_kernel(near, far, weight_ref, gain_ref, *rest):
@@ -304,7 +346,7 @@
 
 def up_kernel(*refs):
     packs, up_out = refs[:-1], refs[-1]
-    kinds, share, pack_width = packs[0].shape
+    kinds, share, _ = packs[0].shape
     columns = up_out.shape[1] // kinds
     me = lax.axis_index("wide") if len(packs) > 1 else 0
     up_out[...] = jnp.zeros_like(up_out)
@@ -312,15 +354,15 @@
         for kind in range(kinds):
             at = pl.multiple_of(((me ^ offset) * kinds + kind) * share, share)
             up_out[pl.ds(at, share), kind * columns : (kind + 1) * columns] = pack[
-                kind, :, pack_width - columns :
+                kind, :, pack.shape[2] - columns :
             ]
 
 
-def final_kernel(width, blocks, near_ref, far_ref, square_ref, bias_ref, *rest):
+def final_kernel(width, inner_count, up_count, near_ref, far_ref, square_ref, bias_ref, *rest):
     query_ref, acc_ref, top_ref, total_ref, cos_ref, sin_ref = rest[:6]
-    inner_refs = rest[6 : 6 + blocks]
-    packs = rest[6 + blocks : 6 + 2 * blocks]
-    keys_out, values_out, attended_out, inner_buffer, up_ref = rest[6 + 2 * blocks :]
+    inner_refs = rest[6 : 6 + inner_count]
+    packs = rest[6 + inner_count : 6 + inner_count + up_count]
+    keys_out, values_out, attended_out, up_ref = rest[6 + inner_count + up_count :]
     up_kernel(*packs, up_ref)
     steps, rows, columns = keys_out.shape
     count = steps * rows
@@ -328,10 +370,9 @@
     per_group = size // count
     kinds = bias_ref.shape[0]
     row_scale = lax.rsqrt(square_ref[:, :1] * (1.0 / width) + norm_eps)
-    me = lax.axis_index("tp") if blocks > 1 else 0
-    for i in range(blocks):
-        inner_buffer[me ^ i] = inner_refs[i][...]
-    inner = jnp.concatenate([inner_buffer[i] for i in range(blocks)], axis=1)
+    inner = inner_refs[0][...]
+    for ref in inner_refs[1:]:
+        inner = inner + ref[...]
     high = inner.astype(jnp.bfloat16)
     low = (inner - high.astype(jnp.float32)).astype(jnp.bfloat16)
     lora = jnp.dot(
@@ -381,18 +422,14 @@
 
 def final_call(shape, width, near, far, square, bias, cached, inner, packs):
     steps, rows, query_width = shape
-    kinds, share, _ = packs[0].shape
-    columns = near.shape[2]
+    kinds, _, columns = near.shape
     small = jax.ShapeDtypeStruct((steps, rows, columns), jnp.bfloat16)
     return pl.pallas_call(
-        functools.partial(final_kernel, width, len(inner)),
+        functools.partial(final_kernel, width, len(inner), len(packs)),
         out_shape=(small, small, jax.ShapeDtypeStruct(shape, jnp.bfloat16)),
         in_specs=[VMEM] * (4 + len(cached) + len(inner) + len(packs)),
         out_specs=(VMEM,) * 3,
-        scratch_shapes=[
-            pltpu.VMEM((len(inner),) + inner[0].shape, jnp.float32),
-            pltpu.VMEM((len(packs) * kinds * share, kinds * columns), jnp.bfloat16),
-        ],
+        scratch_shapes=[pltpu.VMEM((inner[0].shape[1], kinds * columns), jnp.bfloat16)],
         compiler_params=pltpu.CompilerParams(vmem_limit_bytes=8 << 20),
         name="fresh_attention",
     )(near, far, square, bias, *cached, *inner, *packs)
@@ -422,13 +459,16 @@
     gain = input_norm_gain.reshape(width // HD, HD)
     up_part = jnp.transpose(adapter_up_factor, (0, 2, 1))
     direct = wide_count == tp_count == 4
-    tp_parts = [swap(hidden, "tp", offset, tp_count) for offset in (1, 2, 3)]
     if direct:
         pack = pack_call(adapter_down_factor, up_part)
         second = swap(pack, "wide", 2, wide_count)
         first = swap(pack, "wide", 1, wide_count)
+        there = [(3, 15), (12, 0), (6, 9), (9, 6)]
+        visitors = lax.ppermute(hidden, ("wide", "tp"), there)
+    crossed = swap(hidden, "tp", 2, tp_count)
+    beside = swap(hidden, "tp", 1, tp_count)
     near, far = (0, 1), (2, 3)
-    near_weight, gain_rows, bias, mine, *cached = cache_call(
+    near_weight, gain_rows, bias, mine, my_down, *cached = cache_call(
         near,
         lengths,
         queries,
@@ -437,18 +477,24 @@
         gain,
         key_value_bias,
         hidden,
+        adapter_down_factor,
         key_value_weight,
     )
+    relayed, gain_rows = lax.optimization_barrier((crossed, gain_rows))
+    relayed = swap(relayed, "tp", 1, tp_count)
     if direct:
-        third, gain_rows = lax.optimization_barrier((second, gain_rows))
-        packs = [pack, first, second, swap(third, "wide", 1, wide_count)]
+        inner = visiting_call(tp_count, visitors, gain_rows, my_down)
+        inner = lax.ppermute(inner, ("wide", "tp"), [(b, a) for a, b in there])
+        packs = [pack, first, second, swap(up_part, "wide", 3, wide_count)]
     scaled, near_scaled, far_scaled, square, far_weight = scale_call(
-        near, far, key_value_weight, gain_rows, [mine] + tp_parts
+        near, far, key_value_weight, gain_rows, (mine, beside, crossed, relayed)
     )
     if direct:
-        inner = inner_call(scaled, packs)
-        inner, far_scaled = lax.optimization_barrier((inner, far_scaled))
-        inner = [inner] + [swap(inner, "tp", offset, tp_count) for offset in (1, 2, 3)]
+        inner = inner_call(scaled, inner, packs[:3])
+        inner, near_scaled, far_scaled = lax.optimization_barrier(
+            (inner, near_scaled, far_scaled)
+        )
+        inner = [inner] + [swap(inner, "tp", offset, tp_count) for offset in (3, 2, 1)]
     else:
         down = lax.all_gather(adapter_down_factor, "wide", axis=2, tiled=True)
         down = down.reshape(kinds * ranks, width)

time: 25.5 us -> 28.4 us (1.11)
  starting transfers between devices: 10 us -> 14.7 us
  waiting for transfers between devices: 4.12 us -> 1.65 us
  Pallas kernels: 8.82 us -> 9.28 us
    ppermute x0 -> x2, starting transfers between devices: none -> 2.79 us  [the longest x1 1.51 us: on_device(): inner = lax.ppermute(inner, ('wide', 'tp'), [(b, a) for a, b in there])]
    ppermute x9, waiting for transfers between devices: 4.12 us -> 1.65 us  [swap(): return lax.ppermute(block, axis, [(i, i ^ offset) for i in range(count)])]
    ppermute x9, starting transfers between devices: 10 us -> 11.9 us  [swap(): return lax.ppermute(block, axis, [(i, i ^ offset) for i in range(count)])]
    pallas_call x2 -> x3, Pallas kernels: 1.81 us -> 2.09 us  [the longest x1 1.5 us: final_call(): pl.pallas_call(functools.partial(final_kernel, width, len(inner), len(pac...]
  transfers between devices with their start and end apart: 9 -> 11, of which waited for: 4 -> 1; matrix products, arithmetic and copies ran while one was open for 7% -> 6% of each run, Pallas kernels for 24% -> 28%
where the time goes in v12:
time: 28.4 us; the launch traced here: 28.1 us
  starting transfers between devices  14.7 us (52%)
  Pallas kernels  9.28 us (33%)
  matrix products  1.67 us (6%)
  waiting for transfers between devices  1.65 us (6%)
  between operations  0.76 us (3%)
    ppermute x9, starting transfers between devices, swap(): return lax.ppermute(block, axis, [(i, i ^ offset) for i in range(count)])  11.9 us
    pallas_call x1, Pallas kernels, cache_call(): pl.pallas_call(functools.partial(cache_kernel, near), out_shape=(pltpu.VM...  3.87 us
    pallas_call x1, Pallas kernels, scale_call(): pl.pallas_call(functools.partial(scale_kernel, near, far), out_shape=(plt...  2.38 us
    dot_general x2, matrix products, on_device(): jnp.einsum('md,dkc->kmc', x, y, preferred_element_type=jnp.float32)  1.67 us
    ppermute x9, waiting for transfers between devices, swap(): return lax.ppermute(block, axis, [(i, i ^ offset) for i in range(count)])  1.65 us
    ppermute x1, starting transfers between devices, on_device(): inner = lax.ppermute(inner, ('wide', 'tp'), [(b, a) for a, b in there])  1.51 us
    pallas_call x1, Pallas kernels, final_call(): pl.pallas_call(functools.partial(final_kernel, width, len(inner), len(pac...  1.5 us
    ppermute x1, starting transfers between devices, on_device(): visitors = lax.ppermute(hidden, ('wide', 'tp'), there)  1.28 us
  transfers between devices with their start and end apart: 11, of which 1 were waited for; matrix products, arithmetic and copies ran while one was open for 6% of the time, Pallas kernels for 28%

profile of v12, /device:TPU:0, one launch (start us, length us, event | category | flops | bytes accessed | tf_op | source)
XLA Modules:
  0.0 28.1 jit_solution(11755462467279819922)
XLA Ops:
  0.6 3.0 %collective-permute-start = (bf16[4,8,2048]{2,1,0:T(8,128)(2,1)}, bf16[4,8,2048]{2,1,0:T(8,128)(2,1)S(1)}, u32[]{:S(2)}, u32[]{:S(2)}) collective-permute-start(bf16[4,8,2048]{2,1,0:T(8,128)(2,1)} %hidden_ref.1), channel_id=1, source_target_pairs={{0,2},{1,3},{2,0},{3,1},{4,6},{5,7},{6,4},{7,5},{8,10},{9,11},{10,... | collective-permute-start | bytes 393224 | tf_op jit(solution)/shard_map/ppermute | solution.py:439
  3.6 1.3 %collective-permute-start.3 = (bf16[4,8,2048]{2,1,0:T(8,128)(2,1)}, bf16[4,8,2048]{2,1,0:T(8,128)(2,1)S(1)}, u32[]{:S(2)}, u32[]{:S(2)}) collective-permute-start(bf16[4,8,2048]{2,1,0:T(8,128)(2,1)} %hidden_ref.1), channel_id=1, source_target_pairs={{3,15},{12,0},{6,9},{9,6},{19,31},{28,16},{22,25},{25,22}} | collective-permute-start | bytes 393224 | tf_op jit(solution)/shard_map/ppermute | solution.py:467
  4.9 0.9 %pack_factors.1.rest_0_.rest_10_ = bf16[2,16,2304]{2,1,0:T(8,128)(2,1)S(1)} custom-call(bf16[2,64,2048]{2,1,0:T(8,128)(2,1)} %down_ref.3, bf16[2,16,256]{2,1,0:T(8,128)(2,1)} %bitcast.13), custom_call_target="tpu_custom_call" | custom-call | tf_op jit(solution)/shard_map/pack_factors/pallas_call | solution.py:223
  5.9 2.0 %collective-permute-start.6 = (bf16[2,16,2304]{2,1,0:T(8,128)(2,1)S(1)}, bf16[2,16,2304]{2,1,0:T(8,128)(2,1)S(1)}, u32[]{:S(2)}, u32[]{:S(2)}) collective-permute-start(bf16[2,16,2304]{2,1,0:T(8,128)(2,1)S(1)} %pack_factors.1.rest_0_.rest_10_), channel_id=1, source_target_pairs={{0,8},{4,12},{8,0},{12,4},{1,9},{5,13},{9,1},{13,5},{2,10},{6,14},... | collective-permute-start | bytes 442376 | tf_op jit(solution)/shard_map/ppermute | solution.py:439
  7.9 3.0 %collective-permute-start.5 = (bf16[2,16,2304]{2,1,0:T(8,128)(2,1)S(1)}, bf16[2,16,2304]{2,1,0:T(8,128)(2,1)S(1)}, u32[]{:S(2)}, u32[]{:S(2)}) collective-permute-start(bf16[2,16,2304]{2,1,0:T(8,128)(2,1)S(1)} %pack_factors.1.rest_0_.rest_10_), channel_id=1, source_target_pairs={{0,4},{4,0},{8,12},{12,8},{1,5},{5,1},{9,13},{13,9},{2,6},{6,2},{1... | collective-permute-start | bytes 442376 | tf_op jit(solution)/shard_map/ppermute | solution.py:439
  10.9 0.0 collective-permute-start.1
  10.9 0.0 copy-start
  10.9 3.9 %cache_attention.1 = (bf16[4096,2,256]{2,1,0:T(2,128)(2,1)S(1)}, f32[64,128]{1,0:T(8,128)S(1)}, bf16[2,256]{1,0:T(2,128)(2,1)S(1)}, bf16[4,8,2048]{2,1,0:T(8,128...) custom-call(s32[8]{0:T(128)} %lengths_ref.1, ...), custom_call_target="tpu_custom_call" | custom-call | flops 140509184 | bytes 9437184 | tf_op jit(solution)/shard_map/cache_attention/pallas_call | solution.py:168
  14.8 0.0 collective-permute-done.rest_2_
  14.8 0.6 %collective-permute-start.2 = (bf16[4,8,2048]{2,1,0:T(8,128)(2,1)S(1)}, bf16[4,8,2048]{2,1,0:T(8,128)(2,1)S(1)}, u32[]{:S(2)}, u32[]{:S(2)}) collective-permute-start(bf16[4,8,2048]{2,1,0:T(8,128)(2,1)S(1)} %collective-permute-done.rest_2_), channel_id=1, source_target_pairs={{0,1},{1,0},{2,3},{3,2},{4,5},{5,4},{6,7},{7,6},{8,9},{9,8},{10,11... | collective-permute-start | bytes 393224 | tf_op jit(solution)/shard_map/ppermute | solution.py:439
  15.4 0.0 collective-permute-done.3.hidden_ref
  15.4 0.3 visiting_rows.1
  15.7 1.5 %collective-permute-start.4 = (f32[32,128]{1,0:T(8,128)S(1)}, f32[32,128]{1,0:T(8,128)S(1)}, u32[]{:S(2)}, u32[]{:S(2)}) collective-permute-start(f32[32,128]{1,0:T(8,128)S(1)} %visiting_rows.1), channel_id=1, source_target_pairs={{15,3},{0,12},{9,6},{6,9},{31,19},{16,28},{25,22},{22,25}} | collective-permute-start | bytes 49160 | tf_op jit(solution)/shard_map/ppermute | solution.py:487
  17.2 0.0 collective-permute-done.1.rest_1_
  17.2 0.0 copy-done
  17.2 0.1 collective-permute-start.10
  17.3 0.0 collective-permute-done.2.rest_3_
  17.3 2.4 %scale_features.1 = (bf16[32,8192]{1,0:T(8,128)(2,1)S(1)}, bf16[32,4096]{1,0:T(8,128)(2,1)S(1)}, bf16[32,4096]{1,0:T(8,128)(2,1)S(1)}, f32[32,128]{1,0:T(8,128)S(1)}, bf16[4096,2,256]{2,1,0:T(2,128)(2,1)S(1)}) custom-call(bf16[8192,2,256]{2,1,0:T(2,128)(2,1)} %weight_ref.3, f32[64,128]{1,0:T(8,128)S(1)} %get-tuple-element.26.gain_ref, ...), custom_call_target="tpu_custom_call" | custom-call | bytes 5242880 | tf_op jit(solution)/shard_map/scale_features/pallas_call | solution.py:329
  19.7 0.0 collective-permute-done.4.far_ref
  19.7 0.0 collective-permute-done.6.rest_2_.rest_12_
  19.7 0.0 collective-permute-done.5.rest_1_.rest_11_
  19.7 0.3 %rank_inner.1.rest_6_ = f32[32,128]{1,0:T(8,128)S(1)} custom-call(bf16[32,8192]{1,0:T(8,128)(2,1)S(1)} %get-tuple-element.29.scaled_ref, f32[32,128]{1,0:T(8,128)S(1)} %collective-permute-done.4.far_ref, bf16[2,16,2304]{2,1,0:T(8,128)(2,1)S(1)} %pack_factors.1.rest_0_.rest_10_, bf16[2,16,2304]{2,1,0:T(8,128)(2,1)S(1)} %collective-permute-done.5.rest_1_.rest_11_, ...), custom_call_target="tpu_custom_call" | custom-call | tf_op jit(solution)/shard_map/rank_inner/pallas_call | solution.py:290
  20.1 0.1 collective-permute-start.9
  20.1 3.1 %collective-permute-start.8 = (f32[32,128]{1,0:T(8,128)S(1)}, f32[32,128]{1,0:T(8,128)S(1)}, u32[]{:S(2)}, u32[]{:S(2)}) collective-permute-start(f32[32,128]{1,0:T(8,128)S(1)} %rank_inner.1.rest_6_), channel_id=1, source_target_pairs={{0,2},{1,3},{2,0},{3,1},{4,6},{5,7},{6,4},{7,5},{8,10},{9,11},{10,... | collective-permute-start | bytes 49160 | tf_op jit(solution)/shard_map/ppermute | solution.py:439
  23.3 0.0 collective-permute-start.7
  23.3 0.8 %fusion.7.far_ref = f32[2,32,256]{2,1,0:T(8,128)S(1)} fusion(bf16[4096,2,256]{2,1,0:T(2,128)(2,1)S(1)} %get-tuple-element.34, bf16[32,4096]{1,0:T(8,128)(2,1)S(1)} %get-tuple-element.35), kind=kOutput, calls=%fused_computation.5 | convolution fusion | flops 134217728 | bytes 4521984 | tf_op jit(solution)/shard_map/md,dkc->kmc/dot_general | solution.py:504
  24.1 0.8 %fusion.4.near_ref = f32[2,32,256]{2,1,0:T(8,128)S(1)} fusion(bf16[4096,2,256]{2,1,0:T(2,128)(2,1)S(1)} %get-tuple-element.24, bf16[32,4096]{1,0:T(8,128)(2,1)S(1)} %get-tuple-element.33), kind=kOutput, calls=%fused_computation.4 | convolution fusion | flops 134217728 | bytes 4521984 | tf_op jit(solution)/shard_map/md,dkc->kmc/dot_general | solution.py:504
  24.9 0.0 collective-permute-done.10.rest_13_
  24.9 0.0 collective-permute-done.9.rest_9_
  24.9 0.0 collective-permute-done.8.rest_8_
  25.0 1.6 %collective-permute-done.7.rest_7_ = f32[32,128]{1,0:T(8,128)S(1)} collective-permute-done((f32[32,128]{1,0:T(8,128)S(1)}, f32[32,128]{1,0:T(8,128)S(1)}, u32[]{:S(2)}, u32[]{:S(2)}) %collective-permute-start.7) | collective-permute-done | bytes 16416 | tf_op jit(solution)/shard_map/ppermute | solution.py:439
  26.6 1.5 %fresh_attention.1 = (bf16[4,8,256]{2,1,0:T(8,128)(2,1)}, bf16[4,8,256]{2,1,0:T(8,128)(2,1)}, bf16[4,8,2048]{2,1,0:T(8,128)(2,1)}) custom-call(f32[2,32,256]{2,1,0:T(8,128)S(1)} %fusion.4.near_ref, f32[2,32,256]{2,1,0:T(8,128)S(1)} %fusion.7.far_ref, f32[32,128]{1,0:T(8,128)S(1)} %get-tuple-element.36.square_ref, ...), custom_call_target="tpu_custom_call" | custom-call | tf_op jit(solution)/shard_map/fresh_attention/pallas_call | solution.py:427
Async XLA Ops:
  0.6 14.2 %collective-permute-start = (bf16[4,8,2048]{2,1,0:T(8,128)(2,1)}, bf16[4,8,2048]{2,1,0:T(8,128)(2,1)S(1)}, u32[]{:S(2)}, u32[]{:S(2)}) collective-permute-start(bf16[4,8,2048]{2,1,0:T(8,128)(2,1)} %hidden_ref.1), channel_id=1, source_target_pairs={{0,2},{1,3},{2,0},{3,1},{4,6},{5,7},{6,4},{7,5},{8,10},{9,11},{10,... | collective-permute-start | bytes 393224 | tf_op jit(solution)/shard_map/ppermute | solution.py:439
  3.6 11.8 %collective-permute-start.3 = (bf16[4,8,2048]{2,1,0:T(8,128)(2,1)}, bf16[4,8,2048]{2,1,0:T(8,128)(2,1)S(1)}, u32[]{:S(2)}, u32[]{:S(2)}) collective-permute-start(bf16[4,8,2048]{2,1,0:T(8,128)(2,1)} %hidden_ref.1), channel_id=1, source_target_pairs={{3,15},{12,0},{6,9},{9,6},{19,31},{28,16},{22,25},{25,22}} | collective-permute-start | bytes 393224 | tf_op jit(solution)/shard_map/ppermute | solution.py:467
  5.9 13.8 %collective-permute-start.6 = (bf16[2,16,2304]{2,1,0:T(8,128)(2,1)S(1)}, bf16[2,16,2304]{2,1,0:T(8,128)(2,1)S(1)}, u32[]{:S(2)}, u32[]{:S(2)}) collective-permute-start(bf16[2,16,2304]{2,1,0:T(8,128)(2,1)S(1)} %pack_factors.1.rest_0_.rest_10_), channel_id=1, source_target_pairs={{0,8},{4,12},{8,0},{12,4},{1,9},{5,13},{9,1},{13,5},{2,10},{6,14},... | collective-permute-start | bytes 442376 | tf_op jit(solution)/shard_map/ppermute | solution.py:439
  7.9 11.8 %collective-permute-start.5 = (bf16[2,16,2304]{2,1,0:T(8,128)(2,1)S(1)}, bf16[2,16,2304]{2,1,0:T(8,128)(2,1)S(1)}, u32[]{:S(2)}, u32[]{:S(2)}) collective-permute-start(bf16[2,16,2304]{2,1,0:T(8,128)(2,1)S(1)} %pack_factors.1.rest_0_.rest_10_), channel_id=1, source_target_pairs={{0,4},{4,0},{8,12},{12,8},{1,5},{5,1},{9,13},{13,9},{2,6},{6,2},{1... | collective-permute-start | bytes 442376 | tf_op jit(solution)/shard_map/ppermute | solution.py:439
  10.9 6.3 %collective-permute-start.1 = (bf16[4,8,2048]{2,1,0:T(8,128)(2,1)}, bf16[4,8,2048]{2,1,0:T(8,128)(2,1)S(1)}, u32[]{:S(2)}, u32[]{:S(2)}) collective-permute-start(bf16[4,8,2048]{2,1,0:T(8,128)(2,1)} %hidden_ref.1), channel_id=1, source_target_pairs={{0,1},{1,0},{2,3},{3,2},{4,5},{5,4},{6,7},{7,6},{8,9},{9,8},{10,11... | collective-permute-start | bytes 393224 | tf_op jit(solution)/shard_map/ppermute | solution.py:439
  10.9 6.3 %copy-start = (bf16[2,256,16]{1,2,0:T(8,128)(2,1)S(1)}, bf16[2,256,16]{1,2,0:T(8,128)(2,1)}, u32[]{:S(2)}) copy-start(bf16[2,256,16]{1,2,0:T(8,128)(2,1)} %param.15) | copy-start | bytes 49156
  14.8 2.5 %collective-permute-start.2 = (bf16[4,8,2048]{2,1,0:T(8,128)(2,1)S(1)}, bf16[4,8,2048]{2,1,0:T(8,128)(2,1)S(1)}, u32[]{:S(2)}, u32[]{:S(2)}) collective-permute-start(bf16[4,8,2048]{2,1,0:T(8,128)(2,1)S(1)} %collective-permute-done.rest_2_), channel_id=1, source_target_pairs={{0,1},{1,0},{2,3},{3,2},{4,5},{5,4},{6,7},{7,6},{8,9},{9,8},{10,11... | collective-permute-start | bytes 393224 | tf_op jit(solution)/shard_map/ppermute | solution.py:439
  15.7 4.0 %collective-permute-start.4 = (f32[32,128]{1,0:T(8,128)S(1)}, f32[32,128]{1,0:T(8,128)S(1)}, u32[]{:S(2)}, u32[]{:S(2)}) collective-permute-start(f32[32,128]{1,0:T(8,128)S(1)} %visiting_rows.1), channel_id=1, source_target_pairs={{15,3},{0,12},{9,6},{6,9},{31,19},{16,28},{25,22},{22,25}} | collective-permute-start | bytes 49160 | tf_op jit(solution)/shard_map/ppermute | solution.py:487
  17.2 7.7 %collective-permute-start.10 = (bf16[2,16,256]{2,1,0:T(8,128)(2,1)S(1)}, bf16[2,16,256]{2,1,0:T(8,128)(2,1)S(1)}, u32[]{:S(2)}, u32[]{:S(2)}) collective-permute-start(bf16[2,16,256]{2,1,0:T(8,128)(2,1)S(1)} %bitcast.14), channel_id=1, source_target_pairs={{0,12},{4,8},{8,4},{12,0},{1,13},{5,9},{9,5},{13,1},{2,14},{6,10},... | collective-permute-start | bytes 49160 | tf_op jit(solution)/shard_map/ppermute | solution.py:439
  20.1 4.9 %collective-permute-start.9 = (f32[32,128]{1,0:T(8,128)S(1)}, f32[32,128]{1,0:T(8,128)S(1)}, u32[]{:S(2)}, u32[]{:S(2)}) collective-permute-start(f32[32,128]{1,0:T(8,128)S(1)} %rank_inner.1.rest_6_), channel_id=1, source_target_pairs={{0,1},{1,0},{2,3},{3,2},{4,5},{5,4},{6,7},{7,6},{8,9},{9,8},{10,11... | collective-permute-start | bytes 49160 | tf_op jit(solution)/shard_map/ppermute | solution.py:439
  20.1 4.8 %collective-permute-start.8 = (f32[32,128]{1,0:T(8,128)S(1)}, f32[32,128]{1,0:T(8,128)S(1)}, u32[]{:S(2)}, u32[]{:S(2)}) collective-permute-start(f32[32,128]{1,0:T(8,128)S(1)} %rank_inner.1.rest_6_), channel_id=1, source_target_pairs={{0,2},{1,3},{2,0},{3,1},{4,6},{5,7},{6,4},{7,5},{8,10},{9,11},{10,... | collective-permute-start | bytes 49160 | tf_op jit(solution)/shard_map/ppermute | solution.py:439
  23.3 3.3 %collective-permute-start.7 = (f32[32,128]{1,0:T(8,128)S(1)}, f32[32,128]{1,0:T(8,128)S(1)}, u32[]{:S(2)}, u32[]{:S(2)}) collective-permute-start(f32[32,128]{1,0:T(8,128)S(1)} %rank_inner.1.rest_6_), channel_id=1, source_target_pairs={{0,3},{1,2},{2,1},{3,0},{4,7},{5,6},{6,5},{7,4},{8,11},{9,10},{10,... | collective-permute-start | bytes 49160 | tf_op jit(solution)/shard_map/ppermute | solution.py:439

commit v13 on v10

--- a/solution.py
+++ b/solution.py
@@ -229,25 +229,29 @@
 def inner_kernel(scaled_ref, *rest):
     packs, out_ref = rest[:-1], rest[-1]
     me = lax.axis_index("wide")
-    width = scaled_ref.shape[1] // len(packs)
+    shares = len(packs)
+    kinds, share, _ = packs[0].shape
+    width = scaled_ref.shape[1] // shares
     total = []
     for offset, pack in enumerate(packs):
         total.append(
             lax.dot_general(
                 scaled_ref[:, pl.ds(pl.multiple_of((me ^ offset) * width, width), width)],
-                pack[:, :, :width].reshape(out_ref.shape[1], width),
+                pack[:, :, :width].reshape(kinds * share, width),
                 (((1,), (1,)), ((), ())),
                 preferred_element_type=jnp.float32,
             )
         )
-    out_ref[...] = sum(total[1:], total[0])
+    total = jnp.concatenate([sum(total[1:], total[0])] * shares, axis=1)
+    lane = lax.broadcasted_iota(jnp.int32, total.shape, 1)
+    out_ref[...] = jnp.where(lane // (kinds * share) == lax.axis_index("tp"), total, 0.0)
 
 
 def inner_call(scaled, packs):
     kinds, share, _ = packs[0].shape
     return pl.pallas_call(
         inner_kernel,
-        out_shape=jax.ShapeDtypeStruct((scaled.shape[0], kinds * share), jnp.float32),
+        out_shape=pltpu.VMEM((scaled.shape[0], len(packs) * kinds * share), jnp.float32),
         in_specs=[VMEM] * (1 + len(packs)),
         out_specs=VMEM,
         compiler_params=pltpu.CompilerParams(vmem_limit_bytes=8 << 20),
@@ -316,11 +320,11 @@
             ]
 
 
-def final_kernel(width, blocks, near_ref, far_ref, square_ref, bias_ref, *rest):
+def final_kernel(width, inner_count, up_count, near_ref, far_ref, square_ref, bias_ref, *rest):
     query_ref, acc_ref, top_ref, total_ref, cos_ref, sin_ref = rest[:6]
-    inner_refs = rest[6 : 6 + blocks]
-    packs = rest[6 + blocks : 6 + 2 * blocks]
-    keys_out, values_out, attended_out, inner_buffer, up_ref = rest[6 + 2 * blocks :]
+    inner_refs = rest[6 : 6 + inner_count]
+    packs = rest[6 + inner_count : 6 + inner_count + up_count]
+    keys_out, values_out, attended_out, up_ref = rest[6 + inner_count + up_count :]
     up_kernel(*packs, up_ref)
     steps, rows, columns = keys_out.shape
     count = steps * rows
@@ -328,10 +332,9 @@
     per_group = size // count
     kinds = bias_ref.shape[0]
     row_scale = lax.rsqrt(square_ref[:, :1] * (1.0 / width) + norm_eps)
-    me = lax.axis_index("tp") if blocks > 1 else 0
-    for i in range(blocks):
-        inner_buffer[me ^ i] = inner_refs[i][...]
-    inner = jnp.concatenate([inner_buffer[i] for i in range(blocks)], axis=1)
+    inner = inner_refs[0][...]
+    for ref in inner_refs[1:]:
+        inner = inner + ref[...]
     high = inner.astype(jnp.bfloat16)
     low = (inner - high.astype(jnp.float32)).astype(jnp.bfloat16)
     lora = jnp.dot(
@@ -381,21 +384,21 @@
 
 def final_call(shape, width, near, far, square, bias, cached, inner, packs):
     steps, rows, query_width = shape
-    kinds, share, _ = packs[0].shape
-    columns = near.shape[2]
+    kinds, _, columns = near.shape
     small = jax.ShapeDtypeStruct((steps, rows, columns), jnp.bfloat16)
     return pl.pallas_call(
-        functools.partial(final_kernel, width, len(inner)),
+        functools.partial(final_kernel, width, len(inner), len(packs)),
         out_shape=(small, small, jax.ShapeDtypeStruct(shape, jnp.bfloat16)),
         in_specs=[VMEM] * (4 + len(cached) + len(inner) + len(packs)),
         out_specs=(VMEM,) * 3,
-        scratch_shapes=[
-            pltpu.VMEM((len(inner),) + inner[0].shape, jnp.float32),
-            pltpu.VMEM((len(packs) * kinds * share, kinds * columns), jnp.bfloat16),
-        ],
+        scratch_shapes=[pltpu.VMEM((inner[0].shape[1], kinds * columns), jnp.bfloat16)],
         compiler_params=pltpu.CompilerParams(vmem_limit_bytes=8 << 20),
         name="fresh_attention",
     )(near, far, square, bias, *cached, *inner, *packs)
+
+
+def dot(rows, weight):
+    return jnp.einsum("md,dkc->kmc", rows, weight, preferred_element_type=jnp.float32)
 
 
 def swap(block, axis, offset, count):
@@ -446,18 +449,19 @@
         near, far, key_value_weight, gain_rows, [mine] + tp_parts
     )
     if direct:
+        near_base = dot(near_scaled, near_weight)
+        scaled, near_base = lax.optimization_barrier((scaled, near_base))
         inner = inner_call(scaled, packs)
+        inner = inner + swap(inner, "tp", 1, tp_count)
         inner, far_scaled = lax.optimization_barrier((inner, far_scaled))
-        inner = [inner] + [swap(inner, "tp", offset, tp_count) for offset in (1, 2, 3)]
+        inner = [inner, swap(inner, "tp", 2, tp_count)]
     else:
+        near_base = dot(near_scaled, near_weight)
         down = lax.all_gather(adapter_down_factor, "wide", axis=2, tiled=True)
         down = down.reshape(kinds * ranks, width)
         inner = [jnp.einsum("rd,kd->rk", scaled, down, preferred_element_type=jnp.float32)]
         packs = [lax.all_gather(up_part, "wide", axis=1, tiled=True)]
-    near_base, far_base = [
-        jnp.einsum("md,dkc->kmc", x, y, preferred_element_type=jnp.float32)
-        for x, y in ((near_scaled, near_weight), (far_scaled, far_weight))
-    ]
+    far_base = dot(far_scaled, far_weight)
     return final_call(
         queries.shape, width, near_base, far_base, square, bias, cached, inner, packs
     )

time: 25.5 us -> 25.7 us (level)
  waiting for transfers between devices: 4.12 us -> 4.47 us
    ppermute x9 -> x8, waiting for transfers between devices: 4.12 us -> 4.47 us  [swap(): return lax.ppermute(block, axis, [(i, i ^ offset) for i in range(count)])]
    ppermute x9 -> x8, starting transfers between devices: 10 us -> 9.82 us  [swap(): return lax.ppermute(block, axis, [(i, i ^ offset) for i in range(count)])]
  transfers between devices with their start and end apart: 9 -> 8, of which waited for: 4 -> 4; matrix products, arithmetic and copies ran while one was open for 7% -> 7% of each run, Pallas kernels for 24% -> 24%
where the time goes in v13:
time: 25.7 us; the launch traced here: 25.5 us
  starting transfers between devices  9.82 us (38%)
  Pallas kernels  8.85 us (34%)
  waiting for transfers between devices  4.47 us (17%)
  matrix products  1.67 us (6%)
  between operations  0.69 us (3%)
    ppermute x8, starting transfers between devices, swap(): return lax.ppermute(block, axis, [(i, i ^ offset) for i in range(count)])  9.82 us
    ppermute x8, waiting for transfers between devices, swap(): return lax.ppermute(block, axis, [(i, i ^ offset) for i in range(count)])  4.47 us
    pallas_call x1, Pallas kernels, cache_call(): pl.pallas_call(functools.partial(cache_kernel, near), out_shape=(pltpu.VM...  3.7 us
    pallas_call x1, Pallas kernels, scale_call(): pl.pallas_call(functools.partial(scale_kernel, near, far), out_shape=(plt...  2.37 us
    dot_general x2, matrix products, dot(): jnp.einsum('md,dkc->kmc', rows, weight, preferred_element_type=jnp.float32)  1.67 us
    pallas_call x1, Pallas kernels, final_call(): pl.pallas_call(functools.partial(final_kernel, width, len(inner), len(pac...  1.5 us
    pallas_call x1, Pallas kernels, pack_call(): pl.pallas_call(pack_kernel, out_shape=pltpu.VMEM((kinds, share, down.shap...  0.93 us
  transfers between devices with their start and end apart: 8, of which 4 were waited for; matrix products, arithmetic and copies ran while one was open for 7% of the time, Pallas kernels for 24%

profile of v13, /device:TPU:0, one launch (start us, length us, event | category | flops | bytes accessed | tf_op | source)
XLA Modules:
  0.0 25.5 jit_solution(11120168847624721627)
XLA Ops:
  0.6 0.9 %pack_factors.1.rest_0_.rest_8_ = bf16[2,16,2304]{2,1,0:T(8,128)(2,1)S(1)} custom-call(bf16[2,64,2048]{2,1,0:T(8,128)(2,1)} %down_ref.1, bf16[2,16,256]{2,1,0:T(8,128)(2,1)} %bitcast.13), custom_call_target="tpu_custom_call" | custom-call | tf_op jit(solution)/shard_map/pack_factors/pallas_call | solution.py:219
  1.6 4.1 %collective-permute-start = (bf16[2,16,2304]{2,1,0:T(8,128)(2,1)S(1)}, bf16[2,16,2304]{2,1,0:T(8,128)(2,1)S(1)}, u32[]{:S(2)}, u32[]{:S(2)}) collective-permute-start(bf16[2,16,2304]{2,1,0:T(8,128)(2,1)S(1)} %pack_factors.1.rest_0_.rest_8_), channel_id=1, source_target_pairs={{0,8},{4,12},{8,0},{12,4},{1,9},{5,13},{9,1},{13,5},{2,10},{6,14},... | collective-permute-start | bytes 442376 | tf_op jit(solution)/shard_map/ppermute | solution.py:405
  5.7 0.0 collective-permute-start.1
  5.7 1.5 %collective-permute-start.2 = (bf16[4,8,2048]{2,1,0:T(8,128)(2,1)}, bf16[4,8,2048]{2,1,0:T(8,128)(2,1)S(1)}, u32[]{:S(2)}, u32[]{:S(2)}) collective-permute-start(bf16[4,8,2048]{2,1,0:T(8,128)(2,1)} %hidden_ref.1), channel_id=1, source_target_pairs={{0,2},{1,3},{2,0},{3,1},{4,6},{5,7},{6,4},{7,5},{8,10},{9,11},{10,... | collective-permute-start | bytes 393224 | tf_op jit(solution)/shard_map/ppermute | solution.py:405
  7.2 0.4 %collective-permute-start.3 = (bf16[4,8,2048]{2,1,0:T(8,128)(2,1)}, bf16[4,8,2048]{2,1,0:T(8,128)(2,1)S(1)}, u32[]{:S(2)}, u32[]{:S(2)}) collective-permute-start(bf16[4,8,2048]{2,1,0:T(8,128)(2,1)} %hidden_ref.1), channel_id=1, source_target_pairs={{0,3},{1,2},{2,1},{3,0},{4,7},{5,6},{6,5},{7,4},{8,11},{9,10},{10,... | collective-permute-start | bytes 393224 | tf_op jit(solution)/shard_map/ppermute | solution.py:405
  7.5 1.6 %collective-permute-start.4 = (bf16[2,16,2304]{2,1,0:T(8,128)(2,1)S(1)}, bf16[2,16,2304]{2,1,0:T(8,128)(2,1)S(1)}, u32[]{:S(2)}, u32[]{:S(2)}) collective-permute-start(bf16[2,16,2304]{2,1,0:T(8,128)(2,1)S(1)} %pack_factors.1.rest_0_.rest_8_), channel_id=1, source_target_pairs={{0,4},{4,0},{8,12},{12,8},{1,5},{5,1},{9,13},{13,9},{2,6},{6,2},{1... | collective-permute-start | bytes 442376 | tf_op jit(solution)/shard_map/ppermute | solution.py:405
  9.1 3.7 %cache_attention.1 = (bf16[4096,2,256]{2,1,0:T(2,128)(2,1)S(1)}, f32[64,128]{1,0:T(8,128)S(1)}, bf16[2,256]{1,0:T(2,128)(2,1)S(1)}, bf16[4,8,2048]{2,1,0:T(8,128...) custom-call(s32[8]{0:T(128)} %lengths_ref.1, ...), custom_call_target="tpu_custom_call" | custom-call | flops 140509184 | bytes 9437184 | tf_op jit(solution)/shard_map/cache_attention/pallas_call | solution.py:165
  12.8 0.0 collective-permute-done.rest_2_.rest_10_
  12.8 0.6 %collective-permute-start.5 = (bf16[2,16,2304]{2,1,0:T(8,128)(2,1)S(1)}, bf16[2,16,2304]{2,1,0:T(8,128)(2,1)S(1)}, u32[]{:S(2)}, u32[]{:S(2)}) collective-permute-start(bf16[2,16,2304]{2,1,0:T(8,128)(2,1)S(1)} %collective-permute-done.rest_2_.rest_10_), channel_id=1, source_target_pairs={{0,4},{4,0},{8,12},{12,8},{1,5},{5,1},{9,13},{13,9},{2,6},{6,2},{1... | collective-permute-start | bytes 442376 | tf_op jit(solution)/shard_map/ppermute | solution.py:405
  13.4 0.0 collective-permute-done.1.rest_1_
  13.5 0.0 collective-permute-done.2.rest_2_
  13.5 0.8 %collective-permute-done.3.rest_3_ = bf16[4,8,2048]{2,1,0:T(8,128)(2,1)S(1)} collective-permute-done((bf16[4,8,2048]{2,1,0:T(8,128)(2,1)}, bf16[4,8,2048]{2,1,0:T(8,128)(2,1)S(1)}, u32[]{:S(2)}, u32[]{:S(2)}) %collective-permute-start.3) | collective-permute-done | bytes 131104 | tf_op jit(solution)/shard_map/ppermute | solution.py:405
  14.2 2.4 %scale_features.1 = (bf16[32,8192]{1,0:T(8,128)(2,1)S(1)}, bf16[32,4096]{1,0:T(8,128)(2,1)S(1)}, bf16[32,4096]{1,0:T(8,128)(2,1)S(1)}, f32[32,128]{1,0:T(8,128)S(1)}, bf16[4096,2,256]{2,1,0:T(2,128)(2,1)S(1)}) custom-call(bf16[8192,2,256]{2,1,0:T(2,128)(2,1)} %weight_ref.3, f32[64,128]{1,0:T(8,128)S(1)} %get-tuple-element.25.gain_ref, ...), custom_call_target="tpu_custom_call" | custom-call | bytes 5242880 | tf_op jit(solution)/shard_map/scale_features/pallas_call | solution.py:291
  16.6 0.8 %fusion.4.near_ref = f32[2,32,256]{2,1,0:T(8,128)S(1)} fusion(bf16[4096,2,256]{2,1,0:T(2,128)(2,1)S(1)} %get-tuple-element.28, bf16[32,4096]{1,0:T(8,128)(2,1)S(1)} %get-tuple-element.29), kind=kOutput, calls=%fused_computation.4 | convolution fusion | flops 134217728 | bytes 4521984 | tf_op jit(solution)/shard_map/md,dkc->kmc/dot_general | solution.py:401
  17.4 0.0 collective-permute-done.4.rest_1_.rest_9_
  17.4 1.2 %collective-permute-done.5.rest_3_.rest_11_ = bf16[2,16,2304]{2,1,0:T(8,128)(2,1)S(1)} collective-permute-done((bf16[2,16,2304]{2,1,0:T(8,128)(2,1)S(1)}, bf16[2,16,2304]{2,1,0:T(8,128)(2,1)S(1)}, u32[]{:S(2)}, u32[]{:S(2)}) %collective-permute-start.5) | collective-permute-done | bytes 147488 | tf_op jit(solution)/shard_map/ppermute | solution.py:405
  18.7 0.3 %rank_inner.1 = f32[32,128]{1,0:T(8,128)S(1)} custom-call(bf16[32,8192]{1,0:T(8,128)(2,1)S(1)} %get-tuple-element.32.scaled_ref, bf16[2,16,2304]{2,1,0:T(8,128)(2,1)S(1)} %pack_factors.1.rest_0_.rest_8_, bf16[2,16,2304]{2,1,0:T(8,128)(2,1)S(1)} %collective-permute-done.4.rest_1_.rest_9_, bf16[2,16,2304]{2,1,0:T(8,128)(2,1)S(1)} %collective-permute-done.rest_2_.rest_10_, ...), custom_call_target="tpu_custom_call" | custom-call | tf_op jit(solution)/shard_map/rank_inner/pallas_call | solution.py:252
  19.0 0.1 collective-permute-start.6
  19.1 1.2 %collective-permute-done.6 = f32[32,128]{1,0:T(8,128)S(1)} collective-permute-done((f32[32,128]{1,0:T(8,128)S(1)}, f32[32,128]{1,0:T(8,128)S(1)}, u32[]{:S(2)}, u32[]{:S(2)}) %collective-permute-start.6) | collective-permute-done | bytes 16416 | tf_op jit(solution)/shard_map/ppermute | solution.py:405
  20.3 1.6 %collective-permute-start.7 = (f32[32,128]{1,0:T(8,128)S(1)}, f32[32,128]{1,0:T(8,128)S(1)}, u32[]{:S(2)}, u32[]{:S(2)}) collective-permute-start(f32[32,128]{1,0:T(8,128)S(1)} %add.3.rest_6_), channel_id=1, source_target_pairs={{0,2},{1,3},{2,0},{3,1},{4,6},{5,7},{6,4},{7,5},{8,10},{9,11},{10,... | collective-permute-start | bytes 49160 | tf_op jit(solution)/shard_map/ppermute | solution.py:405
  21.9 0.8 %fusion.7.far_ref = f32[2,32,256]{2,1,0:T(8,128)S(1)} fusion(bf16[4096,2,256]{2,1,0:T(2,128)(2,1)S(1)} %get-tuple-element.31, bf16[32,4096]{1,0:T(8,128)(2,1)S(1)} %get-tuple-element.35), kind=kOutput, calls=%fused_computation.5 | convolution fusion | flops 134217728 | bytes 4521984 | tf_op jit(solution)/shard_map/md,dkc->kmc/dot_general | solution.py:401
  22.7 1.3 %collective-permute-done.7.rest_7_ = f32[32,128]{1,0:T(8,128)S(1)} collective-permute-done((f32[32,128]{1,0:T(8,128)S(1)}, f32[32,128]{1,0:T(8,128)S(1)}, u32[]{:S(2)}, u32[]{:S(2)}) %collective-permute-start.7) | collective-permute-done | bytes 16416 | tf_op jit(solution)/shard_map/ppermute | solution.py:405
  24.0 1.5 %fresh_attention.1 = (bf16[4,8,256]{2,1,0:T(8,128)(2,1)}, bf16[4,8,256]{2,1,0:T(8,128)(2,1)}, bf16[4,8,2048]{2,1,0:T(8,128)(2,1)}) custom-call(f32[2,32,256]{2,1,0:T(8,128)S(1)} %fusion.4.near_ref, f32[2,32,256]{2,1,0:T(8,128)S(1)} %fusion.7.far_ref, f32[32,128]{1,0:T(8,128)S(1)} %get-tuple-element.36.square_ref, ...), custom_call_target="tpu_custom_call" | custom-call | tf_op jit(solution)/shard_map/fresh_attention/pallas_call | solution.py:389
  (1 shorter events, 0.0 us)
Async XLA Ops:
  1.6 11.3 %collective-permute-start = (bf16[2,16,2304]{2,1,0:T(8,128)(2,1)S(1)}, bf16[2,16,2304]{2,1,0:T(8,128)(2,1)S(1)}, u32[]{:S(2)}, u32[]{:S(2)}) collective-permute-start(bf16[2,16,2304]{2,1,0:T(8,128)(2,1)S(1)} %pack_factors.1.rest_0_.rest_8_), channel_id=1, source_target_pairs={{0,8},{4,12},{8,0},{12,4},{1,9},{5,13},{9,1},{13,5},{2,10},{6,14},... | collective-permute-start | bytes 442376 | tf_op jit(solution)/shard_map/ppermute | solution.py:405
  5.7 7.8 %collective-permute-start.1 = (bf16[4,8,2048]{2,1,0:T(8,128)(2,1)}, bf16[4,8,2048]{2,1,0:T(8,128)(2,1)S(1)}, u32[]{:S(2)}, u32[]{:S(2)}) collective-permute-start(bf16[4,8,2048]{2,1,0:T(8,128)(2,1)} %hidden_ref.1), channel_id=1, source_target_pairs={{0,1},{1,0},{2,3},{3,2},{4,5},{5,4},{6,7},{7,6},{8,9},{9,8},{10,11... | collective-permute-start | bytes 393224 | tf_op jit(solution)/shard_map/ppermute | solution.py:405
  5.7 7.8 %collective-permute-start.2 = (bf16[4,8,2048]{2,1,0:T(8,128)(2,1)}, bf16[4,8,2048]{2,1,0:T(8,128)(2,1)S(1)}, u32[]{:S(2)}, u32[]{:S(2)}) collective-permute-start(bf16[4,8,2048]{2,1,0:T(8,128)(2,1)} %hidden_ref.1), channel_id=1, source_target_pairs={{0,2},{1,3},{2,0},{3,1},{4,6},{5,7},{6,4},{7,5},{8,10},{9,11},{10,... | collective-permute-start | bytes 393224 | tf_op jit(solution)/shard_map/ppermute | solution.py:405
  7.2 7.0 %collective-permute-start.3 = (bf16[4,8,2048]{2,1,0:T(8,128)(2,1)}, bf16[4,8,2048]{2,1,0:T(8,128)(2,1)S(1)}, u32[]{:S(2)}, u32[]{:S(2)}) collective-permute-start(bf16[4,8,2048]{2,1,0:T(8,128)(2,1)} %hidden_ref.1), channel_id=1, source_target_pairs={{0,3},{1,2},{2,1},{3,0},{4,7},{5,6},{6,5},{7,4},{8,11},{9,10},{10,... | collective-permute-start | bytes 393224 | tf_op jit(solution)/shard_map/ppermute | solution.py:405
  7.5 9.9 %collective-permute-start.4 = (bf16[2,16,2304]{2,1,0:T(8,128)(2,1)S(1)}, bf16[2,16,2304]{2,1,0:T(8,128)(2,1)S(1)}, u32[]{:S(2)}, u32[]{:S(2)}) collective-permute-start(bf16[2,16,2304]{2,1,0:T(8,128)(2,1)S(1)} %pack_factors.1.rest_0_.rest_8_), channel_id=1, source_target_pairs={{0,4},{4,0},{8,12},{12,8},{1,5},{5,1},{9,13},{13,9},{2,6},{6,2},{1... | collective-permute-start | bytes 442376 | tf_op jit(solution)/shard_map/ppermute | solution.py:405
  12.8 5.8 %collective-permute-start.5 = (bf16[2,16,2304]{2,1,0:T(8,128)(2,1)S(1)}, bf16[2,16,2304]{2,1,0:T(8,128)(2,1)S(1)}, u32[]{:S(2)}, u32[]{:S(2)}) collective-permute-start(bf16[2,16,2304]{2,1,0:T(8,128)(2,1)S(1)} %collective-permute-done.rest_2_.rest_10_), channel_id=1, source_target_pairs={{0,4},{4,0},{8,12},{12,8},{1,5},{5,1},{9,13},{13,9},{2,6},{6,2},{1... | collective-permute-start | bytes 442376 | tf_op jit(solution)/shard_map/ppermute | solution.py:405
  19.0 1.2 %collective-permute-start.6 = (f32[32,128]{1,0:T(8,128)S(1)}, f32[32,128]{1,0:T(8,128)S(1)}, u32[]{:S(2)}, u32[]{:S(2)}) collective-permute-start(f32[32,128]{1,0:T(8,128)S(1)} %rank_inner.1), channel_id=1, source_target_pairs={{0,1},{1,0},{2,3},{3,2},{4,5},{5,4},{6,7},{7,6},{8,9},{9,8},{10,11... | collective-permute-start | bytes 49160 | tf_op jit(solution)/shard_map/ppermute | solution.py:405
  20.3 3.7 %collective-permute-start.7 = (f32[32,128]{1,0:T(8,128)S(1)}, f32[32,128]{1,0:T(8,128)S(1)}, u32[]{:S(2)}, u32[]{:S(2)}) collective-permute-start(f32[32,128]{1,0:T(8,128)S(1)} %add.3.rest_6_), channel_id=1, source_target_pairs={{0,2},{1,3},{2,0},{3,1},{4,6},{5,7},{6,4},{7,5},{8,10},{9,11},{10,... | collective-permute-start | bytes 49160 | tf_op jit(solution)/shard_map/ppermute | solution.py:405

commit v14 on v10

--- a/solution.py
+++ b/solution.py
@@ -422,11 +422,11 @@
     gain = input_norm_gain.reshape(width // HD, HD)
     up_part = jnp.transpose(adapter_up_factor, (0, 2, 1))
     direct = wide_count == tp_count == 4
-    tp_parts = [swap(hidden, "tp", offset, tp_count) for offset in (1, 2, 3)]
     if direct:
         pack = pack_call(adapter_down_factor, up_part)
         second = swap(pack, "wide", 2, wide_count)
         first = swap(pack, "wide", 1, wide_count)
+    beside, crossed = [swap(hidden, "tp", offset, tp_count) for offset in (1, 2)]
     near, far = (0, 1), (2, 3)
     near_weight, gain_rows, bias, mine, *cached = cache_call(
         near,
@@ -442,8 +442,14 @@
     if direct:
         third, gain_rows = lax.optimization_barrier((second, gain_rows))
         packs = [pack, first, second, swap(third, "wide", 1, wide_count)]
+        relayed, first, beside = lax.optimization_barrier((crossed, first, beside))
+        packs[1] = first
+    else:
+        relayed = crossed
+    relayed, gain_rows = lax.optimization_barrier((relayed, gain_rows))
+    relayed = swap(relayed, "tp", 1, tp_count)
     scaled, near_scaled, far_scaled, square, far_weight = scale_call(
-        near, far, key_value_weight, gain_rows, [mine] + tp_parts
+        near, far, key_value_weight, gain_rows, (mine, beside, crossed, relayed)
     )
     if direct:
         inner = inner_call(scaled, packs)

time: 25.5 us -> 26 us (1.020)
  starting transfers between devices: 10 us -> 10.5 us
    ppermute x9, starting transfers between devices: 10 us -> 10.5 us  [swap(): return lax.ppermute(block, axis, [(i, i ^ offset) for i in range(count)])]
  transfers between devices with their start and end apart: 9 -> 9, of which waited for: 4 -> 5; matrix products, arithmetic and copies ran while one was open for 7% -> 6% of each run, Pallas kernels for 24% -> 24%
where the time goes in v14:
time: 26 us; the launch traced here: 25.8 us
  starting transfers between devices  10.5 us (40%)
  Pallas kernels  8.82 us (34%)
  waiting for transfers between devices  4.15 us (16%)
  matrix products  1.67 us (6%)
  between operations  0.67 us (3%)
    ppermute x9, starting transfers between devices, swap(): return lax.ppermute(block, axis, [(i, i ^ offset) for i in range(count)])  10.5 us
    ppermute x9, waiting for transfers between devices, swap(): return lax.ppermute(block, axis, [(i, i ^ offset) for i in range(count)])  4.15 us
    pallas_call x1, Pallas kernels, cache_call(): pl.pallas_call(functools.partial(cache_kernel, near), out_shape=(pltpu.VM...  3.7 us
    pallas_call x1, Pallas kernels, scale_call(): pl.pallas_call(functools.partial(scale_kernel, near, far), out_shape=(plt...  2.37 us
    dot_general x2, matrix products, on_device(): jnp.einsum('md,dkc->kmc', x, y, preferred_element_type=jnp.float32)  1.67 us
    pallas_call x1, Pallas kernels, final_call(): pl.pallas_call(functools.partial(final_kernel, width, len(inner)), out_sh...  1.55 us
    pallas_call x1, Pallas kernels, pack_call(): pl.pallas_call(pack_kernel, out_shape=pltpu.VMEM((kinds, share, down.shap...  0.93 us
  transfers between devices with their start and end apart: 9, of which 5 were waited for; matrix products, arithmetic and copies ran while one was open for 6% of the time, Pallas kernels for 24%

profile of v14, /device:TPU:0, one launch (start us, length us, event | category | flops | bytes accessed | tf_op | source)
XLA Modules:
  0.0 25.8 jit_solution(1900782625536986384)
XLA Ops:
  0.6 0.9 %pack_factors.1.rest_0_.rest_10_ = bf16[2,16,2304]{2,1,0:T(8,128)(2,1)S(1)} custom-call(bf16[2,64,2048]{2,1,0:T(8,128)(2,1)} %down_ref.1, bf16[2,16,256]{2,1,0:T(8,128)(2,1)} %bitcast.13), custom_call_target="tpu_custom_call" | custom-call | tf_op jit(solution)/shard_map/pack_factors/pallas_call | solution.py:219
  1.6 4.1 %collective-permute-start.3 = (bf16[2,16,2304]{2,1,0:T(8,128)(2,1)S(1)}, bf16[2,16,2304]{2,1,0:T(8,128)(2,1)S(1)}, u32[]{:S(2)}, u32[]{:S(2)}) collective-permute-start(bf16[2,16,2304]{2,1,0:T(8,128)(2,1)S(1)} %pack_factors.1.rest_0_.rest_10_), channel_id=1, source_target_pairs={{0,8},{4,12},{8,0},{12,4},{1,9},{5,13},{9,1},{13,5},{2,10},{6,14},... | collective-permute-start | bytes 442376 | tf_op jit(solution)/shard_map/ppermute | solution.py:402
  5.7 1.6 %collective-permute-start.1 = (bf16[2,16,2304]{2,1,0:T(8,128)(2,1)S(1)}, bf16[2,16,2304]{2,1,0:T(8,128)(2,1)S(1)}, u32[]{:S(2)}, u32[]{:S(2)}) collective-permute-start(bf16[2,16,2304]{2,1,0:T(8,128)(2,1)S(1)} %pack_factors.1.rest_0_.rest_10_), channel_id=1, source_target_pairs={{0,4},{4,0},{8,12},{12,8},{1,5},{5,1},{9,13},{13,9},{2,6},{6,2},{1... | collective-permute-start | bytes 442376 | tf_op jit(solution)/shard_map/ppermute | solution.py:402
  7.2 1.5 %collective-permute-start = (bf16[4,8,2048]{2,1,0:T(8,128)(2,1)}, bf16[4,8,2048]{2,1,0:T(8,128)(2,1)S(1)}, u32[]{:S(2)}, u32[]{:S(2)}) collective-permute-start(bf16[4,8,2048]{2,1,0:T(8,128)(2,1)} %hidden_ref.1), channel_id=1, source_target_pairs={{0,2},{1,3},{2,0},{3,1},{4,6},{5,7},{6,4},{7,5},{8,10},{9,11},{10,... | collective-permute-start | bytes 393224 | tf_op jit(solution)/shard_map/ppermute | solution.py:402
  8.7 0.0 collective-permute-start.2
  8.7 3.7 %cache_attention.1 = (bf16[4096,2,256]{2,1,0:T(2,128)(2,1)S(1)}, f32[64,128]{1,0:T(8,128)S(1)}, bf16[2,256]{1,0:T(2,128)(2,1)S(1)}, bf16[4,8,2048]{2,1,0:T(8,128...) custom-call(s32[8]{0:T(128)} %lengths_ref.1, ...), custom_call_target="tpu_custom_call" | custom-call | flops 140509184 | bytes 9437184 | tf_op jit(solution)/shard_map/cache_attention/pallas_call | solution.py:165
  12.5 0.3 %collective-permute-done.3.rest_2_.rest_12_ = bf16[2,16,2304]{2,1,0:T(8,128)(2,1)S(1)} collective-permute-done((bf16[2,16,2304]{2,1,0:T(8,128)(2,1)S(1)}, bf16[2,16,2304]{2,1,0:T(8,128)(2,1)S(1)}, u32[]{:S(2)}, u32[]{:S(2)}) %collective-permute-start.3) | collective-permute-done | bytes 147488 | tf_op jit(solution)/shard_map/ppermute | solution.py:402
  12.8 0.0 collective-permute-done.rest_2_
  12.8 0.0 collective-permute-done.2.rest_1_
  12.8 0.2 collective-permute-done.1.rest_1_.rest_11_
  13.0 0.1 collective-permute-start.4
  13.1 1.4 %collective-permute-start.5 = (bf16[2,16,2304]{2,1,0:T(8,128)(2,1)S(1)}, bf16[2,16,2304]{2,1,0:T(8,128)(2,1)S(1)}, u32[]{:S(2)}, u32[]{:S(2)}) collective-permute-start(bf16[2,16,2304]{2,1,0:T(8,128)(2,1)S(1)} %collective-permute-done.3.rest_2_.rest_12_), channel_id=1, source_target_pairs={{0,4},{4,0},{8,12},{12,8},{1,5},{5,1},{9,13},{13,9},{2,6},{6,2},{1... | collective-permute-start | bytes 442376 | tf_op jit(solution)/shard_map/ppermute | solution.py:402
  14.5 0.0 collective-permute-done.4.rest_3_
  14.5 2.4 %scale_features.1 = (bf16[32,8192]{1,0:T(8,128)(2,1)S(1)}, bf16[32,4096]{1,0:T(8,128)(2,1)S(1)}, bf16[32,4096]{1,0:T(8,128)(2,1)S(1)}, f32[32,128]{1,0:T(8,128)S(1)}, bf16[4096,2,256]{2,1,0:T(2,128)(2,1)S(1)}) custom-call(bf16[8192,2,256]{2,1,0:T(2,128)(2,1)} %weight_ref.3, f32[64,128]{1,0:T(8,128)S(1)} %get-tuple-element.31.gain_ref, ...), custom_call_target="tpu_custom_call" | custom-call | bytes 5242880 | tf_op jit(solution)/shard_map/scale_features/pallas_call | solution.py:287
  16.9 0.8 %fusion.4.near_ref = f32[2,32,256]{2,1,0:T(8,128)S(1)} fusion(bf16[4096,2,256]{2,1,0:T(2,128)(2,1)S(1)} %get-tuple-element.27, bf16[32,4096]{1,0:T(8,128)(2,1)S(1)} %get-tuple-element.35), kind=kOutput, calls=%fused_computation.4 | convolution fusion | flops 134217728 | bytes 4521984 | tf_op jit(solution)/shard_map/md,dkc->kmc/dot_general | solution.py:464
  17.7 1.6 %collective-permute-done.5.rest_3_.rest_13_ = bf16[2,16,2304]{2,1,0:T(8,128)(2,1)S(1)} collective-permute-done((bf16[2,16,2304]{2,1,0:T(8,128)(2,1)S(1)}, bf16[2,16,2304]{2,1,0:T(8,128)(2,1)S(1)}, u32[]{:S(2)}, u32[]{:S(2)}) %collective-permute-start.5) | collective-permute-done | bytes 147488 | tf_op jit(solution)/shard_map/ppermute | solution.py:402
  19.3 0.3 %rank_inner.1.rest_6_ = f32[32,32]{1,0:T(8,128)S(1)} custom-call(bf16[32,8192]{1,0:T(8,128)(2,1)S(1)} %get-tuple-element.37.scaled_ref, bf16[2,16,2304]{2,1,0:T(8,128)(2,1)S(1)} %pack_factors.1.rest_0_.rest_10_, bf16[2,16,2304]{2,1,0:T(8,128)(2,1)S(1)} %collective-permute-done.1.rest_1_.rest_11_, ...), custom_call_target="tpu_custom_call" | custom-call | tf_op jit(solution)/shard_map/rank_inner/pallas_call | solution.py:248
  19.5 0.0 collective-permute-start.6
  19.5 1.6 %collective-permute-start.7 = (f32[32,32]{1,0:T(8,128)S(1)}, f32[32,32]{1,0:T(8,128)S(1)}, u32[]{:S(2)}, u32[]{:S(2)}) collective-permute-start(f32[32,32]{1,0:T(8,128)S(1)} %rank_inner.1.rest_6_), channel_id=1, source_target_pairs={{0,2},{1,3},{2,0},{3,1},{4,6},{5,7},{6,4},{7,5},{8,10},{9,11},{10,... | collective-permute-start | bytes 12296 | tf_op jit(solution)/shard_map/ppermute | solution.py:402
  21.1 0.3 %collective-permute-start.8 = (f32[32,32]{1,0:T(8,128)S(1)}, f32[32,32]{1,0:T(8,128)S(1)}, u32[]{:S(2)}, u32[]{:S(2)}) collective-permute-start(f32[32,32]{1,0:T(8,128)S(1)} %rank_inner.1.rest_6_), channel_id=1, source_target_pairs={{0,3},{1,2},{2,1},{3,0},{4,7},{5,6},{6,5},{7,4},{8,11},{9,10},{10,... | collective-permute-start | bytes 12296 | tf_op jit(solution)/shard_map/ppermute | solution.py:402
  21.4 0.8 %fusion.7.far_ref = f32[2,32,256]{2,1,0:T(8,128)S(1)} fusion(bf16[4096,2,256]{2,1,0:T(2,128)(2,1)S(1)} %get-tuple-element.36, bf16[32,4096]{1,0:T(8,128)(2,1)S(1)} %get-tuple-element.41), kind=kOutput, calls=%fused_computation.5 | convolution fusion | flops 134217728 | bytes 4521984 | tf_op jit(solution)/shard_map/md,dkc->kmc/dot_general | solution.py:464
  22.2 0.0 collective-permute-done.6.rest_7_
  22.2 1.1 %collective-permute-done.7.rest_8_ = f32[32,32]{1,0:T(8,128)S(1)} collective-permute-done((f32[32,32]{1,0:T(8,128)S(1)}, f32[32,32]{1,0:T(8,128)S(1)}, u32[]{:S(2)}, u32[]{:S(2)}) %collective-permute-start.7) | collective-permute-done | bytes 4128 | tf_op jit(solution)/shard_map/ppermute | solution.py:402
  23.3 0.9 %collective-permute-done.8.rest_9_ = f32[32,32]{1,0:T(8,128)S(1)} collective-permute-done((f32[32,32]{1,0:T(8,128)S(1)}, f32[32,32]{1,0:T(8,128)S(1)}, u32[]{:S(2)}, u32[]{:S(2)}) %collective-permute-start.8) | collective-permute-done | bytes 4128 | tf_op jit(solution)/shard_map/ppermute | solution.py:402
  24.3 1.5 %fresh_attention.1 = (bf16[4,8,256]{2,1,0:T(8,128)(2,1)}, bf16[4,8,256]{2,1,0:T(8,128)(2,1)}, bf16[4,8,2048]{2,1,0:T(8,128)(2,1)}) custom-call(f32[2,32,256]{2,1,0:T(8,128)S(1)} %fusion.4.near_ref, f32[2,32,256]{2,1,0:T(8,128)S(1)} %fusion.7.far_ref, f32[32,128]{1,0:T(8,128)S(1)} %get-tuple-element.42.square_ref, ...), custom_call_target="tpu_custom_call" | custom-call | tf_op jit(solution)/shard_map/fresh_attention/pallas_call | solution.py:387
Async XLA Ops:
  1.6 11.2 %collective-permute-start.3 = (bf16[2,16,2304]{2,1,0:T(8,128)(2,1)S(1)}, bf16[2,16,2304]{2,1,0:T(8,128)(2,1)S(1)}, u32[]{:S(2)}, u32[]{:S(2)}) collective-permute-start(bf16[2,16,2304]{2,1,0:T(8,128)(2,1)S(1)} %pack_factors.1.rest_0_.rest_10_), channel_id=1, source_target_pairs={{0,8},{4,12},{8,0},{12,4},{1,9},{5,13},{9,1},{13,5},{2,10},{6,14},... | collective-permute-start | bytes 442376 | tf_op jit(solution)/shard_map/ppermute | solution.py:402
  5.7 7.3 %collective-permute-start.1 = (bf16[2,16,2304]{2,1,0:T(8,128)(2,1)S(1)}, bf16[2,16,2304]{2,1,0:T(8,128)(2,1)S(1)}, u32[]{:S(2)}, u32[]{:S(2)}) collective-permute-start(bf16[2,16,2304]{2,1,0:T(8,128)(2,1)S(1)} %pack_factors.1.rest_0_.rest_10_), channel_id=1, source_target_pairs={{0,4},{4,0},{8,12},{12,8},{1,5},{5,1},{9,13},{13,9},{2,6},{6,2},{1... | collective-permute-start | bytes 442376 | tf_op jit(solution)/shard_map/ppermute | solution.py:402
  7.2 5.5 %collective-permute-start = (bf16[4,8,2048]{2,1,0:T(8,128)(2,1)}, bf16[4,8,2048]{2,1,0:T(8,128)(2,1)S(1)}, u32[]{:S(2)}, u32[]{:S(2)}) collective-permute-start(bf16[4,8,2048]{2,1,0:T(8,128)(2,1)} %hidden_ref.1), channel_id=1, source_target_pairs={{0,2},{1,3},{2,0},{3,1},{4,6},{5,7},{6,4},{7,5},{8,10},{9,11},{10,... | collective-permute-start | bytes 393224 | tf_op jit(solution)/shard_map/ppermute | solution.py:402
  8.7 4.1 %collective-permute-start.2 = (bf16[4,8,2048]{2,1,0:T(8,128)(2,1)}, bf16[4,8,2048]{2,1,0:T(8,128)(2,1)S(1)}, u32[]{:S(2)}, u32[]{:S(2)}) collective-permute-start(bf16[4,8,2048]{2,1,0:T(8,128)(2,1)} %hidden_ref.1), channel_id=1, source_target_pairs={{0,1},{1,0},{2,3},{3,2},{4,5},{5,4},{6,7},{7,6},{8,9},{9,8},{10,11... | collective-permute-start | bytes 393224 | tf_op jit(solution)/shard_map/ppermute | solution.py:402
  13.0 1.5 %collective-permute-start.4 = (bf16[4,8,2048]{2,1,0:T(8,128)(2,1)S(1)}, bf16[4,8,2048]{2,1,0:T(8,128)(2,1)S(1)}, u32[]{:S(2)}, u32[]{:S(2)}) collective-permute-start(bf16[4,8,2048]{2,1,0:T(8,128)(2,1)S(1)} %collective-permute-done.rest_2_), channel_id=1, source_target_pairs={{0,1},{1,0},{2,3},{3,2},{4,5},{5,4},{6,7},{7,6},{8,9},{9,8},{10,11... | collective-permute-start | bytes 393224 | tf_op jit(solution)/shard_map/ppermute | solution.py:402
  13.1 6.2 %collective-permute-start.5 = (bf16[2,16,2304]{2,1,0:T(8,128)(2,1)S(1)}, bf16[2,16,2304]{2,1,0:T(8,128)(2,1)S(1)}, u32[]{:S(2)}, u32[]{:S(2)}) collective-permute-start(bf16[2,16,2304]{2,1,0:T(8,128)(2,1)S(1)} %collective-permute-done.3.rest_2_.rest_12_), channel_id=1, source_target_pairs={{0,4},{4,0},{8,12},{12,8},{1,5},{5,1},{9,13},{13,9},{2,6},{6,2},{1... | collective-permute-start | bytes 442376 | tf_op jit(solution)/shard_map/ppermute | solution.py:402
  19.5 2.7 %collective-permute-start.6 = (f32[32,32]{1,0:T(8,128)S(1)}, f32[32,32]{1,0:T(8,128)S(1)}, u32[]{:S(2)}, u32[]{:S(2)}) collective-permute-start(f32[32,32]{1,0:T(8,128)S(1)} %rank_inner.1.rest_6_), channel_id=1, source_target_pairs={{0,1},{1,0},{2,3},{3,2},{4,5},{5,4},{6,7},{7,6},{8,9},{9,8},{10,11... | collective-permute-start | bytes 12296 | tf_op jit(solution)/shard_map/ppermute | solution.py:402
  19.5 3.8 %collective-permute-start.7 = (f32[32,32]{1,0:T(8,128)S(1)}, f32[32,32]{1,0:T(8,128)S(1)}, u32[]{:S(2)}, u32[]{:S(2)}) collective-permute-start(f32[32,32]{1,0:T(8,128)S(1)} %rank_inner.1.rest_6_), channel_id=1, source_target_pairs={{0,2},{1,3},{2,0},{3,1},{4,6},{5,7},{6,4},{7,5},{8,10},{9,11},{10,... | collective-permute-start | bytes 12296 | tf_op jit(solution)/shard_map/ppermute | solution.py:402
  21.1 3.2 %collective-permute-start.8 = (f32[32,32]{1,0:T(8,128)S(1)}, f32[32,32]{1,0:T(8,128)S(1)}, u32[]{:S(2)}, u32[]{:S(2)}) collective-permute-start(f32[32,32]{1,0:T(8,128)S(1)} %rank_inner.1.rest_6_), channel_id=1, source_target_pairs={{0,3},{1,2},{2,1},{3,0},{4,7},{5,6},{6,5},{7,4},{8,11},{9,10},{10,... | collective-permute-start | bytes 12296 | tf_op jit(solution)/shard_map/ppermute | solution.py:402

commit v15 on v10

--- a/solution.py
+++ b/solution.py
@@ -59,6 +59,7 @@
     gain_out,
     bias_out,
     hidden_out,
+    query_rows,
     query_out,
     acc_out,
     top_out,
@@ -114,14 +115,15 @@
         sin_out[pl.ds(step * rows, rows)] = jnp.where(second, sine, -sine)
     copies[1].wait()
     for group in range(groups):
-        query_out[group] = query_block(queries, group, per_group)
+        query_rows[group] = query_block(queries, group, per_group)
+        query_out[group] = query_rows[group].astype(jnp.bfloat16)
 
     place = lax.broadcasted_iota(jnp.int32, (lines, cache_span), 1)
     for i in range(2):
         copies[2 + i].wait()
         for row in range(i * half_rows, (i + 1) * half_rows):
             for group in range(groups):
-                query = query_out[group, pl.ds(row, lines, stride=rows), :].astype(jnp.bfloat16)
+                query = query_rows[group, pl.ds(row, lines, stride=rows), :].astype(jnp.bfloat16)
                 score_buffer[row * groups + group] = lax.dot_general(
                     query,
                     key_buffer[row, :, pl.ds(group * HD, HD)],
@@ -170,6 +172,7 @@
             pltpu.VMEM(bias.shape, bias.dtype),
             pltpu.VMEM(hidden.shape, hidden.dtype),
             pltpu.VMEM(block, jnp.float32),
+            pltpu.VMEM(block, jnp.bfloat16),
             pltpu.VMEM(block, jnp.float32),
             pltpu.VMEM(block, jnp.float32),
             pltpu.VMEM(block, jnp.float32),
@@ -177,7 +180,7 @@
             pltpu.VMEM(table, jnp.float32),
         ),
         in_specs=[HBM] * len(operands),
-        out_specs=(VMEM,) * 10,
+        out_specs=(VMEM,) * 11,
         scratch_shapes=[
             pltpu.SMEM(lengths.shape, jnp.int32),
             pltpu.VMEM(queries.shape, queries.dtype),
@@ -316,12 +319,22 @@
             ]
 
 
+def up_call(packs, columns):
+    kinds, share, _ = packs[0].shape
+    return pl.pallas_call(
+        up_kernel,
+        out_shape=pltpu.VMEM((len(packs) * kinds * share, kinds * columns), packs[0].dtype),
+        in_specs=[VMEM] * len(packs),
+        out_specs=VMEM,
+        compiler_params=pltpu.CompilerParams(vmem_limit_bytes=8 << 20),
+        name="lay_out_up",
+    )(*packs)
+
+
 def final_kernel(width, blocks, near_ref, far_ref, square_ref, bias_ref, *rest):
     query_ref, acc_ref, top_ref, total_ref, cos_ref, sin_ref = rest[:6]
     inner_refs = rest[6 : 6 + blocks]
-    packs = rest[6 + blocks : 6 + 2 * blocks]
-    keys_out, values_out, attended_out, inner_buffer, up_ref = rest[6 + 2 * blocks :]
-    up_kernel(*packs, up_ref)
+    up_ref, keys_out, values_out, attended_out, inner_buffer = rest[6 + blocks :]
     steps, rows, columns = keys_out.shape
     count = steps * rows
     groups, size, _ = query_ref.shape
@@ -357,7 +370,7 @@
             keys_out[step, :, at] = key[step * rows : (step + 1) * rows]
             values_out[step, :, at] = value[step * rows : (step + 1) * rows]
         scores = lax.dot_general(
-            query_ref[group].astype(jnp.bfloat16),
+            query_ref[group],
             key,
             (((1,), (1,)), ((), ())),
             preferred_element_type=jnp.float32,
@@ -379,23 +392,19 @@
                 attended_out[step, :, lanes] = attended[tile : tile + rows]
 
 
-def final_call(shape, width, near, far, square, bias, cached, inner, packs):
+def final_call(shape, width, near, far, square, bias, cached, inner, up):
     steps, rows, query_width = shape
-    kinds, share, _ = packs[0].shape
     columns = near.shape[2]
     small = jax.ShapeDtypeStruct((steps, rows, columns), jnp.bfloat16)
     return pl.pallas_call(
         functools.partial(final_kernel, width, len(inner)),
         out_shape=(small, small, jax.ShapeDtypeStruct(shape, jnp.bfloat16)),
-        in_specs=[VMEM] * (4 + len(cached) + len(inner) + len(packs)),
+        in_specs=[VMEM] * (5 + len(cached) + len(inner)),
         out_specs=(VMEM,) * 3,
-        scratch_shapes=[
-            pltpu.VMEM((len(inner),) + inner[0].shape, jnp.float32),
-            pltpu.VMEM((len(packs) * kinds * share, kinds * columns), jnp.bfloat16),
-        ],
+        scratch_shapes=[pltpu.VMEM((len(inner),) + inner[0].shape, jnp.float32)],
         compiler_params=pltpu.CompilerParams(vmem_limit_bytes=8 << 20),
         name="fresh_attention",
-    )(near, far, square, bias, *cached, *inner, *packs)
+    )(near, far, square, bias, *cached, *inner, up)
 
 
 def swap(block, axis, offset, count):
@@ -428,7 +437,7 @@
         second = swap(pack, "wide", 2, wide_count)
         first = swap(pack, "wide", 1, wide_count)
     near, far = (0, 1), (2, 3)
-    near_weight, gain_rows, bias, mine, *cached = cache_call(
+    near_weight, gain_rows, bias, mine, _, *cached = cache_call(
         near,
         lengths,
         queries,
@@ -447,7 +456,7 @@
     )
     if direct:
         inner = inner_call(scaled, packs)
-        inner, far_scaled = lax.optimization_barrier((inner, far_scaled))
+        inner, far_scaled, packs = lax.optimization_barrier((inner, far_scaled, packs))
         inner = [inner] + [swap(inner, "tp", offset, tp_count) for offset in (1, 2, 3)]
     else:
         down = lax.all_gather(adapter_down_factor, "wide", axis=2, tiled=True)
@@ -458,8 +467,9 @@
         jnp.einsum("md,dkc->kmc", x, y, preferred_element_type=jnp.float32)
         for x, y in ((near_scaled, near_weight), (far_scaled, far_weight))
     ]
+    up = up_call(packs, bias.shape[1])
     return final_call(
-        queries.shape, width, near_base, far_base, square, bias, cached, inner, packs
+        queries.shape, width, near_base, far_base, square, bias, cached, inner, up
     )
 
 

time: 25.5 us -> 26.1 us (1.024)
  Pallas kernels: 8.82 us -> 9.56 us
    pallas_call x1, Pallas kernels: 3.7 us -> 4.41 us  [cache_call(): pl.pallas_call(functools.partial(cache_kernel, near), out_shape=(pltpu.VM...]
  transfers between devices with their start and end apart: 9 -> 9, of which waited for: 4 -> 4; matrix products, arithmetic and copies ran while one was open for 7% -> 6% of each run, Pallas kernels for 24% -> 26%
where the time goes in v15:
time: 26.1 us; the launch traced here: 25.9 us
  starting transfers between devices  9.92 us (38%)
  Pallas kernels  9.56 us (37%)
  waiting for transfers between devices  4.07 us (16%)
  matrix products  1.67 us (6%)
  between operations  0.7 us (3%)
    ppermute x9, starting transfers between devices, swap(): return lax.ppermute(block, axis, [(i, i ^ offset) for i in range(count)])  9.92 us
    pallas_call x1, Pallas kernels, cache_call(): pl.pallas_call(functools.partial(cache_kernel, near), out_shape=(pltpu.VM...  4.41 us
    ppermute x9, waiting for transfers between devices, swap(): return lax.ppermute(block, axis, [(i, i ^ offset) for i in range(count)])  4.07 us
    pallas_call x1, Pallas kernels, scale_call(): pl.pallas_call(functools.partial(scale_kernel, near, far), out_shape=(plt...  2.37 us
    dot_general x2, matrix products, on_device(): jnp.einsum('md,dkc->kmc', x, y, preferred_element_type=jnp.float32)  1.67 us
    pallas_call x1, Pallas kernels, final_call(): pl.pallas_call(functools.partial(final_kernel, width, len(inner)), out_sh...  1.55 us
    pallas_call x1, Pallas kernels, pack_call(): pl.pallas_call(pack_kernel, out_shape=pltpu.VMEM((kinds, share, down.shap...  0.93 us
  transfers between devices with their start and end apart: 9, of which 4 were waited for; matrix products, arithmetic and copies ran while one was open for 6% of the time, Pallas kernels for 26%

profile of v15, /device:TPU:0, one launch (start us, length us, event | category | flops | bytes accessed | tf_op | source)
XLA Modules:
  0.0 25.9 jit_solution(520151388797697542)
XLA Ops:
  0.6 0.9 %pack_factors.1.rest_0_.refs_0_ = bf16[2,16,2304]{2,1,0:T(8,128)(2,1)S(1)} custom-call(bf16[2,64,2048]{2,1,0:T(8,128)(2,1)} %down_ref.1, bf16[2,16,256]{2,1,0:T(8,128)(2,1)} %bitcast.13), custom_call_target="tpu_custom_call" | custom-call | tf_op jit(solution)/shard_map/pack_factors/pallas_call | solution.py:222
  1.6 4.1 %collective-permute-start = (bf16[2,16,2304]{2,1,0:T(8,128)(2,1)S(1)}, bf16[2,16,2304]{2,1,0:T(8,128)(2,1)S(1)}, u32[]{:S(2)}, u32[]{:S(2)}) collective-permute-start(bf16[2,16,2304]{2,1,0:T(8,128)(2,1)S(1)} %pack_factors.1.rest_0_.refs_0_), channel_id=1, source_target_pairs={{0,8},{4,12},{8,0},{12,4},{1,9},{5,13},{9,1},{13,5},{2,10},{6,14},... | collective-permute-start | bytes 442376 | tf_op jit(solution)/shard_map/ppermute | solution.py:411
  5.7 0.0 collective-permute-start.1
  5.7 1.5 %collective-permute-start.2 = (bf16[4,8,2048]{2,1,0:T(8,128)(2,1)}, bf16[4,8,2048]{2,1,0:T(8,128)(2,1)S(1)}, u32[]{:S(2)}, u32[]{:S(2)}) collective-permute-start(bf16[4,8,2048]{2,1,0:T(8,128)(2,1)} %hidden_ref.1), channel_id=1, source_target_pairs={{0,2},{1,3},{2,0},{3,1},{4,6},{5,7},{6,4},{7,5},{8,10},{9,11},{10,... | collective-permute-start | bytes 393224 | tf_op jit(solution)/shard_map/ppermute | solution.py:411
  7.2 0.4 %collective-permute-start.3 = (bf16[4,8,2048]{2,1,0:T(8,128)(2,1)}, bf16[4,8,2048]{2,1,0:T(8,128)(2,1)S(1)}, u32[]{:S(2)}, u32[]{:S(2)}) collective-permute-start(bf16[4,8,2048]{2,1,0:T(8,128)(2,1)} %hidden_ref.1), channel_id=1, source_target_pairs={{0,3},{1,2},{2,1},{3,0},{4,7},{5,6},{6,5},{7,4},{8,11},{9,10},{10,... | collective-permute-start | bytes 393224 | tf_op jit(solution)/shard_map/ppermute | solution.py:411
  7.5 1.6 %collective-permute-start.4 = (bf16[2,16,2304]{2,1,0:T(8,128)(2,1)S(1)}, bf16[2,16,2304]{2,1,0:T(8,128)(2,1)S(1)}, u32[]{:S(2)}, u32[]{:S(2)}) collective-permute-start(bf16[2,16,2304]{2,1,0:T(8,128)(2,1)S(1)} %pack_factors.1.rest_0_.refs_0_), channel_id=1, source_target_pairs={{0,4},{4,0},{8,12},{12,8},{1,5},{5,1},{9,13},{13,9},{2,6},{6,2},{1... | collective-permute-start | bytes 442376 | tf_op jit(solution)/shard_map/ppermute | solution.py:411
  9.1 4.4 %cache_attention.1 = (bf16[4096,2,256]{2,1,0:T(2,128)(2,1)S(1)}, f32[64,128]{1,0:T(8,128)S(1)}, bf16[2,256]{1,0:T(2,128)(2,1)S(1)}, bf16[4,8,2048]{2,1,0:T(8,128...) custom-call(s32[8]{0:T(128)} %lengths_ref.1, ...), custom_call_target="tpu_custom_call" | custom-call | flops 140509184 | bytes 9437184 | tf_op jit(solution)/shard_map/cache_attention/pallas_call | solution.py:167
  13.5 0.0 collective-permute-done.rest_2_.refs_2_
  13.5 0.5 %collective-permute-start.5 = (bf16[2,16,2304]{2,1,0:T(8,128)(2,1)S(1)}, bf16[2,16,2304]{2,1,0:T(8,128)(2,1)S(1)}, u32[]{:S(2)}, u32[]{:S(2)}) collective-permute-start(bf16[2,16,2304]{2,1,0:T(8,128)(2,1)S(1)} %collective-permute-done.rest_2_.refs_2_), channel_id=1, source_target_pairs={{0,4},{4,0},{8,12},{12,8},{1,5},{5,1},{9,13},{13,9},{2,6},{6,2},{1... | collective-permute-start | bytes 442376 | tf_op jit(solution)/shard_map/ppermute | solution.py:411
  14.1 0.0 collective-permute-done.1.rest_1_
  14.1 0.0 collective-permute-done.2.rest_2_
  14.1 0.2 collective-permute-done.3.rest_3_
  14.2 2.4 %scale_features.1 = (bf16[32,8192]{1,0:T(8,128)(2,1)S(1)}, bf16[32,4096]{1,0:T(8,128)(2,1)S(1)}, bf16[32,4096]{1,0:T(8,128)(2,1)S(1)}, f32[32,128]{1,0:T(8,128)S(1)}, bf16[4096,2,256]{2,1,0:T(2,128)(2,1)S(1)}) custom-call(bf16[8192,2,256]{2,1,0:T(2,128)(2,1)} %weight_ref.3, f32[64,128]{1,0:T(8,128)S(1)} %get-tuple-element.28.gain_ref, ...), custom_call_target="tpu_custom_call" | custom-call | bytes 5242880 | tf_op jit(solution)/shard_map/scale_features/pallas_call | solution.py:290
  16.6 0.8 %fusion.4.near_ref = f32[2,32,256]{2,1,0:T(8,128)S(1)} fusion(bf16[4096,2,256]{2,1,0:T(2,128)(2,1)S(1)} %get-tuple-element.26, bf16[32,4096]{1,0:T(8,128)(2,1)S(1)} %get-tuple-element.30), kind=kOutput, calls=%fused_computation.4 | convolution fusion | flops 134217728 | bytes 4521984 | tf_op jit(solution)/shard_map/md,dkc->kmc/dot_general | solution.py:467
  17.4 0.0 collective-permute-done.4.rest_1_.refs_1_
  17.4 1.9 %collective-permute-done.5.rest_3_.refs_3_ = bf16[2,16,2304]{2,1,0:T(8,128)(2,1)S(1)} collective-permute-done((bf16[2,16,2304]{2,1,0:T(8,128)(2,1)S(1)}, bf16[2,16,2304]{2,1,0:T(8,128)(2,1)S(1)}, u32[]{:S(2)}, u32[]{:S(2)}) %collective-permute-start.5) | collective-permute-done | bytes 147488 | tf_op jit(solution)/shard_map/ppermute | solution.py:411
  19.4 0.3 %rank_inner.1.rest_6_ = f32[32,32]{1,0:T(8,128)S(1)} custom-call(bf16[32,8192]{1,0:T(8,128)(2,1)S(1)} %get-tuple-element.32.scaled_ref, bf16[2,16,2304]{2,1,0:T(8,128)(2,1)S(1)} %pack_factors.1.rest_0_.refs_0_, bf16[2,16,2304]{2,1,0:T(8,128)(2,1)S(1)} %collective-permute-done.4.rest_1_.refs_1_, ...), custom_call_target="tpu_custom_call" | custom-call | tf_op jit(solution)/shard_map/rank_inner/pallas_call | solution.py:251
  19.6 0.0 collective-permute-start.6
  19.6 1.6 %collective-permute-start.7 = (f32[32,32]{1,0:T(8,128)S(1)}, f32[32,32]{1,0:T(8,128)S(1)}, u32[]{:S(2)}, u32[]{:S(2)}) collective-permute-start(f32[32,32]{1,0:T(8,128)S(1)} %rank_inner.1.rest_6_), channel_id=1, source_target_pairs={{0,2},{1,3},{2,0},{3,1},{4,6},{5,7},{6,4},{7,5},{8,10},{9,11},{10,... | collective-permute-start | bytes 12296 | tf_op jit(solution)/shard_map/ppermute | solution.py:411
  21.2 0.3 %collective-permute-start.8 = (f32[32,32]{1,0:T(8,128)S(1)}, f32[32,32]{1,0:T(8,128)S(1)}, u32[]{:S(2)}, u32[]{:S(2)}) collective-permute-start(f32[32,32]{1,0:T(8,128)S(1)} %rank_inner.1.rest_6_), channel_id=1, source_target_pairs={{0,3},{1,2},{2,1},{3,0},{4,7},{5,6},{6,5},{7,4},{8,11},{9,10},{10,... | collective-permute-start | bytes 12296 | tf_op jit(solution)/shard_map/ppermute | solution.py:411
  21.5 0.8 %fusion.7.far_ref = f32[2,32,256]{2,1,0:T(8,128)S(1)} fusion(bf16[4096,2,256]{2,1,0:T(2,128)(2,1)S(1)} %get-tuple-element.31, bf16[32,4096]{1,0:T(8,128)(2,1)S(1)} %get-tuple-element.35), kind=kOutput, calls=%fused_computation.5 | convolution fusion | flops 134217728 | bytes 4521984 | tf_op jit(solution)/shard_map/md,dkc->kmc/dot_general | solution.py:467
  22.4 0.0 collective-permute-done.6.rest_7_
  22.4 1.1 %collective-permute-done.7.rest_8_ = f32[32,32]{1,0:T(8,128)S(1)} collective-permute-done((f32[32,32]{1,0:T(8,128)S(1)}, f32[32,32]{1,0:T(8,128)S(1)}, u32[]{:S(2)}, u32[]{:S(2)}) %collective-permute-start.7) | collective-permute-done | bytes 4128 | tf_op jit(solution)/shard_map/ppermute | solution.py:411
  23.5 0.9 %collective-permute-done.8.rest_9_ = f32[32,32]{1,0:T(8,128)S(1)} collective-permute-done((f32[32,32]{1,0:T(8,128)S(1)}, f32[32,32]{1,0:T(8,128)S(1)}, u32[]{:S(2)}, u32[]{:S(2)}) %collective-permute-start.8) | collective-permute-done | bytes 4128 | tf_op jit(solution)/shard_map/ppermute | solution.py:411
  24.4 1.5 %fresh_attention.1 = (bf16[4,8,256]{2,1,0:T(8,128)(2,1)}, bf16[4,8,256]{2,1,0:T(8,128)(2,1)}, bf16[4,8,2048]{2,1,0:T(8,128)(2,1)}) custom-call(f32[2,32,256]{2,1,0:T(8,128)S(1)} %fusion.4.near_ref, f32[2,32,256]{2,1,0:T(8,128)S(1)} %fusion.7.far_ref, f32[32,128]{1,0:T(8,128)S(1)} %get-tuple-element.36.square_ref, ...), custom_call_target="tpu_custom_call" | custom-call | tf_op jit(solution)/shard_map/fresh_attention/pallas_call | solution.py:399
  (1 shorter events, 0.0 us)
Async XLA Ops:
  1.6 12.0 %collective-permute-start = (bf16[2,16,2304]{2,1,0:T(8,128)(2,1)S(1)}, bf16[2,16,2304]{2,1,0:T(8,128)(2,1)S(1)}, u32[]{:S(2)}, u32[]{:S(2)}) collective-permute-start(bf16[2,16,2304]{2,1,0:T(8,128)(2,1)S(1)} %pack_factors.1.rest_0_.refs_0_), channel_id=1, source_target_pairs={{0,8},{4,12},{8,0},{12,4},{1,9},{5,13},{9,1},{13,5},{2,10},{6,14},... | collective-permute-start | bytes 442376 | tf_op jit(solution)/shard_map/ppermute | solution.py:411
  5.7 8.4 %collective-permute-start.1 = (bf16[4,8,2048]{2,1,0:T(8,128)(2,1)}, bf16[4,8,2048]{2,1,0:T(8,128)(2,1)S(1)}, u32[]{:S(2)}, u32[]{:S(2)}) collective-permute-start(bf16[4,8,2048]{2,1,0:T(8,128)(2,1)} %hidden_ref.1), channel_id=1, source_target_pairs={{0,1},{1,0},{2,3},{3,2},{4,5},{5,4},{6,7},{7,6},{8,9},{9,8},{10,11... | collective-permute-start | bytes 393224 | tf_op jit(solution)/shard_map/ppermute | solution.py:411
  5.7 8.4 %collective-permute-start.2 = (bf16[4,8,2048]{2,1,0:T(8,128)(2,1)}, bf16[4,8,2048]{2,1,0:T(8,128)(2,1)S(1)}, u32[]{:S(2)}, u32[]{:S(2)}) collective-permute-start(bf16[4,8,2048]{2,1,0:T(8,128)(2,1)} %hidden_ref.1), channel_id=1, source_target_pairs={{0,2},{1,3},{2,0},{3,1},{4,6},{5,7},{6,4},{7,5},{8,10},{9,11},{10,... | collective-permute-start | bytes 393224 | tf_op jit(solution)/shard_map/ppermute | solution.py:411
  7.2 7.0 %collective-permute-start.3 = (bf16[4,8,2048]{2,1,0:T(8,128)(2,1)}, bf16[4,8,2048]{2,1,0:T(8,128)(2,1)S(1)}, u32[]{:S(2)}, u32[]{:S(2)}) collective-permute-start(bf16[4,8,2048]{2,1,0:T(8,128)(2,1)} %hidden_ref.1), channel_id=1, source_target_pairs={{0,3},{1,2},{2,1},{3,0},{4,7},{5,6},{6,5},{7,4},{8,11},{9,10},{10,... | collective-permute-start | bytes 393224 | tf_op jit(solution)/shard_map/ppermute | solution.py:411
  7.5 9.9 %collective-permute-start.4 = (bf16[2,16,2304]{2,1,0:T(8,128)(2,1)S(1)}, bf16[2,16,2304]{2,1,0:T(8,128)(2,1)S(1)}, u32[]{:S(2)}, u32[]{:S(2)}) collective-permute-start(bf16[2,16,2304]{2,1,0:T(8,128)(2,1)S(1)} %pack_factors.1.rest_0_.refs_0_), channel_id=1, source_target_pairs={{0,4},{4,0},{8,12},{12,8},{1,5},{5,1},{9,13},{13,9},{2,6},{6,2},{1... | collective-permute-start | bytes 442376 | tf_op jit(solution)/shard_map/ppermute | solution.py:411
  13.5 5.8 %collective-permute-start.5 = (bf16[2,16,2304]{2,1,0:T(8,128)(2,1)S(1)}, bf16[2,16,2304]{2,1,0:T(8,128)(2,1)S(1)}, u32[]{:S(2)}, u32[]{:S(2)}) collective-permute-start(bf16[2,16,2304]{2,1,0:T(8,128)(2,1)S(1)} %collective-permute-done.rest_2_.refs_2_), channel_id=1, source_target_pairs={{0,4},{4,0},{8,12},{12,8},{1,5},{5,1},{9,13},{13,9},{2,6},{6,2},{1... | collective-permute-start | bytes 442376 | tf_op jit(solution)/shard_map/ppermute | solution.py:411
  19.6 2.8 %collective-permute-start.6 = (f32[32,32]{1,0:T(8,128)S(1)}, f32[32,32]{1,0:T(8,128)S(1)}, u32[]{:S(2)}, u32[]{:S(2)}) collective-permute-start(f32[32,32]{1,0:T(8,128)S(1)} %rank_inner.1.rest_6_), channel_id=1, source_target_pairs={{0,1},{1,0},{2,3},{3,2},{4,5},{5,4},{6,7},{7,6},{8,9},{9,8},{10,11... | collective-permute-start | bytes 12296 | tf_op jit(solution)/shard_map/ppermute | solution.py:411
  19.6 3.8 %collective-permute-start.7 = (f32[32,32]{1,0:T(8,128)S(1)}, f32[32,32]{1,0:T(8,128)S(1)}, u32[]{:S(2)}, u32[]{:S(2)}) collective-permute-start(f32[32,32]{1,0:T(8,128)S(1)} %rank_inner.1.rest_6_), channel_id=1, source_target_pairs={{0,2},{1,3},{2,0},{3,1},{4,6},{5,7},{6,4},{7,5},{8,10},{9,11},{10,... | collective-permute-start | bytes 12296 | tf_op jit(solution)/shard_map/ppermute | solution.py:411
  21.2 3.2 %collective-permute-start.8 = (f32[32,32]{1,0:T(8,128)S(1)}, f32[32,32]{1,0:T(8,128)S(1)}, u32[]{:S(2)}, u32[]{:S(2)}) collective-permute-start(f32[32,32]{1,0:T(8,128)S(1)} %rank_inner.1.rest_6_), channel_id=1, source_target_pairs={{0,3},{1,2},{2,1},{3,0},{4,7},{5,6},{6,5},{7,4},{8,11},{9,10},{10,... | collective-permute-start | bytes 12296 | tf_op jit(solution)/shard_map/ppermute | solution.py:411

commit v16 on v15

--- a/solution.py
+++ b/solution.py
@@ -46,7 +46,6 @@
 
 
 def cache_kernel(
-    near,
     lengths_ref,
     query_ref,
     key_ref,
@@ -54,8 +53,6 @@
     gain_ref,
     bias_ref,
     hidden_ref,
-    weight_ref,
-    near_out,
     gain_out,
     bias_out,
     hidden_out,
@@ -73,7 +70,6 @@
     value_buffer,
     score_buffer,
     sems,
-    weight_sems,
 ):
     steps, rows, query_width = query_ref.shape
     cache_span = key_ref.shape[1]
@@ -96,7 +92,6 @@
     copies = [pltpu.make_async_copy(*pair, sems.at[i]) for i, pair in enumerate(copies)]
     for copy in copies:
         copy.start()
-    copies += copy_blocks(near, hidden_ref.shape[2], weight_ref, near_out, weight_sems)
 
     copies[0].wait()
     lane = lax.broadcasted_iota(jnp.int32, (rows, HD), 1)
@@ -155,19 +150,17 @@
         copy.wait()
 
 
-def cache_call(near, lengths, queries, keys, values, gain, bias, hidden, weight):
+def cache_call(lengths, queries, keys, values, gain, bias, hidden):
     steps, rows, query_width = queries.shape
     cache_span, key_width = keys.shape[1:]
     groups = key_width // HD
     lines = steps * (query_width // key_width)
     block = (groups, lines * rows, HD)
     table = (steps * rows, HD)
-    operands = (lengths, queries, keys, values, gain, bias, hidden, weight)
-    part = hidden.shape[2]
+    operands = (lengths, queries, keys, values, gain, bias, hidden)
     return pl.pallas_call(
-        functools.partial(cache_kernel, near),
+        cache_kernel,
         out_shape=(
-            pltpu.VMEM((len(near) * part,) + weight.shape[1:], weight.dtype),
             pltpu.VMEM(gain.shape, jnp.float32),
             pltpu.VMEM(bias.shape, bias.dtype),
             pltpu.VMEM(hidden.shape, hidden.dtype),
@@ -180,7 +173,7 @@
             pltpu.VMEM(table, jnp.float32),
         ),
         in_specs=[HBM] * len(operands),
-        out_specs=(VMEM,) * 11,
+        out_specs=(VMEM,) * 10,
         scratch_shapes=[
             pltpu.SMEM(lengths.shape, jnp.int32),
             pltpu.VMEM(queries.shape, queries.dtype),
@@ -189,10 +182,9 @@
             pltpu.VMEM(values.shape, values.dtype),
             pltpu.VMEM((rows * groups, lines, cache_span), jnp.float32),
             pltpu.SemaphoreType.DMA((9,)),
-            pltpu.SemaphoreType.DMA((len(near),)),
         ],
         compiler_params=pltpu.CompilerParams(vmem_limit_bytes=16 << 20),
-        cost_estimate=pl.CostEstimate(flops=2 * 67 << 20, bytes_accessed=9 << 20, transcendentals=0),
+        cost_estimate=pl.CostEstimate(flops=2 * 67 << 20, bytes_accessed=5 << 20, transcendentals=0),
         name="cache_attention",
     )(*[pltpu.with_memory_space_constraint(x, pltpu.HBM) for x in operands])
 
@@ -229,80 +221,116 @@
     )(*[pltpu.with_memory_space_constraint(x, pltpu.HBM) for x in (down, up)])
 
 
-def inner_kernel(scaled_ref, *rest):
-    packs, out_ref = rest[:-1], rest[-1]
+def scaled_block(part, gain_ref, block):
+    steps, rows, width = part.shape
+    chunks = width // HD
+    gain = gain_ref[pl.ds(pl.multiple_of(block * chunks, chunks), chunks)]
+    values = rows_of(part)
+    squares = jnp.zeros((steps * rows, HD), jnp.float32)
+    scaled = []
+    for i in range(chunks):
+        chunk = values[:, i * HD : (i + 1) * HD]
+        squares += chunk * chunk
+        scaled.append((chunk * gain[i : i + 1]).astype(jnp.bfloat16))
+    return jnp.concatenate(scaled, axis=1), squares
+
+
+def scale_kernel(near, far, weight_ref, gain_ref, *rest):
+    scaled_out, near_out, far_out, square_out, near_weight, far_weight, near_sems, far_sems = rest[-8:]
+    parts = rest[:-8]
+    width = parts[0].shape[2]
+    copies = copy_blocks(near, width, weight_ref, near_weight, near_sems)
+    copies += copy_blocks(far, width, weight_ref, far_weight, far_sems)
+    me = lax.axis_index("tp")
+    offsets = near + far
+    total = None
+    for k, part in enumerate(parts):
+        block = me ^ offsets[k]
+        scaled, squares = scaled_block(part, gain_ref, block)
+        total = squares if total is None else total + squares
+        scaled_out[:, pl.ds(pl.multiple_of(block * width, width), width)] = scaled
+        if k < len(near):
+            near_out[:, k * width : (k + 1) * width] = scaled
+        else:
+            i = k - len(near)
+            far_out[:, i * width : (i + 1) * width] = scaled
+    at = pl.ds(pl.multiple_of((me ^ offsets[-1]) * width, width), width)
+    scaled_out[:, at] = jnp.zeros_like(scaled)
+    square_out[...] = total
+    for copy in copies:
+        copy.wait()
+
+
+def scale_call(near, far, weight, gain, parts):
+    steps, rows, width = parts[0].shape
+    count = steps * rows
+    return pl.pallas_call(
+        functools.partial(scale_kernel, near, far),
+        out_shape=(
+            pltpu.VMEM((count, (len(near) + len(far)) * width), jnp.bfloat16),
+            pltpu.VMEM((count, len(near) * width), jnp.bfloat16),
+            pltpu.VMEM((count, (len(far) - 1) * width), jnp.bfloat16),
+            pltpu.VMEM((count, HD), jnp.float32),
+            pltpu.VMEM((len(near) * width,) + weight.shape[1:], weight.dtype),
+            pltpu.VMEM((len(far) * width,) + weight.shape[1:], weight.dtype),
+        ),
+        in_specs=[HBM] + [VMEM] * (1 + len(parts)),
+        out_specs=(VMEM,) * 6,
+        scratch_shapes=[
+            pltpu.SemaphoreType.DMA((len(near),)),
+            pltpu.SemaphoreType.DMA((len(far),)),
+        ],
+        compiler_params=pltpu.CompilerParams(vmem_limit_bytes=8 << 20),
+        cost_estimate=pl.CostEstimate(flops=0, bytes_accessed=9 << 20, transcendentals=0),
+        name="scale_features",
+    )(pltpu.with_memory_space_constraint(weight, pltpu.HBM), gain, *parts)
+
+
+def inner_kernel(last, scaled_ref, far_ref, square_ref, gain_ref, part_ref, *rest):
+    far_out, square_out = rest[-2:]
+    packs, inner_out = (rest[:-3], rest[-3]) if len(rest) > 2 else ((), None)
+    block = lax.axis_index("tp") ^ last
+    late, squares = scaled_block(part_ref, gain_ref, block)
+    width = late.shape[1]
+    far_out[:, : far_ref.shape[1]] = far_ref[...]
+    far_out[:, far_ref.shape[1] :] = late
+    squares = jnp.sum(squares + square_ref[...], axis=1, keepdims=True)
+    square_out[...] = jnp.broadcast_to(squares, square_out.shape)
+    if not packs:
+        return
     me = lax.axis_index("wide")
-    width = scaled_ref.shape[1] // len(packs)
     total = []
     for offset, pack in enumerate(packs):
+        mine = me ^ offset
+        early = scaled_ref[:, pl.ds(pl.multiple_of(mine * width, width), width)]
         total.append(
             lax.dot_general(
-                scaled_ref[:, pl.ds(pl.multiple_of((me ^ offset) * width, width), width)],
-                pack[:, :, :width].reshape(out_ref.shape[1], width),
+                jnp.where(mine == block, late, early),
+                pack[:, :, :width].reshape(inner_out.shape[1], width),
                 (((1,), (1,)), ((), ())),
                 preferred_element_type=jnp.float32,
             )
         )
-    out_ref[...] = sum(total[1:], total[0])
-
-
-def inner_call(scaled, packs):
-    kinds, share, _ = packs[0].shape
+    inner_out[...] = sum(total[1:], total[0])
+
+
+def inner_call(last, scaled, far, square, gain, part, packs):
+    count, width = far.shape[0], part.shape[2]
+    shapes = [
+        pltpu.VMEM((count, far.shape[1] + width), far.dtype),
+        pltpu.VMEM(square.shape, jnp.float32),
+    ]
+    if packs:
+        kinds, share, _ = packs[0].shape
+        shapes = [pltpu.VMEM((count, kinds * share), jnp.float32)] + shapes
     return pl.pallas_call(
-        inner_kernel,
-        out_shape=jax.ShapeDtypeStruct((scaled.shape[0], kinds * share), jnp.float32),
-        in_specs=[VMEM] * (1 + len(packs)),
-        out_specs=VMEM,
+        functools.partial(inner_kernel, last),
+        out_shape=tuple(shapes),
+        in_specs=[VMEM] * (5 + len(packs)),
+        out_specs=(VMEM,) * len(shapes),
         compiler_params=pltpu.CompilerParams(vmem_limit_bytes=8 << 20),
         name="rank_inner",
-    )(scaled, *packs)
-
-
-def scale_kernel(near, far, weight_ref, gain_ref, *rest):
-    parts = rest[:-6]
-    scaled_out, near_out, far_out, square_out, weight_out, sems = rest[-6:]
-    steps, rows, width = parts[0].shape
-    chunks = width // HD
-    copies = copy_blocks(far, width, weight_ref, weight_out, sems)
-    me = lax.axis_index("tp")
-    squares = jnp.zeros(square_out.shape, jnp.float32)
-    for k, (offset, part) in enumerate(zip(near + far, parts)):
-        block = me ^ offset
-        gain = gain_ref[pl.ds(pl.multiple_of(block * chunks, chunks), chunks)]
-        values = rows_of(part)
-        scaled = []
-        for i in range(chunks):
-            chunk = values[:, i * HD : (i + 1) * HD]
-            squares += chunk * chunk
-            scaled.append((chunk * gain[i : i + 1]).astype(jnp.bfloat16))
-        at = pl.ds(pl.multiple_of(block * width, width), width)
-        scaled = jnp.concatenate(scaled, axis=1)
-        scaled_out[:, at] = scaled
-        out, i = (near_out, k) if k < len(near) else (far_out, k - len(near))
-        out[:, i * width : (i + 1) * width] = scaled
-    square_out[...] = jnp.broadcast_to(jnp.sum(squares, axis=1, keepdims=True), squares.shape)
-    for copy in copies:
-        copy.wait()
-
-
-def scale_call(near, far, weight, gain, parts):
-    steps, rows, width = parts[0].shape
-    return pl.pallas_call(
-        functools.partial(scale_kernel, near, far),
-        out_shape=(
-            pltpu.VMEM((steps * rows, len(parts) * width), jnp.bfloat16),
-            pltpu.VMEM((steps * rows, len(near) * width), jnp.bfloat16),
-            pltpu.VMEM((steps * rows, len(far) * width), jnp.bfloat16),
-            pltpu.VMEM((steps * rows, HD), jnp.float32),
-            pltpu.VMEM((len(far) * width,) + weight.shape[1:], weight.dtype),
-        ),
-        in_specs=[HBM] + [VMEM] * (1 + len(parts)),
-        out_specs=(VMEM,) * 5,
-        scratch_shapes=[pltpu.SemaphoreType.DMA((len(far),))],
-        compiler_params=pltpu.CompilerParams(vmem_limit_bytes=8 << 20),
-        cost_estimate=pl.CostEstimate(flops=0, bytes_accessed=5 << 20, transcendentals=0),
-        name="scale_features",
-    )(pltpu.with_memory_space_constraint(weight, pltpu.HBM), gain, *parts)
+    )(scaled, far, square, gain, part, *packs)
 
 
 def up_kernel(*refs):
@@ -407,6 +435,10 @@
     )(near, far, square, bias, *cached, *inner, up)
 
 
+def dot(rows, weight):
+    return jnp.einsum("md,dkc->kmc", rows, weight, preferred_element_type=jnp.float32)
+
+
 def swap(block, axis, offset, count):
     return lax.ppermute(block, axis, [(i, i ^ offset) for i in range(count)])
 
@@ -437,36 +469,34 @@
         second = swap(pack, "wide", 2, wide_count)
         first = swap(pack, "wide", 1, wide_count)
     near, far = (0, 1), (2, 3)
-    near_weight, gain_rows, bias, mine, _, *cached = cache_call(
-        near,
-        lengths,
-        queries,
-        stored_rotated_keys,
-        stored_value_rows,
-        gain,
-        key_value_bias,
-        hidden,
-        key_value_weight,
+    gain_rows, bias, mine, _, *cached = cache_call(
+        lengths, queries, stored_rotated_keys, stored_value_rows, gain, key_value_bias, hidden
     )
     if direct:
         third, gain_rows = lax.optimization_barrier((second, gain_rows))
         packs = [pack, first, second, swap(third, "wide", 1, wide_count)]
-    scaled, near_scaled, far_scaled, square, far_weight = scale_call(
-        near, far, key_value_weight, gain_rows, [mine] + tp_parts
-    )
+    scaled, near_scaled, far_scaled, square, near_weight, far_weight = scale_call(
+        near, far, key_value_weight, gain_rows, [mine] + tp_parts[:2]
+    )
+    near_base = dot(near_scaled, near_weight)
     if direct:
-        inner = inner_call(scaled, packs)
+        scaled, near_base = lax.optimization_barrier((scaled, near_base))
+        inner, far_scaled, square = inner_call(
+            far[-1], scaled, far_scaled, square, gain_rows, tp_parts[2], packs
+        )
         inner, far_scaled, packs = lax.optimization_barrier((inner, far_scaled, packs))
         inner = [inner] + [swap(inner, "tp", offset, tp_count) for offset in (1, 2, 3)]
     else:
+        far_scaled, square = inner_call(
+            far[-1], scaled, far_scaled, square, gain_rows, tp_parts[2], []
+        )
         down = lax.all_gather(adapter_down_factor, "wide", axis=2, tiled=True)
-        down = down.reshape(kinds * ranks, width)
-        inner = [jnp.einsum("rd,kd->rk", scaled, down, preferred_element_type=jnp.float32)]
+        rows_full = lax.all_gather(hidden, "tp", axis=2, tiled=True).astype(jnp.float32)
+        rows_full = (rows_full * input_norm_gain.astype(jnp.float32)).astype(jnp.bfloat16)
+        inner = jnp.einsum("srd,kad->srka", rows_full, down, preferred_element_type=jnp.float32)
+        inner = [inner.reshape(steps * rows, kinds * ranks)]
         packs = [lax.all_gather(up_part, "wide", axis=1, tiled=True)]
-    near_base, far_base = [
-        jnp.einsum("md,dkc->kmc", x, y, preferred_element_type=jnp.float32)
-        for x, y in ((near_scaled, near_weight), (far_scaled, far_weight))
-    ]
+    far_base = dot(far_scaled, far_weight)
     up = up_call(packs, bias.shape[1])
     return final_call(
         queries.shape, width, near_base, far_base, square, bias, cached, inner, up

time: 26.1 us -> 25.8 us (0.989)
  waiting for transfers between devices: 4.07 us -> 3.36 us
  Pallas kernels: 9.56 us -> 10.1 us
    pallas_call x1, Pallas kernels: 2.37 us -> 3.52 us  [scale_call(): pl.pallas_call(functools.partial(scale_kernel, near, far), out_shape=(plt...]
    ppermute x9, waiting for transfers between devices: 4.07 us -> 3.36 us  [swap(): return lax.ppermute(block, axis, [(i, i ^ offset) for i in range(count)])]
    pallas_call x2, Pallas kernels: 4.68 us -> 4.04 us  [the longest x1 3.75 us: cache_call(): pl.pallas_call(cache_kernel, out_shape=(pltpu.VMEM(gain.shape, jnp.float3...]
  transfers between devices with their start and end apart: 9 -> 9, of which waited for: 4 -> 4; matrix products, arithmetic and copies ran while one was open for 6% -> 6% of each run, Pallas kernels for 26% -> 28%
where the time goes in v16:
time: 25.8 us; the launch traced here: 25.6 us
  Pallas kernels  10.1 us (39%)
  starting transfers between devices  9.84 us (38%)
  waiting for transfers between devices  3.36 us (13%)
  matrix products  1.64 us (6%)
  between operations  0.7 us (3%)
    ppermute x9, starting transfers between devices, swap(): return lax.ppermute(block, axis, [(i, i ^ offset) for i in range(count)])  9.84 us
    pallas_call x1, Pallas kernels, cache_call(): pl.pallas_call(cache_kernel, out_shape=(pltpu.VMEM(gain.shape, jnp.float3...  3.75 us
    pallas_call x1, Pallas kernels, scale_call(): pl.pallas_call(functools.partial(scale_kernel, near, far), out_shape=(plt...  3.52 us
    ppermute x9, waiting for transfers between devices, swap(): return lax.ppermute(block, axis, [(i, i ^ offset) for i in range(count)])  3.36 us
    dot_general x2, matrix products, dot(): jnp.einsum('md,dkc->kmc', rows, weight, preferred_element_type=jnp.float32)  1.64 us
    pallas_call x1, Pallas kernels, final_call(): pl.pallas_call(functools.partial(final_kernel, width, len(inner)), out_sh...  1.54 us
    pallas_call x1, Pallas kernels, pack_call(): pl.pallas_call(pack_kernel, out_shape=pltpu.VMEM((kinds, share, down.shap...  0.93 us
  transfers between devices with their start and end apart: 9, of which 4 were waited for; matrix products, arithmetic and copies ran while one was open for 6% of the time, Pallas kernels for 28%

profile of v16, /device:TPU:0, one launch (start us, length us, event | category | flops | bytes accessed | tf_op | source)
XLA Modules:
  0.0 25.6 jit_solution(15595182037294506784)
XLA Ops:
  0.6 0.9 %pack_factors.1.rest_0_.refs_0_ = bf16[2,16,2304]{2,1,0:T(8,128)(2,1)S(1)} custom-call(bf16[2,64,2048]{2,1,0:T(8,128)(2,1)} %down_ref.1, bf16[2,16,256]{2,1,0:T(8,128)(2,1)} %bitcast.13), custom_call_target="tpu_custom_call" | custom-call | tf_op jit(solution)/shard_map/pack_factors/pallas_call | solution.py:214
  1.6 4.1 %collective-permute-start = (bf16[2,16,2304]{2,1,0:T(8,128)(2,1)S(1)}, bf16[2,16,2304]{2,1,0:T(8,128)(2,1)S(1)}, u32[]{:S(2)}, u32[]{:S(2)}) collective-permute-start(bf16[2,16,2304]{2,1,0:T(8,128)(2,1)S(1)} %pack_factors.1.rest_0_.refs_0_), channel_id=1, source_target_pairs={{0,8},{4,12},{8,0},{12,4},{1,9},{5,13},{9,1},{13,5},{2,10},{6,14},... | collective-permute-start | bytes 442376 | tf_op jit(solution)/shard_map/ppermute | solution.py:443
  5.7 0.0 collective-permute-start.1
  5.7 1.5 %collective-permute-start.2 = (bf16[4,8,2048]{2,1,0:T(8,128)(2,1)}, bf16[4,8,2048]{2,1,0:T(8,128)(2,1)S(1)}, u32[]{:S(2)}, u32[]{:S(2)}) collective-permute-start(bf16[4,8,2048]{2,1,0:T(8,128)(2,1)} %hidden_ref.1), channel_id=1, source_target_pairs={{0,2},{1,3},{2,0},{3,1},{4,6},{5,7},{6,4},{7,5},{8,10},{9,11},{10,... | collective-permute-start | bytes 393224 | tf_op jit(solution)/shard_map/ppermute | solution.py:443
  7.2 1.6 %collective-permute-start.4 = (bf16[2,16,2304]{2,1,0:T(8,128)(2,1)S(1)}, bf16[2,16,2304]{2,1,0:T(8,128)(2,1)S(1)}, u32[]{:S(2)}, u32[]{:S(2)}) collective-permute-start(bf16[2,16,2304]{2,1,0:T(8,128)(2,1)S(1)} %pack_factors.1.rest_0_.refs_0_), channel_id=1, source_target_pairs={{0,4},{4,0},{8,12},{12,8},{1,5},{5,1},{9,13},{13,9},{2,6},{6,2},{1... | collective-permute-start | bytes 442376 | tf_op jit(solution)/shard_map/ppermute | solution.py:443
  8.7 0.1 collective-permute-start.3
  8.8 3.7 %cache_attention.1 = (f32[64,128]{1,0:T(8,128)S(1)}, bf16[2,256]{1,0:T(2,128)(2,1)S(1)}, bf16[4,8,2048]{2,1,0:T(8,128)(2,1)S(1)}, f32[2,256,128]{2,1,0:T(8,128)}...) custom-call(s32[8]{0:T(128)} %lengths_ref.1, ...), custom_call_target="tpu_custom_call" | custom-call | flops 140509184 | bytes 5242880 | tf_op jit(solution)/shard_map/cache_attention/pallas_call | solution.py:161
  12.6 0.2 collective-permute-done.rest_2_.refs_2_
  12.8 0.7 %collective-permute-start.5 = (bf16[2,16,2304]{2,1,0:T(8,128)(2,1)S(1)}, bf16[2,16,2304]{2,1,0:T(8,128)(2,1)S(1)}, u32[]{:S(2)}, u32[]{:S(2)}) collective-permute-start(bf16[2,16,2304]{2,1,0:T(8,128)(2,1)S(1)} %collective-permute-done.rest_2_.refs_2_), channel_id=1, source_target_pairs={{0,4},{4,0},{8,12},{12,8},{1,5},{5,1},{9,13},{13,9},{2,6},{6,2},{1... | collective-permute-start | bytes 442376 | tf_op jit(solution)/shard_map/ppermute | solution.py:443
  13.4 0.0 collective-permute-done.1.rest_1_
  13.4 0.0 collective-permute-done.2.rest_2_
  13.5 3.5 %scale_features.1 = (bf16[32,8192]{1,0:T(8,128)(2,1)S(1)}, bf16[32,4096]{1,0:T(8,128)(2,1)S(1)}, bf16[32,2048]{1,0:T(8,128)(2,1)S(1)}, f32[32,128]{1,0:T(8,128)S...) custom-call(bf16[8192,2,256]{2,1,0:T(2,128)(2,1)} %weight_ref.1, ...), custom_call_target="tpu_custom_call" | custom-call | bytes 9437184 | tf_op jit(solution)/shard_map/scale_features/pallas_call | solution.py:267
  17.0 0.8 %fusion.4.near_ref = f32[2,32,256]{2,1,0:T(8,128)S(1)} fusion(bf16[4096,2,256]{2,1,0:T(2,128)(2,1)S(1)} %get-tuple-element.35, bf16[32,4096]{1,0:T(8,128)(2,1)S(1)} %get-tuple-element.36), kind=kOutput, calls=%fused_computation.4 | convolution fusion | flops 134217728 | bytes 4521984 | tf_op jit(solution)/shard_map/md,dkc->kmc/dot_general | solution.py:439
  17.8 0.0 collective-permute-done.3.part_ref
  17.8 0.0 collective-permute-done.4.rest_1_.refs_1_
  17.8 1.2 %collective-permute-done.5.rest_3_.refs_3_ = bf16[2,16,2304]{2,1,0:T(8,128)(2,1)S(1)} collective-permute-done((bf16[2,16,2304]{2,1,0:T(8,128)(2,1)S(1)}, bf16[2,16,2304]{2,1,0:T(8,128)(2,1)S(1)}, u32[]{:S(2)}, u32[]{:S(2)}) %collective-permute-start.5) | collective-permute-done | bytes 147488 | tf_op jit(solution)/shard_map/ppermute | solution.py:443
  19.0 0.3 %rank_inner.1 = (f32[32,32]{1,0:T(8,128)S(1)}, bf16[32,4096]{1,0:T(8,128)(2,1)S(1)}, f32[32,128]{1,0:T(8,128)S(1)}) custom-call(bf16[32,8192]{1,0:T(8,128)(2,1)S(1)} %get-tuple-element.39.scaled_ref, bf16[32,2048]{1,0:T(8,128)(2,1)S(1)} %get-tuple-element.40.far_ref, f32[32,128]{1,0:T(8,128)S(1)} %get-tuple-element.41.square_ref, ...), custom_call_target="tpu_custom_call" | custom-call | tf_op jit(solution)/shard_map/rank_inner/pallas_call | solution.py:326
  19.3 0.1 collective-permute-start.6
  19.3 1.6 %collective-permute-start.7 = (f32[32,32]{1,0:T(8,128)S(1)}, f32[32,32]{1,0:T(8,128)S(1)}, u32[]{:S(2)}, u32[]{:S(2)}) collective-permute-start(f32[32,32]{1,0:T(8,128)S(1)} %get-tuple-element.54.rest_6_), channel_id=1, source_target_pairs={{0,2},{1,3},{2,0},{3,1},{4,6},{5,7},{6,4},{7,5},{8,10},{9,11},{10,... | collective-permute-start | bytes 12296 | tf_op jit(solution)/shard_map/ppermute | solution.py:443
  20.9 0.3 %collective-permute-start.8 = (f32[32,32]{1,0:T(8,128)S(1)}, f32[32,32]{1,0:T(8,128)S(1)}, u32[]{:S(2)}, u32[]{:S(2)}) collective-permute-start(f32[32,32]{1,0:T(8,128)S(1)} %get-tuple-element.54.rest_6_), channel_id=1, source_target_pairs={{0,3},{1,2},{2,1},{3,0},{4,7},{5,6},{6,5},{7,4},{8,11},{9,10},{10,... | collective-permute-start | bytes 12296 | tf_op jit(solution)/shard_map/ppermute | solution.py:443
  21.2 0.8 %fusion.7.far_ref = f32[2,32,256]{2,1,0:T(8,128)S(1)} fusion(bf16[4096,2,256]{2,1,0:T(2,128)(2,1)S(1)} %get-tuple-element.38, bf16[32,4096]{1,0:T(8,128)(2,1)S(1)} %get-tuple-element.45), kind=kOutput, calls=%fused_computation.5 | convolution fusion | flops 134217728 | bytes 4521984 | tf_op jit(solution)/shard_map/md,dkc->kmc/dot_general | solution.py:439
  22.1 0.0 collective-permute-done.6.rest_7_
  22.1 1.1 %collective-permute-done.7.rest_8_ = f32[32,32]{1,0:T(8,128)S(1)} collective-permute-done((f32[32,32]{1,0:T(8,128)S(1)}, f32[32,32]{1,0:T(8,128)S(1)}, u32[]{:S(2)}, u32[]{:S(2)}) %collective-permute-start.7) | collective-permute-done | bytes 4128 | tf_op jit(solution)/shard_map/ppermute | solution.py:443
  23.1 0.9 %collective-permute-done.8.rest_9_ = f32[32,32]{1,0:T(8,128)S(1)} collective-permute-done((f32[32,32]{1,0:T(8,128)S(1)}, f32[32,32]{1,0:T(8,128)S(1)}, u32[]{:S(2)}, u32[]{:S(2)}) %collective-permute-start.8) | collective-permute-done | bytes 4128 | tf_op jit(solution)/shard_map/ppermute | solution.py:443
  24.1 1.5 %fresh_attention.1 = (bf16[4,8,256]{2,1,0:T(8,128)(2,1)}, bf16[4,8,256]{2,1,0:T(8,128)(2,1)}, bf16[4,8,2048]{2,1,0:T(8,128)(2,1)}) custom-call(f32[2,32,256]{2,1,0:T(8,128)S(1)} %fusion.4.near_ref, f32[2,32,256]{2,1,0:T(8,128)S(1)} %fusion.7.far_ref, f32[32,128]{1,0:T(8,128)S(1)} %get-tuple-element.46.square_ref, ...), custom_call_target="tpu_custom_call" | custom-call | tf_op jit(solution)/shard_map/fresh_attention/pallas_call | solution.py:427
  (1 shorter events, 0.0 us)
Async XLA Ops:
  1.6 11.2 %collective-permute-start = (bf16[2,16,2304]{2,1,0:T(8,128)(2,1)S(1)}, bf16[2,16,2304]{2,1,0:T(8,128)(2,1)S(1)}, u32[]{:S(2)}, u32[]{:S(2)}) collective-permute-start(bf16[2,16,2304]{2,1,0:T(8,128)(2,1)S(1)} %pack_factors.1.rest_0_.refs_0_), channel_id=1, source_target_pairs={{0,8},{4,12},{8,0},{12,4},{1,9},{5,13},{9,1},{13,5},{2,10},{6,14},... | collective-permute-start | bytes 442376 | tf_op jit(solution)/shard_map/ppermute | solution.py:443
  5.7 7.8 %collective-permute-start.1 = (bf16[4,8,2048]{2,1,0:T(8,128)(2,1)}, bf16[4,8,2048]{2,1,0:T(8,128)(2,1)S(1)}, u32[]{:S(2)}, u32[]{:S(2)}) collective-permute-start(bf16[4,8,2048]{2,1,0:T(8,128)(2,1)} %hidden_ref.1), channel_id=1, source_target_pairs={{0,1},{1,0},{2,3},{3,2},{4,5},{5,4},{6,7},{7,6},{8,9},{9,8},{10,11... | collective-permute-start | bytes 393224 | tf_op jit(solution)/shard_map/ppermute | solution.py:443
  5.7 7.8 %collective-permute-start.2 = (bf16[4,8,2048]{2,1,0:T(8,128)(2,1)}, bf16[4,8,2048]{2,1,0:T(8,128)(2,1)S(1)}, u32[]{:S(2)}, u32[]{:S(2)}) collective-permute-start(bf16[4,8,2048]{2,1,0:T(8,128)(2,1)} %hidden_ref.1), channel_id=1, source_target_pairs={{0,2},{1,3},{2,0},{3,1},{4,6},{5,7},{6,4},{7,5},{8,10},{9,11},{10,... | collective-permute-start | bytes 393224 | tf_op jit(solution)/shard_map/ppermute | solution.py:443
  7.2 10.6 %collective-permute-start.4 = (bf16[2,16,2304]{2,1,0:T(8,128)(2,1)S(1)}, bf16[2,16,2304]{2,1,0:T(8,128)(2,1)S(1)}, u32[]{:S(2)}, u32[]{:S(2)}) collective-permute-start(bf16[2,16,2304]{2,1,0:T(8,128)(2,1)S(1)} %pack_factors.1.rest_0_.refs_0_), channel_id=1, source_target_pairs={{0,4},{4,0},{8,12},{12,8},{1,5},{5,1},{9,13},{13,9},{2,6},{6,2},{1... | collective-permute-start | bytes 442376 | tf_op jit(solution)/shard_map/ppermute | solution.py:443
  8.7 9.1 %collective-permute-start.3 = (bf16[4,8,2048]{2,1,0:T(8,128)(2,1)}, bf16[4,8,2048]{2,1,0:T(8,128)(2,1)S(1)}, u32[]{:S(2)}, u32[]{:S(2)}) collective-permute-start(bf16[4,8,2048]{2,1,0:T(8,128)(2,1)} %hidden_ref.1), channel_id=1, source_target_pairs={{0,3},{1,2},{2,1},{3,0},{4,7},{5,6},{6,5},{7,4},{8,11},{9,10},{10,... | collective-permute-start | bytes 393224 | tf_op jit(solution)/shard_map/ppermute | solution.py:443
  12.8 6.2 %collective-permute-start.5 = (bf16[2,16,2304]{2,1,0:T(8,128)(2,1)S(1)}, bf16[2,16,2304]{2,1,0:T(8,128)(2,1)S(1)}, u32[]{:S(2)}, u32[]{:S(2)}) collective-permute-start(bf16[2,16,2304]{2,1,0:T(8,128)(2,1)S(1)} %collective-permute-done.rest_2_.refs_2_), channel_id=1, source_target_pairs={{0,4},{4,0},{8,12},{12,8},{1,5},{5,1},{9,13},{13,9},{2,6},{6,2},{1... | collective-permute-start | bytes 442376 | tf_op jit(solution)/shard_map/ppermute | solution.py:443
  19.3 2.8 %collective-permute-start.6 = (f32[32,32]{1,0:T(8,128)S(1)}, f32[32,32]{1,0:T(8,128)S(1)}, u32[]{:S(2)}, u32[]{:S(2)}) collective-permute-start(f32[32,32]{1,0:T(8,128)S(1)} %get-tuple-element.54.rest_6_), channel_id=1, source_target_pairs={{0,1},{1,0},{2,3},{3,2},{4,5},{5,4},{6,7},{7,6},{8,9},{9,8},{10,11... | collective-permute-start | bytes 12296 | tf_op jit(solution)/shard_map/ppermute | solution.py:443
  19.3 3.8 %collective-permute-start.7 = (f32[32,32]{1,0:T(8,128)S(1)}, f32[32,32]{1,0:T(8,128)S(1)}, u32[]{:S(2)}, u32[]{:S(2)}) collective-permute-start(f32[32,32]{1,0:T(8,128)S(1)} %get-tuple-element.54.rest_6_), channel_id=1, source_target_pairs={{0,2},{1,3},{2,0},{3,1},{4,6},{5,7},{6,4},{7,5},{8,10},{9,11},{10,... | collective-permute-start | bytes 12296 | tf_op jit(solution)/shard_map/ppermute | solution.py:443
  20.9 3.2 %collective-permute-start.8 = (f32[32,32]{1,0:T(8,128)S(1)}, f32[32,32]{1,0:T(8,128)S(1)}, u32[]{:S(2)}, u32[]{:S(2)}) collective-permute-start(f32[32,32]{1,0:T(8,128)S(1)} %get-tuple-element.54.rest_6_), channel_id=1, source_target_pairs={{0,3},{1,2},{2,1},{3,0},{4,7},{5,6},{6,5},{7,4},{8,11},{9,10},{10,... | collective-permute-start | bytes 12296 | tf_op jit(solution)/shard_map/ppermute | solution.py:443

commit v17 on v16

--- a/solution.py
+++ b/solution.py
@@ -56,13 +56,10 @@
     gain_out,
     bias_out,
     hidden_out,
-    query_rows,
     query_out,
     acc_out,
     top_out,
     total_out,
-    cos_out,
-    sin_out,
     lengths,
     queries,
     gain_buffer,
@@ -94,31 +91,16 @@
         copy.start()
 
     copies[0].wait()
-    lane = lax.broadcasted_iota(jnp.int32, (rows, HD), 1)
-    half = HD // 2
-    second = lane >= half
-    index = jnp.where(second, lane - half, lane).astype(jnp.float32)
-    inv_freq = jnp.exp(index * (-2.0 * math.log(rope_base) / HD))
-    row_index = lax.broadcasted_iota(jnp.int32, (rows, HD), 0)
-    row_lengths = jnp.zeros((rows, HD), jnp.int32)
-    for row in range(rows):
-        row_lengths = jnp.where(row_index == row, lengths[row], row_lengths)
-    for step in range(steps):
-        angles = (row_lengths + step).astype(jnp.float32) * inv_freq
-        sine = jnp.sin(angles)
-        cos_out[pl.ds(step * rows, rows)] = jnp.cos(angles)
-        sin_out[pl.ds(step * rows, rows)] = jnp.where(second, sine, -sine)
     copies[1].wait()
     for group in range(groups):
-        query_rows[group] = query_block(queries, group, per_group)
-        query_out[group] = query_rows[group].astype(jnp.bfloat16)
+        query_out[group] = query_block(queries, group, per_group)
 
     place = lax.broadcasted_iota(jnp.int32, (lines, cache_span), 1)
     for i in range(2):
         copies[2 + i].wait()
         for row in range(i * half_rows, (i + 1) * half_rows):
             for group in range(groups):
-                query = query_rows[group, pl.ds(row, lines, stride=rows), :].astype(jnp.bfloat16)
+                query = query_out[group, pl.ds(row, lines, stride=rows), :].astype(jnp.bfloat16)
                 score_buffer[row * groups + group] = lax.dot_general(
                     query,
                     key_buffer[row, :, pl.ds(group * HD, HD)],
@@ -156,7 +138,6 @@
     groups = key_width // HD
     lines = steps * (query_width // key_width)
     block = (groups, lines * rows, HD)
-    table = (steps * rows, HD)
     operands = (lengths, queries, keys, values, gain, bias, hidden)
     return pl.pallas_call(
         cache_kernel,
@@ -165,15 +146,12 @@
             pltpu.VMEM(bias.shape, bias.dtype),
             pltpu.VMEM(hidden.shape, hidden.dtype),
             pltpu.VMEM(block, jnp.float32),
-            pltpu.VMEM(block, jnp.bfloat16),
             pltpu.VMEM(block, jnp.float32),
             pltpu.VMEM(block, jnp.float32),
             pltpu.VMEM(block, jnp.float32),
-            pltpu.VMEM(table, jnp.float32),
-            pltpu.VMEM(table, jnp.float32),
         ),
         in_specs=[HBM] * len(operands),
-        out_specs=(VMEM,) * 10,
+        out_specs=(VMEM,) * 7,
         scratch_shapes=[
             pltpu.SMEM(lengths.shape, jnp.int32),
             pltpu.VMEM(queries.shape, queries.dtype),
@@ -235,10 +213,30 @@
     return jnp.concatenate(scaled, axis=1), squares
 
 
-def scale_kernel(near, far, weight_ref, gain_ref, *rest):
-    scaled_out, near_out, far_out, square_out, near_weight, far_weight, near_sems, far_sems = rest[-8:]
-    parts = rest[:-8]
-    width = parts[0].shape[2]
+def rotation_tables(lengths, steps, rows, cos_out, sin_out):
+    lane = lax.broadcasted_iota(jnp.int32, (rows, HD), 1)
+    half = HD // 2
+    second = lane >= half
+    index = jnp.where(second, lane - half, lane).astype(jnp.float32)
+    inv_freq = jnp.exp(index * (-2.0 * math.log(rope_base) / HD))
+    row_index = lax.broadcasted_iota(jnp.int32, (rows, HD), 0)
+    row_lengths = jnp.zeros((rows, HD), jnp.int32)
+    for row in range(rows):
+        row_lengths = jnp.where(row_index == row, lengths[row], row_lengths)
+    for step in range(steps):
+        angles = (row_lengths + step).astype(jnp.float32) * inv_freq
+        sine = jnp.sin(angles)
+        cos_out[pl.ds(step * rows, rows)] = jnp.cos(angles)
+        sin_out[pl.ds(step * rows, rows)] = jnp.where(second, sine, -sine)
+
+
+def scale_kernel(near, far, lengths_ref, weight_ref, gain_ref, *rest):
+    scaled_out, near_out, far_out, square_out, near_weight, far_weight, cos_out, sin_out = rest[-12:-4]
+    lengths, length_sem, near_sems, far_sems = rest[-4:]
+    parts = rest[:-12]
+    steps, rows, width = parts[0].shape
+    length_copy = pltpu.make_async_copy(lengths_ref, lengths, length_sem)
+    length_copy.start()
     copies = copy_blocks(near, width, weight_ref, near_weight, near_sems)
     copies += copy_blocks(far, width, weight_ref, far_weight, far_sems)
     me = lax.axis_index("tp")
@@ -257,11 +255,13 @@
     at = pl.ds(pl.multiple_of((me ^ offsets[-1]) * width, width), width)
     scaled_out[:, at] = jnp.zeros_like(scaled)
     square_out[...] = total
+    length_copy.wait()
+    rotation_tables(lengths, steps, rows, cos_out, sin_out)
     for copy in copies:
         copy.wait()
 
 
-def scale_call(near, far, weight, gain, parts):
+def scale_call(near, far, lengths, weight, gain, parts):
     steps, rows, width = parts[0].shape
     count = steps * rows
     return pl.pallas_call(
@@ -273,17 +273,21 @@
             pltpu.VMEM((count, HD), jnp.float32),
             pltpu.VMEM((len(near) * width,) + weight.shape[1:], weight.dtype),
             pltpu.VMEM((len(far) * width,) + weight.shape[1:], weight.dtype),
+            pltpu.VMEM((count, HD), jnp.float32),
+            pltpu.VMEM((count, HD), jnp.float32),
         ),
-        in_specs=[HBM] + [VMEM] * (1 + len(parts)),
-        out_specs=(VMEM,) * 6,
+        in_specs=[HBM] * 2 + [VMEM] * (1 + len(parts)),
+        out_specs=(VMEM,) * 8,
         scratch_shapes=[
+            pltpu.SMEM(lengths.shape, jnp.int32),
+            pltpu.SemaphoreType.DMA,
             pltpu.SemaphoreType.DMA((len(near),)),
             pltpu.SemaphoreType.DMA((len(far),)),
         ],
         compiler_params=pltpu.CompilerParams(vmem_limit_bytes=8 << 20),
         cost_estimate=pl.CostEstimate(flops=0, bytes_accessed=9 << 20, transcendentals=0),
         name="scale_features",
-    )(pltpu.with_memory_space_constraint(weight, pltpu.HBM), gain, *parts)
+    )(*[pltpu.with_memory_space_constraint(x, pltpu.HBM) for x in (lengths, weight)], gain, *parts)
 
 
 def inner_kernel(last, scaled_ref, far_ref, square_ref, gain_ref, part_ref, *rest):
@@ -398,7 +402,7 @@
             keys_out[step, :, at] = key[step * rows : (step + 1) * rows]
             values_out[step, :, at] = value[step * rows : (step + 1) * rows]
         scores = lax.dot_general(
-            query_ref[group],
+            query_ref[group].astype(jnp.bfloat16),
             key,
             (((1,), (1,)), ((), ())),
             preferred_element_type=jnp.float32,
@@ -469,14 +473,14 @@
         second = swap(pack, "wide", 2, wide_count)
         first = swap(pack, "wide", 1, wide_count)
     near, far = (0, 1), (2, 3)
-    gain_rows, bias, mine, _, *cached = cache_call(
+    gain_rows, bias, mine, *cached = cache_call(
         lengths, queries, stored_rotated_keys, stored_value_rows, gain, key_value_bias, hidden
     )
     if direct:
         third, gain_rows = lax.optimization_barrier((second, gain_rows))
         packs = [pack, first, second, swap(third, "wide", 1, wide_count)]
-    scaled, near_scaled, far_scaled, square, near_weight, far_weight = scale_call(
-        near, far, key_value_weight, gain_rows, [mine] + tp_parts[:2]
+    scaled, near_scaled, far_scaled, square, near_weight, far_weight, *tables = scale_call(
+        near, far, lengths, key_value_weight, gain_rows, [mine] + tp_parts[:2]
     )
     near_base = dot(near_scaled, near_weight)
     if direct:
@@ -499,7 +503,7 @@
     far_base = dot(far_scaled, far_weight)
     up = up_call(packs, bias.shape[1])
     return final_call(
-        queries.shape, width, near_base, far_base, square, bias, cached, inner, up
+        queries.shape, width, near_base, far_base, square, bias, cached + tables, inner, up
     )
 
 

time: 25.8 us -> 25.1 us (0.973)
  Pallas kernels: 10.1 us -> 9.37 us
    pallas_call x1, Pallas kernels: 3.75 us -> 3.04 us  [cache_call(): pl.pallas_call(cache_kernel, out_shape=(pltpu.VMEM(gain.shape, jnp.float3...]
  transfers between devices with their start and end apart: 9 -> 9, of which waited for: 4 -> 4; matrix products, arithmetic and copies ran while one was open for 6% -> 7% of each run, Pallas kernels for 28% -> 27%
where the time goes in v17:
time: 25.1 us; the launch traced here: 24.9 us
  starting transfers between devices  9.84 us (39%)
  Pallas kernels  9.37 us (37%)
  waiting for transfers between devices  3.35 us (13%)
  matrix products  1.64 us (7%)
  between operations  0.7 us (3%)
    ppermute x9, starting transfers between devices, swap(): return lax.ppermute(block, axis, [(i, i ^ offset) for i in range(count)])  9.84 us
    pallas_call x1, Pallas kernels, scale_call(): pl.pallas_call(functools.partial(scale_kernel, near, far), out_shape=(plt...  3.53 us
    ppermute x9, waiting for transfers between devices, swap(): return lax.ppermute(block, axis, [(i, i ^ offset) for i in range(count)])  3.35 us
    pallas_call x1, Pallas kernels, cache_call(): pl.pallas_call(cache_kernel, out_shape=(pltpu.VMEM(gain.shape, jnp.float3...  3.04 us
    dot_general x2, matrix products, dot(): jnp.einsum('md,dkc->kmc', rows, weight, preferred_element_type=jnp.float32)  1.64 us
    pallas_call x1, Pallas kernels, final_call(): pl.pallas_call(functools.partial(final_kernel, width, len(inner)), out_sh...  1.54 us
    pallas_call x1, Pallas kernels, pack_call(): pl.pallas_call(pack_kernel, out_shape=pltpu.VMEM((kinds, share, down.shap...  0.93 us
  transfers between devices with their start and end apart: 9, of which 4 were waited for; matrix products, arithmetic and copies ran while one was open for 7% of the time, Pallas kernels for 27%

profile of v17, /device:TPU:0, one launch (start us, length us, event | category | flops | bytes accessed | tf_op | source)
XLA Modules:
  0.0 24.9 jit_solution(11846287294639039147)
XLA Ops:
  0.6 0.9 %pack_factors.1.rest_0_.refs_0_ = bf16[2,16,2304]{2,1,0:T(8,128)(2,1)S(1)} custom-call(bf16[2,64,2048]{2,1,0:T(8,128)(2,1)} %down_ref.1, bf16[2,16,256]{2,1,0:T(8,128)(2,1)} %bitcast.13), custom_call_target="tpu_custom_call" | custom-call | tf_op jit(solution)/shard_map/pack_factors/pallas_call | solution.py:192
  1.6 4.1 %collective-permute-start = (bf16[2,16,2304]{2,1,0:T(8,128)(2,1)S(1)}, bf16[2,16,2304]{2,1,0:T(8,128)(2,1)S(1)}, u32[]{:S(2)}, u32[]{:S(2)}) collective-permute-start(bf16[2,16,2304]{2,1,0:T(8,128)(2,1)S(1)} %pack_factors.1.rest_0_.refs_0_), channel_id=1, source_target_pairs={{0,8},{4,12},{8,0},{12,4},{1,9},{5,13},{9,1},{13,5},{2,10},{6,14},... | collective-permute-start | bytes 442376 | tf_op jit(solution)/shard_map/ppermute | solution.py:447
  5.7 0.0 collective-permute-start.1
  5.7 1.5 %collective-permute-start.2 = (bf16[4,8,2048]{2,1,0:T(8,128)(2,1)}, bf16[4,8,2048]{2,1,0:T(8,128)(2,1)S(1)}, u32[]{:S(2)}, u32[]{:S(2)}) collective-permute-start(bf16[4,8,2048]{2,1,0:T(8,128)(2,1)} %hidden_ref.1), channel_id=1, source_target_pairs={{0,2},{1,3},{2,0},{3,1},{4,6},{5,7},{6,4},{7,5},{8,10},{9,11},{10,... | collective-permute-start | bytes 393224 | tf_op jit(solution)/shard_map/ppermute | solution.py:447
  7.2 1.6 %collective-permute-start.4 = (bf16[2,16,2304]{2,1,0:T(8,128)(2,1)S(1)}, bf16[2,16,2304]{2,1,0:T(8,128)(2,1)S(1)}, u32[]{:S(2)}, u32[]{:S(2)}) collective-permute-start(bf16[2,16,2304]{2,1,0:T(8,128)(2,1)S(1)} %pack_factors.1.rest_0_.refs_0_), channel_id=1, source_target_pairs={{0,4},{4,0},{8,12},{12,8},{1,5},{5,1},{9,13},{13,9},{2,6},{6,2},{1... | collective-permute-start | bytes 442376 | tf_op jit(solution)/shard_map/ppermute | solution.py:447
  8.7 0.1 collective-permute-start.3
  8.8 3.0 %cache_attention.1 = (f32[64,128]{1,0:T(8,128)S(1)}, bf16[2,256]{1,0:T(2,128)(2,1)S(1)}, bf16[4,8,2048]{2,1,0:T(8,128)(2,1)S(1)}, f32[2,256,128]{2,1,0:T(8,128)S...) custom-call(s32[8]{0:T(128)} %lengths_ref.3, ...), custom_call_target="tpu_custom_call" | custom-call | flops 140509184 | bytes 5242880 | tf_op jit(solution)/shard_map/cache_attention/pallas_call | solution.py:142
  11.9 0.9 %collective-permute-done.rest_2_.refs_2_ = bf16[2,16,2304]{2,1,0:T(8,128)(2,1)S(1)} collective-permute-done((bf16[2,16,2304]{2,1,0:T(8,128)(2,1)S(1)}, bf16[2,16,2304]{2,1,0:T(8,128)(2,1)S(1)}, u32[]{:S(2)}, u32[]{:S(2)}) %collective-permute-start) | collective-permute-done | bytes 147488 | tf_op jit(solution)/shard_map/ppermute | solution.py:447
  12.8 0.7 %collective-permute-start.5 = (bf16[2,16,2304]{2,1,0:T(8,128)(2,1)S(1)}, bf16[2,16,2304]{2,1,0:T(8,128)(2,1)S(1)}, u32[]{:S(2)}, u32[]{:S(2)}) collective-permute-start(bf16[2,16,2304]{2,1,0:T(8,128)(2,1)S(1)} %collective-permute-done.rest_2_.refs_2_), channel_id=1, source_target_pairs={{0,4},{4,0},{8,12},{12,8},{1,5},{5,1},{9,13},{13,9},{2,6},{6,2},{1... | collective-permute-start | bytes 442376 | tf_op jit(solution)/shard_map/ppermute | solution.py:447
  13.4 0.0 collective-permute-done.1.rest_1_
  13.4 0.0 collective-permute-done.2.rest_2_
  13.5 3.5 %scale_features.1 = (bf16[32,8192]{1,0:T(8,128)(2,1)S(1)}, bf16[32,4096]{1,0:T(8,128)(2,1)S(1)}, bf16[32,2048]{1,0:T(8,128)(2,1)S(1)}, f32[32,128]{1,0:T(8,128)S...) custom-call(s32[8]{0:T(128)} %lengths_ref.3, ...), custom_call_target="tpu_custom_call" | custom-call | bytes 9437184 | tf_op jit(solution)/shard_map/scale_features/pallas_call | solution.py:267
  17.0 0.8 %fusion.4.near_ref = f32[2,32,256]{2,1,0:T(8,128)S(1)} fusion(bf16[4096,2,256]{2,1,0:T(2,128)(2,1)S(1)} %get-tuple-element.35, bf16[32,4096]{1,0:T(8,128)(2,1)S(1)} %get-tuple-element.36), kind=kOutput, calls=%fused_computation.4 | convolution fusion | flops 134217728 | bytes 4521984 | tf_op jit(solution)/shard_map/md,dkc->kmc/dot_general | solution.py:443
  17.8 0.0 collective-permute-done.3.part_ref
  17.8 0.0 collective-permute-done.4.rest_1_.refs_1_
  17.8 0.4 %collective-permute-done.5.rest_3_.refs_3_ = bf16[2,16,2304]{2,1,0:T(8,128)(2,1)S(1)} collective-permute-done((bf16[2,16,2304]{2,1,0:T(8,128)(2,1)S(1)}, bf16[2,16,2304]{2,1,0:T(8,128)(2,1)S(1)}, u32[]{:S(2)}, u32[]{:S(2)}) %collective-permute-start.5) | collective-permute-done | bytes 147488 | tf_op jit(solution)/shard_map/ppermute | solution.py:447
  18.3 0.3 %rank_inner.1 = (f32[32,32]{1,0:T(8,128)S(1)}, bf16[32,4096]{1,0:T(8,128)(2,1)S(1)}, f32[32,128]{1,0:T(8,128)S(1)}) custom-call(bf16[32,8192]{1,0:T(8,128)(2,1)S(1)} %get-tuple-element.39.scaled_ref, bf16[32,2048]{1,0:T(8,128)(2,1)S(1)} %get-tuple-element.40.far_ref, f32[32,128]{1,0:T(8,128)S(1)} %get-tuple-element.41.square_ref, ...), custom_call_target="tpu_custom_call" | custom-call | tf_op jit(solution)/shard_map/rank_inner/pallas_call | solution.py:330
  18.6 0.1 collective-permute-start.6
  18.6 1.6 %collective-permute-start.7 = (f32[32,32]{1,0:T(8,128)S(1)}, f32[32,32]{1,0:T(8,128)S(1)}, u32[]{:S(2)}, u32[]{:S(2)}) collective-permute-start(f32[32,32]{1,0:T(8,128)S(1)} %get-tuple-element.54.rest_6_), channel_id=1, source_target_pairs={{0,2},{1,3},{2,0},{3,1},{4,6},{5,7},{6,4},{7,5},{8,10},{9,11},{10,... | collective-permute-start | bytes 12296 | tf_op jit(solution)/shard_map/ppermute | solution.py:447
  20.2 0.3 %collective-permute-start.8 = (f32[32,32]{1,0:T(8,128)S(1)}, f32[32,32]{1,0:T(8,128)S(1)}, u32[]{:S(2)}, u32[]{:S(2)}) collective-permute-start(f32[32,32]{1,0:T(8,128)S(1)} %get-tuple-element.54.rest_6_), channel_id=1, source_target_pairs={{0,3},{1,2},{2,1},{3,0},{4,7},{5,6},{6,5},{7,4},{8,11},{9,10},{10,... | collective-permute-start | bytes 12296 | tf_op jit(solution)/shard_map/ppermute | solution.py:447
  20.5 0.8 %fusion.7.far_ref = f32[2,32,256]{2,1,0:T(8,128)S(1)} fusion(bf16[4096,2,256]{2,1,0:T(2,128)(2,1)S(1)} %get-tuple-element.38, bf16[32,4096]{1,0:T(8,128)(2,1)S(1)} %get-tuple-element.45), kind=kOutput, calls=%fused_computation.5 | convolution fusion | flops 134217728 | bytes 4521984 | tf_op jit(solution)/shard_map/md,dkc->kmc/dot_general | solution.py:443
  21.4 0.0 collective-permute-done.6.rest_7_
  21.4 1.1 %collective-permute-done.7.rest_8_ = f32[32,32]{1,0:T(8,128)S(1)} collective-permute-done((f32[32,32]{1,0:T(8,128)S(1)}, f32[32,32]{1,0:T(8,128)S(1)}, u32[]{:S(2)}, u32[]{:S(2)}) %collective-permute-start.7) | collective-permute-done | bytes 4128 | tf_op jit(solution)/shard_map/ppermute | solution.py:447
  22.4 0.9 %collective-permute-done.8.rest_9_ = f32[32,32]{1,0:T(8,128)S(1)} collective-permute-done((f32[32,32]{1,0:T(8,128)S(1)}, f32[32,32]{1,0:T(8,128)S(1)}, u32[]{:S(2)}, u32[]{:S(2)}) %collective-permute-start.8) | collective-permute-done | bytes 4128 | tf_op jit(solution)/shard_map/ppermute | solution.py:447
  23.4 1.5 %fresh_attention.1 = (bf16[4,8,256]{2,1,0:T(8,128)(2,1)}, bf16[4,8,256]{2,1,0:T(8,128)(2,1)}, bf16[4,8,2048]{2,1,0:T(8,128)(2,1)}) custom-call(f32[2,32,256]{2,1,0:T(8,128)S(1)} %fusion.4.near_ref, f32[2,32,256]{2,1,0:T(8,128)S(1)} %fusion.7.far_ref, f32[32,128]{1,0:T(8,128)S(1)} %get-tuple-element.46.square_ref, ...), custom_call_target="tpu_custom_call" | custom-call | tf_op jit(solution)/shard_map/fresh_attention/pallas_call | solution.py:431
  (1 shorter events, 0.0 us)
Async XLA Ops:
  1.6 11.2 %collective-permute-start = (bf16[2,16,2304]{2,1,0:T(8,128)(2,1)S(1)}, bf16[2,16,2304]{2,1,0:T(8,128)(2,1)S(1)}, u32[]{:S(2)}, u32[]{:S(2)}) collective-permute-start(bf16[2,16,2304]{2,1,0:T(8,128)(2,1)S(1)} %pack_factors.1.rest_0_.refs_0_), channel_id=1, source_target_pairs={{0,8},{4,12},{8,0},{12,4},{1,9},{5,13},{9,1},{13,5},{2,10},{6,14},... | collective-permute-start | bytes 442376 | tf_op jit(solution)/shard_map/ppermute | solution.py:447
  5.7 7.8 %collective-permute-start.1 = (bf16[4,8,2048]{2,1,0:T(8,128)(2,1)}, bf16[4,8,2048]{2,1,0:T(8,128)(2,1)S(1)}, u32[]{:S(2)}, u32[]{:S(2)}) collective-permute-start(bf16[4,8,2048]{2,1,0:T(8,128)(2,1)} %hidden_ref.1), channel_id=1, source_target_pairs={{0,1},{1,0},{2,3},{3,2},{4,5},{5,4},{6,7},{7,6},{8,9},{9,8},{10,11... | collective-permute-start | bytes 393224 | tf_op jit(solution)/shard_map/ppermute | solution.py:447
  5.7 7.8 %collective-permute-start.2 = (bf16[4,8,2048]{2,1,0:T(8,128)(2,1)}, bf16[4,8,2048]{2,1,0:T(8,128)(2,1)S(1)}, u32[]{:S(2)}, u32[]{:S(2)}) collective-permute-start(bf16[4,8,2048]{2,1,0:T(8,128)(2,1)} %hidden_ref.1), channel_id=1, source_target_pairs={{0,2},{1,3},{2,0},{3,1},{4,6},{5,7},{6,4},{7,5},{8,10},{9,11},{10,... | collective-permute-start | bytes 393224 | tf_op jit(solution)/shard_map/ppermute | solution.py:447
  7.2 10.7 %collective-permute-start.4 = (bf16[2,16,2304]{2,1,0:T(8,128)(2,1)S(1)}, bf16[2,16,2304]{2,1,0:T(8,128)(2,1)S(1)}, u32[]{:S(2)}, u32[]{:S(2)}) collective-permute-start(bf16[2,16,2304]{2,1,0:T(8,128)(2,1)S(1)} %pack_factors.1.rest_0_.refs_0_), channel_id=1, source_target_pairs={{0,4},{4,0},{8,12},{12,8},{1,5},{5,1},{9,13},{13,9},{2,6},{6,2},{1... | collective-permute-start | bytes 442376 | tf_op jit(solution)/shard_map/ppermute | solution.py:447
  8.7 9.1 %collective-permute-start.3 = (bf16[4,8,2048]{2,1,0:T(8,128)(2,1)}, bf16[4,8,2048]{2,1,0:T(8,128)(2,1)S(1)}, u32[]{:S(2)}, u32[]{:S(2)}) collective-permute-start(bf16[4,8,2048]{2,1,0:T(8,128)(2,1)} %hidden_ref.1), channel_id=1, source_target_pairs={{0,3},{1,2},{2,1},{3,0},{4,7},{5,6},{6,5},{7,4},{8,11},{9,10},{10,... | collective-permute-start | bytes 393224 | tf_op jit(solution)/shard_map/ppermute | solution.py:447
  12.8 5.5 %collective-permute-start.5 = (bf16[2,16,2304]{2,1,0:T(8,128)(2,1)S(1)}, bf16[2,16,2304]{2,1,0:T(8,128)(2,1)S(1)}, u32[]{:S(2)}, u32[]{:S(2)}) collective-permute-start(bf16[2,16,2304]{2,1,0:T(8,128)(2,1)S(1)} %collective-permute-done.rest_2_.refs_2_), channel_id=1, source_target_pairs={{0,4},{4,0},{8,12},{12,8},{1,5},{5,1},{9,13},{13,9},{2,6},{6,2},{1... | collective-permute-start | bytes 442376 | tf_op jit(solution)/shard_map/ppermute | solution.py:447
  18.6 2.8 %collective-permute-start.6 = (f32[32,32]{1,0:T(8,128)S(1)}, f32[32,32]{1,0:T(8,128)S(1)}, u32[]{:S(2)}, u32[]{:S(2)}) collective-permute-start(f32[32,32]{1,0:T(8,128)S(1)} %get-tuple-element.54.rest_6_), channel_id=1, source_target_pairs={{0,1},{1,0},{2,3},{3,2},{4,5},{5,4},{6,7},{7,6},{8,9},{9,8},{10,11... | collective-permute-start | bytes 12296 | tf_op jit(solution)/shard_map/ppermute | solution.py:447
  18.6 3.8 %collective-permute-start.7 = (f32[32,32]{1,0:T(8,128)S(1)}, f32[32,32]{1,0:T(8,128)S(1)}, u32[]{:S(2)}, u32[]{:S(2)}) collective-permute-start(f32[32,32]{1,0:T(8,128)S(1)} %get-tuple-element.54.rest_6_), channel_id=1, source_target_pairs={{0,2},{1,3},{2,0},{3,1},{4,6},{5,7},{6,4},{7,5},{8,10},{9,11},{10,... | collective-permute-start | bytes 12296 | tf_op jit(solution)/shard_map/ppermute | solution.py:447
  20.2 3.2 %collective-permute-start.8 = (f32[32,32]{1,0:T(8,128)S(1)}, f32[32,32]{1,0:T(8,128)S(1)}, u32[]{:S(2)}, u32[]{:S(2)}) collective-permute-start(f32[32,32]{1,0:T(8,128)S(1)} %get-tuple-element.54.rest_6_), channel_id=1, source_target_pairs={{0,3},{1,2},{2,1},{3,0},{4,7},{5,6},{6,5},{7,4},{8,11},{9,10},{10,... | collective-permute-start | bytes 12296 | tf_op jit(solution)/shard_map/ppermute | solution.py:447

commit v18 on v17

--- a/solution.py
+++ b/solution.py
@@ -46,6 +46,7 @@
 
 
 def cache_kernel(
+    near,
     lengths_ref,
     query_ref,
     key_ref,
@@ -53,6 +54,8 @@
     gain_ref,
     bias_ref,
     hidden_ref,
+    weight_ref,
+    near_out,
     gain_out,
     bias_out,
     hidden_out,
@@ -67,6 +70,7 @@
     value_buffer,
     score_buffer,
     sems,
+    weight_sems,
 ):
     steps, rows, query_width = query_ref.shape
     cache_span = key_ref.shape[1]
@@ -89,6 +93,7 @@
     copies = [pltpu.make_async_copy(*pair, sems.at[i]) for i, pair in enumerate(copies)]
     for copy in copies:
         copy.start()
+    copies += copy_blocks(near, hidden_ref.shape[2], weight_ref, near_out, weight_sems)
 
     copies[0].wait()
     copies[1].wait()
@@ -132,16 +137,18 @@
         copy.wait()
 
 
-def cache_call(lengths, queries, keys, values, gain, bias, hidden):
+def cache_call(near, lengths, queries, keys, values, gain, bias, hidden, weight):
     steps, rows, query_width = queries.shape
     cache_span, key_width = keys.shape[1:]
     groups = key_width // HD
     lines = steps * (query_width // key_width)
     block = (groups, lines * rows, HD)
-    operands = (lengths, queries, keys, values, gain, bias, hidden)
+    operands = (lengths, queries, keys, values, gain, bias, hidden, weight)
+    near_weight = (len(near) * hidden.shape[2],) + weight.shape[1:]
     return pl.pallas_call(
-        cache_kernel,
+        functools.partial(cache_kernel, near),
         out_shape=(
+            pltpu.VMEM(near_weight, weight.dtype),
             pltpu.VMEM(gain.shape, jnp.float32),
             pltpu.VMEM(bias.shape, bias.dtype),
             pltpu.VMEM(hidden.shape, hidden.dtype),
@@ -151,7 +158,7 @@
             pltpu.VMEM(block, jnp.float32),
         ),
         in_specs=[HBM] * len(operands),
-        out_specs=(VMEM,) * 7,
+        out_specs=(VMEM,) * 8,
         scratch_shapes=[
             pltpu.SMEM(lengths.shape, jnp.int32),
             pltpu.VMEM(queries.shape, queries.dtype),
@@ -160,6 +167,7 @@
             pltpu.VMEM(values.shape, values.dtype),
             pltpu.VMEM((rows * groups, lines, cache_span), jnp.float32),
             pltpu.SemaphoreType.DMA((9,)),
+            pltpu.SemaphoreType.DMA((len(near),)),
         ],
         compiler_params=pltpu.CompilerParams(vmem_limit_bytes=16 << 20),
         cost_estimate=pl.CostEstimate(flops=2 * 67 << 20, bytes_accessed=5 << 20, transcendentals=0),
@@ -175,16 +183,17 @@
     share = out_ref.shape[1]
     width = down_ref.shape[2]
     at = pl.ds(pl.multiple_of(lax.axis_index("tp") * share, share), share)
-    down = pltpu.make_async_copy(
-        down_ref.at[:, at, :], out_ref.at[:, :, pl.ds(0, width)], sems.at[0]
-    )
-    up = pltpu.make_async_copy(
-        up_ref, out_ref.at[:, :, pl.ds(width, up_ref.shape[2])], sems.at[1]
-    )
-    down.start()
-    up.start()
-    down.wait()
-    up.wait()
+    copies = [(up_ref, out_ref.at[:, :, pl.ds(width, up_ref.shape[2])])]
+    half = width // 2
+    for kind in range(down_ref.shape[0]):
+        for first in (0, half):
+            lanes = pl.ds(first, half)
+            copies.append((down_ref.at[kind, at, lanes], out_ref.at[kind, :, lanes]))
+    copies = [pltpu.make_async_copy(*pair, sems.at[i]) for i, pair in enumerate(copies)]
+    for copy in copies:
+        copy.start()
+    for copy in copies:
+        copy.wait()
 
 
 def pack_call(down, up):
@@ -194,7 +203,7 @@
         out_shape=pltpu.VMEM((kinds, share, down.shape[2] + columns), down.dtype),
         in_specs=[HBM] * 2,
         out_specs=VMEM,
-        scratch_shapes=[pltpu.SemaphoreType.DMA((2,))],
+        scratch_shapes=[pltpu.SemaphoreType.DMA((1 + 2 * kinds,))],
         name="pack_factors",
     )(*[pltpu.with_memory_space_constraint(x, pltpu.HBM) for x in (down, up)])
 
@@ -231,14 +240,13 @@
 
 
 def scale_kernel(near, far, lengths_ref, weight_ref, gain_ref, *rest):
-    scaled_out, near_out, far_out, square_out, near_weight, far_weight, cos_out, sin_out = rest[-12:-4]
-    lengths, length_sem, near_sems, far_sems = rest[-4:]
-    parts = rest[:-12]
+    scaled_out, near_out, far_out, square_out, far_weight, cos_out, sin_out = rest[-10:-3]
+    lengths, length_sem, far_sems = rest[-3:]
+    parts = rest[:-10]
     steps, rows, width = parts[0].shape
     length_copy = pltpu.make_async_copy(lengths_ref, lengths, length_sem)
     length_copy.start()
-    copies = copy_blocks(near, width, weight_ref, near_weight, near_sems)
-    copies += copy_blocks(far, width, weight_ref, far_weight, far_sems)
+    copies = copy_blocks(far, width, weight_ref, far_weight, far_sems)
     me = lax.axis_index("tp")
     offsets = near + far
     total = None
@@ -271,17 +279,15 @@
             pltpu.VMEM((count, len(near) * width), jnp.bfloat16),
             pltpu.VMEM((count, (len(far) - 1) * width), jnp.bfloat16),
             pltpu.VMEM((count, HD), jnp.float32),
-            pltpu.VMEM((len(near) * width,) + weight.shape[1:], weight.dtype),
             pltpu.VMEM((len(far) * width,) + weight.shape[1:], weight.dtype),
             pltpu.VMEM((count, HD), jnp.float32),
             pltpu.VMEM((count, HD), jnp.float32),
         ),
         in_specs=[HBM] * 2 + [VMEM] * (1 + len(parts)),
-        out_specs=(VMEM,) * 8,
+        out_specs=(VMEM,) * 7,
         scratch_shapes=[
             pltpu.SMEM(lengths.shape, jnp.int32),
             pltpu.SemaphoreType.DMA,
-            pltpu.SemaphoreType.DMA((len(near),)),
             pltpu.SemaphoreType.DMA((len(far),)),
         ],
         compiler_params=pltpu.CompilerParams(vmem_limit_bytes=8 << 20),
@@ -310,12 +316,16 @@
         total.append(
             lax.dot_general(
                 jnp.where(mine == block, late, early),
-                pack[:, :, :width].reshape(inner_out.shape[1], width),
+                pack[:, :, :width].reshape(pack.shape[0] * pack.shape[1], width),
                 (((1,), (1,)), ((), ())),
                 preferred_element_type=jnp.float32,
             )
         )
-    inner_out[...] = sum(total[1:], total[0])
+    total = sum(total[1:], total[0])
+    lines = inner_out.shape[0]
+    inner_out[...] = jnp.concatenate(
+        [total[i : i + lines] for i in range(0, total.shape[0], lines)], axis=1
+    )
 
 
 def inner_call(last, scaled, far, square, gain, part, packs):
@@ -326,7 +336,7 @@
     ]
     if packs:
         kinds, share, _ = packs[0].shape
-        shapes = [pltpu.VMEM((count, kinds * share), jnp.float32)] + shapes
+        shapes = [pltpu.VMEM((count * kinds * share // HD, HD), jnp.float32)] + shapes
     return pl.pallas_call(
         functools.partial(inner_kernel, last),
         out_shape=tuple(shapes),
@@ -376,7 +386,17 @@
     me = lax.axis_index("tp") if blocks > 1 else 0
     for i in range(blocks):
         inner_buffer[me ^ i] = inner_refs[i][...]
-    inner = jnp.concatenate([inner_buffer[i] for i in range(blocks)], axis=1)
+    lines = inner_buffer.shape[1]
+    share = inner_buffer.shape[2] * lines // count
+    inner = jnp.concatenate(
+        [
+            jnp.concatenate(
+                [inner_buffer[i, :, j * share : (j + 1) * share] for i in range(blocks)], axis=1
+            )
+            for j in range(count // lines)
+        ],
+        axis=0,
+    )
     high = inner.astype(jnp.bfloat16)
     low = (inner - high.astype(jnp.float32)).astype(jnp.bfloat16)
     lora = jnp.dot(
@@ -473,13 +493,21 @@
         second = swap(pack, "wide", 2, wide_count)
         first = swap(pack, "wide", 1, wide_count)
     near, far = (0, 1), (2, 3)
-    gain_rows, bias, mine, *cached = cache_call(
-        lengths, queries, stored_rotated_keys, stored_value_rows, gain, key_value_bias, hidden
+    near_weight, gain_rows, bias, mine, *cached = cache_call(
+        near,
+        lengths,
+        queries,
+        stored_rotated_keys,
+        stored_value_rows,
+        gain,
+        key_value_bias,
+        hidden,
+        key_value_weight,
     )
     if direct:
         third, gain_rows = lax.optimization_barrier((second, gain_rows))
         packs = [pack, first, second, swap(third, "wide", 1, wide_count)]
-    scaled, near_scaled, far_scaled, square, near_weight, far_weight, *tables = scale_call(
+    scaled, near_scaled, far_scaled, square, far_weight, *tables = scale_call(
         near, far, lengths, key_value_weight, gain_rows, [mine] + tp_parts[:2]
     )
     near_base = dot(near_scaled, near_weight)

time: 25.1 us -> 25.6 us (1.020)
  waiting for transfers between devices: 3.35 us -> 4.47 us
  Pallas kernels: 9.37 us -> 8.77 us
    pallas_call x1, Pallas kernels: 3.53 us -> 2.26 us  [scale_call(): pl.pallas_call(functools.partial(scale_kernel, near, far), out_shape=(plt...]
    ppermute x9, waiting for transfers between devices: 3.35 us -> 4.47 us  [swap(): return lax.ppermute(block, axis, [(i, i ^ offset) for i in range(count)])]
    pallas_call x1, Pallas kernels: 3.04 us -> 3.7 us  [cache_call(): pl.pallas_call(functools.partial(cache_kernel, near), out_shape=(pltpu.VM...]
  transfers between devices with their start and end apart: 9 -> 9, of which waited for: 4 -> 4; matrix products, arithmetic and copies ran while one was open for 7% -> 7% of each run, Pallas kernels for 27% -> 24%
where the time goes in v18:
time: 25.6 us; the launch traced here: 25.4 us
  starting transfers between devices  9.81 us (38%)
  Pallas kernels  8.77 us (34%)
  waiting for transfers between devices  4.47 us (17%)
  matrix products  1.66 us (6%)
  between operations  0.7 us (3%)
    ppermute x9, starting transfers between devices, swap(): return lax.ppermute(block, axis, [(i, i ^ offset) for i in range(count)])  9.81 us
    ppermute x9, waiting for transfers between devices, swap(): return lax.ppermute(block, axis, [(i, i ^ offset) for i in range(count)])  4.47 us
    pallas_call x1, Pallas kernels, cache_call(): pl.pallas_call(functools.partial(cache_kernel, near), out_shape=(pltpu.VM...  3.7 us
    pallas_call x1, Pallas kernels, scale_call(): pl.pallas_call(functools.partial(scale_kernel, near, far), out_shape=(plt...  2.26 us
    dot_general x2, matrix products, dot(): jnp.einsum('md,dkc->kmc', rows, weight, preferred_element_type=jnp.float32)  1.66 us
    pallas_call x1, Pallas kernels, final_call(): pl.pallas_call(functools.partial(final_kernel, width, len(inner)), out_sh...  1.54 us
    pallas_call x1, Pallas kernels, pack_call(): pl.pallas_call(pack_kernel, out_shape=pltpu.VMEM((kinds, share, down.shap...  0.87 us
  transfers between devices with their start and end apart: 9, of which 4 were waited for; matrix products, arithmetic and copies ran while one was open for 7% of the time, Pallas kernels for 24%

profile of v18, /device:TPU:0, one launch (start us, length us, event | category | flops | bytes accessed | tf_op | source)
XLA Modules:
  0.0 25.4 jit_solution(3475977586774747146)
XLA Ops:
  0.6 0.9 %pack_factors.1.rest_0_.refs_0_ = bf16[2,16,2304]{2,1,0:T(8,128)(2,1)S(1)} custom-call(bf16[2,64,2048]{2,1,0:T(8,128)(2,1)} %down_ref.1, bf16[2,16,256]{2,1,0:T(8,128)(2,1)} %bitcast.13), custom_call_target="tpu_custom_call" | custom-call | tf_op jit(solution)/shard_map/pack_factors/pallas_call | solution.py:201
  1.5 4.1 %collective-permute-start = (bf16[2,16,2304]{2,1,0:T(8,128)(2,1)S(1)}, bf16[2,16,2304]{2,1,0:T(8,128)(2,1)S(1)}, u32[]{:S(2)}, u32[]{:S(2)}) collective-permute-start(bf16[2,16,2304]{2,1,0:T(8,128)(2,1)S(1)} %pack_factors.1.rest_0_.refs_0_), channel_id=1, source_target_pairs={{0,8},{4,12},{8,0},{12,4},{1,9},{5,13},{9,1},{13,5},{2,10},{6,14},... | collective-permute-start | bytes 442376 | tf_op jit(solution)/shard_map/ppermute | solution.py:467
  5.6 0.0 collective-permute-start.1
  5.6 1.5 %collective-permute-start.2 = (bf16[4,8,2048]{2,1,0:T(8,128)(2,1)}, bf16[4,8,2048]{2,1,0:T(8,128)(2,1)S(1)}, u32[]{:S(2)}, u32[]{:S(2)}) collective-permute-start(bf16[4,8,2048]{2,1,0:T(8,128)(2,1)} %hidden_ref.1), channel_id=1, source_target_pairs={{0,2},{1,3},{2,0},{3,1},{4,6},{5,7},{6,4},{7,5},{8,10},{9,11},{10,... | collective-permute-start | bytes 393224 | tf_op jit(solution)/shard_map/ppermute | solution.py:467
  7.1 1.6 %collective-permute-start.4 = (bf16[2,16,2304]{2,1,0:T(8,128)(2,1)S(1)}, bf16[2,16,2304]{2,1,0:T(8,128)(2,1)S(1)}, u32[]{:S(2)}, u32[]{:S(2)}) collective-permute-start(bf16[2,16,2304]{2,1,0:T(8,128)(2,1)S(1)} %pack_factors.1.rest_0_.refs_0_), channel_id=1, source_target_pairs={{0,4},{4,0},{8,12},{12,8},{1,5},{5,1},{9,13},{13,9},{2,6},{6,2},{1... | collective-permute-start | bytes 442376 | tf_op jit(solution)/shard_map/ppermute | solution.py:467
  8.7 0.1 collective-permute-start.3
  8.8 3.7 %cache_attention.1 = (bf16[4096,2,256]{2,1,0:T(2,128)(2,1)S(1)}, f32[64,128]{1,0:T(8,128)S(1)}, bf16[2,256]{1,0:T(2,128)(2,1)S(1)}, bf16[4,8,2048]{2,1,0:T(8,128...) custom-call(s32[8]{0:T(128)} %lengths_ref.3, ...), custom_call_target="tpu_custom_call" | custom-call | flops 140509184 | bytes 5242880 | tf_op jit(solution)/shard_map/cache_attention/pallas_call | solution.py:148
  12.5 0.2 collective-permute-done.rest_2_.refs_2_
  12.7 0.7 %collective-permute-start.5 = (bf16[2,16,2304]{2,1,0:T(8,128)(2,1)S(1)}, bf16[2,16,2304]{2,1,0:T(8,128)(2,1)S(1)}, u32[]{:S(2)}, u32[]{:S(2)}) collective-permute-start(bf16[2,16,2304]{2,1,0:T(8,128)(2,1)S(1)} %collective-permute-done.rest_2_.refs_2_), channel_id=1, source_target_pairs={{0,4},{4,0},{8,12},{12,8},{1,5},{5,1},{9,13},{13,9},{2,6},{6,2},{1... | collective-permute-start | bytes 442376 | tf_op jit(solution)/shard_map/ppermute | solution.py:467
  13.4 0.0 collective-permute-done.1.rest_1_
  13.4 0.0 collective-permute-done.2.rest_2_
  13.4 2.3 %scale_features.1 = (bf16[32,8192]{1,0:T(8,128)(2,1)S(1)}, bf16[32,4096]{1,0:T(8,128)(2,1)S(1)}, bf16[32,2048]{1,0:T(8,128)(2,1)S(1)}, f32[32,128]{1,0:T(8,128)S...) custom-call(s32[8]{0:T(128)} %lengths_ref.3, ...), custom_call_target="tpu_custom_call" | custom-call | bytes 9437184 | tf_op jit(solution)/shard_map/scale_features/pallas_call | solution.py:275
  15.7 0.8 %fusion.4.near_ref = f32[2,32,256]{2,1,0:T(8,128)S(1)} fusion(bf16[4096,2,256]{2,1,0:T(2,128)(2,1)S(1)} %get-tuple-element.35, bf16[32,4096]{1,0:T(8,128)(2,1)S(1)} %get-tuple-element.36), kind=kOutput, calls=%fused_computation.4 | convolution fusion | flops 134217728 | bytes 4521984 | tf_op jit(solution)/shard_map/md,dkc->kmc/dot_general | solution.py:463
  16.5 0.0 collective-permute-done.3.part_ref
  16.5 0.0 collective-permute-done.4.rest_1_.refs_1_
  16.5 2.4 %collective-permute-done.5.rest_3_.refs_3_ = bf16[2,16,2304]{2,1,0:T(8,128)(2,1)S(1)} collective-permute-done((bf16[2,16,2304]{2,1,0:T(8,128)(2,1)S(1)}, bf16[2,16,2304]{2,1,0:T(8,128)(2,1)S(1)}, u32[]{:S(2)}, u32[]{:S(2)}) %collective-permute-start.5) | collective-permute-done | bytes 147488 | tf_op jit(solution)/shard_map/ppermute | solution.py:467
  18.9 0.4 %rank_inner.1 = (f32[8,128]{1,0:T(8,128)S(1)}, bf16[32,4096]{1,0:T(8,128)(2,1)S(1)}, f32[32,128]{1,0:T(8,128)S(1)}) custom-call(bf16[32,8192]{1,0:T(8,128)(2,1)S(1)} %get-tuple-element.39.scaled_ref, bf16[32,2048]{1,0:T(8,128)(2,1)S(1)} %get-tuple-element.40.far_ref, f32[32,128]{1,0:T(8,128)S(1)} %get-tuple-element.41.square_ref, ...), custom_call_target="tpu_custom_call" | custom-call | tf_op jit(solution)/shard_map/rank_inner/pallas_call | solution.py:340
  19.2 0.0 collective-permute-start.6
  19.3 1.6 %collective-permute-start.7 = (f32[8,128]{1,0:T(8,128)S(1)}, f32[8,128]{1,0:T(8,128)S(1)}, u32[]{:S(2)}, u32[]{:S(2)}) collective-permute-start(f32[8,128]{1,0:T(8,128)S(1)} %get-tuple-element.54.rest_6_), channel_id=1, source_target_pairs={{0,2},{1,3},{2,0},{3,1},{4,6},{5,7},{6,4},{7,5},{8,10},{9,11},{10,... | collective-permute-start | bytes 12296 | tf_op jit(solution)/shard_map/ppermute | solution.py:467
  20.8 0.3 %collective-permute-start.8 = (f32[8,128]{1,0:T(8,128)S(1)}, f32[8,128]{1,0:T(8,128)S(1)}, u32[]{:S(2)}, u32[]{:S(2)}) collective-permute-start(f32[8,128]{1,0:T(8,128)S(1)} %get-tuple-element.54.rest_6_), channel_id=1, source_target_pairs={{0,3},{1,2},{2,1},{3,0},{4,7},{5,6},{6,5},{7,4},{8,11},{9,10},{10,... | collective-permute-start | bytes 12296 | tf_op jit(solution)/shard_map/ppermute | solution.py:467
  21.1 0.8 %fusion.7.far_ref = f32[2,32,256]{2,1,0:T(8,128)S(1)} fusion(bf16[4096,2,256]{2,1,0:T(2,128)(2,1)S(1)} %get-tuple-element.38, bf16[32,4096]{1,0:T(8,128)(2,1)S(1)} %get-tuple-element.45), kind=kOutput, calls=%fused_computation.5 | convolution fusion | flops 134217728 | bytes 4521984 | tf_op jit(solution)/shard_map/md,dkc->kmc/dot_general | solution.py:463
  22.0 0.0 collective-permute-done.6.rest_7_
  22.0 0.9 %collective-permute-done.7.rest_8_ = f32[8,128]{1,0:T(8,128)S(1)} collective-permute-done((f32[8,128]{1,0:T(8,128)S(1)}, f32[8,128]{1,0:T(8,128)S(1)}, u32[]{:S(2)}, u32[]{:S(2)}) %collective-permute-start.7) | collective-permute-done | bytes 4128 | tf_op jit(solution)/shard_map/ppermute | solution.py:467
  22.9 0.9 %collective-permute-done.8.rest_9_ = f32[8,128]{1,0:T(8,128)S(1)} collective-permute-done((f32[8,128]{1,0:T(8,128)S(1)}, f32[8,128]{1,0:T(8,128)S(1)}, u32[]{:S(2)}, u32[]{:S(2)}) %collective-permute-start.8) | collective-permute-done | bytes 4128 | tf_op jit(solution)/shard_map/ppermute | solution.py:467
  23.9 1.5 %fresh_attention.1 = (bf16[4,8,256]{2,1,0:T(8,128)(2,1)}, bf16[4,8,256]{2,1,0:T(8,128)(2,1)}, bf16[4,8,2048]{2,1,0:T(8,128)(2,1)}) custom-call(f32[2,32,256]{2,1,0:T(8,128)S(1)} %fusion.4.near_ref, f32[2,32,256]{2,1,0:T(8,128)S(1)} %fusion.7.far_ref, f32[32,128]{1,0:T(8,128)S(1)} %get-tuple-element.46.square_ref, ...), custom_call_target="tpu_custom_call" | custom-call | tf_op jit(solution)/shard_map/fresh_attention/pallas_call | solution.py:451
  (1 shorter events, 0.0 us)
Async XLA Ops:
  1.5 11.2 %collective-permute-start = (bf16[2,16,2304]{2,1,0:T(8,128)(2,1)S(1)}, bf16[2,16,2304]{2,1,0:T(8,128)(2,1)S(1)}, u32[]{:S(2)}, u32[]{:S(2)}) collective-permute-start(bf16[2,16,2304]{2,1,0:T(8,128)(2,1)S(1)} %pack_factors.1.rest_0_.refs_0_), channel_id=1, source_target_pairs={{0,8},{4,12},{8,0},{12,4},{1,9},{5,13},{9,1},{13,5},{2,10},{6,14},... | collective-permute-start | bytes 442376 | tf_op jit(solution)/shard_map/ppermute | solution.py:467
  5.6 7.8 %collective-permute-start.1 = (bf16[4,8,2048]{2,1,0:T(8,128)(2,1)}, bf16[4,8,2048]{2,1,0:T(8,128)(2,1)S(1)}, u32[]{:S(2)}, u32[]{:S(2)}) collective-permute-start(bf16[4,8,2048]{2,1,0:T(8,128)(2,1)} %hidden_ref.1), channel_id=1, source_target_pairs={{0,1},{1,0},{2,3},{3,2},{4,5},{5,4},{6,7},{7,6},{8,9},{9,8},{10,11... | collective-permute-start | bytes 393224 | tf_op jit(solution)/shard_map/ppermute | solution.py:467
  5.6 7.8 %collective-permute-start.2 = (bf16[4,8,2048]{2,1,0:T(8,128)(2,1)}, bf16[4,8,2048]{2,1,0:T(8,128)(2,1)S(1)}, u32[]{:S(2)}, u32[]{:S(2)}) collective-permute-start(bf16[4,8,2048]{2,1,0:T(8,128)(2,1)} %hidden_ref.1), channel_id=1, source_target_pairs={{0,2},{1,3},{2,0},{3,1},{4,6},{5,7},{6,4},{7,5},{8,10},{9,11},{10,... | collective-permute-start | bytes 393224 | tf_op jit(solution)/shard_map/ppermute | solution.py:467
  7.1 9.4 %collective-permute-start.4 = (bf16[2,16,2304]{2,1,0:T(8,128)(2,1)S(1)}, bf16[2,16,2304]{2,1,0:T(8,128)(2,1)S(1)}, u32[]{:S(2)}, u32[]{:S(2)}) collective-permute-start(bf16[2,16,2304]{2,1,0:T(8,128)(2,1)S(1)} %pack_factors.1.rest_0_.refs_0_), channel_id=1, source_target_pairs={{0,4},{4,0},{8,12},{12,8},{1,5},{5,1},{9,13},{13,9},{2,6},{6,2},{1... | collective-permute-start | bytes 442376 | tf_op jit(solution)/shard_map/ppermute | solution.py:467
  8.7 7.8 %collective-permute-start.3 = (bf16[4,8,2048]{2,1,0:T(8,128)(2,1)}, bf16[4,8,2048]{2,1,0:T(8,128)(2,1)S(1)}, u32[]{:S(2)}, u32[]{:S(2)}) collective-permute-start(bf16[4,8,2048]{2,1,0:T(8,128)(2,1)} %hidden_ref.1), channel_id=1, source_target_pairs={{0,3},{1,2},{2,1},{3,0},{4,7},{5,6},{6,5},{7,4},{8,11},{9,10},{10,... | collective-permute-start | bytes 393224 | tf_op jit(solution)/shard_map/ppermute | solution.py:467
  12.7 6.1 %collective-permute-start.5 = (bf16[2,16,2304]{2,1,0:T(8,128)(2,1)S(1)}, bf16[2,16,2304]{2,1,0:T(8,128)(2,1)S(1)}, u32[]{:S(2)}, u32[]{:S(2)}) collective-permute-start(bf16[2,16,2304]{2,1,0:T(8,128)(2,1)S(1)} %collective-permute-done.rest_2_.refs_2_), channel_id=1, source_target_pairs={{0,4},{4,0},{8,12},{12,8},{1,5},{5,1},{9,13},{13,9},{2,6},{6,2},{1... | collective-permute-start | bytes 442376 | tf_op jit(solution)/shard_map/ppermute | solution.py:467
  19.2 2.8 %collective-permute-start.6 = (f32[8,128]{1,0:T(8,128)S(1)}, f32[8,128]{1,0:T(8,128)S(1)}, u32[]{:S(2)}, u32[]{:S(2)}) collective-permute-start(f32[8,128]{1,0:T(8,128)S(1)} %get-tuple-element.54.rest_6_), channel_id=1, source_target_pairs={{0,1},{1,0},{2,3},{3,2},{4,5},{5,4},{6,7},{7,6},{8,9},{9,8},{10,11... | collective-permute-start | bytes 12296 | tf_op jit(solution)/shard_map/ppermute | solution.py:467
  19.3 3.7 %collective-permute-start.7 = (f32[8,128]{1,0:T(8,128)S(1)}, f32[8,128]{1,0:T(8,128)S(1)}, u32[]{:S(2)}, u32[]{:S(2)}) collective-permute-start(f32[8,128]{1,0:T(8,128)S(1)} %get-tuple-element.54.rest_6_), channel_id=1, source_target_pairs={{0,2},{1,3},{2,0},{3,1},{4,6},{5,7},{6,4},{7,5},{8,10},{9,11},{10,... | collective-permute-start | bytes 12296 | tf_op jit(solution)/shard_map/ppermute | solution.py:467
  20.8 3.0 %collective-permute-start.8 = (f32[8,128]{1,0:T(8,128)S(1)}, f32[8,128]{1,0:T(8,128)S(1)}, u32[]{:S(2)}, u32[]{:S(2)}) collective-permute-start(f32[8,128]{1,0:T(8,128)S(1)} %get-tuple-element.54.rest_6_), channel_id=1, source_target_pairs={{0,3},{1,2},{2,1},{3,0},{4,7},{5,6},{6,5},{7,4},{8,11},{9,10},{10,... | collective-permute-start | bytes 12296 | tf_op jit(solution)/shard_map/ppermute | solution.py:467

commit v19 on v17

--- a/solution.py
+++ b/solution.py
@@ -175,16 +175,17 @@
     share = out_ref.shape[1]
     width = down_ref.shape[2]
     at = pl.ds(pl.multiple_of(lax.axis_index("tp") * share, share), share)
-    down = pltpu.make_async_copy(
-        down_ref.at[:, at, :], out_ref.at[:, :, pl.ds(0, width)], sems.at[0]
-    )
-    up = pltpu.make_async_copy(
-        up_ref, out_ref.at[:, :, pl.ds(width, up_ref.shape[2])], sems.at[1]
-    )
-    down.start()
-    up.start()
-    down.wait()
-    up.wait()
+    copies = [(up_ref, out_ref.at[:, :, pl.ds(width, up_ref.shape[2])])]
+    half = width // 2
+    for kind in range(down_ref.shape[0]):
+        for first in (0, half):
+            lanes = pl.ds(first, half)
+            copies.append((down_ref.at[kind, at, lanes], out_ref.at[kind, :, lanes]))
+    copies = [pltpu.make_async_copy(*pair, sems.at[i]) for i, pair in enumerate(copies)]
+    for copy in copies:
+        copy.start()
+    for copy in copies:
+        copy.wait()
 
 
 def pack_call(down, up):
@@ -194,7 +195,7 @@
         out_shape=pltpu.VMEM((kinds, share, down.shape[2] + columns), down.dtype),
         in_specs=[HBM] * 2,
         out_specs=VMEM,
-        scratch_shapes=[pltpu.SemaphoreType.DMA((2,))],
+        scratch_shapes=[pltpu.SemaphoreType.DMA((1 + 2 * kinds,))],
         name="pack_factors",
     )(*[pltpu.with_memory_space_constraint(x, pltpu.HBM) for x in (down, up)])
 
@@ -230,30 +231,24 @@
         sin_out[pl.ds(step * rows, rows)] = jnp.where(second, sine, -sine)
 
 
-def scale_kernel(near, far, lengths_ref, weight_ref, gain_ref, *rest):
-    scaled_out, near_out, far_out, square_out, near_weight, far_weight, cos_out, sin_out = rest[-12:-4]
+def scale_kernel(early, near, far, lengths_ref, weight_ref, gain_ref, *rest):
+    scaled_out, early_out, square_out, near_weight, far_weight, cos_out, sin_out = rest[-11:-4]
     lengths, length_sem, near_sems, far_sems = rest[-4:]
-    parts = rest[:-12]
+    parts = rest[:-11]
     steps, rows, width = parts[0].shape
     length_copy = pltpu.make_async_copy(lengths_ref, lengths, length_sem)
     length_copy.start()
     copies = copy_blocks(near, width, weight_ref, near_weight, near_sems)
     copies += copy_blocks(far, width, weight_ref, far_weight, far_sems)
     me = lax.axis_index("tp")
-    offsets = near + far
+    scaled_out[...] = jnp.zeros_like(scaled_out)
     total = None
-    for k, part in enumerate(parts):
-        block = me ^ offsets[k]
+    for k, (offset, part) in enumerate(zip(early, parts)):
+        block = me ^ offset
         scaled, squares = scaled_block(part, gain_ref, block)
         total = squares if total is None else total + squares
         scaled_out[:, pl.ds(pl.multiple_of(block * width, width), width)] = scaled
-        if k < len(near):
-            near_out[:, k * width : (k + 1) * width] = scaled
-        else:
-            i = k - len(near)
-            far_out[:, i * width : (i + 1) * width] = scaled
-    at = pl.ds(pl.multiple_of((me ^ offsets[-1]) * width, width), width)
-    scaled_out[:, at] = jnp.zeros_like(scaled)
+        early_out[:, k * width : (k + 1) * width] = scaled
     square_out[...] = total
     length_copy.wait()
     rotation_tables(lengths, steps, rows, cos_out, sin_out)
@@ -261,15 +256,14 @@
         copy.wait()
 
 
-def scale_call(near, far, lengths, weight, gain, parts):
+def scale_call(early, near, far, lengths, weight, gain, parts):
     steps, rows, width = parts[0].shape
     count = steps * rows
     return pl.pallas_call(
-        functools.partial(scale_kernel, near, far),
+        functools.partial(scale_kernel, early, near, far),
         out_shape=(
             pltpu.VMEM((count, (len(near) + len(far)) * width), jnp.bfloat16),
-            pltpu.VMEM((count, len(near) * width), jnp.bfloat16),
-            pltpu.VMEM((count, (len(far) - 1) * width), jnp.bfloat16),
+            pltpu.VMEM((count, len(early) * width), jnp.bfloat16),
             pltpu.VMEM((count, HD), jnp.float32),
             pltpu.VMEM((len(near) * width,) + weight.shape[1:], weight.dtype),
             pltpu.VMEM((len(far) * width,) + weight.shape[1:], weight.dtype),
@@ -277,7 +271,7 @@
             pltpu.VMEM((count, HD), jnp.float32),
         ),
         in_specs=[HBM] * 2 + [VMEM] * (1 + len(parts)),
-        out_specs=(VMEM,) * 8,
+        out_specs=(VMEM,) * 7,
         scratch_shapes=[
             pltpu.SMEM(lengths.shape, jnp.int32),
             pltpu.SemaphoreType.DMA,
@@ -290,15 +284,21 @@
     )(*[pltpu.with_memory_space_constraint(x, pltpu.HBM) for x in (lengths, weight)], gain, *parts)
 
 
-def inner_kernel(last, scaled_ref, far_ref, square_ref, gain_ref, part_ref, *rest):
-    far_out, square_out = rest[-2:]
-    packs, inner_out = (rest[:-3], rest[-3]) if len(rest) > 2 else ((), None)
-    block = lax.axis_index("tp") ^ last
-    late, squares = scaled_block(part_ref, gain_ref, block)
-    width = late.shape[1]
-    far_out[:, : far_ref.shape[1]] = far_ref[...]
-    far_out[:, far_ref.shape[1] :] = late
-    squares = jnp.sum(squares + square_ref[...], axis=1, keepdims=True)
+def inner_kernel(late, scaled_ref, early_ref, square_ref, gain_ref, *rest):
+    parts, rest = rest[: len(late)], rest[len(late) :]
+    outs, square_out = rest[-1 - len(late) : -1], rest[-1]
+    packs, inner_out = (rest[: -2 - len(late)], rest[-2 - len(late)]) if len(rest) > 1 + len(late) else ((), None)
+    squares = square_ref[...]
+    blocks = []
+    for k, (offset, part) in enumerate(zip(late, parts)):
+        block = lax.axis_index("tp") ^ offset
+        scaled, more = scaled_block(part, gain_ref, block)
+        squares += more
+        blocks.append((block, scaled))
+        width = scaled.shape[1]
+        outs[k][:, :width] = early_ref[:, k * width : (k + 1) * width]
+        outs[k][:, width:] = scaled
+    squares = jnp.sum(squares, axis=1, keepdims=True)
     square_out[...] = jnp.broadcast_to(squares, square_out.shape)
     if not packs:
         return
@@ -306,10 +306,12 @@
     total = []
     for offset, pack in enumerate(packs):
         mine = me ^ offset
-        early = scaled_ref[:, pl.ds(pl.multiple_of(mine * width, width), width)]
+        rows = scaled_ref[:, pl.ds(pl.multiple_of(mine * width, width), width)]
+        for block, scaled in blocks:
+            rows = jnp.where(mine == block, scaled, rows)
         total.append(
             lax.dot_general(
-                jnp.where(mine == block, late, early),
+                rows,
                 pack[:, :, :width].reshape(inner_out.shape[1], width),
                 (((1,), (1,)), ((), ())),
                 preferred_element_type=jnp.float32,
@@ -318,23 +320,21 @@
     inner_out[...] = sum(total[1:], total[0])
 
 
-def inner_call(last, scaled, far, square, gain, part, packs):
-    count, width = far.shape[0], part.shape[2]
-    shapes = [
-        pltpu.VMEM((count, far.shape[1] + width), far.dtype),
-        pltpu.VMEM(square.shape, jnp.float32),
-    ]
+def inner_call(late, scaled, early, square, gain, parts, packs):
+    count, width = scaled.shape[0], parts[0].shape[2]
+    shapes = [pltpu.VMEM((count, 2 * width), scaled.dtype) for _ in late]
+    shapes.append(pltpu.VMEM(square.shape, jnp.float32))
     if packs:
         kinds, share, _ = packs[0].shape
         shapes = [pltpu.VMEM((count, kinds * share), jnp.float32)] + shapes
     return pl.pallas_call(
-        functools.partial(inner_kernel, last),
+        functools.partial(inner_kernel, late),
         out_shape=tuple(shapes),
-        in_specs=[VMEM] * (5 + len(packs)),
+        in_specs=[VMEM] * (4 + len(parts) + len(packs)),
         out_specs=(VMEM,) * len(shapes),
         compiler_params=pltpu.CompilerParams(vmem_limit_bytes=8 << 20),
         name="rank_inner",
-    )(scaled, far, square, gain, part, *packs)
+    )(scaled, early, square, gain, *parts, *packs)
 
 
 def up_kernel(*refs):
@@ -467,32 +467,36 @@
     gain = input_norm_gain.reshape(width // HD, HD)
     up_part = jnp.transpose(adapter_up_factor, (0, 2, 1))
     direct = wide_count == tp_count == 4
-    tp_parts = [swap(hidden, "tp", offset, tp_count) for offset in (1, 2, 3)]
+    beside, crossed = [swap(hidden, "tp", offset, tp_count) for offset in (1, 2)]
     if direct:
         pack = pack_call(adapter_down_factor, up_part)
         second = swap(pack, "wide", 2, wide_count)
         first = swap(pack, "wide", 1, wide_count)
     near, far = (0, 1), (2, 3)
+    early, late = (0, 2), (1, 3)
     gain_rows, bias, mine, *cached = cache_call(
         lengths, queries, stored_rotated_keys, stored_value_rows, gain, key_value_bias, hidden
     )
+    relayed, gain_rows = lax.optimization_barrier((crossed, gain_rows))
+    relayed = swap(relayed, "tp", 1, tp_count)
     if direct:
         third, gain_rows = lax.optimization_barrier((second, gain_rows))
         packs = [pack, first, second, swap(third, "wide", 1, wide_count)]
-    scaled, near_scaled, far_scaled, square, near_weight, far_weight, *tables = scale_call(
-        near, far, lengths, key_value_weight, gain_rows, [mine] + tp_parts[:2]
-    )
-    near_base = dot(near_scaled, near_weight)
+    scaled, early_scaled, square, near_weight, far_weight, *tables = scale_call(
+        early, near, far, lengths, key_value_weight, gain_rows, (mine, crossed)
+    )
+    late_parts = (beside, relayed)
     if direct:
-        scaled, near_base = lax.optimization_barrier((scaled, near_base))
-        inner, far_scaled, square = inner_call(
-            far[-1], scaled, far_scaled, square, gain_rows, tp_parts[2], packs
-        )
-        inner, far_scaled, packs = lax.optimization_barrier((inner, far_scaled, packs))
+        inner, near_scaled, far_scaled, square = inner_call(
+            late, scaled, early_scaled, square, gain_rows, late_parts, packs
+        )
+        inner, far_scaled, near_scaled, packs = lax.optimization_barrier(
+            (inner, far_scaled, near_scaled, packs)
+        )
         inner = [inner] + [swap(inner, "tp", offset, tp_count) for offset in (1, 2, 3)]
     else:
-        far_scaled, square = inner_call(
-            far[-1], scaled, far_scaled, square, gain_rows, tp_parts[2], []
+        near_scaled, far_scaled, square = inner_call(
+            late, scaled, early_scaled, square, gain_rows, late_parts, []
         )
         down = lax.all_gather(adapter_down_factor, "wide", axis=2, tiled=True)
         rows_full = lax.all_gather(hidden, "tp", axis=2, tiled=True).astype(jnp.float32)
@@ -500,6 +504,7 @@
         inner = jnp.einsum("srd,kad->srka", rows_full, down, preferred_element_type=jnp.float32)
         inner = [inner.reshape(steps * rows, kinds * ranks)]
         packs = [lax.all_gather(up_part, "wide", axis=1, tiled=True)]
+    near_base = dot(near_scaled, near_weight)
     far_base = dot(far_scaled, far_weight)
     up = up_call(packs, bias.shape[1])
     return final_call(

time: 25.1 us -> 24.5 us (0.976)
  waiting for transfers between devices: 3.35 us -> 2.38 us
  starting transfers between devices: 9.84 us -> 10.2 us
    ppermute x9, waiting for transfers between devices: 3.35 us -> 2.38 us  [swap(): return lax.ppermute(block, axis, [(i, i ^ offset) for i in range(count)])]
    ppermute x9, starting transfers between devices: 9.84 us -> 10.2 us  [swap(): return lax.ppermute(block, axis, [(i, i ^ offset) for i in range(count)])]
  transfers between devices with their start and end apart: 9 -> 9, of which waited for: 4 -> 3; matrix products, arithmetic and copies ran while one was open for 7% -> 7% of each run, Pallas kernels for 27% -> 27%
where the time goes in v19:
time: 24.5 us; the launch traced here: 24.4 us
  starting transfers between devices  10.2 us (42%)
  Pallas kernels  9.37 us (38%)
  waiting for transfers between devices  2.38 us (10%)
  matrix products  1.66 us (7%)
  between operations  0.72 us (3%)
    ppermute x9, starting transfers between devices, swap(): return lax.ppermute(block, axis, [(i, i ^ offset) for i in range(count)])  10.2 us
    pallas_call x1, Pallas kernels, scale_call(): pl.pallas_call(functools.partial(scale_kernel, early, near, far), out_sha...  3.53 us
    pallas_call x1, Pallas kernels, cache_call(): pl.pallas_call(cache_kernel, out_shape=(pltpu.VMEM(gain.shape, jnp.float3...  3.04 us
    ppermute x9, waiting for transfers between devices, swap(): return lax.ppermute(block, axis, [(i, i ^ offset) for i in range(count)])  2.38 us
    dot_general x2, matrix products, dot(): jnp.einsum('md,dkc->kmc', rows, weight, preferred_element_type=jnp.float32)  1.66 us
    pallas_call x1, Pallas kernels, final_call(): pl.pallas_call(functools.partial(final_kernel, width, len(inner)), out_sh...  1.54 us
    pallas_call x1, Pallas kernels, pack_call(): pl.pallas_call(pack_kernel, out_shape=pltpu.VMEM((kinds, share, down.shap...  0.9 us
  transfers between devices with their start and end apart: 9, of which 3 were waited for; matrix products, arithmetic and copies ran while one was open for 7% of the time, Pallas kernels for 27%

profile of v19, /device:TPU:0, one launch (start us, length us, event | category | flops | bytes accessed | tf_op | source)
XLA Modules:
  0.0 24.4 jit_solution(8106025068076140313)
XLA Ops:
  0.6 0.0 copy-start
  0.6 0.9 %pack_factors.1.rest_2_.refs_0_ = bf16[2,16,2304]{2,1,0:T(8,128)(2,1)S(1)} custom-call(bf16[2,64,2048]{2,1,0:T(8,128)(2,1)} %down_ref.1, bf16[2,16,256]{2,1,0:T(8,128)(2,1)} %bitcast.13), custom_call_target="tpu_custom_call" | custom-call | tf_op jit(solution)/shard_map/pack_factors/pallas_call | solution.py:193
  1.6 4.1 %collective-permute-start = (bf16[2,16,2304]{2,1,0:T(8,128)(2,1)S(1)}, bf16[2,16,2304]{2,1,0:T(8,128)(2,1)S(1)}, u32[]{:S(2)}, u32[]{:S(2)}) collective-permute-start(bf16[2,16,2304]{2,1,0:T(8,128)(2,1)S(1)} %pack_factors.1.rest_2_.refs_0_), channel_id=1, source_target_pairs={{0,8},{4,12},{8,0},{12,4},{1,9},{5,13},{9,1},{13,5},{2,10},{6,14},... | collective-permute-start | bytes 442376 | tf_op jit(solution)/shard_map/ppermute | solution.py:447
  5.7 1.5 %collective-permute-start.1 = (bf16[4,8,2048]{2,1,0:T(8,128)(2,1)}, bf16[4,8,2048]{2,1,0:T(8,128)(2,1)S(1)}, u32[]{:S(2)}, u32[]{:S(2)}) collective-permute-start(bf16[4,8,2048]{2,1,0:T(8,128)(2,1)} %hidden_ref.1), channel_id=1, source_target_pairs={{0,2},{1,3},{2,0},{3,1},{4,6},{5,7},{6,4},{7,5},{8,10},{9,11},{10,... | collective-permute-start | bytes 393224 | tf_op jit(solution)/shard_map/ppermute | solution.py:447
  7.1 1.6 %collective-permute-start.4 = (bf16[2,16,2304]{2,1,0:T(8,128)(2,1)S(1)}, bf16[2,16,2304]{2,1,0:T(8,128)(2,1)S(1)}, u32[]{:S(2)}, u32[]{:S(2)}) collective-permute-start(bf16[2,16,2304]{2,1,0:T(8,128)(2,1)S(1)} %pack_factors.1.rest_2_.refs_0_), channel_id=1, source_target_pairs={{0,4},{4,0},{8,12},{12,8},{1,5},{5,1},{9,13},{13,9},{2,6},{6,2},{1... | collective-permute-start | bytes 442376 | tf_op jit(solution)/shard_map/ppermute | solution.py:447
  8.7 3.0 %cache_attention.1 = (f32[64,128]{1,0:T(8,128)S(1)}, bf16[2,256]{1,0:T(2,128)(2,1)S(1)}, bf16[4,8,2048]{2,1,0:T(8,128)(2,1)S(1)}, f32[2,256,128]{2,1,0:T(8,128)S...) custom-call(s32[8]{0:T(128)} %lengths_ref.3, ...), custom_call_target="tpu_custom_call" | custom-call | flops 140509184 | bytes 5242880 | tf_op jit(solution)/shard_map/cache_attention/pallas_call | solution.py:142
  11.8 0.0 collective-permute-done.1.rest_1_
  11.8 1.0 %collective-permute-done.rest_4_.refs_2_ = bf16[2,16,2304]{2,1,0:T(8,128)(2,1)S(1)} collective-permute-done((bf16[2,16,2304]{2,1,0:T(8,128)(2,1)S(1)}, bf16[2,16,2304]{2,1,0:T(8,128)(2,1)S(1)}, u32[]{:S(2)}, u32[]{:S(2)}) %collective-permute-start) | collective-permute-done | bytes 147488 | tf_op jit(solution)/shard_map/ppermute | solution.py:447
  12.8 0.7 %collective-permute-start.5 = (bf16[2,16,2304]{2,1,0:T(8,128)(2,1)S(1)}, bf16[2,16,2304]{2,1,0:T(8,128)(2,1)S(1)}, u32[]{:S(2)}, u32[]{:S(2)}) collective-permute-start(bf16[2,16,2304]{2,1,0:T(8,128)(2,1)S(1)} %collective-permute-done.rest_4_.refs_2_), channel_id=1, source_target_pairs={{0,4},{4,0},{8,12},{12,8},{1,5},{5,1},{9,13},{13,9},{2,6},{6,2},{1... | collective-permute-start | bytes 442376 | tf_op jit(solution)/shard_map/ppermute | solution.py:447
  13.4 0.0 copy-done
  13.4 0.0 collective-permute-start.2
  13.4 0.5 %collective-permute-start.3 = (bf16[4,8,2048]{2,1,0:T(8,128)(2,1)S(1)}, bf16[4,8,2048]{2,1,0:T(8,128)(2,1)S(1)}, u32[]{:S(2)}, u32[]{:S(2)}) collective-permute-start(bf16[4,8,2048]{2,1,0:T(8,128)(2,1)S(1)} %collective-permute-done.1.rest_1_), channel_id=1, source_target_pairs={{0,1},{1,0},{2,3},{3,2},{4,5},{5,4},{6,7},{7,6},{8,9},{9,8},{10,11... | collective-permute-start | bytes 393224 | tf_op jit(solution)/shard_map/ppermute | solution.py:447
  13.9 3.5 %scale_features.1 = (bf16[32,8192]{1,0:T(8,128)(2,1)S(1)}, bf16[32,4096]{1,0:T(8,128)(2,1)S(1)}, f32[32,128]{1,0:T(8,128)S(1)}, bf16[4096,2,256]{2,1,0:T(2,128)(...) custom-call(s32[8]{0:T(128)} %lengths_ref.3, ...), custom_call_target="tpu_custom_call" | custom-call | bytes 9437184 | tf_op jit(solution)/shard_map/scale_features/pallas_call | solution.py:262
  17.5 0.0 collective-permute-done.2.rest_0_
  17.5 0.0 collective-permute-done.4.rest_3_.refs_1_
  17.5 0.0 collective-permute-done.3.rest_1_
  17.5 0.4 %collective-permute-done.5.rest_5_.refs_3_ = bf16[2,16,2304]{2,1,0:T(8,128)(2,1)S(1)} collective-permute-done((bf16[2,16,2304]{2,1,0:T(8,128)(2,1)S(1)}, bf16[2,16,2304]{2,1,0:T(8,128)(2,1)S(1)}, u32[]{:S(2)}, u32[]{:S(2)}) %collective-permute-start.5) | collective-permute-done | bytes 147488 | tf_op jit(solution)/shard_map/ppermute | solution.py:447
  17.9 0.3 %rank_inner.1 = (f32[32,32]{1,0:T(8,128)S(1)}, bf16[32,4096]{1,0:T(8,128)(2,1)S(1)}, bf16[32,4096]{1,0:T(8,128)(2,1)S(1)}, f32[32,128]{1,0:T(8,128)S(1)}) custom-call(bf16[32,8192]{1,0:T(8,128)(2,1)S(1)} %get-tuple-element.37.scaled_ref, bf16[32,4096]{1,0:T(8,128)(2,1)S(1)} %get-tuple-element.38.early_ref, f32[32,128]{1,0:T(8,128)S(1)} %get-tuple-element.39.square_ref, ...), custom_call_target="tpu_custom_call" | custom-call | tf_op jit(solution)/shard_map/rank_inner/pallas_call | solution.py:330
  18.2 0.7 %collective-permute-start.8 = (f32[32,32]{1,0:T(8,128)S(1)}, f32[32,32]{1,0:T(8,128)S(1)}, u32[]{:S(2)}, u32[]{:S(2)}) collective-permute-start(f32[32,32]{1,0:T(8,128)S(1)} %get-tuple-element.56.rest_6_), channel_id=1, source_target_pairs={{0,3},{1,2},{2,1},{3,0},{4,7},{5,6},{6,5},{7,4},{8,11},{9,10},{10,... | collective-permute-start | bytes 12296 | tf_op jit(solution)/shard_map/ppermute | solution.py:447
  18.9 1.0 %collective-permute-start.7 = (f32[32,32]{1,0:T(8,128)S(1)}, f32[32,32]{1,0:T(8,128)S(1)}, u32[]{:S(2)}, u32[]{:S(2)}) collective-permute-start(f32[32,32]{1,0:T(8,128)S(1)} %get-tuple-element.56.rest_6_), channel_id=1, source_target_pairs={{0,2},{1,3},{2,0},{3,1},{4,6},{5,7},{6,4},{7,5},{8,10},{9,11},{10,... | collective-permute-start | bytes 12296 | tf_op jit(solution)/shard_map/ppermute | solution.py:447
  19.9 0.2 %collective-permute-start.6 = (f32[32,32]{1,0:T(8,128)S(1)}, f32[32,32]{1,0:T(8,128)S(1)}, u32[]{:S(2)}, u32[]{:S(2)}) collective-permute-start(f32[32,32]{1,0:T(8,128)S(1)} %get-tuple-element.56.rest_6_), channel_id=1, source_target_pairs={{0,1},{1,0},{2,3},{3,2},{4,5},{5,4},{6,7},{7,6},{8,9},{9,8},{10,11... | collective-permute-start | bytes 12296 | tf_op jit(solution)/shard_map/ppermute | solution.py:447
  20.1 0.8 %fusion.7.far_ref = f32[2,32,256]{2,1,0:T(8,128)S(1)} fusion(bf16[4096,2,256]{2,1,0:T(2,128)(2,1)S(1)} %get-tuple-element.46, bf16[32,4096]{1,0:T(8,128)(2,1)S(1)} %get-tuple-element.47), kind=kOutput, calls=%fused_computation.5 | convolution fusion | flops 134217728 | bytes 4521984 | tf_op jit(solution)/shard_map/md,dkc->kmc/dot_general | solution.py:443
  20.9 0.8 %fusion.4.near_ref = f32[2,32,256]{2,1,0:T(8,128)S(1)} fusion(bf16[4096,2,256]{2,1,0:T(2,128)(2,1)S(1)} %get-tuple-element.36, bf16[32,4096]{1,0:T(8,128)(2,1)S(1)} %get-tuple-element.45), kind=kOutput, calls=%fused_computation.4 | convolution fusion | flops 134217728 | bytes 4521984 | tf_op jit(solution)/shard_map/md,dkc->kmc/dot_general | solution.py:443
  21.8 0.0 collective-permute-done.8.rest_9_
  21.8 1.0 %collective-permute-done.7.rest_8_ = f32[32,32]{1,0:T(8,128)S(1)} collective-permute-done((f32[32,32]{1,0:T(8,128)S(1)}, f32[32,32]{1,0:T(8,128)S(1)}, u32[]{:S(2)}, u32[]{:S(2)}) %collective-permute-start.7) | collective-permute-done | bytes 4128 | tf_op jit(solution)/shard_map/ppermute | solution.py:447
  22.8 0.0 collective-permute-done.6.rest_7_
  22.8 1.5 %fresh_attention.1 = (bf16[4,8,256]{2,1,0:T(8,128)(2,1)}, bf16[4,8,256]{2,1,0:T(8,128)(2,1)}, bf16[4,8,2048]{2,1,0:T(8,128)(2,1)}) custom-call(f32[2,32,256]{2,1,0:T(8,128)S(1)} %fusion.4.near_ref, f32[2,32,256]{2,1,0:T(8,128)S(1)} %fusion.7.far_ref, f32[32,128]{1,0:T(8,128)S(1)} %get-tuple-element.48.square_ref, ...), custom_call_target="tpu_custom_call" | custom-call | tf_op jit(solution)/shard_map/fresh_attention/pallas_call | solution.py:431
  (1 shorter events, 0.0 us)
Async XLA Ops:
  0.6 12.8 %copy-start = (bf16[4,8,2048]{2,1,0:T(8,128)(2,1)S(1)}, bf16[4,8,2048]{2,1,0:T(8,128)(2,1)}, u32[]{:S(2)}) copy-start(bf16[4,8,2048]{2,1,0:T(8,128)(2,1)} %hidden_ref.1) | copy-start | bytes 393220
  1.6 11.2 %collective-permute-start = (bf16[2,16,2304]{2,1,0:T(8,128)(2,1)S(1)}, bf16[2,16,2304]{2,1,0:T(8,128)(2,1)S(1)}, u32[]{:S(2)}, u32[]{:S(2)}) collective-permute-start(bf16[2,16,2304]{2,1,0:T(8,128)(2,1)S(1)} %pack_factors.1.rest_2_.refs_0_), channel_id=1, source_target_pairs={{0,8},{4,12},{8,0},{12,4},{1,9},{5,13},{9,1},{13,5},{2,10},{6,14},... | collective-permute-start | bytes 442376 | tf_op jit(solution)/shard_map/ppermute | solution.py:447
  5.7 6.1 %collective-permute-start.1 = (bf16[4,8,2048]{2,1,0:T(8,128)(2,1)}, bf16[4,8,2048]{2,1,0:T(8,128)(2,1)S(1)}, u32[]{:S(2)}, u32[]{:S(2)}) collective-permute-start(bf16[4,8,2048]{2,1,0:T(8,128)(2,1)} %hidden_ref.1), channel_id=1, source_target_pairs={{0,2},{1,3},{2,0},{3,1},{4,6},{5,7},{6,4},{7,5},{8,10},{9,11},{10,... | collective-permute-start | bytes 393224 | tf_op jit(solution)/shard_map/ppermute | solution.py:447
  7.1 10.3 %collective-permute-start.4 = (bf16[2,16,2304]{2,1,0:T(8,128)(2,1)S(1)}, bf16[2,16,2304]{2,1,0:T(8,128)(2,1)S(1)}, u32[]{:S(2)}, u32[]{:S(2)}) collective-permute-start(bf16[2,16,2304]{2,1,0:T(8,128)(2,1)S(1)} %pack_factors.1.rest_2_.refs_0_), channel_id=1, source_target_pairs={{0,4},{4,0},{8,12},{12,8},{1,5},{5,1},{9,13},{13,9},{2,6},{6,2},{1... | collective-permute-start | bytes 442376 | tf_op jit(solution)/shard_map/ppermute | solution.py:447
  12.8 5.1 %collective-permute-start.5 = (bf16[2,16,2304]{2,1,0:T(8,128)(2,1)S(1)}, bf16[2,16,2304]{2,1,0:T(8,128)(2,1)S(1)}, u32[]{:S(2)}, u32[]{:S(2)}) collective-permute-start(bf16[2,16,2304]{2,1,0:T(8,128)(2,1)S(1)} %collective-permute-done.rest_4_.refs_2_), channel_id=1, source_target_pairs={{0,4},{4,0},{8,12},{12,8},{1,5},{5,1},{9,13},{13,9},{2,6},{6,2},{1... | collective-permute-start | bytes 442376 | tf_op jit(solution)/shard_map/ppermute | solution.py:447
  13.4 4.0 %collective-permute-start.2 = (bf16[4,8,2048]{2,1,0:T(8,128)(2,1)S(1)}, bf16[4,8,2048]{2,1,0:T(8,128)(2,1)S(1)}, u32[]{:S(2)}, u32[]{:S(2)}) collective-permute-start(bf16[4,8,2048]{2,1,0:T(8,128)(2,1)S(1)} %copy-done), channel_id=1, source_target_pairs={{0,1},{1,0},{2,3},{3,2},{4,5},{5,4},{6,7},{7,6},{8,9},{9,8},{10,11... | collective-permute-start | bytes 393224 | tf_op jit(solution)/shard_map/ppermute | solution.py:447
  13.4 4.1 %collective-permute-start.3 = (bf16[4,8,2048]{2,1,0:T(8,128)(2,1)S(1)}, bf16[4,8,2048]{2,1,0:T(8,128)(2,1)S(1)}, u32[]{:S(2)}, u32[]{:S(2)}) collective-permute-start(bf16[4,8,2048]{2,1,0:T(8,128)(2,1)S(1)} %collective-permute-done.1.rest_1_), channel_id=1, source_target_pairs={{0,1},{1,0},{2,3},{3,2},{4,5},{5,4},{6,7},{7,6},{8,9},{9,8},{10,11... | collective-permute-start | bytes 393224 | tf_op jit(solution)/shard_map/ppermute | solution.py:447
  18.2 3.6 %collective-permute-start.8 = (f32[32,32]{1,0:T(8,128)S(1)}, f32[32,32]{1,0:T(8,128)S(1)}, u32[]{:S(2)}, u32[]{:S(2)}) collective-permute-start(f32[32,32]{1,0:T(8,128)S(1)} %get-tuple-element.56.rest_6_), channel_id=1, source_target_pairs={{0,3},{1,2},{2,1},{3,0},{4,7},{5,6},{6,5},{7,4},{8,11},{9,10},{10,... | collective-permute-start | bytes 12296 | tf_op jit(solution)/shard_map/ppermute | solution.py:447
  18.9 3.9 %collective-permute-start.7 = (f32[32,32]{1,0:T(8,128)S(1)}, f32[32,32]{1,0:T(8,128)S(1)}, u32[]{:S(2)}, u32[]{:S(2)}) collective-permute-start(f32[32,32]{1,0:T(8,128)S(1)} %get-tuple-element.56.rest_6_), channel_id=1, source_target_pairs={{0,2},{1,3},{2,0},{3,1},{4,6},{5,7},{6,4},{7,5},{8,10},{9,11},{10,... | collective-permute-start | bytes 12296 | tf_op jit(solution)/shard_map/ppermute | solution.py:447
  19.9 2.9 %collective-permute-start.6 = (f32[32,32]{1,0:T(8,128)S(1)}, f32[32,32]{1,0:T(8,128)S(1)}, u32[]{:S(2)}, u32[]{:S(2)}) collective-permute-start(f32[32,32]{1,0:T(8,128)S(1)} %get-tuple-element.56.rest_6_), channel_id=1, source_target_pairs={{0,1},{1,0},{2,3},{3,2},{4,5},{5,4},{6,7},{7,6},{8,9},{9,8},{10,11... | collective-permute-start | bytes 12296 | tf_op jit(solution)/shard_map/ppermute | solution.py:447

commit v20 on v19

--- a/solution.py
+++ b/solution.py
@@ -46,6 +46,7 @@
 
 
 def cache_kernel(
+    near,
     lengths_ref,
     query_ref,
     key_ref,
@@ -53,6 +54,8 @@
     gain_ref,
     bias_ref,
     hidden_ref,
+    weight_ref,
+    near_out,
     gain_out,
     bias_out,
     hidden_out,
@@ -67,6 +70,7 @@
     value_buffer,
     score_buffer,
     sems,
+    weight_sems,
 ):
     steps, rows, query_width = query_ref.shape
     cache_span = key_ref.shape[1]
@@ -89,6 +93,7 @@
     copies = [pltpu.make_async_copy(*pair, sems.at[i]) for i, pair in enumerate(copies)]
     for copy in copies:
         copy.start()
+    copies += copy_blocks(near, hidden_ref.shape[2], weight_ref, near_out, weight_sems)
 
     copies[0].wait()
     copies[1].wait()
@@ -132,16 +137,18 @@
         copy.wait()
 
 
-def cache_call(lengths, queries, keys, values, gain, bias, hidden):
+def cache_call(near, lengths, queries, keys, values, gain, bias, hidden, weight):
     steps, rows, query_width = queries.shape
     cache_span, key_width = keys.shape[1:]
     groups = key_width // HD
     lines = steps * (query_width // key_width)
     block = (groups, lines * rows, HD)
-    operands = (lengths, queries, keys, values, gain, bias, hidden)
+    operands = (lengths, queries, keys, values, gain, bias, hidden, weight)
+    near_weight = (len(near) * hidden.shape[2],) + weight.shape[1:]
     return pl.pallas_call(
-        cache_kernel,
+        functools.partial(cache_kernel, near),
         out_shape=(
+            pltpu.VMEM(near_weight, weight.dtype),
             pltpu.VMEM(gain.shape, jnp.float32),
             pltpu.VMEM(bias.shape, bias.dtype),
             pltpu.VMEM(hidden.shape, hidden.dtype),
@@ -151,7 +158,7 @@
             pltpu.VMEM(block, jnp.float32),
         ),
         in_specs=[HBM] * len(operands),
-        out_specs=(VMEM,) * 7,
+        out_specs=(VMEM,) * 8,
         scratch_shapes=[
             pltpu.SMEM(lengths.shape, jnp.int32),
             pltpu.VMEM(queries.shape, queries.dtype),
@@ -160,6 +167,7 @@
             pltpu.VMEM(values.shape, values.dtype),
             pltpu.VMEM((rows * groups, lines, cache_span), jnp.float32),
             pltpu.SemaphoreType.DMA((9,)),
+            pltpu.SemaphoreType.DMA((len(near),)),
         ],
         compiler_params=pltpu.CompilerParams(vmem_limit_bytes=16 << 20),
         cost_estimate=pl.CostEstimate(flops=2 * 67 << 20, bytes_accessed=5 << 20, transcendentals=0),
@@ -231,15 +239,14 @@
         sin_out[pl.ds(step * rows, rows)] = jnp.where(second, sine, -sine)
 
 
-def scale_kernel(early, near, far, lengths_ref, weight_ref, gain_ref, *rest):
-    scaled_out, early_out, square_out, near_weight, far_weight, cos_out, sin_out = rest[-11:-4]
-    lengths, length_sem, near_sems, far_sems = rest[-4:]
-    parts = rest[:-11]
+def scale_kernel(early, far, lengths_ref, weight_ref, gain_ref, *rest):
+    scaled_out, early_out, square_out, far_weight, cos_out, sin_out = rest[-9:-3]
+    lengths, length_sem, far_sems = rest[-3:]
+    parts = rest[:-9]
     steps, rows, width = parts[0].shape
     length_copy = pltpu.make_async_copy(lengths_ref, lengths, length_sem)
     length_copy.start()
-    copies = copy_blocks(near, width, weight_ref, near_weight, near_sems)
-    copies += copy_blocks(far, width, weight_ref, far_weight, far_sems)
+    copies = copy_blocks(far, width, weight_ref, far_weight, far_sems)
     me = lax.axis_index("tp")
     scaled_out[...] = jnp.zeros_like(scaled_out)
     total = None
@@ -256,26 +263,24 @@
         copy.wait()
 
 
-def scale_call(early, near, far, lengths, weight, gain, parts):
+def scale_call(early, blocks, far, lengths, weight, gain, parts):
     steps, rows, width = parts[0].shape
     count = steps * rows
     return pl.pallas_call(
-        functools.partial(scale_kernel, early, near, far),
+        functools.partial(scale_kernel, early, far),
         out_shape=(
-            pltpu.VMEM((count, (len(near) + len(far)) * width), jnp.bfloat16),
+            pltpu.VMEM((count, blocks * width), jnp.bfloat16),
             pltpu.VMEM((count, len(early) * width), jnp.bfloat16),
             pltpu.VMEM((count, HD), jnp.float32),
-            pltpu.VMEM((len(near) * width,) + weight.shape[1:], weight.dtype),
             pltpu.VMEM((len(far) * width,) + weight.shape[1:], weight.dtype),
             pltpu.VMEM((count, HD), jnp.float32),
             pltpu.VMEM((count, HD), jnp.float32),
         ),
         in_specs=[HBM] * 2 + [VMEM] * (1 + len(parts)),
-        out_specs=(VMEM,) * 7,
+        out_specs=(VMEM,) * 6,
         scratch_shapes=[
             pltpu.SMEM(lengths.shape, jnp.int32),
             pltpu.SemaphoreType.DMA,
-            pltpu.SemaphoreType.DMA((len(near),)),
             pltpu.SemaphoreType.DMA((len(far),)),
         ],
         compiler_params=pltpu.CompilerParams(vmem_limit_bytes=8 << 20),
@@ -474,16 +479,24 @@
         first = swap(pack, "wide", 1, wide_count)
     near, far = (0, 1), (2, 3)
     early, late = (0, 2), (1, 3)
-    gain_rows, bias, mine, *cached = cache_call(
-        lengths, queries, stored_rotated_keys, stored_value_rows, gain, key_value_bias, hidden
+    near_weight, gain_rows, bias, mine, *cached = cache_call(
+        near,
+        lengths,
+        queries,
+        stored_rotated_keys,
+        stored_value_rows,
+        gain,
+        key_value_bias,
+        hidden,
+        key_value_weight,
     )
     relayed, gain_rows = lax.optimization_barrier((crossed, gain_rows))
     relayed = swap(relayed, "tp", 1, tp_count)
     if direct:
         third, gain_rows = lax.optimization_barrier((second, gain_rows))
         packs = [pack, first, second, swap(third, "wide", 1, wide_count)]
-    scaled, early_scaled, square, near_weight, far_weight, *tables = scale_call(
-        early, near, far, lengths, key_value_weight, gain_rows, (mine, crossed)
+    scaled, early_scaled, square, far_weight, *tables = scale_call(
+        early, tp_count, far, lengths, key_value_weight, gain_rows, (mine, crossed)
     )
     late_parts = (beside, relayed)
     if direct:

time: 24.5 us -> 23.8 us (0.971)
  Pallas kernels: 9.37 us -> 8.78 us
    pallas_call x2, Pallas kernels: 6.57 us -> 5.99 us  [the longest x1 3.73 us: cache_call(): pl.pallas_call(functools.partial(cache_kernel, near), out_shape=(pltpu.VM...]
  transfers between devices with their start and end apart: 9 -> 9, of which waited for: 3 -> 3; matrix products, arithmetic and copies ran while one was open for 7% -> 7% of each run, Pallas kernels for 27% -> 26%
where the time goes in v20:
time: 23.8 us; the launch traced here: 23.6 us
  starting transfers between devices  10.2 us (43%)
  Pallas kernels  8.78 us (37%)
  waiting for transfers between devices  2.2 us (9%)
  matrix products  1.67 us (7%)
  between operations  0.72 us (3%)
    ppermute x9, starting transfers between devices, swap(): return lax.ppermute(block, axis, [(i, i ^ offset) for i in range(count)])  10.2 us
    pallas_call x1, Pallas kernels, cache_call(): pl.pallas_call(functools.partial(cache_kernel, near), out_shape=(pltpu.VM...  3.73 us
    pallas_call x1, Pallas kernels, scale_call(): pl.pallas_call(functools.partial(scale_kernel, early, far), out_shape=(pl...  2.26 us
    ppermute x9, waiting for transfers between devices, swap(): return lax.ppermute(block, axis, [(i, i ^ offset) for i in range(count)])  2.2 us
    dot_general x2, matrix products, dot(): jnp.einsum('md,dkc->kmc', rows, weight, preferred_element_type=jnp.float32)  1.67 us
    pallas_call x1, Pallas kernels, final_call(): pl.pallas_call(functools.partial(final_kernel, width, len(inner)), out_sh...  1.55 us
    pallas_call x1, Pallas kernels, pack_call(): pl.pallas_call(pack_kernel, out_shape=pltpu.VMEM((kinds, share, down.shap...  0.87 us
  transfers between devices with their start and end apart: 9, of which 3 were waited for; matrix products, arithmetic and copies ran while one was open for 7% of the time, Pallas kernels for 26%

profile of v20, /device:TPU:0, one launch (start us, length us, event | category | flops | bytes accessed | tf_op | source)
XLA Modules:
  0.0 23.6 jit_solution(11167310149897985828)
XLA Ops:
  0.6 0.9 %pack_factors.1.rest_2_.refs_0_ = bf16[2,16,2304]{2,1,0:T(8,128)(2,1)S(1)} custom-call(bf16[2,64,2048]{2,1,0:T(8,128)(2,1)} %down_ref.1, bf16[2,16,256]{2,1,0:T(8,128)(2,1)} %bitcast.13), custom_call_target="tpu_custom_call" | custom-call | tf_op jit(solution)/shard_map/pack_factors/pallas_call | solution.py:201
  1.5 4.1 %collective-permute-start = (bf16[2,16,2304]{2,1,0:T(8,128)(2,1)S(1)}, bf16[2,16,2304]{2,1,0:T(8,128)(2,1)S(1)}, u32[]{:S(2)}, u32[]{:S(2)}) collective-permute-start(bf16[2,16,2304]{2,1,0:T(8,128)(2,1)S(1)} %pack_factors.1.rest_2_.refs_0_), channel_id=1, source_target_pairs={{0,8},{4,12},{8,0},{12,4},{1,9},{5,13},{9,1},{13,5},{2,10},{6,14},... | collective-permute-start | bytes 442376 | tf_op jit(solution)/shard_map/ppermute | solution.py:452
  5.6 1.5 %collective-permute-start.1 = (bf16[4,8,2048]{2,1,0:T(8,128)(2,1)}, bf16[4,8,2048]{2,1,0:T(8,128)(2,1)S(1)}, u32[]{:S(2)}, u32[]{:S(2)}) collective-permute-start(bf16[4,8,2048]{2,1,0:T(8,128)(2,1)} %hidden_ref.1), channel_id=1, source_target_pairs={{0,2},{1,3},{2,0},{3,1},{4,6},{5,7},{6,4},{7,5},{8,10},{9,11},{10,... | collective-permute-start | bytes 393224 | tf_op jit(solution)/shard_map/ppermute | solution.py:452
  7.1 1.6 %collective-permute-start.4 = (bf16[2,16,2304]{2,1,0:T(8,128)(2,1)S(1)}, bf16[2,16,2304]{2,1,0:T(8,128)(2,1)S(1)}, u32[]{:S(2)}, u32[]{:S(2)}) collective-permute-start(bf16[2,16,2304]{2,1,0:T(8,128)(2,1)S(1)} %pack_factors.1.rest_2_.refs_0_), channel_id=1, source_target_pairs={{0,4},{4,0},{8,12},{12,8},{1,5},{5,1},{9,13},{13,9},{2,6},{6,2},{1... | collective-permute-start | bytes 442376 | tf_op jit(solution)/shard_map/ppermute | solution.py:452
  8.7 0.0 copy-start
  8.7 3.7 %cache_attention.1 = (bf16[4096,2,256]{2,1,0:T(2,128)(2,1)S(1)}, f32[64,128]{1,0:T(8,128)S(1)}, bf16[2,256]{1,0:T(2,128)(2,1)S(1)}, bf16[4,8,2048]{2,1,0:T(8,128...) custom-call(s32[8]{0:T(128)} %lengths_ref.3, ...), custom_call_target="tpu_custom_call" | custom-call | flops 140509184 | bytes 5242880 | tf_op jit(solution)/shard_map/cache_attention/pallas_call | solution.py:148
  12.4 0.0 collective-permute-done.1.rest_1_
  12.4 0.3 %collective-permute-done.rest_4_.refs_2_ = bf16[2,16,2304]{2,1,0:T(8,128)(2,1)S(1)} collective-permute-done((bf16[2,16,2304]{2,1,0:T(8,128)(2,1)S(1)}, bf16[2,16,2304]{2,1,0:T(8,128)(2,1)S(1)}, u32[]{:S(2)}, u32[]{:S(2)}) %collective-permute-start) | collective-permute-done | bytes 147488 | tf_op jit(solution)/shard_map/ppermute | solution.py:452
  12.7 0.7 %collective-permute-start.5 = (bf16[2,16,2304]{2,1,0:T(8,128)(2,1)S(1)}, bf16[2,16,2304]{2,1,0:T(8,128)(2,1)S(1)}, u32[]{:S(2)}, u32[]{:S(2)}) collective-permute-start(bf16[2,16,2304]{2,1,0:T(8,128)(2,1)S(1)} %collective-permute-done.rest_4_.refs_2_), channel_id=1, source_target_pairs={{0,4},{4,0},{8,12},{12,8},{1,5},{5,1},{9,13},{13,9},{2,6},{6,2},{1... | collective-permute-start | bytes 442376 | tf_op jit(solution)/shard_map/ppermute | solution.py:452
  13.4 0.0 copy-done
  13.4 0.0 collective-permute-start.2
  13.4 0.5 %collective-permute-start.3 = (bf16[4,8,2048]{2,1,0:T(8,128)(2,1)S(1)}, bf16[4,8,2048]{2,1,0:T(8,128)(2,1)S(1)}, u32[]{:S(2)}, u32[]{:S(2)}) collective-permute-start(bf16[4,8,2048]{2,1,0:T(8,128)(2,1)S(1)} %collective-permute-done.1.rest_1_), channel_id=1, source_target_pairs={{0,1},{1,0},{2,3},{3,2},{4,5},{5,4},{6,7},{7,6},{8,9},{9,8},{10,11... | collective-permute-start | bytes 393224 | tf_op jit(solution)/shard_map/ppermute | solution.py:452
  13.9 2.3 %scale_features.1 = (bf16[32,8192]{1,0:T(8,128)(2,1)S(1)}, bf16[32,4096]{1,0:T(8,128)(2,1)S(1)}, f32[32,128]{1,0:T(8,128)S(1)}, bf16[4096,2,256]{2,1,0:T(2,128)(...) custom-call(s32[8]{0:T(128)} %lengths_ref.3, bf16[8192,2,256]{2,1,0:T(2,128)(2,1)} %weight_ref.3, ...), custom_call_target="tpu_custom_call" | custom-call | bytes 9437184 | tf_op jit(solution)/shard_map/scale_features/pallas_call | solution.py:269
  16.2 0.0 collective-permute-done.2.rest_0_
  16.2 0.0 collective-permute-done.4.rest_3_.refs_1_
  16.2 0.0 collective-permute-done.3.rest_1_
  16.2 1.7 %collective-permute-done.5.rest_5_.refs_3_ = bf16[2,16,2304]{2,1,0:T(8,128)(2,1)S(1)} collective-permute-done((bf16[2,16,2304]{2,1,0:T(8,128)(2,1)S(1)}, bf16[2,16,2304]{2,1,0:T(8,128)(2,1)S(1)}, u32[]{:S(2)}, u32[]{:S(2)}) %collective-permute-start.5) | collective-permute-done | bytes 147488 | tf_op jit(solution)/shard_map/ppermute | solution.py:452
  17.9 0.3 %rank_inner.1 = (f32[32,32]{1,0:T(8,128)S(1)}, bf16[32,4096]{1,0:T(8,128)(2,1)S(1)}, bf16[32,4096]{1,0:T(8,128)(2,1)S(1)}, f32[32,128]{1,0:T(8,128)S(1)}) custom-call(bf16[32,8192]{1,0:T(8,128)(2,1)S(1)} %get-tuple-element.37.scaled_ref, bf16[32,4096]{1,0:T(8,128)(2,1)S(1)} %get-tuple-element.38.early_ref, f32[32,128]{1,0:T(8,128)S(1)} %get-tuple-element.39.square_ref, ...), custom_call_target="tpu_custom_call" | custom-call | tf_op jit(solution)/shard_map/rank_inner/pallas_call | solution.py:335
  18.2 0.0 collective-permute-start.8
  18.2 1.6 %collective-permute-start.7 = (f32[32,32]{1,0:T(8,128)S(1)}, f32[32,32]{1,0:T(8,128)S(1)}, u32[]{:S(2)}, u32[]{:S(2)}) collective-permute-start(f32[32,32]{1,0:T(8,128)S(1)} %get-tuple-element.56.rest_6_), channel_id=1, source_target_pairs={{0,2},{1,3},{2,0},{3,1},{4,6},{5,7},{6,4},{7,5},{8,10},{9,11},{10,... | collective-permute-start | bytes 12296 | tf_op jit(solution)/shard_map/ppermute | solution.py:452
  19.8 0.2 %collective-permute-start.6 = (f32[32,32]{1,0:T(8,128)S(1)}, f32[32,32]{1,0:T(8,128)S(1)}, u32[]{:S(2)}, u32[]{:S(2)}) collective-permute-start(f32[32,32]{1,0:T(8,128)S(1)} %get-tuple-element.56.rest_6_), channel_id=1, source_target_pairs={{0,1},{1,0},{2,3},{3,2},{4,5},{5,4},{6,7},{7,6},{8,9},{9,8},{10,11... | collective-permute-start | bytes 12296 | tf_op jit(solution)/shard_map/ppermute | solution.py:452
  20.1 0.8 %fusion.7.far_ref = f32[2,32,256]{2,1,0:T(8,128)S(1)} fusion(bf16[4096,2,256]{2,1,0:T(2,128)(2,1)S(1)} %get-tuple-element.46, bf16[32,4096]{1,0:T(8,128)(2,1)S(1)} %get-tuple-element.47), kind=kOutput, calls=%fused_computation.5 | convolution fusion | flops 134217728 | bytes 4521984 | tf_op jit(solution)/shard_map/md,dkc->kmc/dot_general | solution.py:448
  20.9 0.8 %fusion.4.near_ref = f32[2,32,256]{2,1,0:T(8,128)S(1)} fusion(bf16[4096,2,256]{2,1,0:T(2,128)(2,1)S(1)} %get-tuple-element.32, bf16[32,4096]{1,0:T(8,128)(2,1)S(1)} %get-tuple-element.45), kind=kOutput, calls=%fused_computation.4 | convolution fusion | flops 134217728 | bytes 4521984 | tf_op jit(solution)/shard_map/md,dkc->kmc/dot_general | solution.py:448
  21.8 0.0 collective-permute-done.8.rest_9_
  21.8 0.2 collective-permute-done.7.rest_8_
  22.0 0.0 collective-permute-done.6.rest_7_
  22.0 1.6 %fresh_attention.1 = (bf16[4,8,256]{2,1,0:T(8,128)(2,1)}, bf16[4,8,256]{2,1,0:T(8,128)(2,1)}, bf16[4,8,2048]{2,1,0:T(8,128)(2,1)}) custom-call(f32[2,32,256]{2,1,0:T(8,128)S(1)} %fusion.4.near_ref, f32[2,32,256]{2,1,0:T(8,128)S(1)} %fusion.7.far_ref, f32[32,128]{1,0:T(8,128)S(1)} %get-tuple-element.48.square_ref, ...), custom_call_target="tpu_custom_call" | custom-call | tf_op jit(solution)/shard_map/fresh_attention/pallas_call | solution.py:436
  (1 shorter events, 0.0 us)
Async XLA Ops:
  1.5 11.2 %collective-permute-start = (bf16[2,16,2304]{2,1,0:T(8,128)(2,1)S(1)}, bf16[2,16,2304]{2,1,0:T(8,128)(2,1)S(1)}, u32[]{:S(2)}, u32[]{:S(2)}) collective-permute-start(bf16[2,16,2304]{2,1,0:T(8,128)(2,1)S(1)} %pack_factors.1.rest_2_.refs_0_), channel_id=1, source_target_pairs={{0,8},{4,12},{8,0},{12,4},{1,9},{5,13},{9,1},{13,5},{2,10},{6,14},... | collective-permute-start | bytes 442376 | tf_op jit(solution)/shard_map/ppermute | solution.py:452
  5.6 6.8 %collective-permute-start.1 = (bf16[4,8,2048]{2,1,0:T(8,128)(2,1)}, bf16[4,8,2048]{2,1,0:T(8,128)(2,1)S(1)}, u32[]{:S(2)}, u32[]{:S(2)}) collective-permute-start(bf16[4,8,2048]{2,1,0:T(8,128)(2,1)} %hidden_ref.1), channel_id=1, source_target_pairs={{0,2},{1,3},{2,0},{3,1},{4,6},{5,7},{6,4},{7,5},{8,10},{9,11},{10,... | collective-permute-start | bytes 393224 | tf_op jit(solution)/shard_map/ppermute | solution.py:452
  7.1 9.1 %collective-permute-start.4 = (bf16[2,16,2304]{2,1,0:T(8,128)(2,1)S(1)}, bf16[2,16,2304]{2,1,0:T(8,128)(2,1)S(1)}, u32[]{:S(2)}, u32[]{:S(2)}) collective-permute-start(bf16[2,16,2304]{2,1,0:T(8,128)(2,1)S(1)} %pack_factors.1.rest_2_.refs_0_), channel_id=1, source_target_pairs={{0,4},{4,0},{8,12},{12,8},{1,5},{5,1},{9,13},{13,9},{2,6},{6,2},{1... | collective-permute-start | bytes 442376 | tf_op jit(solution)/shard_map/ppermute | solution.py:452
  8.7 4.7 %copy-start = (bf16[4,8,2048]{2,1,0:T(8,128)(2,1)S(1)}, bf16[4,8,2048]{2,1,0:T(8,128)(2,1)}, u32[]{:S(2)}) copy-start(bf16[4,8,2048]{2,1,0:T(8,128)(2,1)} %hidden_ref.1) | copy-start | bytes 393220
  12.7 5.1 %collective-permute-start.5 = (bf16[2,16,2304]{2,1,0:T(8,128)(2,1)S(1)}, bf16[2,16,2304]{2,1,0:T(8,128)(2,1)S(1)}, u32[]{:S(2)}, u32[]{:S(2)}) collective-permute-start(bf16[2,16,2304]{2,1,0:T(8,128)(2,1)S(1)} %collective-permute-done.rest_4_.refs_2_), channel_id=1, source_target_pairs={{0,4},{4,0},{8,12},{12,8},{1,5},{5,1},{9,13},{13,9},{2,6},{6,2},{1... | collective-permute-start | bytes 442376 | tf_op jit(solution)/shard_map/ppermute | solution.py:452
  13.4 2.8 %collective-permute-start.2 = (bf16[4,8,2048]{2,1,0:T(8,128)(2,1)S(1)}, bf16[4,8,2048]{2,1,0:T(8,128)(2,1)S(1)}, u32[]{:S(2)}, u32[]{:S(2)}) collective-permute-start(bf16[4,8,2048]{2,1,0:T(8,128)(2,1)S(1)} %copy-done), channel_id=1, source_target_pairs={{0,1},{1,0},{2,3},{3,2},{4,5},{5,4},{6,7},{7,6},{8,9},{9,8},{10,11... | collective-permute-start | bytes 393224 | tf_op jit(solution)/shard_map/ppermute | solution.py:452
  13.4 2.8 %collective-permute-start.3 = (bf16[4,8,2048]{2,1,0:T(8,128)(2,1)S(1)}, bf16[4,8,2048]{2,1,0:T(8,128)(2,1)S(1)}, u32[]{:S(2)}, u32[]{:S(2)}) collective-permute-start(bf16[4,8,2048]{2,1,0:T(8,128)(2,1)S(1)} %collective-permute-done.1.rest_1_), channel_id=1, source_target_pairs={{0,1},{1,0},{2,3},{3,2},{4,5},{5,4},{6,7},{7,6},{8,9},{9,8},{10,11... | collective-permute-start | bytes 393224 | tf_op jit(solution)/shard_map/ppermute | solution.py:452
  18.2 3.6 %collective-permute-start.8 = (f32[32,32]{1,0:T(8,128)S(1)}, f32[32,32]{1,0:T(8,128)S(1)}, u32[]{:S(2)}, u32[]{:S(2)}) collective-permute-start(f32[32,32]{1,0:T(8,128)S(1)} %get-tuple-element.56.rest_6_), channel_id=1, source_target_pairs={{0,3},{1,2},{2,1},{3,0},{4,7},{5,6},{6,5},{7,4},{8,11},{9,10},{10,... | collective-permute-start | bytes 12296 | tf_op jit(solution)/shard_map/ppermute | solution.py:452
  18.2 3.8 %collective-permute-start.7 = (f32[32,32]{1,0:T(8,128)S(1)}, f32[32,32]{1,0:T(8,128)S(1)}, u32[]{:S(2)}, u32[]{:S(2)}) collective-permute-start(f32[32,32]{1,0:T(8,128)S(1)} %get-tuple-element.56.rest_6_), channel_id=1, source_target_pairs={{0,2},{1,3},{2,0},{3,1},{4,6},{5,7},{6,4},{7,5},{8,10},{9,11},{10,... | collective-permute-start | bytes 12296 | tf_op jit(solution)/shard_map/ppermute | solution.py:452
  19.8 2.2 %collective-permute-start.6 = (f32[32,32]{1,0:T(8,128)S(1)}, f32[32,32]{1,0:T(8,128)S(1)}, u32[]{:S(2)}, u32[]{:S(2)}) collective-permute-start(f32[32,32]{1,0:T(8,128)S(1)} %get-tuple-element.56.rest_6_), channel_id=1, source_target_pairs={{0,1},{1,0},{2,3},{3,2},{4,5},{5,4},{6,7},{7,6},{8,9},{9,8},{10,11... | collective-permute-start | bytes 12296 | tf_op jit(solution)/shard_map/ppermute | solution.py:452

commit v21 on v20

--- a/solution.py
+++ b/solution.py
@@ -368,6 +368,12 @@
     )(*packs)
 
 
+def split_index(index, count):
+    if count & (count - 1) == 0:
+        return index >> (count.bit_length() - 1), index & (count - 1)
+    return index // count, index % count
+
+
 def final_kernel(width, blocks, near_ref, far_ref, square_ref, bias_ref, *rest):
     query_ref, acc_ref, top_ref, total_ref, cos_ref, sin_ref = rest[:6]
     inner_refs = rest[6 : 6 + blocks]
@@ -397,7 +403,10 @@
     cosine, sine = cos_ref[...], sin_ref[...]
     line = lax.broadcasted_iota(jnp.int32, (size, count), 0)
     other = lax.broadcasted_iota(jnp.int32, (size, count), 1)
-    live = (line % rows == other % rows) & (other // rows <= line // rows % steps)
+    line_step, line_row = split_index(line, rows)
+    other_step, other_row = split_index(other, rows)
+    line_step = split_index(line_step, steps)[1]
+    live = (line_row == other_row) & (other_step <= line_step)
     for group in range(groups):
         at = slice(group * HD, (group + 1) * HD)
         key = linear[0][:, at]
@@ -421,7 +430,7 @@
         acc = acc_ref[group] * keep + jnp.dot(
             exps.astype(jnp.bfloat16), value, preferred_element_type=jnp.float32
         )
-        attended = (acc / total).astype(jnp.bfloat16)
+        attended = (acc * (1.0 / total)).astype(jnp.bfloat16)
         for head in range(per_group):
             lanes = pl.ds((group * per_group + head) * HD, HD)
             for step in range(steps):

time: 23.8 us -> 23.8 us (level)
  no operation moved by 1% of the time
where the time goes in v21:
time: 23.8 us; the launch traced here: 23.6 us
  starting transfers between devices  10.2 us (43%)
  Pallas kernels  8.78 us (37%)
  waiting for transfers between devices  2.2 us (9%)
  matrix products  1.67 us (7%)
  between operations  0.72 us (3%)
    ppermute x9, starting transfers between devices, swap(): return lax.ppermute(block, axis, [(i, i ^ offset) for i in range(count)])  10.2 us
    pallas_call x1, Pallas kernels, cache_call(): pl.pallas_call(functools.partial(cache_kernel, near), out_shape=(pltpu.VM...  3.73 us
    pallas_call x1, Pallas kernels, scale_call(): pl.pallas_call(functools.partial(scale_kernel, early, far), out_shape=(pl...  2.26 us
    ppermute x9, waiting for transfers between devices, swap(): return lax.ppermute(block, axis, [(i, i ^ offset) for i in range(count)])  2.2 us
    dot_general x2, matrix products, dot(): jnp.einsum('md,dkc->kmc', rows, weight, preferred_element_type=jnp.float32)  1.67 us
    pallas_call x1, Pallas kernels, final_call(): pl.pallas_call(functools.partial(final_kernel, width, len(inner)), out_sh...  1.55 us
    pallas_call x1, Pallas kernels, pack_call(): pl.pallas_call(pack_kernel, out_shape=pltpu.VMEM((kinds, share, down.shap...  0.87 us
  transfers between devices with their start and end apart: 9, of which 3 were waited for; matrix products, arithmetic and copies ran while one was open for 7% of the time, Pallas kernels for 26%

profile of v21, /device:TPU:0, one launch (start us, length us, event | category | flops | bytes accessed | tf_op | source)
XLA Modules:
  0.0 23.6 jit_solution(13679987880669171623)
XLA Ops:
  0.6 0.9 %pack_factors.1.rest_2_.refs_0_ = bf16[2,16,2304]{2,1,0:T(8,128)(2,1)S(1)} custom-call(bf16[2,64,2048]{2,1,0:T(8,128)(2,1)} %down_ref.1, bf16[2,16,256]{2,1,0:T(8,128)(2,1)} %bitcast.13), custom_call_target="tpu_custom_call" | custom-call | tf_op jit(solution)/shard_map/pack_factors/pallas_call | solution.py:201
  1.5 4.1 %collective-permute-start = (bf16[2,16,2304]{2,1,0:T(8,128)(2,1)S(1)}, bf16[2,16,2304]{2,1,0:T(8,128)(2,1)S(1)}, u32[]{:S(2)}, u32[]{:S(2)}) collective-permute-start(bf16[2,16,2304]{2,1,0:T(8,128)(2,1)S(1)} %pack_factors.1.rest_2_.refs_0_), channel_id=1, source_target_pairs={{0,8},{4,12},{8,0},{12,4},{1,9},{5,13},{9,1},{13,5},{2,10},{6,14},... | collective-permute-start | bytes 442376 | tf_op jit(solution)/shard_map/ppermute | solution.py:461
  5.6 1.5 %collective-permute-start.1 = (bf16[4,8,2048]{2,1,0:T(8,128)(2,1)}, bf16[4,8,2048]{2,1,0:T(8,128)(2,1)S(1)}, u32[]{:S(2)}, u32[]{:S(2)}) collective-permute-start(bf16[4,8,2048]{2,1,0:T(8,128)(2,1)} %hidden_ref.1), channel_id=1, source_target_pairs={{0,2},{1,3},{2,0},{3,1},{4,6},{5,7},{6,4},{7,5},{8,10},{9,11},{10,... | collective-permute-start | bytes 393224 | tf_op jit(solution)/shard_map/ppermute | solution.py:461
  7.1 1.6 %collective-permute-start.4 = (bf16[2,16,2304]{2,1,0:T(8,128)(2,1)S(1)}, bf16[2,16,2304]{2,1,0:T(8,128)(2,1)S(1)}, u32[]{:S(2)}, u32[]{:S(2)}) collective-permute-start(bf16[2,16,2304]{2,1,0:T(8,128)(2,1)S(1)} %pack_factors.1.rest_2_.refs_0_), channel_id=1, source_target_pairs={{0,4},{4,0},{8,12},{12,8},{1,5},{5,1},{9,13},{13,9},{2,6},{6,2},{1... | collective-permute-start | bytes 442376 | tf_op jit(solution)/shard_map/ppermute | solution.py:461
  8.7 0.0 copy-start
  8.7 3.7 %cache_attention.1 = (bf16[4096,2,256]{2,1,0:T(2,128)(2,1)S(1)}, f32[64,128]{1,0:T(8,128)S(1)}, bf16[2,256]{1,0:T(2,128)(2,1)S(1)}, bf16[4,8,2048]{2,1,0:T(8,128...) custom-call(s32[8]{0:T(128)} %lengths_ref.3, ...), custom_call_target="tpu_custom_call" | custom-call | flops 140509184 | bytes 5242880 | tf_op jit(solution)/shard_map/cache_attention/pallas_call | solution.py:148
  12.4 0.0 collective-permute-done.1.rest_1_
  12.4 0.3 %collective-permute-done.rest_4_.refs_2_ = bf16[2,16,2304]{2,1,0:T(8,128)(2,1)S(1)} collective-permute-done((bf16[2,16,2304]{2,1,0:T(8,128)(2,1)S(1)}, bf16[2,16,2304]{2,1,0:T(8,128)(2,1)S(1)}, u32[]{:S(2)}, u32[]{:S(2)}) %collective-permute-start) | collective-permute-done | bytes 147488 | tf_op jit(solution)/shard_map/ppermute | solution.py:461
  12.7 0.7 %collective-permute-start.5 = (bf16[2,16,2304]{2,1,0:T(8,128)(2,1)S(1)}, bf16[2,16,2304]{2,1,0:T(8,128)(2,1)S(1)}, u32[]{:S(2)}, u32[]{:S(2)}) collective-permute-start(bf16[2,16,2304]{2,1,0:T(8,128)(2,1)S(1)} %collective-permute-done.rest_4_.refs_2_), channel_id=1, source_target_pairs={{0,4},{4,0},{8,12},{12,8},{1,5},{5,1},{9,13},{13,9},{2,6},{6,2},{1... | collective-permute-start | bytes 442376 | tf_op jit(solution)/shard_map/ppermute | solution.py:461
  13.4 0.0 copy-done
  13.4 0.0 collective-permute-start.2
  13.4 0.5 %collective-permute-start.3 = (bf16[4,8,2048]{2,1,0:T(8,128)(2,1)S(1)}, bf16[4,8,2048]{2,1,0:T(8,128)(2,1)S(1)}, u32[]{:S(2)}, u32[]{:S(2)}) collective-permute-start(bf16[4,8,2048]{2,1,0:T(8,128)(2,1)S(1)} %collective-permute-done.1.rest_1_), channel_id=1, source_target_pairs={{0,1},{1,0},{2,3},{3,2},{4,5},{5,4},{6,7},{7,6},{8,9},{9,8},{10,11... | collective-permute-start | bytes 393224 | tf_op jit(solution)/shard_map/ppermute | solution.py:461
  13.9 2.3 %scale_features.1 = (bf16[32,8192]{1,0:T(8,128)(2,1)S(1)}, bf16[32,4096]{1,0:T(8,128)(2,1)S(1)}, f32[32,128]{1,0:T(8,128)S(1)}, bf16[4096,2,256]{2,1,0:T(2,128)(...) custom-call(s32[8]{0:T(128)} %lengths_ref.3, bf16[8192,2,256]{2,1,0:T(2,128)(2,1)} %weight_ref.3, ...), custom_call_target="tpu_custom_call" | custom-call | bytes 9437184 | tf_op jit(solution)/shard_map/scale_features/pallas_call | solution.py:269
  16.2 0.0 collective-permute-done.2.rest_0_
  16.2 0.0 collective-permute-done.4.rest_3_.refs_1_
  16.2 0.0 collective-permute-done.3.rest_1_
  16.2 1.7 %collective-permute-done.5.rest_5_.refs_3_ = bf16[2,16,2304]{2,1,0:T(8,128)(2,1)S(1)} collective-permute-done((bf16[2,16,2304]{2,1,0:T(8,128)(2,1)S(1)}, bf16[2,16,2304]{2,1,0:T(8,128)(2,1)S(1)}, u32[]{:S(2)}, u32[]{:S(2)}) %collective-permute-start.5) | collective-permute-done | bytes 147488 | tf_op jit(solution)/shard_map/ppermute | solution.py:461
  17.9 0.3 %rank_inner.1 = (f32[32,32]{1,0:T(8,128)S(1)}, bf16[32,4096]{1,0:T(8,128)(2,1)S(1)}, bf16[32,4096]{1,0:T(8,128)(2,1)S(1)}, f32[32,128]{1,0:T(8,128)S(1)}) custom-call(bf16[32,8192]{1,0:T(8,128)(2,1)S(1)} %get-tuple-element.37.scaled_ref, bf16[32,4096]{1,0:T(8,128)(2,1)S(1)} %get-tuple-element.38.early_ref, f32[32,128]{1,0:T(8,128)S(1)} %get-tuple-element.39.square_ref, ...), custom_call_target="tpu_custom_call" | custom-call | tf_op jit(solution)/shard_map/rank_inner/pallas_call | solution.py:335
  18.2 0.0 collective-permute-start.8
  18.2 1.6 %collective-permute-start.7 = (f32[32,32]{1,0:T(8,128)S(1)}, f32[32,32]{1,0:T(8,128)S(1)}, u32[]{:S(2)}, u32[]{:S(2)}) collective-permute-start(f32[32,32]{1,0:T(8,128)S(1)} %get-tuple-element.56.rest_6_), channel_id=1, source_target_pairs={{0,2},{1,3},{2,0},{3,1},{4,6},{5,7},{6,4},{7,5},{8,10},{9,11},{10,... | collective-permute-start | bytes 12296 | tf_op jit(solution)/shard_map/ppermute | solution.py:461
  19.8 0.2 %collective-permute-start.6 = (f32[32,32]{1,0:T(8,128)S(1)}, f32[32,32]{1,0:T(8,128)S(1)}, u32[]{:S(2)}, u32[]{:S(2)}) collective-permute-start(f32[32,32]{1,0:T(8,128)S(1)} %get-tuple-element.56.rest_6_), channel_id=1, source_target_pairs={{0,1},{1,0},{2,3},{3,2},{4,5},{5,4},{6,7},{7,6},{8,9},{9,8},{10,11... | collective-permute-start | bytes 12296 | tf_op jit(solution)/shard_map/ppermute | solution.py:461
  20.1 0.8 %fusion.7.far_ref = f32[2,32,256]{2,1,0:T(8,128)S(1)} fusion(bf16[4096,2,256]{2,1,0:T(2,128)(2,1)S(1)} %get-tuple-element.46, bf16[32,4096]{1,0:T(8,128)(2,1)S(1)} %get-tuple-element.47), kind=kOutput, calls=%fused_computation.5 | convolution fusion | flops 134217728 | bytes 4521984 | tf_op jit(solution)/shard_map/md,dkc->kmc/dot_general | solution.py:457
  20.9 0.8 %fusion.4.near_ref = f32[2,32,256]{2,1,0:T(8,128)S(1)} fusion(bf16[4096,2,256]{2,1,0:T(2,128)(2,1)S(1)} %get-tuple-element.32, bf16[32,4096]{1,0:T(8,128)(2,1)S(1)} %get-tuple-element.45), kind=kOutput, calls=%fused_computation.4 | convolution fusion | flops 134217728 | bytes 4521984 | tf_op jit(solution)/shard_map/md,dkc->kmc/dot_general | solution.py:457
  21.8 0.0 collective-permute-done.8.rest_9_
  21.8 0.2 collective-permute-done.7.rest_8_
  22.0 0.0 collective-permute-done.6.rest_7_
  22.0 1.5 %fresh_attention.1 = (bf16[4,8,256]{2,1,0:T(8,128)(2,1)}, bf16[4,8,256]{2,1,0:T(8,128)(2,1)}, bf16[4,8,2048]{2,1,0:T(8,128)(2,1)}) custom-call(f32[2,32,256]{2,1,0:T(8,128)S(1)} %fusion.4.near_ref, f32[2,32,256]{2,1,0:T(8,128)S(1)} %fusion.7.far_ref, f32[32,128]{1,0:T(8,128)S(1)} %get-tuple-element.48.square_ref, ...), custom_call_target="tpu_custom_call" | custom-call | tf_op jit(solution)/shard_map/fresh_attention/pallas_call | solution.py:445
  (1 shorter events, 0.0 us)
Async XLA Ops:
  1.5 11.2 %collective-permute-start = (bf16[2,16,2304]{2,1,0:T(8,128)(2,1)S(1)}, bf16[2,16,2304]{2,1,0:T(8,128)(2,1)S(1)}, u32[]{:S(2)}, u32[]{:S(2)}) collective-permute-start(bf16[2,16,2304]{2,1,0:T(8,128)(2,1)S(1)} %pack_factors.1.rest_2_.refs_0_), channel_id=1, source_target_pairs={{0,8},{4,12},{8,0},{12,4},{1,9},{5,13},{9,1},{13,5},{2,10},{6,14},... | collective-permute-start | bytes 442376 | tf_op jit(solution)/shard_map/ppermute | solution.py:461
  5.6 6.8 %collective-permute-start.1 = (bf16[4,8,2048]{2,1,0:T(8,128)(2,1)}, bf16[4,8,2048]{2,1,0:T(8,128)(2,1)S(1)}, u32[]{:S(2)}, u32[]{:S(2)}) collective-permute-start(bf16[4,8,2048]{2,1,0:T(8,128)(2,1)} %hidden_ref.1), channel_id=1, source_target_pairs={{0,2},{1,3},{2,0},{3,1},{4,6},{5,7},{6,4},{7,5},{8,10},{9,11},{10,... | collective-permute-start | bytes 393224 | tf_op jit(solution)/shard_map/ppermute | solution.py:461
  7.1 9.1 %collective-permute-start.4 = (bf16[2,16,2304]{2,1,0:T(8,128)(2,1)S(1)}, bf16[2,16,2304]{2,1,0:T(8,128)(2,1)S(1)}, u32[]{:S(2)}, u32[]{:S(2)}) collective-permute-start(bf16[2,16,2304]{2,1,0:T(8,128)(2,1)S(1)} %pack_factors.1.rest_2_.refs_0_), channel_id=1, source_target_pairs={{0,4},{4,0},{8,12},{12,8},{1,5},{5,1},{9,13},{13,9},{2,6},{6,2},{1... | collective-permute-start | bytes 442376 | tf_op jit(solution)/shard_map/ppermute | solution.py:461
  8.7 4.7 %copy-start = (bf16[4,8,2048]{2,1,0:T(8,128)(2,1)S(1)}, bf16[4,8,2048]{2,1,0:T(8,128)(2,1)}, u32[]{:S(2)}) copy-start(bf16[4,8,2048]{2,1,0:T(8,128)(2,1)} %hidden_ref.1) | copy-start | bytes 393220
  12.7 5.1 %collective-permute-start.5 = (bf16[2,16,2304]{2,1,0:T(8,128)(2,1)S(1)}, bf16[2,16,2304]{2,1,0:T(8,128)(2,1)S(1)}, u32[]{:S(2)}, u32[]{:S(2)}) collective-permute-start(bf16[2,16,2304]{2,1,0:T(8,128)(2,1)S(1)} %collective-permute-done.rest_4_.refs_2_), channel_id=1, source_target_pairs={{0,4},{4,0},{8,12},{12,8},{1,5},{5,1},{9,13},{13,9},{2,6},{6,2},{1... | collective-permute-start | bytes 442376 | tf_op jit(solution)/shard_map/ppermute | solution.py:461
  13.4 2.8 %collective-permute-start.2 = (bf16[4,8,2048]{2,1,0:T(8,128)(2,1)S(1)}, bf16[4,8,2048]{2,1,0:T(8,128)(2,1)S(1)}, u32[]{:S(2)}, u32[]{:S(2)}) collective-permute-start(bf16[4,8,2048]{2,1,0:T(8,128)(2,1)S(1)} %copy-done), channel_id=1, source_target_pairs={{0,1},{1,0},{2,3},{3,2},{4,5},{5,4},{6,7},{7,6},{8,9},{9,8},{10,11... | collective-permute-start | bytes 393224 | tf_op jit(solution)/shard_map/ppermute | solution.py:461
  13.4 2.8 %collective-permute-start.3 = (bf16[4,8,2048]{2,1,0:T(8,128)(2,1)S(1)}, bf16[4,8,2048]{2,1,0:T(8,128)(2,1)S(1)}, u32[]{:S(2)}, u32[]{:S(2)}) collective-permute-start(bf16[4,8,2048]{2,1,0:T(8,128)(2,1)S(1)} %collective-permute-done.1.rest_1_), channel_id=1, source_target_pairs={{0,1},{1,0},{2,3},{3,2},{4,5},{5,4},{6,7},{7,6},{8,9},{9,8},{10,11... | collective-permute-start | bytes 393224 | tf_op jit(solution)/shard_map/ppermute | solution.py:461
  18.2 3.6 %collective-permute-start.8 = (f32[32,32]{1,0:T(8,128)S(1)}, f32[32,32]{1,0:T(8,128)S(1)}, u32[]{:S(2)}, u32[]{:S(2)}) collective-permute-start(f32[32,32]{1,0:T(8,128)S(1)} %get-tuple-element.56.rest_6_), channel_id=1, source_target_pairs={{0,3},{1,2},{2,1},{3,0},{4,7},{5,6},{6,5},{7,4},{8,11},{9,10},{10,... | collective-permute-start | bytes 12296 | tf_op jit(solution)/shard_map/ppermute | solution.py:461
  18.2 3.8 %collective-permute-start.7 = (f32[32,32]{1,0:T(8,128)S(1)}, f32[32,32]{1,0:T(8,128)S(1)}, u32[]{:S(2)}, u32[]{:S(2)}) collective-permute-start(f32[32,32]{1,0:T(8,128)S(1)} %get-tuple-element.56.rest_6_), channel_id=1, source_target_pairs={{0,2},{1,3},{2,0},{3,1},{4,6},{5,7},{6,4},{7,5},{8,10},{9,11},{10,... | collective-permute-start | bytes 12296 | tf_op jit(solution)/shard_map/ppermute | solution.py:461
  19.8 2.2 %collective-permute-start.6 = (f32[32,32]{1,0:T(8,128)S(1)}, f32[32,32]{1,0:T(8,128)S(1)}, u32[]{:S(2)}, u32[]{:S(2)}) collective-permute-start(f32[32,32]{1,0:T(8,128)S(1)} %get-tuple-element.56.rest_6_), channel_id=1, source_target_pairs={{0,1},{1,0},{2,3},{3,2},{4,5},{5,4},{6,7},{7,6},{8,9},{9,8},{10,11... | collective-permute-start | bytes 12296 | tf_op jit(solution)/shard_map/ppermute | solution.py:461

commit v22 on v21

--- a/solution.py
+++ b/solution.py
@@ -377,7 +377,8 @@
 def final_kernel(width, blocks, near_ref, far_ref, square_ref, bias_ref, *rest):
     query_ref, acc_ref, top_ref, total_ref, cos_ref, sin_ref = rest[:6]
     inner_refs = rest[6 : 6 + blocks]
-    up_ref, keys_out, values_out, attended_out, inner_buffer = rest[6 + blocks :]
+    up_ref, keys_ref, values_ref, attended_ref = rest[6 + blocks : 10 + blocks]
+    inner_buffer, keys_out, values_out, attended_out, sems = rest[10 + blocks :]
     steps, rows, columns = keys_out.shape
     count = steps * rows
     groups, size, _ = query_ref.shape
@@ -407,6 +408,13 @@
     other_step, other_row = split_index(other, rows)
     line_step = split_index(line_step, steps)[1]
     live = (line_row == other_row) & (other_step <= line_step)
+    copies = []
+
+    def send(source, target):
+        copies.append(pltpu.make_async_copy(source, target, sems.at[len(copies)]))
+        copies[-1].start()
+
+    keys, values = [], []
     for group in range(groups):
         at = slice(group * HD, (group + 1) * HD)
         key = linear[0][:, at]
@@ -415,9 +423,14 @@
         for step in range(steps):
             keys_out[step, :, at] = key[step * rows : (step + 1) * rows]
             values_out[step, :, at] = value[step * rows : (step + 1) * rows]
+        keys.append(key)
+        values.append(value)
+    send(keys_out, keys_ref)
+    send(values_out, values_ref)
+    for group in range(groups):
         scores = lax.dot_general(
             query_ref[group].astype(jnp.bfloat16),
-            key,
+            keys[group],
             (((1,), (1,)), ((), ())),
             preferred_element_type=jnp.float32,
         )
@@ -428,7 +441,7 @@
         keep = jnp.exp(old_top - top)
         total = total_ref[group][:, :1] * keep + jnp.sum(exps, axis=1, keepdims=True)
         acc = acc_ref[group] * keep + jnp.dot(
-            exps.astype(jnp.bfloat16), value, preferred_element_type=jnp.float32
+            exps.astype(jnp.bfloat16), values[group], preferred_element_type=jnp.float32
         )
         attended = (acc * (1.0 / total)).astype(jnp.bfloat16)
         for head in range(per_group):
@@ -436,6 +449,12 @@
             for step in range(steps):
                 tile = (head * steps + step) * rows
                 attended_out[step, :, lanes] = attended[tile : tile + rows]
+    for group in range(groups):
+        lanes = pl.ds(group * per_group * HD, per_group * HD)
+        for step in range(steps):
+            send(attended_out.at[step, :, lanes], attended_ref.at[step, :, lanes])
+    for copy in copies:
+        copy.wait()
 
 
 def final_call(shape, width, near, far, square, bias, cached, inner, up):
@@ -446,8 +465,14 @@
         functools.partial(final_kernel, width, len(inner)),
         out_shape=(small, small, jax.ShapeDtypeStruct(shape, jnp.bfloat16)),
         in_specs=[VMEM] * (5 + len(cached) + len(inner)),
-        out_specs=(VMEM,) * 3,
-        scratch_shapes=[pltpu.VMEM((len(inner),) + inner[0].shape, jnp.float32)],
+        out_specs=(HBM,) * 3,
+        scratch_shapes=[
+            pltpu.VMEM((len(inner),) + inner[0].shape, jnp.float32),
+            pltpu.VMEM(small.shape, small.dtype),
+            pltpu.VMEM(small.shape, small.dtype),
+            pltpu.VMEM(shape, jnp.bfloat16),
+            pltpu.SemaphoreType.DMA((2 + columns // HD * steps,)),
+        ],
         compiler_params=pltpu.CompilerParams(vmem_limit_bytes=8 << 20),
         name="fresh_attention",
     )(near, far, square, bias, *cached, *inner, up)

time: 23.8 us -> 23.9 us (level)
  transfers between devices with their start and end apart: 9 -> 9, of which waited for: 3 -> 3; matrix products, arithmetic and copies ran while one was open for 7% -> 7% of each run, Pallas kernels for 26% -> 25%
where the time goes in v22:
time: 23.9 us; the launch traced here: 23.7 us
  starting transfers between devices  10.2 us (43%)
  Pallas kernels  8.85 us (37%)
  waiting for transfers between devices  2.2 us (9%)
  matrix products  1.67 us (7%)
  between operations  0.72 us (3%)
    ppermute x9, starting transfers between devices, swap(): return lax.ppermute(block, axis, [(i, i ^ offset) for i in range(count)])  10.2 us
    pallas_call x1, Pallas kernels, cache_call(): pl.pallas_call(functools.partial(cache_kernel, near), out_shape=(pltpu.VM...  3.73 us
    pallas_call x1, Pallas kernels, scale_call(): pl.pallas_call(functools.partial(scale_kernel, early, far), out_shape=(pl...  2.26 us
    ppermute x9, waiting for transfers between devices, swap(): return lax.ppermute(block, axis, [(i, i ^ offset) for i in range(count)])  2.2 us
    dot_general x2, matrix products, dot(): jnp.einsum('md,dkc->kmc', rows, weight, preferred_element_type=jnp.float32)  1.67 us
    pallas_call x1, Pallas kernels, final_call(): pl.pallas_call(functools.partial(final_kernel, width, len(inner)), out_sh...  1.62 us
    pallas_call x1, Pallas kernels, pack_call(): pl.pallas_call(pack_kernel, out_shape=pltpu.VMEM((kinds, share, down.shap...  0.87 us
  transfers between devices with their start and end apart: 9, of which 3 were waited for; matrix products, arithmetic and copies ran while one was open for 7% of the time, Pallas kernels for 25%

profile of v22, /device:TPU:0, one launch (start us, length us, event | category | flops | bytes accessed | tf_op | source)
XLA Modules:
  0.0 23.7 jit_solution(14275549827766652068)
XLA Ops:
  0.6 0.9 %pack_factors.1.rest_2_.refs_0_ = bf16[2,16,2304]{2,1,0:T(8,128)(2,1)S(1)} custom-call(bf16[2,64,2048]{2,1,0:T(8,128)(2,1)} %down_ref.1, bf16[2,16,256]{2,1,0:T(8,128)(2,1)} %bitcast.13), custom_call_target="tpu_custom_call" | custom-call | tf_op jit(solution)/shard_map/pack_factors/pallas_call | solution.py:201
  1.5 4.1 %collective-permute-start = (bf16[2,16,2304]{2,1,0:T(8,128)(2,1)S(1)}, bf16[2,16,2304]{2,1,0:T(8,128)(2,1)S(1)}, u32[]{:S(2)}, u32[]{:S(2)}) collective-permute-start(bf16[2,16,2304]{2,1,0:T(8,128)(2,1)S(1)} %pack_factors.1.rest_2_.refs_0_), channel_id=1, source_target_pairs={{0,8},{4,12},{8,0},{12,4},{1,9},{5,13},{9,1},{13,5},{2,10},{6,14},... | collective-permute-start | bytes 442376 | tf_op jit(solution)/shard_map/ppermute | solution.py:486
  5.6 1.5 %collective-permute-start.1 = (bf16[4,8,2048]{2,1,0:T(8,128)(2,1)}, bf16[4,8,2048]{2,1,0:T(8,128)(2,1)S(1)}, u32[]{:S(2)}, u32[]{:S(2)}) collective-permute-start(bf16[4,8,2048]{2,1,0:T(8,128)(2,1)} %hidden_ref.1), channel_id=1, source_target_pairs={{0,2},{1,3},{2,0},{3,1},{4,6},{5,7},{6,4},{7,5},{8,10},{9,11},{10,... | collective-permute-start | bytes 393224 | tf_op jit(solution)/shard_map/ppermute | solution.py:486
  7.1 1.6 %collective-permute-start.4 = (bf16[2,16,2304]{2,1,0:T(8,128)(2,1)S(1)}, bf16[2,16,2304]{2,1,0:T(8,128)(2,1)S(1)}, u32[]{:S(2)}, u32[]{:S(2)}) collective-permute-start(bf16[2,16,2304]{2,1,0:T(8,128)(2,1)S(1)} %pack_factors.1.rest_2_.refs_0_), channel_id=1, source_target_pairs={{0,4},{4,0},{8,12},{12,8},{1,5},{5,1},{9,13},{13,9},{2,6},{6,2},{1... | collective-permute-start | bytes 442376 | tf_op jit(solution)/shard_map/ppermute | solution.py:486
  8.7 0.0 copy-start
  8.7 3.7 %cache_attention.1 = (bf16[4096,2,256]{2,1,0:T(2,128)(2,1)S(1)}, f32[64,128]{1,0:T(8,128)S(1)}, bf16[2,256]{1,0:T(2,128)(2,1)S(1)}, bf16[4,8,2048]{2,1,0:T(8,128...) custom-call(s32[8]{0:T(128)} %lengths_ref.3, ...), custom_call_target="tpu_custom_call" | custom-call | flops 140509184 | bytes 5242880 | tf_op jit(solution)/shard_map/cache_attention/pallas_call | solution.py:148
  12.4 0.0 collective-permute-done.1.rest_1_
  12.4 0.3 %collective-permute-done.rest_4_.refs_2_ = bf16[2,16,2304]{2,1,0:T(8,128)(2,1)S(1)} collective-permute-done((bf16[2,16,2304]{2,1,0:T(8,128)(2,1)S(1)}, bf16[2,16,2304]{2,1,0:T(8,128)(2,1)S(1)}, u32[]{:S(2)}, u32[]{:S(2)}) %collective-permute-start) | collective-permute-done | bytes 147488 | tf_op jit(solution)/shard_map/ppermute | solution.py:486
  12.7 0.7 %collective-permute-start.5 = (bf16[2,16,2304]{2,1,0:T(8,128)(2,1)S(1)}, bf16[2,16,2304]{2,1,0:T(8,128)(2,1)S(1)}, u32[]{:S(2)}, u32[]{:S(2)}) collective-permute-start(bf16[2,16,2304]{2,1,0:T(8,128)(2,1)S(1)} %collective-permute-done.rest_4_.refs_2_), channel_id=1, source_target_pairs={{0,4},{4,0},{8,12},{12,8},{1,5},{5,1},{9,13},{13,9},{2,6},{6,2},{1... | collective-permute-start | bytes 442376 | tf_op jit(solution)/shard_map/ppermute | solution.py:486
  13.4 0.0 copy-done
  13.4 0.0 collective-permute-start.2
  13.4 0.5 %collective-permute-start.3 = (bf16[4,8,2048]{2,1,0:T(8,128)(2,1)S(1)}, bf16[4,8,2048]{2,1,0:T(8,128)(2,1)S(1)}, u32[]{:S(2)}, u32[]{:S(2)}) collective-permute-start(bf16[4,8,2048]{2,1,0:T(8,128)(2,1)S(1)} %collective-permute-done.1.rest_1_), channel_id=1, source_target_pairs={{0,1},{1,0},{2,3},{3,2},{4,5},{5,4},{6,7},{7,6},{8,9},{9,8},{10,11... | collective-permute-start | bytes 393224 | tf_op jit(solution)/shard_map/ppermute | solution.py:486
  13.9 2.3 %scale_features.1 = (bf16[32,8192]{1,0:T(8,128)(2,1)S(1)}, bf16[32,4096]{1,0:T(8,128)(2,1)S(1)}, f32[32,128]{1,0:T(8,128)S(1)}, bf16[4096,2,256]{2,1,0:T(2,128)(...) custom-call(s32[8]{0:T(128)} %lengths_ref.3, bf16[8192,2,256]{2,1,0:T(2,128)(2,1)} %weight_ref.3, ...), custom_call_target="tpu_custom_call" | custom-call | bytes 9437184 | tf_op jit(solution)/shard_map/scale_features/pallas_call | solution.py:269
  16.2 0.0 collective-permute-done.2.rest_0_
  16.2 0.0 collective-permute-done.4.rest_3_.refs_1_
  16.2 0.0 collective-permute-done.3.rest_1_
  16.2 1.7 %collective-permute-done.5.rest_5_.refs_3_ = bf16[2,16,2304]{2,1,0:T(8,128)(2,1)S(1)} collective-permute-done((bf16[2,16,2304]{2,1,0:T(8,128)(2,1)S(1)}, bf16[2,16,2304]{2,1,0:T(8,128)(2,1)S(1)}, u32[]{:S(2)}, u32[]{:S(2)}) %collective-permute-start.5) | collective-permute-done | bytes 147488 | tf_op jit(solution)/shard_map/ppermute | solution.py:486
  17.9 0.3 %rank_inner.1 = (f32[32,32]{1,0:T(8,128)S(1)}, bf16[32,4096]{1,0:T(8,128)(2,1)S(1)}, bf16[32,4096]{1,0:T(8,128)(2,1)S(1)}, f32[32,128]{1,0:T(8,128)S(1)}) custom-call(bf16[32,8192]{1,0:T(8,128)(2,1)S(1)} %get-tuple-element.37.scaled_ref, bf16[32,4096]{1,0:T(8,128)(2,1)S(1)} %get-tuple-element.38.early_ref, f32[32,128]{1,0:T(8,128)S(1)} %get-tuple-element.39.square_ref, ...), custom_call_target="tpu_custom_call" | custom-call | tf_op jit(solution)/shard_map/rank_inner/pallas_call | solution.py:335
  18.2 0.0 collective-permute-start.8
  18.2 1.6 %collective-permute-start.7 = (f32[32,32]{1,0:T(8,128)S(1)}, f32[32,32]{1,0:T(8,128)S(1)}, u32[]{:S(2)}, u32[]{:S(2)}) collective-permute-start(f32[32,32]{1,0:T(8,128)S(1)} %get-tuple-element.56.rest_6_), channel_id=1, source_target_pairs={{0,2},{1,3},{2,0},{3,1},{4,6},{5,7},{6,4},{7,5},{8,10},{9,11},{10,... | collective-permute-start | bytes 12296 | tf_op jit(solution)/shard_map/ppermute | solution.py:486
  19.8 0.2 %collective-permute-start.6 = (f32[32,32]{1,0:T(8,128)S(1)}, f32[32,32]{1,0:T(8,128)S(1)}, u32[]{:S(2)}, u32[]{:S(2)}) collective-permute-start(f32[32,32]{1,0:T(8,128)S(1)} %get-tuple-element.56.rest_6_), channel_id=1, source_target_pairs={{0,1},{1,0},{2,3},{3,2},{4,5},{5,4},{6,7},{7,6},{8,9},{9,8},{10,11... | collective-permute-start | bytes 12296 | tf_op jit(solution)/shard_map/ppermute | solution.py:486
  20.1 0.8 %fusion.7.far_ref = f32[2,32,256]{2,1,0:T(8,128)S(1)} fusion(bf16[4096,2,256]{2,1,0:T(2,128)(2,1)S(1)} %get-tuple-element.46, bf16[32,4096]{1,0:T(8,128)(2,1)S(1)} %get-tuple-element.47), kind=kOutput, calls=%fused_computation.5 | convolution fusion | flops 134217728 | bytes 4521984 | tf_op jit(solution)/shard_map/md,dkc->kmc/dot_general | solution.py:482
  20.9 0.8 %fusion.4.near_ref = f32[2,32,256]{2,1,0:T(8,128)S(1)} fusion(bf16[4096,2,256]{2,1,0:T(2,128)(2,1)S(1)} %get-tuple-element.32, bf16[32,4096]{1,0:T(8,128)(2,1)S(1)} %get-tuple-element.45), kind=kOutput, calls=%fused_computation.4 | convolution fusion | flops 134217728 | bytes 4521984 | tf_op jit(solution)/shard_map/md,dkc->kmc/dot_general | solution.py:482
  21.8 0.0 collective-permute-done.8.rest_9_
  21.8 0.2 collective-permute-done.7.rest_8_
  22.0 0.0 collective-permute-done.6.rest_7_
  22.0 1.6 %fresh_attention.1 = (bf16[4,8,256]{2,1,0:T(8,128)(2,1)}, bf16[4,8,256]{2,1,0:T(8,128)(2,1)}, bf16[4,8,2048]{2,1,0:T(8,128)(2,1)}) custom-call(f32[2,32,256]{2,1,0:T(8,128)S(1)} %fusion.4.near_ref, f32[2,32,256]{2,1,0:T(8,128)S(1)} %fusion.7.far_ref, f32[32,128]{1,0:T(8,128)S(1)} %get-tuple-element.48.square_ref, ...), custom_call_target="tpu_custom_call" | custom-call | tf_op jit(solution)/shard_map/fresh_attention/pallas_call | solution.py:464
  (1 shorter events, 0.0 us)
Async XLA Ops:
  1.5 11.2 %collective-permute-start = (bf16[2,16,2304]{2,1,0:T(8,128)(2,1)S(1)}, bf16[2,16,2304]{2,1,0:T(8,128)(2,1)S(1)}, u32[]{:S(2)}, u32[]{:S(2)}) collective-permute-start(bf16[2,16,2304]{2,1,0:T(8,128)(2,1)S(1)} %pack_factors.1.rest_2_.refs_0_), channel_id=1, source_target_pairs={{0,8},{4,12},{8,0},{12,4},{1,9},{5,13},{9,1},{13,5},{2,10},{6,14},... | collective-permute-start | bytes 442376 | tf_op jit(solution)/shard_map/ppermute | solution.py:486
  5.6 6.8 %collective-permute-start.1 = (bf16[4,8,2048]{2,1,0:T(8,128)(2,1)}, bf16[4,8,2048]{2,1,0:T(8,128)(2,1)S(1)}, u32[]{:S(2)}, u32[]{:S(2)}) collective-permute-start(bf16[4,8,2048]{2,1,0:T(8,128)(2,1)} %hidden_ref.1), channel_id=1, source_target_pairs={{0,2},{1,3},{2,0},{3,1},{4,6},{5,7},{6,4},{7,5},{8,10},{9,11},{10,... | collective-permute-start | bytes 393224 | tf_op jit(solution)/shard_map/ppermute | solution.py:486
  7.1 9.1 %collective-permute-start.4 = (bf16[2,16,2304]{2,1,0:T(8,128)(2,1)S(1)}, bf16[2,16,2304]{2,1,0:T(8,128)(2,1)S(1)}, u32[]{:S(2)}, u32[]{:S(2)}) collective-permute-start(bf16[2,16,2304]{2,1,0:T(8,128)(2,1)S(1)} %pack_factors.1.rest_2_.refs_0_), channel_id=1, source_target_pairs={{0,4},{4,0},{8,12},{12,8},{1,5},{5,1},{9,13},{13,9},{2,6},{6,2},{1... | collective-permute-start | bytes 442376 | tf_op jit(solution)/shard_map/ppermute | solution.py:486
  8.7 4.7 %copy-start = (bf16[4,8,2048]{2,1,0:T(8,128)(2,1)S(1)}, bf16[4,8,2048]{2,1,0:T(8,128)(2,1)}, u32[]{:S(2)}) copy-start(bf16[4,8,2048]{2,1,0:T(8,128)(2,1)} %hidden_ref.1) | copy-start | bytes 393220
  12.7 5.1 %collective-permute-start.5 = (bf16[2,16,2304]{2,1,0:T(8,128)(2,1)S(1)}, bf16[2,16,2304]{2,1,0:T(8,128)(2,1)S(1)}, u32[]{:S(2)}, u32[]{:S(2)}) collective-permute-start(bf16[2,16,2304]{2,1,0:T(8,128)(2,1)S(1)} %collective-permute-done.rest_4_.refs_2_), channel_id=1, source_target_pairs={{0,4},{4,0},{8,12},{12,8},{1,5},{5,1},{9,13},{13,9},{2,6},{6,2},{1... | collective-permute-start | bytes 442376 | tf_op jit(solution)/shard_map/ppermute | solution.py:486
  13.4 2.8 %collective-permute-start.2 = (bf16[4,8,2048]{2,1,0:T(8,128)(2,1)S(1)}, bf16[4,8,2048]{2,1,0:T(8,128)(2,1)S(1)}, u32[]{:S(2)}, u32[]{:S(2)}) collective-permute-start(bf16[4,8,2048]{2,1,0:T(8,128)(2,1)S(1)} %copy-done), channel_id=1, source_target_pairs={{0,1},{1,0},{2,3},{3,2},{4,5},{5,4},{6,7},{7,6},{8,9},{9,8},{10,11... | collective-permute-start | bytes 393224 | tf_op jit(solution)/shard_map/ppermute | solution.py:486
  13.4 2.8 %collective-permute-start.3 = (bf16[4,8,2048]{2,1,0:T(8,128)(2,1)S(1)}, bf16[4,8,2048]{2,1,0:T(8,128)(2,1)S(1)}, u32[]{:S(2)}, u32[]{:S(2)}) collective-permute-start(bf16[4,8,2048]{2,1,0:T(8,128)(2,1)S(1)} %collective-permute-done.1.rest_1_), channel_id=1, source_target_pairs={{0,1},{1,0},{2,3},{3,2},{4,5},{5,4},{6,7},{7,6},{8,9},{9,8},{10,11... | collective-permute-start | bytes 393224 | tf_op jit(solution)/shard_map/ppermute | solution.py:486
  18.2 3.6 %collective-permute-start.8 = (f32[32,32]{1,0:T(8,128)S(1)}, f32[32,32]{1,0:T(8,128)S(1)}, u32[]{:S(2)}, u32[]{:S(2)}) collective-permute-start(f32[32,32]{1,0:T(8,128)S(1)} %get-tuple-element.56.rest_6_), channel_id=1, source_target_pairs={{0,3},{1,2},{2,1},{3,0},{4,7},{5,6},{6,5},{7,4},{8,11},{9,10},{10,... | collective-permute-start | bytes 12296 | tf_op jit(solution)/shard_map/ppermute | solution.py:486
  18.2 3.8 %collective-permute-start.7 = (f32[32,32]{1,0:T(8,128)S(1)}, f32[32,32]{1,0:T(8,128)S(1)}, u32[]{:S(2)}, u32[]{:S(2)}) collective-permute-start(f32[32,32]{1,0:T(8,128)S(1)} %get-tuple-element.56.rest_6_), channel_id=1, source_target_pairs={{0,2},{1,3},{2,0},{3,1},{4,6},{5,7},{6,4},{7,5},{8,10},{9,11},{10,... | collective-permute-start | bytes 12296 | tf_op jit(solution)/shard_map/ppermute | solution.py:486
  19.8 2.2 %collective-permute-start.6 = (f32[32,32]{1,0:T(8,128)S(1)}, f32[32,32]{1,0:T(8,128)S(1)}, u32[]{:S(2)}, u32[]{:S(2)}) collective-permute-start(f32[32,32]{1,0:T(8,128)S(1)} %get-tuple-element.56.rest_6_), channel_id=1, source_target_pairs={{0,1},{1,0},{2,3},{3,2},{4,5},{5,4},{6,7},{7,6},{8,9},{9,8},{10,11... | collective-permute-start | bytes 12296 | tf_op jit(solution)/shard_map/ppermute | solution.py:486

commit v23 on v21

--- a/solution.py
+++ b/solution.py
@@ -383,7 +383,8 @@
     groups, size, _ = query_ref.shape
     per_group = size // count
     kinds = bias_ref.shape[0]
-    row_scale = lax.rsqrt(square_ref[:, :1] * (1.0 / width) + norm_eps)
+    row_scale = lax.rsqrt(square_ref[...] * (1.0 / width) + norm_eps)
+    row_scale = jnp.concatenate([row_scale] * groups, axis=1)
     me = lax.axis_index("tp") if blocks > 1 else 0
     for i in range(blocks):
         inner_buffer[me ^ i] = inner_refs[i][...]
@@ -422,11 +423,11 @@
             preferred_element_type=jnp.float32,
         )
         scores = jnp.where(live, scores * score_scale, masked_score)
-        old_top = top_ref[group][:, :1]
+        old_top = top_ref[group]
         top = jnp.maximum(old_top, jnp.max(scores, axis=1, keepdims=True))
-        exps = jnp.exp(scores - top)
+        exps = jnp.exp(scores - top[:, :count])
         keep = jnp.exp(old_top - top)
-        total = total_ref[group][:, :1] * keep + jnp.sum(exps, axis=1, keepdims=True)
+        total = total_ref[group] * keep + jnp.sum(exps, axis=1, keepdims=True)
         acc = acc_ref[group] * keep + jnp.dot(
             exps.astype(jnp.bfloat16), value, preferred_element_type=jnp.float32
         )

time: 23.8 us -> 23.6 us (level)
  no operation moved by 1% of the time
where the time goes in v23:
time: 23.6 us; the launch traced here: 23.4 us
  starting transfers between devices  10.2 us (43%)
  Pallas kernels  8.59 us (36%)
  waiting for transfers between devices  2.2 us (9%)
  matrix products  1.67 us (7%)
  between operations  0.72 us (3%)
    ppermute x9, starting transfers between devices, swap(): return lax.ppermute(block, axis, [(i, i ^ offset) for i in range(count)])  10.2 us
    pallas_call x1, Pallas kernels, cache_call(): pl.pallas_call(functools.partial(cache_kernel, near), out_shape=(pltpu.VM...  3.73 us
    pallas_call x1, Pallas kernels, scale_call(): pl.pallas_call(functools.partial(scale_kernel, early, far), out_shape=(pl...  2.26 us
    ppermute x9, waiting for transfers between devices, swap(): return lax.ppermute(block, axis, [(i, i ^ offset) for i in range(count)])  2.2 us
    dot_general x2, matrix products, dot(): jnp.einsum('md,dkc->kmc', rows, weight, preferred_element_type=jnp.float32)  1.67 us
    pallas_call x1, Pallas kernels, final_call(): pl.pallas_call(functools.partial(final_kernel, width, len(inner)), out_sh...  1.36 us
    pallas_call x1, Pallas kernels, pack_call(): pl.pallas_call(pack_kernel, out_shape=pltpu.VMEM((kinds, share, down.shap...  0.87 us
  transfers between devices with their start and end apart: 9, of which 3 were waited for; matrix products, arithmetic and copies ran while one was open for 7% of the time, Pallas kernels for 26%

profile of v23, /device:TPU:0, one launch (start us, length us, event | category | flops | bytes accessed | tf_op | source)
XLA Modules:
  0.0 23.4 jit_solution(787279913423032569)
XLA Ops:
  0.6 0.9 %pack_factors.1.rest_2_.refs_0_ = bf16[2,16,2304]{2,1,0:T(8,128)(2,1)S(1)} custom-call(bf16[2,64,2048]{2,1,0:T(8,128)(2,1)} %down_ref.1, bf16[2,16,256]{2,1,0:T(8,128)(2,1)} %bitcast.13), custom_call_target="tpu_custom_call" | custom-call | tf_op jit(solution)/shard_map/pack_factors/pallas_call | solution.py:201
  1.5 4.1 %collective-permute-start = (bf16[2,16,2304]{2,1,0:T(8,128)(2,1)S(1)}, bf16[2,16,2304]{2,1,0:T(8,128)(2,1)S(1)}, u32[]{:S(2)}, u32[]{:S(2)}) collective-permute-start(bf16[2,16,2304]{2,1,0:T(8,128)(2,1)S(1)} %pack_factors.1.rest_2_.refs_0_), channel_id=1, source_target_pairs={{0,8},{4,12},{8,0},{12,4},{1,9},{5,13},{9,1},{13,5},{2,10},{6,14},... | collective-permute-start | bytes 442376 | tf_op jit(solution)/shard_map/ppermute | solution.py:462
  5.6 1.5 %collective-permute-start.1 = (bf16[4,8,2048]{2,1,0:T(8,128)(2,1)}, bf16[4,8,2048]{2,1,0:T(8,128)(2,1)S(1)}, u32[]{:S(2)}, u32[]{:S(2)}) collective-permute-start(bf16[4,8,2048]{2,1,0:T(8,128)(2,1)} %hidden_ref.1), channel_id=1, source_target_pairs={{0,2},{1,3},{2,0},{3,1},{4,6},{5,7},{6,4},{7,5},{8,10},{9,11},{10,... | collective-permute-start | bytes 393224 | tf_op jit(solution)/shard_map/ppermute | solution.py:462
  7.1 1.6 %collective-permute-start.4 = (bf16[2,16,2304]{2,1,0:T(8,128)(2,1)S(1)}, bf16[2,16,2304]{2,1,0:T(8,128)(2,1)S(1)}, u32[]{:S(2)}, u32[]{:S(2)}) collective-permute-start(bf16[2,16,2304]{2,1,0:T(8,128)(2,1)S(1)} %pack_factors.1.rest_2_.refs_0_), channel_id=1, source_target_pairs={{0,4},{4,0},{8,12},{12,8},{1,5},{5,1},{9,13},{13,9},{2,6},{6,2},{1... | collective-permute-start | bytes 442376 | tf_op jit(solution)/shard_map/ppermute | solution.py:462
  8.7 0.0 copy-start
  8.7 3.7 %cache_attention.1 = (bf16[4096,2,256]{2,1,0:T(2,128)(2,1)S(1)}, f32[64,128]{1,0:T(8,128)S(1)}, bf16[2,256]{1,0:T(2,128)(2,1)S(1)}, bf16[4,8,2048]{2,1,0:T(8,128...) custom-call(s32[8]{0:T(128)} %lengths_ref.3, ...), custom_call_target="tpu_custom_call" | custom-call | flops 140509184 | bytes 5242880 | tf_op jit(solution)/shard_map/cache_attention/pallas_call | solution.py:148
  12.4 0.0 collective-permute-done.1.rest_1_
  12.4 0.3 %collective-permute-done.rest_4_.refs_2_ = bf16[2,16,2304]{2,1,0:T(8,128)(2,1)S(1)} collective-permute-done((bf16[2,16,2304]{2,1,0:T(8,128)(2,1)S(1)}, bf16[2,16,2304]{2,1,0:T(8,128)(2,1)S(1)}, u32[]{:S(2)}, u32[]{:S(2)}) %collective-permute-start) | collective-permute-done | bytes 147488 | tf_op jit(solution)/shard_map/ppermute | solution.py:462
  12.7 0.7 %collective-permute-start.5 = (bf16[2,16,2304]{2,1,0:T(8,128)(2,1)S(1)}, bf16[2,16,2304]{2,1,0:T(8,128)(2,1)S(1)}, u32[]{:S(2)}, u32[]{:S(2)}) collective-permute-start(bf16[2,16,2304]{2,1,0:T(8,128)(2,1)S(1)} %collective-permute-done.rest_4_.refs_2_), channel_id=1, source_target_pairs={{0,4},{4,0},{8,12},{12,8},{1,5},{5,1},{9,13},{13,9},{2,6},{6,2},{1... | collective-permute-start | bytes 442376 | tf_op jit(solution)/shard_map/ppermute | solution.py:462
  13.4 0.0 copy-done
  13.4 0.0 collective-permute-start.2
  13.4 0.5 %collective-permute-start.3 = (bf16[4,8,2048]{2,1,0:T(8,128)(2,1)S(1)}, bf16[4,8,2048]{2,1,0:T(8,128)(2,1)S(1)}, u32[]{:S(2)}, u32[]{:S(2)}) collective-permute-start(bf16[4,8,2048]{2,1,0:T(8,128)(2,1)S(1)} %collective-permute-done.1.rest_1_), channel_id=1, source_target_pairs={{0,1},{1,0},{2,3},{3,2},{4,5},{5,4},{6,7},{7,6},{8,9},{9,8},{10,11... | collective-permute-start | bytes 393224 | tf_op jit(solution)/shard_map/ppermute | solution.py:462
  13.9 2.3 %scale_features.1 = (bf16[32,8192]{1,0:T(8,128)(2,1)S(1)}, bf16[32,4096]{1,0:T(8,128)(2,1)S(1)}, f32[32,128]{1,0:T(8,128)S(1)}, bf16[4096,2,256]{2,1,0:T(2,128)(...) custom-call(s32[8]{0:T(128)} %lengths_ref.3, bf16[8192,2,256]{2,1,0:T(2,128)(2,1)} %weight_ref.3, ...), custom_call_target="tpu_custom_call" | custom-call | bytes 9437184 | tf_op jit(solution)/shard_map/scale_features/pallas_call | solution.py:269
  16.2 0.0 collective-permute-done.2.rest_0_
  16.2 0.0 collective-permute-done.4.rest_3_.refs_1_
  16.2 0.0 collective-permute-done.3.rest_1_
  16.2 1.7 %collective-permute-done.5.rest_5_.refs_3_ = bf16[2,16,2304]{2,1,0:T(8,128)(2,1)S(1)} collective-permute-done((bf16[2,16,2304]{2,1,0:T(8,128)(2,1)S(1)}, bf16[2,16,2304]{2,1,0:T(8,128)(2,1)S(1)}, u32[]{:S(2)}, u32[]{:S(2)}) %collective-permute-start.5) | collective-permute-done | bytes 147488 | tf_op jit(solution)/shard_map/ppermute | solution.py:462
  17.9 0.3 %rank_inner.1 = (f32[32,32]{1,0:T(8,128)S(1)}, bf16[32,4096]{1,0:T(8,128)(2,1)S(1)}, bf16[32,4096]{1,0:T(8,128)(2,1)S(1)}, f32[32,128]{1,0:T(8,128)S(1)}) custom-call(bf16[32,8192]{1,0:T(8,128)(2,1)S(1)} %get-tuple-element.37.scaled_ref, bf16[32,4096]{1,0:T(8,128)(2,1)S(1)} %get-tuple-element.38.early_ref, f32[32,128]{1,0:T(8,128)S(1)} %get-tuple-element.39.square_ref, ...), custom_call_target="tpu_custom_call" | custom-call | tf_op jit(solution)/shard_map/rank_inner/pallas_call | solution.py:335
  18.2 0.0 collective-permute-start.8
  18.2 1.6 %collective-permute-start.7 = (f32[32,32]{1,0:T(8,128)S(1)}, f32[32,32]{1,0:T(8,128)S(1)}, u32[]{:S(2)}, u32[]{:S(2)}) collective-permute-start(f32[32,32]{1,0:T(8,128)S(1)} %get-tuple-element.56.rest_6_), channel_id=1, source_target_pairs={{0,2},{1,3},{2,0},{3,1},{4,6},{5,7},{6,4},{7,5},{8,10},{9,11},{10,... | collective-permute-start | bytes 12296 | tf_op jit(solution)/shard_map/ppermute | solution.py:462
  19.8 0.2 %collective-permute-start.6 = (f32[32,32]{1,0:T(8,128)S(1)}, f32[32,32]{1,0:T(8,128)S(1)}, u32[]{:S(2)}, u32[]{:S(2)}) collective-permute-start(f32[32,32]{1,0:T(8,128)S(1)} %get-tuple-element.56.rest_6_), channel_id=1, source_target_pairs={{0,1},{1,0},{2,3},{3,2},{4,5},{5,4},{6,7},{7,6},{8,9},{9,8},{10,11... | collective-permute-start | bytes 12296 | tf_op jit(solution)/shard_map/ppermute | solution.py:462
  20.1 0.8 %fusion.7.far_ref = f32[2,32,256]{2,1,0:T(8,128)S(1)} fusion(bf16[4096,2,256]{2,1,0:T(2,128)(2,1)S(1)} %get-tuple-element.46, bf16[32,4096]{1,0:T(8,128)(2,1)S(1)} %get-tuple-element.47), kind=kOutput, calls=%fused_computation.5 | convolution fusion | flops 134217728 | bytes 4521984 | tf_op jit(solution)/shard_map/md,dkc->kmc/dot_general | solution.py:458
  20.9 0.8 %fusion.4.near_ref = f32[2,32,256]{2,1,0:T(8,128)S(1)} fusion(bf16[4096,2,256]{2,1,0:T(2,128)(2,1)S(1)} %get-tuple-element.32, bf16[32,4096]{1,0:T(8,128)(2,1)S(1)} %get-tuple-element.45), kind=kOutput, calls=%fused_computation.4 | convolution fusion | flops 134217728 | bytes 4521984 | tf_op jit(solution)/shard_map/md,dkc->kmc/dot_general | solution.py:458
  21.8 0.0 collective-permute-done.8.rest_9_
  21.8 0.2 collective-permute-done.7.rest_8_
  22.0 0.0 collective-permute-done.6.rest_7_
  22.0 1.4 %fresh_attention.1 = (bf16[4,8,256]{2,1,0:T(8,128)(2,1)}, bf16[4,8,256]{2,1,0:T(8,128)(2,1)}, bf16[4,8,2048]{2,1,0:T(8,128)(2,1)}) custom-call(f32[2,32,256]{2,1,0:T(8,128)S(1)} %fusion.4.near_ref, f32[2,32,256]{2,1,0:T(8,128)S(1)} %fusion.7.far_ref, f32[32,128]{1,0:T(8,128)S(1)} %get-tuple-element.48.square_ref, ...), custom_call_target="tpu_custom_call" | custom-call | tf_op jit(solution)/shard_map/fresh_attention/pallas_call | solution.py:446
  (1 shorter events, 0.0 us)
Async XLA Ops:
  1.5 11.2 %collective-permute-start = (bf16[2,16,2304]{2,1,0:T(8,128)(2,1)S(1)}, bf16[2,16,2304]{2,1,0:T(8,128)(2,1)S(1)}, u32[]{:S(2)}, u32[]{:S(2)}) collective-permute-start(bf16[2,16,2304]{2,1,0:T(8,128)(2,1)S(1)} %pack_factors.1.rest_2_.refs_0_), channel_id=1, source_target_pairs={{0,8},{4,12},{8,0},{12,4},{1,9},{5,13},{9,1},{13,5},{2,10},{6,14},... | collective-permute-start | bytes 442376 | tf_op jit(solution)/shard_map/ppermute | solution.py:462
  5.6 6.8 %collective-permute-start.1 = (bf16[4,8,2048]{2,1,0:T(8,128)(2,1)}, bf16[4,8,2048]{2,1,0:T(8,128)(2,1)S(1)}, u32[]{:S(2)}, u32[]{:S(2)}) collective-permute-start(bf16[4,8,2048]{2,1,0:T(8,128)(2,1)} %hidden_ref.1), channel_id=1, source_target_pairs={{0,2},{1,3},{2,0},{3,1},{4,6},{5,7},{6,4},{7,5},{8,10},{9,11},{10,... | collective-permute-start | bytes 393224 | tf_op jit(solution)/shard_map/ppermute | solution.py:462
  7.1 9.1 %collective-permute-start.4 = (bf16[2,16,2304]{2,1,0:T(8,128)(2,1)S(1)}, bf16[2,16,2304]{2,1,0:T(8,128)(2,1)S(1)}, u32[]{:S(2)}, u32[]{:S(2)}) collective-permute-start(bf16[2,16,2304]{2,1,0:T(8,128)(2,1)S(1)} %pack_factors.1.rest_2_.refs_0_), channel_id=1, source_target_pairs={{0,4},{4,0},{8,12},{12,8},{1,5},{5,1},{9,13},{13,9},{2,6},{6,2},{1... | collective-permute-start | bytes 442376 | tf_op jit(solution)/shard_map/ppermute | solution.py:462
  8.7 4.7 %copy-start = (bf16[4,8,2048]{2,1,0:T(8,128)(2,1)S(1)}, bf16[4,8,2048]{2,1,0:T(8,128)(2,1)}, u32[]{:S(2)}) copy-start(bf16[4,8,2048]{2,1,0:T(8,128)(2,1)} %hidden_ref.1) | copy-start | bytes 393220
  12.7 5.1 %collective-permute-start.5 = (bf16[2,16,2304]{2,1,0:T(8,128)(2,1)S(1)}, bf16[2,16,2304]{2,1,0:T(8,128)(2,1)S(1)}, u32[]{:S(2)}, u32[]{:S(2)}) collective-permute-start(bf16[2,16,2304]{2,1,0:T(8,128)(2,1)S(1)} %collective-permute-done.rest_4_.refs_2_), channel_id=1, source_target_pairs={{0,4},{4,0},{8,12},{12,8},{1,5},{5,1},{9,13},{13,9},{2,6},{6,2},{1... | collective-permute-start | bytes 442376 | tf_op jit(solution)/shard_map/ppermute | solution.py:462
  13.4 2.8 %collective-permute-start.2 = (bf16[4,8,2048]{2,1,0:T(8,128)(2,1)S(1)}, bf16[4,8,2048]{2,1,0:T(8,128)(2,1)S(1)}, u32[]{:S(2)}, u32[]{:S(2)}) collective-permute-start(bf16[4,8,2048]{2,1,0:T(8,128)(2,1)S(1)} %copy-done), channel_id=1, source_target_pairs={{0,1},{1,0},{2,3},{3,2},{4,5},{5,4},{6,7},{7,6},{8,9},{9,8},{10,11... | collective-permute-start | bytes 393224 | tf_op jit(solution)/shard_map/ppermute | solution.py:462
  13.4 2.8 %collective-permute-start.3 = (bf16[4,8,2048]{2,1,0:T(8,128)(2,1)S(1)}, bf16[4,8,2048]{2,1,0:T(8,128)(2,1)S(1)}, u32[]{:S(2)}, u32[]{:S(2)}) collective-permute-start(bf16[4,8,2048]{2,1,0:T(8,128)(2,1)S(1)} %collective-permute-done.1.rest_1_), channel_id=1, source_target_pairs={{0,1},{1,0},{2,3},{3,2},{4,5},{5,4},{6,7},{7,6},{8,9},{9,8},{10,11... | collective-permute-start | bytes 393224 | tf_op jit(solution)/shard_map/ppermute | solution.py:462
  18.2 3.6 %collective-permute-start.8 = (f32[32,32]{1,0:T(8,128)S(1)}, f32[32,32]{1,0:T(8,128)S(1)}, u32[]{:S(2)}, u32[]{:S(2)}) collective-permute-start(f32[32,32]{1,0:T(8,128)S(1)} %get-tuple-element.56.rest_6_), channel_id=1, source_target_pairs={{0,3},{1,2},{2,1},{3,0},{4,7},{5,6},{6,5},{7,4},{8,11},{9,10},{10,... | collective-permute-start | bytes 12296 | tf_op jit(solution)/shard_map/ppermute | solution.py:462
  18.2 3.8 %collective-permute-start.7 = (f32[32,32]{1,0:T(8,128)S(1)}, f32[32,32]{1,0:T(8,128)S(1)}, u32[]{:S(2)}, u32[]{:S(2)}) collective-permute-start(f32[32,32]{1,0:T(8,128)S(1)} %get-tuple-element.56.rest_6_), channel_id=1, source_target_pairs={{0,2},{1,3},{2,0},{3,1},{4,6},{5,7},{6,4},{7,5},{8,10},{9,11},{10,... | collective-permute-start | bytes 12296 | tf_op jit(solution)/shard_map/ppermute | solution.py:462
  19.8 2.2 %collective-permute-start.6 = (f32[32,32]{1,0:T(8,128)S(1)}, f32[32,32]{1,0:T(8,128)S(1)}, u32[]{:S(2)}, u32[]{:S(2)}) collective-permute-start(f32[32,32]{1,0:T(8,128)S(1)} %get-tuple-element.56.rest_6_), channel_id=1, source_target_pairs={{0,1},{1,0},{2,3},{3,2},{4,5},{5,4},{6,7},{7,6},{8,9},{9,8},{10,11... | collective-permute-start | bytes 12296 | tf_op jit(solution)/shard_map/ppermute | solution.py:462

commit v24 on v23

--- a/solution.py
+++ b/solution.py
@@ -239,10 +239,10 @@
         sin_out[pl.ds(step * rows, rows)] = jnp.where(second, sine, -sine)
 
 
-def scale_kernel(early, far, lengths_ref, weight_ref, gain_ref, *rest):
-    scaled_out, early_out, square_out, far_weight, cos_out, sin_out = rest[-9:-3]
+def scale_kernel(early, far, lengths_ref, weight_ref, gain_ref, query_ref, *rest):
+    scaled_out, early_out, square_out, far_weight, query_out, cos_out, sin_out = rest[-10:-3]
     lengths, length_sem, far_sems = rest[-3:]
-    parts = rest[:-9]
+    parts = rest[:-10]
     steps, rows, width = parts[0].shape
     length_copy = pltpu.make_async_copy(lengths_ref, lengths, length_sem)
     length_copy.start()
@@ -257,13 +257,14 @@
         scaled_out[:, pl.ds(pl.multiple_of(block * width, width), width)] = scaled
         early_out[:, k * width : (k + 1) * width] = scaled
     square_out[...] = total
+    query_out[...] = query_ref[...].astype(query_out.dtype)
     length_copy.wait()
     rotation_tables(lengths, steps, rows, cos_out, sin_out)
     for copy in copies:
         copy.wait()
 
 
-def scale_call(early, blocks, far, lengths, weight, gain, parts):
+def scale_call(early, blocks, far, lengths, weight, gain, queries, parts):
     steps, rows, width = parts[0].shape
     count = steps * rows
     return pl.pallas_call(
@@ -273,11 +274,12 @@
             pltpu.VMEM((count, len(early) * width), jnp.bfloat16),
             pltpu.VMEM((count, HD), jnp.float32),
             pltpu.VMEM((len(far) * width,) + weight.shape[1:], weight.dtype),
+            pltpu.VMEM(queries.shape, jnp.bfloat16),
             pltpu.VMEM((count, HD), jnp.float32),
             pltpu.VMEM((count, HD), jnp.float32),
         ),
-        in_specs=[HBM] * 2 + [VMEM] * (1 + len(parts)),
-        out_specs=(VMEM,) * 6,
+        in_specs=[HBM] * 2 + [VMEM] * (2 + len(parts)),
+        out_specs=(VMEM,) * 7,
         scratch_shapes=[
             pltpu.SMEM(lengths.shape, jnp.int32),
             pltpu.SemaphoreType.DMA,
@@ -286,7 +288,7 @@
         compiler_params=pltpu.CompilerParams(vmem_limit_bytes=8 << 20),
         cost_estimate=pl.CostEstimate(flops=0, bytes_accessed=9 << 20, transcendentals=0),
         name="scale_features",
-    )(*[pltpu.with_memory_space_constraint(x, pltpu.HBM) for x in (lengths, weight)], gain, *parts)
+    )(*[pltpu.with_memory_space_constraint(x, pltpu.HBM) for x in (lengths, weight)], gain, queries, *parts)
 
 
 def inner_kernel(late, scaled_ref, early_ref, square_ref, gain_ref, *rest):
@@ -377,7 +379,7 @@
 def final_kernel(width, blocks, near_ref, far_ref, square_ref, bias_ref, *rest):
     query_ref, acc_ref, top_ref, total_ref, cos_ref, sin_ref = rest[:6]
     inner_refs = rest[6 : 6 + blocks]
-    up_ref, keys_out, values_out, attended_out, inner_buffer = rest[6 + blocks :]
+    up_ref, keys_out, values_out, attended_out = rest[6 + blocks :]
     steps, rows, columns = keys_out.shape
     count = steps * rows
     groups, size, _ = query_ref.shape
@@ -386,14 +388,21 @@
     row_scale = lax.rsqrt(square_ref[...] * (1.0 / width) + norm_eps)
     row_scale = jnp.concatenate([row_scale] * groups, axis=1)
     me = lax.axis_index("tp") if blocks > 1 else 0
+    share = inner_refs[0].shape[1]
+    products = []
     for i in range(blocks):
-        inner_buffer[me ^ i] = inner_refs[i][...]
-    inner = jnp.concatenate([inner_buffer[i] for i in range(blocks)], axis=1)
-    high = inner.astype(jnp.bfloat16)
-    low = (inner - high.astype(jnp.float32)).astype(jnp.bfloat16)
-    lora = jnp.dot(
-        jnp.concatenate([high, low], axis=0), up_ref[...], preferred_element_type=jnp.float32
-    )
+        inner = inner_refs[i][...]
+        high = inner.astype(jnp.bfloat16)
+        low = (inner - high.astype(jnp.float32)).astype(jnp.bfloat16)
+        at = pl.multiple_of((me ^ i) * share, share)
+        products.append(
+            jnp.dot(
+                jnp.concatenate([high, low], axis=0),
+                up_ref[pl.ds(at, share), :],
+                preferred_element_type=jnp.float32,
+            )
+        )
+    lora = sum(products[1:], products[0])
     lora = lora[:count] + lora[count:]
     bias = bias_ref[...].astype(jnp.float32)
     linear = []
@@ -417,7 +426,7 @@
             keys_out[step, :, at] = key[step * rows : (step + 1) * rows]
             values_out[step, :, at] = value[step * rows : (step + 1) * rows]
         scores = lax.dot_general(
-            query_ref[group].astype(jnp.bfloat16),
+            query_ref[group],
             key,
             (((1,), (1,)), ((), ())),
             preferred_element_type=jnp.float32,
@@ -448,7 +457,6 @@
         out_shape=(small, small, jax.ShapeDtypeStruct(shape, jnp.bfloat16)),
         in_specs=[VMEM] * (5 + len(cached) + len(inner)),
         out_specs=(VMEM,) * 3,
-        scratch_shapes=[pltpu.VMEM((len(inner),) + inner[0].shape, jnp.float32)],
         compiler_params=pltpu.CompilerParams(vmem_limit_bytes=8 << 20),
         name="fresh_attention",
     )(near, far, square, bias, *cached, *inner, up)
@@ -489,7 +497,7 @@
         first = swap(pack, "wide", 1, wide_count)
     near, far = (0, 1), (2, 3)
     early, late = (0, 2), (1, 3)
-    near_weight, gain_rows, bias, mine, *cached = cache_call(
+    near_weight, gain_rows, bias, mine, query_rows, *cached = cache_call(
         near,
         lengths,
         queries,
@@ -505,8 +513,8 @@
     if direct:
         third, gain_rows = lax.optimization_barrier((second, gain_rows))
         packs = [pack, first, second, swap(third, "wide", 1, wide_count)]
-    scaled, early_scaled, square, far_weight, *tables = scale_call(
-        early, tp_count, far, lengths, key_value_weight, gain_rows, (mine, crossed)
+    scaled, early_scaled, square, far_weight, query_rows, *tables = scale_call(
+        early, tp_count, far, lengths, key_value_weight, gain_rows, query_rows, (mine, crossed)
     )
     late_parts = (beside, relayed)
     if direct:
@@ -531,7 +539,7 @@
     far_base = dot(far_scaled, far_weight)
     up = up_call(packs, bias.shape[1])
     return final_call(
-        queries.shape, width, near_base, far_base, square, bias, cached + tables, inner, up
+        queries.shape, width, near_base, far_base, square, bias, [query_rows] + cached + tables, inner, up
     )
 
 

time: 23.6 us -> 23.6 us (level)
  no operation moved by 1% of the time
where the time goes in v24:
time: 23.6 us; the launch traced here: 23.4 us
  starting transfers between devices  10.2 us (43%)
  Pallas kernels  8.57 us (36%)
  waiting for transfers between devices  2.19 us (9%)
  matrix products  1.68 us (7%)
  between operations  0.72 us (3%)
    ppermute x9, starting transfers between devices, swap(): return lax.ppermute(block, axis, [(i, i ^ offset) for i in range(count)])  10.2 us
    pallas_call x1, Pallas kernels, cache_call(): pl.pallas_call(functools.partial(cache_kernel, near), out_shape=(pltpu.VM...  3.73 us
    pallas_call x1, Pallas kernels, scale_call(): pl.pallas_call(functools.partial(scale_kernel, early, far), out_shape=(pl...  2.26 us
    ppermute x9, waiting for transfers between devices, swap(): return lax.ppermute(block, axis, [(i, i ^ offset) for i in range(count)])  2.19 us
    dot_general x2, matrix products, dot(): jnp.einsum('md,dkc->kmc', rows, weight, preferred_element_type=jnp.float32)  1.68 us
    pallas_call x1, Pallas kernels, final_call(): pl.pallas_call(functools.partial(final_kernel, width, len(inner)), out_sh...  1.34 us
    pallas_call x1, Pallas kernels, pack_call(): pl.pallas_call(pack_kernel, out_shape=pltpu.VMEM((kinds, share, down.shap...  0.87 us
  transfers between devices with their start and end apart: 9, of which 3 were waited for; matrix products, arithmetic and copies ran while one was open for 7% of the time, Pallas kernels for 26%

profile of v24, /device:TPU:0, one launch (start us, length us, event | category | flops | bytes accessed | tf_op | source)
XLA Modules:
  0.0 23.4 jit_solution(9650188974954180489)
XLA Ops:
  0.6 0.9 %pack_factors.1.rest_2_.refs_0_ = bf16[2,16,2304]{2,1,0:T(8,128)(2,1)S(1)} custom-call(bf16[2,64,2048]{2,1,0:T(8,128)(2,1)} %down_ref.1, bf16[2,16,256]{2,1,0:T(8,128)(2,1)} %bitcast.13), custom_call_target="tpu_custom_call" | custom-call | tf_op jit(solution)/shard_map/pack_factors/pallas_call | solution.py:201
  1.5 4.1 %collective-permute-start = (bf16[2,16,2304]{2,1,0:T(8,128)(2,1)S(1)}, bf16[2,16,2304]{2,1,0:T(8,128)(2,1)S(1)}, u32[]{:S(2)}, u32[]{:S(2)}) collective-permute-start(bf16[2,16,2304]{2,1,0:T(8,128)(2,1)S(1)} %pack_factors.1.rest_2_.refs_0_), channel_id=1, source_target_pairs={{0,8},{4,12},{8,0},{12,4},{1,9},{5,13},{9,1},{13,5},{2,10},{6,14},... | collective-permute-start | bytes 442376 | tf_op jit(solution)/shard_map/ppermute | solution.py:470
  5.6 1.5 %collective-permute-start.1 = (bf16[4,8,2048]{2,1,0:T(8,128)(2,1)}, bf16[4,8,2048]{2,1,0:T(8,128)(2,1)S(1)}, u32[]{:S(2)}, u32[]{:S(2)}) collective-permute-start(bf16[4,8,2048]{2,1,0:T(8,128)(2,1)} %hidden_ref.1), channel_id=1, source_target_pairs={{0,2},{1,3},{2,0},{3,1},{4,6},{5,7},{6,4},{7,5},{8,10},{9,11},{10,... | collective-permute-start | bytes 393224 | tf_op jit(solution)/shard_map/ppermute | solution.py:470
  7.1 1.6 %collective-permute-start.4 = (bf16[2,16,2304]{2,1,0:T(8,128)(2,1)S(1)}, bf16[2,16,2304]{2,1,0:T(8,128)(2,1)S(1)}, u32[]{:S(2)}, u32[]{:S(2)}) collective-permute-start(bf16[2,16,2304]{2,1,0:T(8,128)(2,1)S(1)} %pack_factors.1.rest_2_.refs_0_), channel_id=1, source_target_pairs={{0,4},{4,0},{8,12},{12,8},{1,5},{5,1},{9,13},{13,9},{2,6},{6,2},{1... | collective-permute-start | bytes 442376 | tf_op jit(solution)/shard_map/ppermute | solution.py:470
  8.7 0.0 copy-start
  8.7 3.7 %cache_attention.1 = (bf16[4096,2,256]{2,1,0:T(2,128)(2,1)S(1)}, f32[64,128]{1,0:T(8,128)S(1)}, bf16[2,256]{1,0:T(2,128)(2,1)S(1)}, bf16[4,8,2048]{2,1,0:T(8,128...) custom-call(s32[8]{0:T(128)} %lengths_ref.3, ...), custom_call_target="tpu_custom_call" | custom-call | flops 140509184 | bytes 5242880 | tf_op jit(solution)/shard_map/cache_attention/pallas_call | solution.py:148
  12.4 0.0 collective-permute-done.1.rest_1_
  12.4 0.3 %collective-permute-done.rest_4_.refs_2_ = bf16[2,16,2304]{2,1,0:T(8,128)(2,1)S(1)} collective-permute-done((bf16[2,16,2304]{2,1,0:T(8,128)(2,1)S(1)}, bf16[2,16,2304]{2,1,0:T(8,128)(2,1)S(1)}, u32[]{:S(2)}, u32[]{:S(2)}) %collective-permute-start) | collective-permute-done | bytes 147488 | tf_op jit(solution)/shard_map/ppermute | solution.py:470
  12.7 0.7 %collective-permute-start.5 = (bf16[2,16,2304]{2,1,0:T(8,128)(2,1)S(1)}, bf16[2,16,2304]{2,1,0:T(8,128)(2,1)S(1)}, u32[]{:S(2)}, u32[]{:S(2)}) collective-permute-start(bf16[2,16,2304]{2,1,0:T(8,128)(2,1)S(1)} %collective-permute-done.rest_4_.refs_2_), channel_id=1, source_target_pairs={{0,4},{4,0},{8,12},{12,8},{1,5},{5,1},{9,13},{13,9},{2,6},{6,2},{1... | collective-permute-start | bytes 442376 | tf_op jit(solution)/shard_map/ppermute | solution.py:470
  13.4 0.0 copy-done
  13.4 0.0 collective-permute-start.2
  13.4 0.5 %collective-permute-start.3 = (bf16[4,8,2048]{2,1,0:T(8,128)(2,1)S(1)}, bf16[4,8,2048]{2,1,0:T(8,128)(2,1)S(1)}, u32[]{:S(2)}, u32[]{:S(2)}) collective-permute-start(bf16[4,8,2048]{2,1,0:T(8,128)(2,1)S(1)} %collective-permute-done.1.rest_1_), channel_id=1, source_target_pairs={{0,1},{1,0},{2,3},{3,2},{4,5},{5,4},{6,7},{7,6},{8,9},{9,8},{10,11... | collective-permute-start | bytes 393224 | tf_op jit(solution)/shard_map/ppermute | solution.py:470
  13.9 2.3 %scale_features.1 = (bf16[32,8192]{1,0:T(8,128)(2,1)S(1)}, bf16[32,4096]{1,0:T(8,128)(2,1)S(1)}, f32[32,128]{1,0:T(8,128)S(1)}, bf16[4096,2,256]{2,1,0:T(2,128)(...) custom-call(s32[8]{0:T(128)} %lengths_ref.3, ...), custom_call_target="tpu_custom_call" | custom-call | bytes 9437184 | tf_op jit(solution)/shard_map/scale_features/pallas_call | solution.py:270
  16.2 0.0 collective-permute-done.2.rest_0_
  16.2 0.0 collective-permute-done.4.rest_3_.refs_1_
  16.2 0.0 collective-permute-done.3.rest_1_
  16.2 1.7 %collective-permute-done.5.rest_5_.refs_3_ = bf16[2,16,2304]{2,1,0:T(8,128)(2,1)S(1)} collective-permute-done((bf16[2,16,2304]{2,1,0:T(8,128)(2,1)S(1)}, bf16[2,16,2304]{2,1,0:T(8,128)(2,1)S(1)}, u32[]{:S(2)}, u32[]{:S(2)}) %collective-permute-start.5) | collective-permute-done | bytes 147488 | tf_op jit(solution)/shard_map/ppermute | solution.py:470
  17.9 0.3 %rank_inner.1 = (f32[32,32]{1,0:T(8,128)S(1)}, bf16[32,4096]{1,0:T(8,128)(2,1)S(1)}, bf16[32,4096]{1,0:T(8,128)(2,1)S(1)}, f32[32,128]{1,0:T(8,128)S(1)}) custom-call(bf16[32,8192]{1,0:T(8,128)(2,1)S(1)} %get-tuple-element.39.scaled_ref, bf16[32,4096]{1,0:T(8,128)(2,1)S(1)} %get-tuple-element.40.early_ref, f32[32,128]{1,0:T(8,128)S(1)} %get-tuple-element.41.square_ref, ...), custom_call_target="tpu_custom_call" | custom-call | tf_op jit(solution)/shard_map/rank_inner/pallas_call | solution.py:337
  18.2 0.0 collective-permute-start.8
  18.2 1.6 %collective-permute-start.7 = (f32[32,32]{1,0:T(8,128)S(1)}, f32[32,32]{1,0:T(8,128)S(1)}, u32[]{:S(2)}, u32[]{:S(2)}) collective-permute-start(f32[32,32]{1,0:T(8,128)S(1)} %get-tuple-element.58.rest_6_), channel_id=1, source_target_pairs={{0,2},{1,3},{2,0},{3,1},{4,6},{5,7},{6,4},{7,5},{8,10},{9,11},{10,... | collective-permute-start | bytes 12296 | tf_op jit(solution)/shard_map/ppermute | solution.py:470
  19.8 0.2 %collective-permute-start.6 = (f32[32,32]{1,0:T(8,128)S(1)}, f32[32,32]{1,0:T(8,128)S(1)}, u32[]{:S(2)}, u32[]{:S(2)}) collective-permute-start(f32[32,32]{1,0:T(8,128)S(1)} %get-tuple-element.58.rest_6_), channel_id=1, source_target_pairs={{0,1},{1,0},{2,3},{3,2},{4,5},{5,4},{6,7},{7,6},{8,9},{9,8},{10,11... | collective-permute-start | bytes 12296 | tf_op jit(solution)/shard_map/ppermute | solution.py:470
  20.1 0.8 %fusion.7.far_ref = f32[2,32,256]{2,1,0:T(8,128)S(1)} fusion(bf16[4096,2,256]{2,1,0:T(2,128)(2,1)S(1)} %get-tuple-element.48, bf16[32,4096]{1,0:T(8,128)(2,1)S(1)} %get-tuple-element.49), kind=kOutput, calls=%fused_computation.5 | convolution fusion | flops 134217728 | bytes 4521984 | tf_op jit(solution)/shard_map/md,dkc->kmc/dot_general | solution.py:466
  20.9 0.8 %fusion.4.near_ref = f32[2,32,256]{2,1,0:T(8,128)S(1)} fusion(bf16[4096,2,256]{2,1,0:T(2,128)(2,1)S(1)} %get-tuple-element.33, bf16[32,4096]{1,0:T(8,128)(2,1)S(1)} %get-tuple-element.47), kind=kOutput, calls=%fused_computation.4 | convolution fusion | flops 134217728 | bytes 4521984 | tf_op jit(solution)/shard_map/md,dkc->kmc/dot_general | solution.py:466
  21.8 0.0 collective-permute-done.8.rest_9_
  21.8 0.2 collective-permute-done.7.rest_8_
  22.0 0.0 collective-permute-done.6.rest_7_
  22.0 1.3 %fresh_attention.1 = (bf16[4,8,256]{2,1,0:T(8,128)(2,1)}, bf16[4,8,256]{2,1,0:T(8,128)(2,1)}, bf16[4,8,2048]{2,1,0:T(8,128)(2,1)}) custom-call(f32[2,32,256]{2,1,0:T(8,128)S(1)} %fusion.4.near_ref, f32[2,32,256]{2,1,0:T(8,128)S(1)} %fusion.7.far_ref, f32[32,128]{1,0:T(8,128)S(1)} %get-tuple-element.50.square_ref, ...), custom_call_target="tpu_custom_call" | custom-call | tf_op jit(solution)/shard_map/fresh_attention/pallas_call | solution.py:455
  (1 shorter events, 0.0 us)
Async XLA Ops:
  1.5 11.2 %collective-permute-start = (bf16[2,16,2304]{2,1,0:T(8,128)(2,1)S(1)}, bf16[2,16,2304]{2,1,0:T(8,128)(2,1)S(1)}, u32[]{:S(2)}, u32[]{:S(2)}) collective-permute-start(bf16[2,16,2304]{2,1,0:T(8,128)(2,1)S(1)} %pack_factors.1.rest_2_.refs_0_), channel_id=1, source_target_pairs={{0,8},{4,12},{8,0},{12,4},{1,9},{5,13},{9,1},{13,5},{2,10},{6,14},... | collective-permute-start | bytes 442376 | tf_op jit(solution)/shard_map/ppermute | solution.py:470
  5.6 6.8 %collective-permute-start.1 = (bf16[4,8,2048]{2,1,0:T(8,128)(2,1)}, bf16[4,8,2048]{2,1,0:T(8,128)(2,1)S(1)}, u32[]{:S(2)}, u32[]{:S(2)}) collective-permute-start(bf16[4,8,2048]{2,1,0:T(8,128)(2,1)} %hidden_ref.1), channel_id=1, source_target_pairs={{0,2},{1,3},{2,0},{3,1},{4,6},{5,7},{6,4},{7,5},{8,10},{9,11},{10,... | collective-permute-start | bytes 393224 | tf_op jit(solution)/shard_map/ppermute | solution.py:470
  7.1 9.1 %collective-permute-start.4 = (bf16[2,16,2304]{2,1,0:T(8,128)(2,1)S(1)}, bf16[2,16,2304]{2,1,0:T(8,128)(2,1)S(1)}, u32[]{:S(2)}, u32[]{:S(2)}) collective-permute-start(bf16[2,16,2304]{2,1,0:T(8,128)(2,1)S(1)} %pack_factors.1.rest_2_.refs_0_), channel_id=1, source_target_pairs={{0,4},{4,0},{8,12},{12,8},{1,5},{5,1},{9,13},{13,9},{2,6},{6,2},{1... | collective-permute-start | bytes 442376 | tf_op jit(solution)/shard_map/ppermute | solution.py:470
  8.7 4.7 %copy-start = (bf16[4,8,2048]{2,1,0:T(8,128)(2,1)S(1)}, bf16[4,8,2048]{2,1,0:T(8,128)(2,1)}, u32[]{:S(2)}) copy-start(bf16[4,8,2048]{2,1,0:T(8,128)(2,1)} %hidden_ref.1) | copy-start | bytes 393220
  12.7 5.1 %collective-permute-start.5 = (bf16[2,16,2304]{2,1,0:T(8,128)(2,1)S(1)}, bf16[2,16,2304]{2,1,0:T(8,128)(2,1)S(1)}, u32[]{:S(2)}, u32[]{:S(2)}) collective-permute-start(bf16[2,16,2304]{2,1,0:T(8,128)(2,1)S(1)} %collective-permute-done.rest_4_.refs_2_), channel_id=1, source_target_pairs={{0,4},{4,0},{8,12},{12,8},{1,5},{5,1},{9,13},{13,9},{2,6},{6,2},{1... | collective-permute-start | bytes 442376 | tf_op jit(solution)/shard_map/ppermute | solution.py:470
  13.4 2.8 %collective-permute-start.2 = (bf16[4,8,2048]{2,1,0:T(8,128)(2,1)S(1)}, bf16[4,8,2048]{2,1,0:T(8,128)(2,1)S(1)}, u32[]{:S(2)}, u32[]{:S(2)}) collective-permute-start(bf16[4,8,2048]{2,1,0:T(8,128)(2,1)S(1)} %copy-done), channel_id=1, source_target_pairs={{0,1},{1,0},{2,3},{3,2},{4,5},{5,4},{6,7},{7,6},{8,9},{9,8},{10,11... | collective-permute-start | bytes 393224 | tf_op jit(solution)/shard_map/ppermute | solution.py:470
  13.4 2.8 %collective-permute-start.3 = (bf16[4,8,2048]{2,1,0:T(8,128)(2,1)S(1)}, bf16[4,8,2048]{2,1,0:T(8,128)(2,1)S(1)}, u32[]{:S(2)}, u32[]{:S(2)}) collective-permute-start(bf16[4,8,2048]{2,1,0:T(8,128)(2,1)S(1)} %collective-permute-done.1.rest_1_), channel_id=1, source_target_pairs={{0,1},{1,0},{2,3},{3,2},{4,5},{5,4},{6,7},{7,6},{8,9},{9,8},{10,11... | collective-permute-start | bytes 393224 | tf_op jit(solution)/shard_map/ppermute | solution.py:470
  18.2 3.6 %collective-permute-start.8 = (f32[32,32]{1,0:T(8,128)S(1)}, f32[32,32]{1,0:T(8,128)S(1)}, u32[]{:S(2)}, u32[]{:S(2)}) collective-permute-start(f32[32,32]{1,0:T(8,128)S(1)} %get-tuple-element.58.rest_6_), channel_id=1, source_target_pairs={{0,3},{1,2},{2,1},{3,0},{4,7},{5,6},{6,5},{7,4},{8,11},{9,10},{10,... | collective-permute-start | bytes 12296 | tf_op jit(solution)/shard_map/ppermute | solution.py:470
  18.2 3.8 %collective-permute-start.7 = (f32[32,32]{1,0:T(8,128)S(1)}, f32[32,32]{1,0:T(8,128)S(1)}, u32[]{:S(2)}, u32[]{:S(2)}) collective-permute-start(f32[32,32]{1,0:T(8,128)S(1)} %get-tuple-element.58.rest_6_), channel_id=1, source_target_pairs={{0,2},{1,3},{2,0},{3,1},{4,6},{5,7},{6,4},{7,5},{8,10},{9,11},{10,... | collective-permute-start | bytes 12296 | tf_op jit(solution)/shard_map/ppermute | solution.py:470
  19.8 2.2 %collective-permute-start.6 = (f32[32,32]{1,0:T(8,128)S(1)}, f32[32,32]{1,0:T(8,128)S(1)}, u32[]{:S(2)}, u32[]{:S(2)}) collective-permute-start(f32[32,32]{1,0:T(8,128)S(1)} %get-tuple-element.58.rest_6_), channel_id=1, source_target_pairs={{0,1},{1,0},{2,3},{3,2},{4,5},{5,4},{6,7},{7,6},{8,9},{9,8},{10,11... | collective-permute-start | bytes 12296 | tf_op jit(solution)/shard_map/ppermute | solution.py:470

commit v25 on v24

--- a/solution.py
+++ b/solution.py
@@ -291,10 +291,10 @@
     )(*[pltpu.with_memory_space_constraint(x, pltpu.HBM) for x in (lengths, weight)], gain, queries, *parts)
 
 
-def inner_kernel(late, scaled_ref, early_ref, square_ref, gain_ref, *rest):
+def inner_kernel(late, scaled_ref, square_ref, gain_ref, *rest):
     parts, rest = rest[: len(late)], rest[len(late) :]
-    outs, square_out = rest[-1 - len(late) : -1], rest[-1]
-    packs, inner_out = (rest[: -2 - len(late)], rest[-2 - len(late)]) if len(rest) > 1 + len(late) else ((), None)
+    late_out, square_out = rest[-2:]
+    packs, inner_out = (rest[:-3], rest[-3]) if len(rest) > 2 else ((), None)
     squares = square_ref[...]
     blocks = []
     for k, (offset, part) in enumerate(zip(late, parts)):
@@ -303,8 +303,7 @@
         squares += more
         blocks.append((block, scaled))
         width = scaled.shape[1]
-        outs[k][:, :width] = early_ref[:, k * width : (k + 1) * width]
-        outs[k][:, width:] = scaled
+        late_out[:, k * width : (k + 1) * width] = scaled
     squares = jnp.sum(squares, axis=1, keepdims=True)
     square_out[...] = jnp.broadcast_to(squares, square_out.shape)
     if not packs:
@@ -327,21 +326,23 @@
     inner_out[...] = sum(total[1:], total[0])
 
 
-def inner_call(late, scaled, early, square, gain, parts, packs):
+def inner_call(late, scaled, square, gain, parts, packs):
     count, width = scaled.shape[0], parts[0].shape[2]
-    shapes = [pltpu.VMEM((count, 2 * width), scaled.dtype) for _ in late]
-    shapes.append(pltpu.VMEM(square.shape, jnp.float32))
+    shapes = [
+        pltpu.VMEM((count, len(late) * width), scaled.dtype),
+        pltpu.VMEM(square.shape, jnp.float32),
+    ]
     if packs:
         kinds, share, _ = packs[0].shape
         shapes = [pltpu.VMEM((count, kinds * share), jnp.float32)] + shapes
     return pl.pallas_call(
         functools.partial(inner_kernel, late),
         out_shape=tuple(shapes),
-        in_specs=[VMEM] * (4 + len(parts) + len(packs)),
+        in_specs=[VMEM] * (3 + len(parts) + len(packs)),
         out_specs=(VMEM,) * len(shapes),
         compiler_params=pltpu.CompilerParams(vmem_limit_bytes=8 << 20),
         name="rank_inner",
-    )(scaled, early, square, gain, *parts, *packs)
+    )(scaled, square, gain, *parts, *packs)
 
 
 def up_kernel(*refs):
@@ -490,15 +491,14 @@
     gain = input_norm_gain.reshape(width // HD, HD)
     up_part = jnp.transpose(adapter_up_factor, (0, 2, 1))
     direct = wide_count == tp_count == 4
-    beside, crossed = [swap(hidden, "tp", offset, tp_count) for offset in (1, 2)]
+    crossed = swap(hidden, "tp", 2, tp_count)
     if direct:
         pack = pack_call(adapter_down_factor, up_part)
         second = swap(pack, "wide", 2, wide_count)
         first = swap(pack, "wide", 1, wide_count)
-    near, far = (0, 1), (2, 3)
     early, late = (0, 2), (1, 3)
-    near_weight, gain_rows, bias, mine, query_rows, *cached = cache_call(
-        near,
+    early_weight, gain_rows, bias, mine, query_rows, *cached = cache_call(
+        early,
         lengths,
         queries,
         stored_rotated_keys,
@@ -508,38 +508,42 @@
         hidden,
         key_value_weight,
     )
-    relayed, gain_rows = lax.optimization_barrier((crossed, gain_rows))
+    beside = swap(mine, "tp", 1, tp_count)
+    if direct:
+        relayed, third, gain_rows = lax.optimization_barrier((crossed, second, gain_rows))
+    else:
+        relayed = crossed
     relayed = swap(relayed, "tp", 1, tp_count)
     if direct:
-        third, gain_rows = lax.optimization_barrier((second, gain_rows))
         packs = [pack, first, second, swap(third, "wide", 1, wide_count)]
-    scaled, early_scaled, square, far_weight, query_rows, *tables = scale_call(
-        early, tp_count, far, lengths, key_value_weight, gain_rows, query_rows, (mine, crossed)
+    scaled, early_scaled, square, late_weight, query_rows, *tables = scale_call(
+        early, tp_count, late, lengths, key_value_weight, gain_rows, query_rows, (mine, crossed)
     )
     late_parts = (beside, relayed)
+    early_base = dot(early_scaled, early_weight)
     if direct:
-        inner, near_scaled, far_scaled, square = inner_call(
-            late, scaled, early_scaled, square, gain_rows, late_parts, packs
+        scaled, early_base = lax.optimization_barrier((scaled, early_base))
+        inner, late_scaled, square = inner_call(
+            late, scaled, square, gain_rows, late_parts, packs
         )
-        inner, far_scaled, near_scaled, packs = lax.optimization_barrier(
-            (inner, far_scaled, near_scaled, packs)
-        )
-        inner = [inner] + [swap(inner, "tp", offset, tp_count) for offset in (1, 2, 3)]
+        inner, late_scaled, packs = lax.optimization_barrier((inner, late_scaled, packs))
+        diagonal = swap(inner, "tp", 3, tp_count)
+        across = swap(inner, "tp", 2, tp_count)
+        beside = swap(inner, "tp", 1, tp_count)
+        both, beside = lax.optimization_barrier((diagonal + across, beside))
+        inner = [inner, beside, across, diagonal]
     else:
-        near_scaled, far_scaled, square = inner_call(
-            late, scaled, early_scaled, square, gain_rows, late_parts, []
-        )
+        late_scaled, square = inner_call(late, scaled, square, gain_rows, late_parts, [])
         down = lax.all_gather(adapter_down_factor, "wide", axis=2, tiled=True)
         rows_full = lax.all_gather(hidden, "tp", axis=2, tiled=True).astype(jnp.float32)
         rows_full = (rows_full * input_norm_gain.astype(jnp.float32)).astype(jnp.bfloat16)
         inner = jnp.einsum("srd,kad->srka", rows_full, down, preferred_element_type=jnp.float32)
         inner = [inner.reshape(steps * rows, kinds * ranks)]
         packs = [lax.all_gather(up_part, "wide", axis=1, tiled=True)]
-    near_base = dot(near_scaled, near_weight)
-    far_base = dot(far_scaled, far_weight)
+    late_base = dot(late_scaled, late_weight)
     up = up_call(packs, bias.shape[1])
     return final_call(
-        queries.shape, width, near_base, far_base, square, bias, [query_rows] + cached + tables, inner, up
+        queries.shape, width, early_base, late_base, square, bias, [query_rows] + cached + tables, inner, up
     )
 
 

time: 23.6 us -> 24.7 us (1.047)
  waiting for transfers between devices: 2.19 us -> 3.46 us
    ppermute x9, waiting for transfers between devices: 2.19 us -> 3.46 us  [swap(): return lax.ppermute(block, axis, [(i, i ^ offset) for i in range(count)])]
  transfers between devices with their start and end apart: 9 -> 9, of which waited for: 3 -> 4; matrix products, arithmetic and copies ran while one was open for 7% -> 7% of each run, Pallas kernels for 26% -> 25%
where the time goes in v25:
time: 24.7 us; the launch traced here: 24.4 us
  starting transfers between devices  10.1 us (41%)
  Pallas kernels  8.52 us (34%)
  waiting for transfers between devices  3.46 us (14%)
  matrix products  1.67 us (7%)
  between operations  0.71 us (3%)
    ppermute x9, starting transfers between devices, swap(): return lax.ppermute(block, axis, [(i, i ^ offset) for i in range(count)])  10.1 us
    pallas_call x1, Pallas kernels, cache_call(): pl.pallas_call(functools.partial(cache_kernel, near), out_shape=(pltpu.VM...  3.7 us
    ppermute x9, waiting for transfers between devices, swap(): return lax.ppermute(block, axis, [(i, i ^ offset) for i in range(count)])  3.46 us
    pallas_call x1, Pallas kernels, scale_call(): pl.pallas_call(functools.partial(scale_kernel, early, far), out_shape=(pl...  2.26 us
    dot_general x2, matrix products, dot(): jnp.einsum('md,dkc->kmc', rows, weight, preferred_element_type=jnp.float32)  1.67 us
    pallas_call x1, Pallas kernels, final_call(): pl.pallas_call(functools.partial(final_kernel, width, len(inner)), out_sh...  1.34 us
    pallas_call x1, Pallas kernels, pack_call(): pl.pallas_call(pack_kernel, out_shape=pltpu.VMEM((kinds, share, down.shap...  0.87 us
  transfers between devices with their start and end apart: 9, of which 4 were waited for; matrix products, arithmetic and copies ran while one was open for 7% of the time, Pallas kernels for 25%

profile of v25, /device:TPU:0, one launch (start us, length us, event | category | flops | bytes accessed | tf_op | source)
XLA Modules:
  0.0 24.4 jit_solution(537241160582907926)
XLA Ops:
  0.6 0.9 %pack_factors.1.rest_2_.refs_0_ = bf16[2,16,2304]{2,1,0:T(8,128)(2,1)S(1)} custom-call(bf16[2,64,2048]{2,1,0:T(8,128)(2,1)} %down_ref.1, bf16[2,16,256]{2,1,0:T(8,128)(2,1)} %bitcast.13), custom_call_target="tpu_custom_call" | custom-call | tf_op jit(solution)/shard_map/pack_factors/pallas_call | solution.py:201
  1.5 4.1 %collective-permute-start.1 = (bf16[2,16,2304]{2,1,0:T(8,128)(2,1)S(1)}, bf16[2,16,2304]{2,1,0:T(8,128)(2,1)S(1)}, u32[]{:S(2)}, u32[]{:S(2)}) collective-permute-start(bf16[2,16,2304]{2,1,0:T(8,128)(2,1)S(1)} %pack_factors.1.rest_2_.refs_0_), channel_id=1, source_target_pairs={{0,8},{4,12},{8,0},{12,4},{1,9},{5,13},{9,1},{13,5},{2,10},{6,14},... | collective-permute-start | bytes 442376 | tf_op jit(solution)/shard_map/ppermute | solution.py:471
  5.6 1.5 %collective-permute-start = (bf16[4,8,2048]{2,1,0:T(8,128)(2,1)}, bf16[4,8,2048]{2,1,0:T(8,128)(2,1)S(1)}, u32[]{:S(2)}, u32[]{:S(2)}) collective-permute-start(bf16[4,8,2048]{2,1,0:T(8,128)(2,1)} %hidden_ref.1), channel_id=1, source_target_pairs={{0,2},{1,3},{2,0},{3,1},{4,6},{5,7},{6,4},{7,5},{8,10},{9,11},{10,... | collective-permute-start | bytes 393224 | tf_op jit(solution)/shard_map/ppermute | solution.py:471
  7.1 1.6 %collective-permute-start.4 = (bf16[2,16,2304]{2,1,0:T(8,128)(2,1)S(1)}, bf16[2,16,2304]{2,1,0:T(8,128)(2,1)S(1)}, u32[]{:S(2)}, u32[]{:S(2)}) collective-permute-start(bf16[2,16,2304]{2,1,0:T(8,128)(2,1)S(1)} %pack_factors.1.rest_2_.refs_0_), channel_id=1, source_target_pairs={{0,4},{4,0},{8,12},{12,8},{1,5},{5,1},{9,13},{13,9},{2,6},{6,2},{1... | collective-permute-start | bytes 442376 | tf_op jit(solution)/shard_map/ppermute | solution.py:471
  8.7 3.7 %cache_attention.1 = (bf16[4096,2,256]{2,1,0:T(2,128)(2,1)S(1)}, f32[64,128]{1,0:T(8,128)S(1)}, bf16[2,256]{1,0:T(2,128)(2,1)S(1)}, bf16[4,8,2048]{2,1,0:T(8,128...) custom-call(s32[8]{0:T(128)} %lengths_ref.3, ...), custom_call_target="tpu_custom_call" | custom-call | flops 140509184 | bytes 5242880 | tf_op jit(solution)/shard_map/cache_attention/pallas_call | solution.py:148
  12.4 0.1 collective-permute-start.2
  12.5 0.0 collective-permute-done.rest_1_
  12.5 0.2 %collective-permute-done.1.rest_4_.refs_2_ = bf16[2,16,2304]{2,1,0:T(8,128)(2,1)S(1)} collective-permute-done((bf16[2,16,2304]{2,1,0:T(8,128)(2,1)S(1)}, bf16[2,16,2304]{2,1,0:T(8,128)(2,1)S(1)}, u32[]{:S(2)}, u32[]{:S(2)}) %collective-permute-start.1) | collective-permute-done | bytes 147488 | tf_op jit(solution)/shard_map/ppermute | solution.py:471
  12.7 0.7 %collective-permute-start.5 = (bf16[2,16,2304]{2,1,0:T(8,128)(2,1)S(1)}, bf16[2,16,2304]{2,1,0:T(8,128)(2,1)S(1)}, u32[]{:S(2)}, u32[]{:S(2)}) collective-permute-start(bf16[2,16,2304]{2,1,0:T(8,128)(2,1)S(1)} %collective-permute-done.1.rest_4_.refs_2_), channel_id=1, source_target_pairs={{0,4},{4,0},{8,12},{12,8},{1,5},{5,1},{9,13},{13,9},{2,6},{6,2},{1... | collective-permute-start | bytes 442376 | tf_op jit(solution)/shard_map/ppermute | solution.py:471
  13.4 0.0 collective-permute-start.3
  13.4 2.3 %scale_features.1 = (bf16[32,8192]{1,0:T(8,128)(2,1)S(1)}, bf16[32,4096]{1,0:T(8,128)(2,1)S(1)}, f32[32,128]{1,0:T(8,128)S(1)}, bf16[4096,2,256]{2,1,0:T(2,128)(...) custom-call(s32[8]{0:T(128)} %lengths_ref.3, ...), custom_call_target="tpu_custom_call" | custom-call | bytes 9437184 | tf_op jit(solution)/shard_map/scale_features/pallas_call | solution.py:270
  15.7 0.8 %fusion.4.near_ref = f32[2,32,256]{2,1,0:T(8,128)S(1)} fusion(bf16[4096,2,256]{2,1,0:T(2,128)(2,1)S(1)} %get-tuple-element.37, bf16[32,4096]{1,0:T(8,128)(2,1)S(1)} %get-tuple-element.38), kind=kOutput, calls=%fused_computation.4 | convolution fusion | flops 134217728 | bytes 4521984 | tf_op jit(solution)/shard_map/md,dkc->kmc/dot_general | solution.py:467
  16.5 0.0 collective-permute-done.2.rest_0_
  16.5 0.0 collective-permute-done.4.rest_3_.refs_1_
  16.5 0.0 collective-permute-done.3.rest_1_
  16.5 2.2 %collective-permute-done.5.rest_5_.refs_3_ = bf16[2,16,2304]{2,1,0:T(8,128)(2,1)S(1)} collective-permute-done((bf16[2,16,2304]{2,1,0:T(8,128)(2,1)S(1)}, bf16[2,16,2304]{2,1,0:T(8,128)(2,1)S(1)}, u32[]{:S(2)}, u32[]{:S(2)}) %collective-permute-start.5) | collective-permute-done | bytes 147488 | tf_op jit(solution)/shard_map/ppermute | solution.py:471
  18.7 0.3 %rank_inner.1 = (f32[32,32]{1,0:T(8,128)S(1)}, bf16[32,4096]{1,0:T(8,128)(2,1)S(1)}, f32[32,128]{1,0:T(8,128)S(1)}) custom-call(bf16[32,8192]{1,0:T(8,128)(2,1)S(1)} %get-tuple-element.41.scaled_ref, f32[32,128]{1,0:T(8,128)S(1)} %get-tuple-element.42.square_ref, f32[64,128]{1,0:T(8,128)S(1)} %get-tuple-element.33.gain_ref, ...), custom_call_target="tpu_custom_call" | custom-call | tf_op jit(solution)/shard_map/rank_inner/pallas_call | solution.py:338
  19.0 0.7 %collective-permute-start.7 = (f32[32,32]{1,0:T(8,128)S(1)}, f32[32,32]{1,0:T(8,128)S(1)}, u32[]{:S(2)}, u32[]{:S(2)}) collective-permute-start(f32[32,32]{1,0:T(8,128)S(1)} %get-tuple-element.56.rest_6_), channel_id=1, source_target_pairs={{0,2},{1,3},{2,0},{3,1},{4,6},{5,7},{6,4},{7,5},{8,10},{9,11},{10,... | collective-permute-start | bytes 12296 | tf_op jit(solution)/shard_map/ppermute | solution.py:471
  19.7 0.1 collective-permute-start.8
  19.9 1.4 %collective-permute-start.6 = (f32[32,32]{1,0:T(8,128)S(1)}, f32[32,32]{1,0:T(8,128)S(1)}, u32[]{:S(2)}, u32[]{:S(2)}) collective-permute-start(f32[32,32]{1,0:T(8,128)S(1)} %get-tuple-element.56.rest_6_), channel_id=1, source_target_pairs={{0,1},{1,0},{2,3},{3,2},{4,5},{5,4},{6,7},{7,6},{8,9},{9,8},{10,11... | collective-permute-start | bytes 12296 | tf_op jit(solution)/shard_map/ppermute | solution.py:471
  21.2 0.8 %fusion.7.far_ref = f32[2,32,256]{2,1,0:T(8,128)S(1)} fusion(bf16[4096,2,256]{2,1,0:T(2,128)(2,1)S(1)} %get-tuple-element.40, bf16[32,4096]{1,0:T(8,128)(2,1)S(1)} %get-tuple-element.47), kind=kOutput, calls=%fused_computation.5 | convolution fusion | flops 134217728 | bytes 4521984 | tf_op jit(solution)/shard_map/md,dkc->kmc/dot_general | solution.py:467
  22.1 0.0 collective-permute-done.6.rest_7_
  22.1 0.8 %collective-permute-done.7.rest_8_ = f32[32,32]{1,0:T(8,128)S(1)} collective-permute-done((f32[32,32]{1,0:T(8,128)S(1)}, f32[32,32]{1,0:T(8,128)S(1)}, u32[]{:S(2)}, u32[]{:S(2)}) %collective-permute-start.7) | collective-permute-done | bytes 4128 | tf_op jit(solution)/shard_map/ppermute | solution.py:471
  22.9 0.2 collective-permute-done.8.rest_9_
  23.1 1.3 %fresh_attention.1 = (bf16[4,8,256]{2,1,0:T(8,128)(2,1)}, bf16[4,8,256]{2,1,0:T(8,128)(2,1)}, bf16[4,8,2048]{2,1,0:T(8,128)(2,1)}) custom-call(f32[2,32,256]{2,1,0:T(8,128)S(1)} %fusion.4.near_ref, f32[2,32,256]{2,1,0:T(8,128)S(1)} %fusion.7.far_ref, f32[32,128]{1,0:T(8,128)S(1)} %get-tuple-element.48.square_ref, ...), custom_call_target="tpu_custom_call" | custom-call | tf_op jit(solution)/shard_map/fresh_attention/pallas_call | solution.py:456
  (1 shorter events, 0.0 us)
Async XLA Ops:
  1.5 11.2 %collective-permute-start.1 = (bf16[2,16,2304]{2,1,0:T(8,128)(2,1)S(1)}, bf16[2,16,2304]{2,1,0:T(8,128)(2,1)S(1)}, u32[]{:S(2)}, u32[]{:S(2)}) collective-permute-start(bf16[2,16,2304]{2,1,0:T(8,128)(2,1)S(1)} %pack_factors.1.rest_2_.refs_0_), channel_id=1, source_target_pairs={{0,8},{4,12},{8,0},{12,4},{1,9},{5,13},{9,1},{13,5},{2,10},{6,14},... | collective-permute-start | bytes 442376 | tf_op jit(solution)/shard_map/ppermute | solution.py:471
  5.6 6.9 %collective-permute-start = (bf16[4,8,2048]{2,1,0:T(8,128)(2,1)}, bf16[4,8,2048]{2,1,0:T(8,128)(2,1)S(1)}, u32[]{:S(2)}, u32[]{:S(2)}) collective-permute-start(bf16[4,8,2048]{2,1,0:T(8,128)(2,1)} %hidden_ref.1), channel_id=1, source_target_pairs={{0,2},{1,3},{2,0},{3,1},{4,6},{5,7},{6,4},{7,5},{8,10},{9,11},{10,... | collective-permute-start | bytes 393224 | tf_op jit(solution)/shard_map/ppermute | solution.py:471
  7.1 9.4 %collective-permute-start.4 = (bf16[2,16,2304]{2,1,0:T(8,128)(2,1)S(1)}, bf16[2,16,2304]{2,1,0:T(8,128)(2,1)S(1)}, u32[]{:S(2)}, u32[]{:S(2)}) collective-permute-start(bf16[2,16,2304]{2,1,0:T(8,128)(2,1)S(1)} %pack_factors.1.rest_2_.refs_0_), channel_id=1, source_target_pairs={{0,4},{4,0},{8,12},{12,8},{1,5},{5,1},{9,13},{13,9},{2,6},{6,2},{1... | collective-permute-start | bytes 442376 | tf_op jit(solution)/shard_map/ppermute | solution.py:471
  12.4 4.1 %collective-permute-start.2 = (bf16[4,8,2048]{2,1,0:T(8,128)(2,1)S(1)}, bf16[4,8,2048]{2,1,0:T(8,128)(2,1)S(1)}, u32[]{:S(2)}, u32[]{:S(2)}) collective-permute-start(bf16[4,8,2048]{2,1,0:T(8,128)(2,1)S(1)} %get-tuple-element.35.rest_0_), channel_id=1, source_target_pairs={{0,1},{1,0},{2,3},{3,2},{4,5},{5,4},{6,7},{7,6},{8,9},{9,8},{10,11... | collective-permute-start | bytes 393224 | tf_op jit(solution)/shard_map/ppermute | solution.py:471
  12.7 6.0 %collective-permute-start.5 = (bf16[2,16,2304]{2,1,0:T(8,128)(2,1)S(1)}, bf16[2,16,2304]{2,1,0:T(8,128)(2,1)S(1)}, u32[]{:S(2)}, u32[]{:S(2)}) collective-permute-start(bf16[2,16,2304]{2,1,0:T(8,128)(2,1)S(1)} %collective-permute-done.1.rest_4_.refs_2_), channel_id=1, source_target_pairs={{0,4},{4,0},{8,12},{12,8},{1,5},{5,1},{9,13},{13,9},{2,6},{6,2},{1... | collective-permute-start | bytes 442376 | tf_op jit(solution)/shard_map/ppermute | solution.py:471
  13.4 3.1 %collective-permute-start.3 = (bf16[4,8,2048]{2,1,0:T(8,128)(2,1)S(1)}, bf16[4,8,2048]{2,1,0:T(8,128)(2,1)S(1)}, u32[]{:S(2)}, u32[]{:S(2)}) collective-permute-start(bf16[4,8,2048]{2,1,0:T(8,128)(2,1)S(1)} %collective-permute-done.rest_1_), channel_id=1, source_target_pairs={{0,1},{1,0},{2,3},{3,2},{4,5},{5,4},{6,7},{7,6},{8,9},{9,8},{10,11... | collective-permute-start | bytes 393224 | tf_op jit(solution)/shard_map/ppermute | solution.py:471
  19.0 3.8 %collective-permute-start.7 = (f32[32,32]{1,0:T(8,128)S(1)}, f32[32,32]{1,0:T(8,128)S(1)}, u32[]{:S(2)}, u32[]{:S(2)}) collective-permute-start(f32[32,32]{1,0:T(8,128)S(1)} %get-tuple-element.56.rest_6_), channel_id=1, source_target_pairs={{0,2},{1,3},{2,0},{3,1},{4,6},{5,7},{6,4},{7,5},{8,10},{9,11},{10,... | collective-permute-start | bytes 12296 | tf_op jit(solution)/shard_map/ppermute | solution.py:471
  19.7 3.3 %collective-permute-start.8 = (f32[32,32]{1,0:T(8,128)S(1)}, f32[32,32]{1,0:T(8,128)S(1)}, u32[]{:S(2)}, u32[]{:S(2)}) collective-permute-start(f32[32,32]{1,0:T(8,128)S(1)} %get-tuple-element.56.rest_6_), channel_id=1, source_target_pairs={{0,3},{1,2},{2,1},{3,0},{4,7},{5,6},{6,5},{7,4},{8,11},{9,10},{10,... | collective-permute-start | bytes 12296 | tf_op jit(solution)/shard_map/ppermute | solution.py:471
  19.9 2.2 %collective-permute-start.6 = (f32[32,32]{1,0:T(8,128)S(1)}, f32[32,32]{1,0:T(8,128)S(1)}, u32[]{:S(2)}, u32[]{:S(2)}) collective-permute-start(f32[32,32]{1,0:T(8,128)S(1)} %get-tuple-element.56.rest_6_), channel_id=1, source_target_pairs={{0,1},{1,0},{2,3},{3,2},{4,5},{5,4},{6,7},{7,6},{8,9},{9,8},{10,11... | collective-permute-start | bytes 12296 | tf_op jit(solution)/shard_map/ppermute | solution.py:471

commit v26 on v25

--- a/solution.py
+++ b/solution.py
@@ -491,7 +491,7 @@
     gain = input_norm_gain.reshape(width // HD, HD)
     up_part = jnp.transpose(adapter_up_factor, (0, 2, 1))
     direct = wide_count == tp_count == 4
-    crossed = swap(hidden, "tp", 2, tp_count)
+    beside, crossed = [swap(hidden, "tp", offset, tp_count) for offset in (1, 2)]
     if direct:
         pack = pack_call(adapter_down_factor, up_part)
         second = swap(pack, "wide", 2, wide_count)
@@ -508,7 +508,6 @@
         hidden,
         key_value_weight,
     )
-    beside = swap(mine, "tp", 1, tp_count)
     if direct:
         relayed, third, gain_rows = lax.optimization_barrier((crossed, second, gain_rows))
     else:

time: 24.7 us -> 24.7 us (level)
  no operation moved by 1% of the time
where the time goes in v26:
time: 24.7 us; the launch traced here: 24.4 us
  starting transfers between devices  10 us (40%)
  Pallas kernels  8.52 us (34%)
  waiting for transfers between devices  3.54 us (14%)
  matrix products  1.66 us (7%)
  between operations  0.7 us (3%)
    ppermute x9, starting transfers between devices, swap(): return lax.ppermute(block, axis, [(i, i ^ offset) for i in range(count)])  10 us
    pallas_call x1, Pallas kernels, cache_call(): pl.pallas_call(functools.partial(cache_kernel, near), out_shape=(pltpu.VM...  3.7 us
    ppermute x9, waiting for transfers between devices, swap(): return lax.ppermute(block, axis, [(i, i ^ offset) for i in range(count)])  3.54 us
    pallas_call x1, Pallas kernels, scale_call(): pl.pallas_call(functools.partial(scale_kernel, early, far), out_shape=(pl...  2.26 us
    dot_general x2, matrix products, dot(): jnp.einsum('md,dkc->kmc', rows, weight, preferred_element_type=jnp.float32)  1.66 us
    pallas_call x1, Pallas kernels, final_call(): pl.pallas_call(functools.partial(final_kernel, width, len(inner)), out_sh...  1.34 us
    pallas_call x1, Pallas kernels, pack_call(): pl.pallas_call(pack_kernel, out_shape=pltpu.VMEM((kinds, share, down.shap...  0.87 us
  transfers between devices with their start and end apart: 9, of which 4 were waited for; matrix products, arithmetic and copies ran while one was open for 7% of the time, Pallas kernels for 25%

profile of v26, /device:TPU:0, one launch (start us, length us, event | category | flops | bytes accessed | tf_op | source)
XLA Modules:
  0.0 24.4 jit_solution(676813642496395595)
XLA Ops:
  0.6 0.9 %pack_factors.1.rest_2_.refs_0_ = bf16[2,16,2304]{2,1,0:T(8,128)(2,1)S(1)} custom-call(bf16[2,64,2048]{2,1,0:T(8,128)(2,1)} %down_ref.1, bf16[2,16,256]{2,1,0:T(8,128)(2,1)} %bitcast.13), custom_call_target="tpu_custom_call" | custom-call | tf_op jit(solution)/shard_map/pack_factors/pallas_call | solution.py:201
  1.5 4.1 %collective-permute-start.1 = (bf16[2,16,2304]{2,1,0:T(8,128)(2,1)S(1)}, bf16[2,16,2304]{2,1,0:T(8,128)(2,1)S(1)}, u32[]{:S(2)}, u32[]{:S(2)}) collective-permute-start(bf16[2,16,2304]{2,1,0:T(8,128)(2,1)S(1)} %pack_factors.1.rest_2_.refs_0_), channel_id=1, source_target_pairs={{0,8},{4,12},{8,0},{12,4},{1,9},{5,13},{9,1},{13,5},{2,10},{6,14},... | collective-permute-start | bytes 442376 | tf_op jit(solution)/shard_map/ppermute | solution.py:471
  5.6 1.5 %collective-permute-start = (bf16[4,8,2048]{2,1,0:T(8,128)(2,1)}, bf16[4,8,2048]{2,1,0:T(8,128)(2,1)S(1)}, u32[]{:S(2)}, u32[]{:S(2)}) collective-permute-start(bf16[4,8,2048]{2,1,0:T(8,128)(2,1)} %hidden_ref.1), channel_id=1, source_target_pairs={{0,2},{1,3},{2,0},{3,1},{4,6},{5,7},{6,4},{7,5},{8,10},{9,11},{10,... | collective-permute-start | bytes 393224 | tf_op jit(solution)/shard_map/ppermute | solution.py:471
  7.1 1.6 %collective-permute-start.4 = (bf16[2,16,2304]{2,1,0:T(8,128)(2,1)S(1)}, bf16[2,16,2304]{2,1,0:T(8,128)(2,1)S(1)}, u32[]{:S(2)}, u32[]{:S(2)}) collective-permute-start(bf16[2,16,2304]{2,1,0:T(8,128)(2,1)S(1)} %pack_factors.1.rest_2_.refs_0_), channel_id=1, source_target_pairs={{0,4},{4,0},{8,12},{12,8},{1,5},{5,1},{9,13},{13,9},{2,6},{6,2},{1... | collective-permute-start | bytes 442376 | tf_op jit(solution)/shard_map/ppermute | solution.py:471
  8.7 0.0 collective-permute-start.2
  8.7 3.7 %cache_attention.1 = (bf16[4096,2,256]{2,1,0:T(2,128)(2,1)S(1)}, f32[64,128]{1,0:T(8,128)S(1)}, bf16[2,256]{1,0:T(2,128)(2,1)S(1)}, bf16[4,8,2048]{2,1,0:T(8,128...) custom-call(s32[8]{0:T(128)} %lengths_ref.3, ...), custom_call_target="tpu_custom_call" | custom-call | flops 140509184 | bytes 5242880 | tf_op jit(solution)/shard_map/cache_attention/pallas_call | solution.py:148
  12.4 0.0 collective-permute-done.rest_1_
  12.4 0.3 %collective-permute-done.1.rest_4_.refs_2_ = bf16[2,16,2304]{2,1,0:T(8,128)(2,1)S(1)} collective-permute-done((bf16[2,16,2304]{2,1,0:T(8,128)(2,1)S(1)}, bf16[2,16,2304]{2,1,0:T(8,128)(2,1)S(1)}, u32[]{:S(2)}, u32[]{:S(2)}) %collective-permute-start.1) | collective-permute-done | bytes 147488 | tf_op jit(solution)/shard_map/ppermute | solution.py:471
  12.7 0.7 %collective-permute-start.5 = (bf16[2,16,2304]{2,1,0:T(8,128)(2,1)S(1)}, bf16[2,16,2304]{2,1,0:T(8,128)(2,1)S(1)}, u32[]{:S(2)}, u32[]{:S(2)}) collective-permute-start(bf16[2,16,2304]{2,1,0:T(8,128)(2,1)S(1)} %collective-permute-done.1.rest_4_.refs_2_), channel_id=1, source_target_pairs={{0,4},{4,0},{8,12},{12,8},{1,5},{5,1},{9,13},{13,9},{2,6},{6,2},{1... | collective-permute-start | bytes 442376 | tf_op jit(solution)/shard_map/ppermute | solution.py:471
  13.4 0.0 collective-permute-start.3
  13.4 2.3 %scale_features.1 = (bf16[32,8192]{1,0:T(8,128)(2,1)S(1)}, bf16[32,4096]{1,0:T(8,128)(2,1)S(1)}, f32[32,128]{1,0:T(8,128)S(1)}, bf16[4096,2,256]{2,1,0:T(2,128)(...) custom-call(s32[8]{0:T(128)} %lengths_ref.3, ...), custom_call_target="tpu_custom_call" | custom-call | bytes 9437184 | tf_op jit(solution)/shard_map/scale_features/pallas_call | solution.py:270
  15.7 0.8 %fusion.4.near_ref = f32[2,32,256]{2,1,0:T(8,128)S(1)} fusion(bf16[4096,2,256]{2,1,0:T(2,128)(2,1)S(1)} %get-tuple-element.37, bf16[32,4096]{1,0:T(8,128)(2,1)S(1)} %get-tuple-element.38), kind=kOutput, calls=%fused_computation.4 | convolution fusion | flops 134217728 | bytes 4521984 | tf_op jit(solution)/shard_map/md,dkc->kmc/dot_general | solution.py:467
  16.5 0.0 collective-permute-done.2.rest_0_
  16.5 0.0 collective-permute-done.4.rest_3_.refs_1_
  16.5 0.0 collective-permute-done.3.rest_1_
  16.5 2.2 %collective-permute-done.5.rest_5_.refs_3_ = bf16[2,16,2304]{2,1,0:T(8,128)(2,1)S(1)} collective-permute-done((bf16[2,16,2304]{2,1,0:T(8,128)(2,1)S(1)}, bf16[2,16,2304]{2,1,0:T(8,128)(2,1)S(1)}, u32[]{:S(2)}, u32[]{:S(2)}) %collective-permute-start.5) | collective-permute-done | bytes 147488 | tf_op jit(solution)/shard_map/ppermute | solution.py:471
  18.7 0.3 %rank_inner.1 = (f32[32,32]{1,0:T(8,128)S(1)}, bf16[32,4096]{1,0:T(8,128)(2,1)S(1)}, f32[32,128]{1,0:T(8,128)S(1)}) custom-call(bf16[32,8192]{1,0:T(8,128)(2,1)S(1)} %get-tuple-element.41.scaled_ref, f32[32,128]{1,0:T(8,128)S(1)} %get-tuple-element.42.square_ref, f32[64,128]{1,0:T(8,128)S(1)} %get-tuple-element.33.gain_ref, ...), custom_call_target="tpu_custom_call" | custom-call | tf_op jit(solution)/shard_map/rank_inner/pallas_call | solution.py:338
  19.1 0.7 %collective-permute-start.7 = (f32[32,32]{1,0:T(8,128)S(1)}, f32[32,32]{1,0:T(8,128)S(1)}, u32[]{:S(2)}, u32[]{:S(2)}) collective-permute-start(f32[32,32]{1,0:T(8,128)S(1)} %get-tuple-element.56.rest_6_), channel_id=1, source_target_pairs={{0,2},{1,3},{2,0},{3,1},{4,6},{5,7},{6,4},{7,5},{8,10},{9,11},{10,... | collective-permute-start | bytes 12296 | tf_op jit(solution)/shard_map/ppermute | solution.py:471
  19.7 0.1 collective-permute-start.8
  19.9 1.3 %collective-permute-start.6 = (f32[32,32]{1,0:T(8,128)S(1)}, f32[32,32]{1,0:T(8,128)S(1)}, u32[]{:S(2)}, u32[]{:S(2)}) collective-permute-start(f32[32,32]{1,0:T(8,128)S(1)} %get-tuple-element.56.rest_6_), channel_id=1, source_target_pairs={{0,1},{1,0},{2,3},{3,2},{4,5},{5,4},{6,7},{7,6},{8,9},{9,8},{10,11... | collective-permute-start | bytes 12296 | tf_op jit(solution)/shard_map/ppermute | solution.py:471
  21.2 0.8 %fusion.7.far_ref = f32[2,32,256]{2,1,0:T(8,128)S(1)} fusion(bf16[4096,2,256]{2,1,0:T(2,128)(2,1)S(1)} %get-tuple-element.40, bf16[32,4096]{1,0:T(8,128)(2,1)S(1)} %get-tuple-element.47), kind=kOutput, calls=%fused_computation.5 | convolution fusion | flops 134217728 | bytes 4521984 | tf_op jit(solution)/shard_map/md,dkc->kmc/dot_general | solution.py:467
  22.1 0.0 collective-permute-done.6.rest_7_
  22.1 0.8 %collective-permute-done.7.rest_8_ = f32[32,32]{1,0:T(8,128)S(1)} collective-permute-done((f32[32,32]{1,0:T(8,128)S(1)}, f32[32,32]{1,0:T(8,128)S(1)}, u32[]{:S(2)}, u32[]{:S(2)}) %collective-permute-start.7) | collective-permute-done | bytes 4128 | tf_op jit(solution)/shard_map/ppermute | solution.py:471
  22.9 0.2 collective-permute-done.8.rest_9_
  23.1 1.3 %fresh_attention.1 = (bf16[4,8,256]{2,1,0:T(8,128)(2,1)}, bf16[4,8,256]{2,1,0:T(8,128)(2,1)}, bf16[4,8,2048]{2,1,0:T(8,128)(2,1)}) custom-call(f32[2,32,256]{2,1,0:T(8,128)S(1)} %fusion.4.near_ref, f32[2,32,256]{2,1,0:T(8,128)S(1)} %fusion.7.far_ref, f32[32,128]{1,0:T(8,128)S(1)} %get-tuple-element.48.square_ref, ...), custom_call_target="tpu_custom_call" | custom-call | tf_op jit(solution)/shard_map/fresh_attention/pallas_call | solution.py:456
  (1 shorter events, 0.0 us)
Async XLA Ops:
  1.5 11.2 %collective-permute-start.1 = (bf16[2,16,2304]{2,1,0:T(8,128)(2,1)S(1)}, bf16[2,16,2304]{2,1,0:T(8,128)(2,1)S(1)}, u32[]{:S(2)}, u32[]{:S(2)}) collective-permute-start(bf16[2,16,2304]{2,1,0:T(8,128)(2,1)S(1)} %pack_factors.1.rest_2_.refs_0_), channel_id=1, source_target_pairs={{0,8},{4,12},{8,0},{12,4},{1,9},{5,13},{9,1},{13,5},{2,10},{6,14},... | collective-permute-start | bytes 442376 | tf_op jit(solution)/shard_map/ppermute | solution.py:471
  5.6 6.8 %collective-permute-start = (bf16[4,8,2048]{2,1,0:T(8,128)(2,1)}, bf16[4,8,2048]{2,1,0:T(8,128)(2,1)S(1)}, u32[]{:S(2)}, u32[]{:S(2)}) collective-permute-start(bf16[4,8,2048]{2,1,0:T(8,128)(2,1)} %hidden_ref.1), channel_id=1, source_target_pairs={{0,2},{1,3},{2,0},{3,1},{4,6},{5,7},{6,4},{7,5},{8,10},{9,11},{10,... | collective-permute-start | bytes 393224 | tf_op jit(solution)/shard_map/ppermute | solution.py:471
  7.1 9.4 %collective-permute-start.4 = (bf16[2,16,2304]{2,1,0:T(8,128)(2,1)S(1)}, bf16[2,16,2304]{2,1,0:T(8,128)(2,1)S(1)}, u32[]{:S(2)}, u32[]{:S(2)}) collective-permute-start(bf16[2,16,2304]{2,1,0:T(8,128)(2,1)S(1)} %pack_factors.1.rest_2_.refs_0_), channel_id=1, source_target_pairs={{0,4},{4,0},{8,12},{12,8},{1,5},{5,1},{9,13},{13,9},{2,6},{6,2},{1... | collective-permute-start | bytes 442376 | tf_op jit(solution)/shard_map/ppermute | solution.py:471
  8.7 7.8 %collective-permute-start.2 = (bf16[4,8,2048]{2,1,0:T(8,128)(2,1)}, bf16[4,8,2048]{2,1,0:T(8,128)(2,1)S(1)}, u32[]{:S(2)}, u32[]{:S(2)}) collective-permute-start(bf16[4,8,2048]{2,1,0:T(8,128)(2,1)} %hidden_ref.1), channel_id=1, source_target_pairs={{0,1},{1,0},{2,3},{3,2},{4,5},{5,4},{6,7},{7,6},{8,9},{9,8},{10,11... | collective-permute-start | bytes 393224 | tf_op jit(solution)/shard_map/ppermute | solution.py:471
  12.7 6.0 %collective-permute-start.5 = (bf16[2,16,2304]{2,1,0:T(8,128)(2,1)S(1)}, bf16[2,16,2304]{2,1,0:T(8,128)(2,1)S(1)}, u32[]{:S(2)}, u32[]{:S(2)}) collective-permute-start(bf16[2,16,2304]{2,1,0:T(8,128)(2,1)S(1)} %collective-permute-done.1.rest_4_.refs_2_), channel_id=1, source_target_pairs={{0,4},{4,0},{8,12},{12,8},{1,5},{5,1},{9,13},{13,9},{2,6},{6,2},{1... | collective-permute-start | bytes 442376 | tf_op jit(solution)/shard_map/ppermute | solution.py:471
  13.4 3.1 %collective-permute-start.3 = (bf16[4,8,2048]{2,1,0:T(8,128)(2,1)S(1)}, bf16[4,8,2048]{2,1,0:T(8,128)(2,1)S(1)}, u32[]{:S(2)}, u32[]{:S(2)}) collective-permute-start(bf16[4,8,2048]{2,1,0:T(8,128)(2,1)S(1)} %collective-permute-done.rest_1_), channel_id=1, source_target_pairs={{0,1},{1,0},{2,3},{3,2},{4,5},{5,4},{6,7},{7,6},{8,9},{9,8},{10,11... | collective-permute-start | bytes 393224 | tf_op jit(solution)/shard_map/ppermute | solution.py:471
  19.1 3.8 %collective-permute-start.7 = (f32[32,32]{1,0:T(8,128)S(1)}, f32[32,32]{1,0:T(8,128)S(1)}, u32[]{:S(2)}, u32[]{:S(2)}) collective-permute-start(f32[32,32]{1,0:T(8,128)S(1)} %get-tuple-element.56.rest_6_), channel_id=1, source_target_pairs={{0,2},{1,3},{2,0},{3,1},{4,6},{5,7},{6,4},{7,5},{8,10},{9,11},{10,... | collective-permute-start | bytes 12296 | tf_op jit(solution)/shard_map/ppermute | solution.py:471
  19.7 3.3 %collective-permute-start.8 = (f32[32,32]{1,0:T(8,128)S(1)}, f32[32,32]{1,0:T(8,128)S(1)}, u32[]{:S(2)}, u32[]{:S(2)}) collective-permute-start(f32[32,32]{1,0:T(8,128)S(1)} %get-tuple-element.56.rest_6_), channel_id=1, source_target_pairs={{0,3},{1,2},{2,1},{3,0},{4,7},{5,6},{6,5},{7,4},{8,11},{9,10},{10,... | collective-permute-start | bytes 12296 | tf_op jit(solution)/shard_map/ppermute | solution.py:471
  19.9 2.2 %collective-permute-start.6 = (f32[32,32]{1,0:T(8,128)S(1)}, f32[32,32]{1,0:T(8,128)S(1)}, u32[]{:S(2)}, u32[]{:S(2)}) collective-permute-start(f32[32,32]{1,0:T(8,128)S(1)} %get-tuple-element.56.rest_6_), channel_id=1, source_target_pairs={{0,1},{1,0},{2,3},{3,2},{4,5},{5,4},{6,7},{7,6},{8,9},{9,8},{10,11... | collective-permute-start | bytes 12296 | tf_op jit(solution)/shard_map/ppermute | solution.py:471

commit v27 on v24

--- a/solution.py
+++ b/solution.py
@@ -490,7 +490,7 @@
     gain = input_norm_gain.reshape(width // HD, HD)
     up_part = jnp.transpose(adapter_up_factor, (0, 2, 1))
     direct = wide_count == tp_count == 4
-    beside, crossed = [swap(hidden, "tp", offset, tp_count) for offset in (1, 2)]
+    crossed = swap(hidden, "tp", 2, tp_count)
     if direct:
         pack = pack_call(adapter_down_factor, up_part)
         second = swap(pack, "wide", 2, wide_count)
@@ -508,6 +508,7 @@
         hidden,
         key_value_weight,
     )
+    beside = swap(mine, "tp", 1, tp_count)
     relayed, gain_rows = lax.optimization_barrier((crossed, gain_rows))
     relayed = swap(relayed, "tp", 1, tp_count)
     if direct:

time: 23.6 us -> 23.6 us (level)
  no operation moved by 1% of the time
where the time goes in v27:
time: 23.6 us; the launch traced here: 23.4 us
  starting transfers between devices  10.2 us (43%)
  Pallas kernels  8.53 us (36%)
  waiting for transfers between devices  2.23 us (9%)
  matrix products  1.68 us (7%)
  between operations  0.72 us (3%)
    ppermute x9, starting transfers between devices, swap(): return lax.ppermute(block, axis, [(i, i ^ offset) for i in range(count)])  10.2 us
    pallas_call x1, Pallas kernels, cache_call(): pl.pallas_call(functools.partial(cache_kernel, near), out_shape=(pltpu.VM...  3.7 us
    pallas_call x1, Pallas kernels, scale_call(): pl.pallas_call(functools.partial(scale_kernel, early, far), out_shape=(pl...  2.26 us
    ppermute x9, waiting for transfers between devices, swap(): return lax.ppermute(block, axis, [(i, i ^ offset) for i in range(count)])  2.23 us
    dot_general x2, matrix products, dot(): jnp.einsum('md,dkc->kmc', rows, weight, preferred_element_type=jnp.float32)  1.68 us
    pallas_call x1, Pallas kernels, final_call(): pl.pallas_call(functools.partial(final_kernel, width, len(inner)), out_sh...  1.34 us
    pallas_call x1, Pallas kernels, pack_call(): pl.pallas_call(pack_kernel, out_shape=pltpu.VMEM((kinds, share, down.shap...  0.87 us
  transfers between devices with their start and end apart: 9, of which 3 were waited for; matrix products, arithmetic and copies ran while one was open for 7% of the time, Pallas kernels for 26%

profile of v27, /device:TPU:0, one launch (start us, length us, event | category | flops | bytes accessed | tf_op | source)
XLA Modules:
  0.0 23.4 jit_solution(4633950548367788266)
XLA Ops:
  0.6 0.9 %pack_factors.1.rest_2_.refs_0_ = bf16[2,16,2304]{2,1,0:T(8,128)(2,1)S(1)} custom-call(bf16[2,64,2048]{2,1,0:T(8,128)(2,1)} %down_ref.1, bf16[2,16,256]{2,1,0:T(8,128)(2,1)} %bitcast.13), custom_call_target="tpu_custom_call" | custom-call | tf_op jit(solution)/shard_map/pack_factors/pallas_call | solution.py:201
  1.5 4.1 %collective-permute-start = (bf16[2,16,2304]{2,1,0:T(8,128)(2,1)S(1)}, bf16[2,16,2304]{2,1,0:T(8,128)(2,1)S(1)}, u32[]{:S(2)}, u32[]{:S(2)}) collective-permute-start(bf16[2,16,2304]{2,1,0:T(8,128)(2,1)S(1)} %pack_factors.1.rest_2_.refs_0_), channel_id=1, source_target_pairs={{0,8},{4,12},{8,0},{12,4},{1,9},{5,13},{9,1},{13,5},{2,10},{6,14},... | collective-permute-start | bytes 442376 | tf_op jit(solution)/shard_map/ppermute | solution.py:470
  5.6 1.5 %collective-permute-start.1 = (bf16[4,8,2048]{2,1,0:T(8,128)(2,1)}, bf16[4,8,2048]{2,1,0:T(8,128)(2,1)S(1)}, u32[]{:S(2)}, u32[]{:S(2)}) collective-permute-start(bf16[4,8,2048]{2,1,0:T(8,128)(2,1)} %hidden_ref.1), channel_id=1, source_target_pairs={{0,2},{1,3},{2,0},{3,1},{4,6},{5,7},{6,4},{7,5},{8,10},{9,11},{10,... | collective-permute-start | bytes 393224 | tf_op jit(solution)/shard_map/ppermute | solution.py:470
  7.1 1.6 %collective-permute-start.4 = (bf16[2,16,2304]{2,1,0:T(8,128)(2,1)S(1)}, bf16[2,16,2304]{2,1,0:T(8,128)(2,1)S(1)}, u32[]{:S(2)}, u32[]{:S(2)}) collective-permute-start(bf16[2,16,2304]{2,1,0:T(8,128)(2,1)S(1)} %pack_factors.1.rest_2_.refs_0_), channel_id=1, source_target_pairs={{0,4},{4,0},{8,12},{12,8},{1,5},{5,1},{9,13},{13,9},{2,6},{6,2},{1... | collective-permute-start | bytes 442376 | tf_op jit(solution)/shard_map/ppermute | solution.py:470
  8.7 3.7 %cache_attention.1 = (bf16[4096,2,256]{2,1,0:T(2,128)(2,1)S(1)}, f32[64,128]{1,0:T(8,128)S(1)}, bf16[2,256]{1,0:T(2,128)(2,1)S(1)}, bf16[4,8,2048]{2,1,0:T(8,128...) custom-call(s32[8]{0:T(128)} %lengths_ref.3, ...), custom_call_target="tpu_custom_call" | custom-call | flops 140509184 | bytes 5242880 | tf_op jit(solution)/shard_map/cache_attention/pallas_call | solution.py:148
  12.4 0.0 collective-permute-done.1.rest_1_
  12.4 0.3 %collective-permute-done.rest_4_.refs_2_ = bf16[2,16,2304]{2,1,0:T(8,128)(2,1)S(1)} collective-permute-done((bf16[2,16,2304]{2,1,0:T(8,128)(2,1)S(1)}, bf16[2,16,2304]{2,1,0:T(8,128)(2,1)S(1)}, u32[]{:S(2)}, u32[]{:S(2)}) %collective-permute-start) | collective-permute-done | bytes 147488 | tf_op jit(solution)/shard_map/ppermute | solution.py:470
  12.7 0.7 %collective-permute-start.5 = (bf16[2,16,2304]{2,1,0:T(8,128)(2,1)S(1)}, bf16[2,16,2304]{2,1,0:T(8,128)(2,1)S(1)}, u32[]{:S(2)}, u32[]{:S(2)}) collective-permute-start(bf16[2,16,2304]{2,1,0:T(8,128)(2,1)S(1)} %collective-permute-done.rest_4_.refs_2_), channel_id=1, source_target_pairs={{0,4},{4,0},{8,12},{12,8},{1,5},{5,1},{9,13},{13,9},{2,6},{6,2},{1... | collective-permute-start | bytes 442376 | tf_op jit(solution)/shard_map/ppermute | solution.py:470
  13.4 0.0 collective-permute-start.2
  13.4 0.5 %collective-permute-start.3 = (bf16[4,8,2048]{2,1,0:T(8,128)(2,1)S(1)}, bf16[4,8,2048]{2,1,0:T(8,128)(2,1)S(1)}, u32[]{:S(2)}, u32[]{:S(2)}) collective-permute-start(bf16[4,8,2048]{2,1,0:T(8,128)(2,1)S(1)} %collective-permute-done.1.rest_1_), channel_id=1, source_target_pairs={{0,1},{1,0},{2,3},{3,2},{4,5},{5,4},{6,7},{7,6},{8,9},{9,8},{10,11... | collective-permute-start | bytes 393224 | tf_op jit(solution)/shard_map/ppermute | solution.py:470
  13.9 2.3 %scale_features.1 = (bf16[32,8192]{1,0:T(8,128)(2,1)S(1)}, bf16[32,4096]{1,0:T(8,128)(2,1)S(1)}, f32[32,128]{1,0:T(8,128)S(1)}, bf16[4096,2,256]{2,1,0:T(2,128)(...) custom-call(s32[8]{0:T(128)} %lengths_ref.3, ...), custom_call_target="tpu_custom_call" | custom-call | bytes 9437184 | tf_op jit(solution)/shard_map/scale_features/pallas_call | solution.py:270
  16.2 0.0 collective-permute-done.2.rest_0_
  16.2 0.0 collective-permute-done.4.rest_3_.refs_1_
  16.2 0.0 collective-permute-done.3.rest_1_
  16.2 1.7 %collective-permute-done.5.rest_5_.refs_3_ = bf16[2,16,2304]{2,1,0:T(8,128)(2,1)S(1)} collective-permute-done((bf16[2,16,2304]{2,1,0:T(8,128)(2,1)S(1)}, bf16[2,16,2304]{2,1,0:T(8,128)(2,1)S(1)}, u32[]{:S(2)}, u32[]{:S(2)}) %collective-permute-start.5) | collective-permute-done | bytes 147488 | tf_op jit(solution)/shard_map/ppermute | solution.py:470
  17.9 0.3 %rank_inner.1 = (f32[32,32]{1,0:T(8,128)S(1)}, bf16[32,4096]{1,0:T(8,128)(2,1)S(1)}, bf16[32,4096]{1,0:T(8,128)(2,1)S(1)}, f32[32,128]{1,0:T(8,128)S(1)}) custom-call(bf16[32,8192]{1,0:T(8,128)(2,1)S(1)} %get-tuple-element.39.scaled_ref, bf16[32,4096]{1,0:T(8,128)(2,1)S(1)} %get-tuple-element.40.early_ref, f32[32,128]{1,0:T(8,128)S(1)} %get-tuple-element.41.square_ref, ...), custom_call_target="tpu_custom_call" | custom-call | tf_op jit(solution)/shard_map/rank_inner/pallas_call | solution.py:337
  18.2 0.0 collective-permute-start.8
  18.2 1.6 %collective-permute-start.7 = (f32[32,32]{1,0:T(8,128)S(1)}, f32[32,32]{1,0:T(8,128)S(1)}, u32[]{:S(2)}, u32[]{:S(2)}) collective-permute-start(f32[32,32]{1,0:T(8,128)S(1)} %get-tuple-element.58.rest_6_), channel_id=1, source_target_pairs={{0,2},{1,3},{2,0},{3,1},{4,6},{5,7},{6,4},{7,5},{8,10},{9,11},{10,... | collective-permute-start | bytes 12296 | tf_op jit(solution)/shard_map/ppermute | solution.py:470
  19.8 0.2 %collective-permute-start.6 = (f32[32,32]{1,0:T(8,128)S(1)}, f32[32,32]{1,0:T(8,128)S(1)}, u32[]{:S(2)}, u32[]{:S(2)}) collective-permute-start(f32[32,32]{1,0:T(8,128)S(1)} %get-tuple-element.58.rest_6_), channel_id=1, source_target_pairs={{0,1},{1,0},{2,3},{3,2},{4,5},{5,4},{6,7},{7,6},{8,9},{9,8},{10,11... | collective-permute-start | bytes 12296 | tf_op jit(solution)/shard_map/ppermute | solution.py:470
  20.1 0.8 %fusion.7.far_ref = f32[2,32,256]{2,1,0:T(8,128)S(1)} fusion(bf16[4096,2,256]{2,1,0:T(2,128)(2,1)S(1)} %get-tuple-element.48, bf16[32,4096]{1,0:T(8,128)(2,1)S(1)} %get-tuple-element.49), kind=kOutput, calls=%fused_computation.5 | convolution fusion | flops 134217728 | bytes 4521984 | tf_op jit(solution)/shard_map/md,dkc->kmc/dot_general | solution.py:466
  20.9 0.8 %fusion.4.near_ref = f32[2,32,256]{2,1,0:T(8,128)S(1)} fusion(bf16[4096,2,256]{2,1,0:T(2,128)(2,1)S(1)} %get-tuple-element.33, bf16[32,4096]{1,0:T(8,128)(2,1)S(1)} %get-tuple-element.47), kind=kOutput, calls=%fused_computation.4 | convolution fusion | flops 134217728 | bytes 4521984 | tf_op jit(solution)/shard_map/md,dkc->kmc/dot_general | solution.py:466
  21.8 0.0 collective-permute-done.8.rest_9_
  21.8 0.2 collective-permute-done.7.rest_8_
  22.0 0.0 collective-permute-done.6.rest_7_
  22.0 1.3 %fresh_attention.1 = (bf16[4,8,256]{2,1,0:T(8,128)(2,1)}, bf16[4,8,256]{2,1,0:T(8,128)(2,1)}, bf16[4,8,2048]{2,1,0:T(8,128)(2,1)}) custom-call(f32[2,32,256]{2,1,0:T(8,128)S(1)} %fusion.4.near_ref, f32[2,32,256]{2,1,0:T(8,128)S(1)} %fusion.7.far_ref, f32[32,128]{1,0:T(8,128)S(1)} %get-tuple-element.50.square_ref, ...), custom_call_target="tpu_custom_call" | custom-call | tf_op jit(solution)/shard_map/fresh_attention/pallas_call | solution.py:455
  (1 shorter events, 0.0 us)
Async XLA Ops:
  1.5 11.2 %collective-permute-start = (bf16[2,16,2304]{2,1,0:T(8,128)(2,1)S(1)}, bf16[2,16,2304]{2,1,0:T(8,128)(2,1)S(1)}, u32[]{:S(2)}, u32[]{:S(2)}) collective-permute-start(bf16[2,16,2304]{2,1,0:T(8,128)(2,1)S(1)} %pack_factors.1.rest_2_.refs_0_), channel_id=1, source_target_pairs={{0,8},{4,12},{8,0},{12,4},{1,9},{5,13},{9,1},{13,5},{2,10},{6,14},... | collective-permute-start | bytes 442376 | tf_op jit(solution)/shard_map/ppermute | solution.py:470
  5.6 6.8 %collective-permute-start.1 = (bf16[4,8,2048]{2,1,0:T(8,128)(2,1)}, bf16[4,8,2048]{2,1,0:T(8,128)(2,1)S(1)}, u32[]{:S(2)}, u32[]{:S(2)}) collective-permute-start(bf16[4,8,2048]{2,1,0:T(8,128)(2,1)} %hidden_ref.1), channel_id=1, source_target_pairs={{0,2},{1,3},{2,0},{3,1},{4,6},{5,7},{6,4},{7,5},{8,10},{9,11},{10,... | collective-permute-start | bytes 393224 | tf_op jit(solution)/shard_map/ppermute | solution.py:470
  7.1 9.1 %collective-permute-start.4 = (bf16[2,16,2304]{2,1,0:T(8,128)(2,1)S(1)}, bf16[2,16,2304]{2,1,0:T(8,128)(2,1)S(1)}, u32[]{:S(2)}, u32[]{:S(2)}) collective-permute-start(bf16[2,16,2304]{2,1,0:T(8,128)(2,1)S(1)} %pack_factors.1.rest_2_.refs_0_), channel_id=1, source_target_pairs={{0,4},{4,0},{8,12},{12,8},{1,5},{5,1},{9,13},{13,9},{2,6},{6,2},{1... | collective-permute-start | bytes 442376 | tf_op jit(solution)/shard_map/ppermute | solution.py:470
  12.7 5.1 %collective-permute-start.5 = (bf16[2,16,2304]{2,1,0:T(8,128)(2,1)S(1)}, bf16[2,16,2304]{2,1,0:T(8,128)(2,1)S(1)}, u32[]{:S(2)}, u32[]{:S(2)}) collective-permute-start(bf16[2,16,2304]{2,1,0:T(8,128)(2,1)S(1)} %collective-permute-done.rest_4_.refs_2_), channel_id=1, source_target_pairs={{0,4},{4,0},{8,12},{12,8},{1,5},{5,1},{9,13},{13,9},{2,6},{6,2},{1... | collective-permute-start | bytes 442376 | tf_op jit(solution)/shard_map/ppermute | solution.py:470
  13.4 2.8 %collective-permute-start.2 = (bf16[4,8,2048]{2,1,0:T(8,128)(2,1)S(1)}, bf16[4,8,2048]{2,1,0:T(8,128)(2,1)S(1)}, u32[]{:S(2)}, u32[]{:S(2)}) collective-permute-start(bf16[4,8,2048]{2,1,0:T(8,128)(2,1)S(1)} %get-tuple-element.38.rest_0_), channel_id=1, source_target_pairs={{0,1},{1,0},{2,3},{3,2},{4,5},{5,4},{6,7},{7,6},{8,9},{9,8},{10,11... | collective-permute-start | bytes 393224 | tf_op jit(solution)/shard_map/ppermute | solution.py:470
  13.4 2.8 %collective-permute-start.3 = (bf16[4,8,2048]{2,1,0:T(8,128)(2,1)S(1)}, bf16[4,8,2048]{2,1,0:T(8,128)(2,1)S(1)}, u32[]{:S(2)}, u32[]{:S(2)}) collective-permute-start(bf16[4,8,2048]{2,1,0:T(8,128)(2,1)S(1)} %collective-permute-done.1.rest_1_), channel_id=1, source_target_pairs={{0,1},{1,0},{2,3},{3,2},{4,5},{5,4},{6,7},{7,6},{8,9},{9,8},{10,11... | collective-permute-start | bytes 393224 | tf_op jit(solution)/shard_map/ppermute | solution.py:470
  18.2 3.6 %collective-permute-start.8 = (f32[32,32]{1,0:T(8,128)S(1)}, f32[32,32]{1,0:T(8,128)S(1)}, u32[]{:S(2)}, u32[]{:S(2)}) collective-permute-start(f32[32,32]{1,0:T(8,128)S(1)} %get-tuple-element.58.rest_6_), channel_id=1, source_target_pairs={{0,3},{1,2},{2,1},{3,0},{4,7},{5,6},{6,5},{7,4},{8,11},{9,10},{10,... | collective-permute-start | bytes 12296 | tf_op jit(solution)/shard_map/ppermute | solution.py:470
  18.2 3.8 %collective-permute-start.7 = (f32[32,32]{1,0:T(8,128)S(1)}, f32[32,32]{1,0:T(8,128)S(1)}, u32[]{:S(2)}, u32[]{:S(2)}) collective-permute-start(f32[32,32]{1,0:T(8,128)S(1)} %get-tuple-element.58.rest_6_), channel_id=1, source_target_pairs={{0,2},{1,3},{2,0},{3,1},{4,6},{5,7},{6,4},{7,5},{8,10},{9,11},{10,... | collective-permute-start | bytes 12296 | tf_op jit(solution)/shard_map/ppermute | solution.py:470
  19.8 2.2 %collective-permute-start.6 = (f32[32,32]{1,0:T(8,128)S(1)}, f32[32,32]{1,0:T(8,128)S(1)}, u32[]{:S(2)}, u32[]{:S(2)}) collective-permute-start(f32[32,32]{1,0:T(8,128)S(1)} %get-tuple-element.58.rest_6_), channel_id=1, source_target_pairs={{0,1},{1,0},{2,3},{3,2},{4,5},{5,4},{6,7},{7,6},{8,9},{9,8},{10,11... | collective-permute-start | bytes 12296 | tf_op jit(solution)/shard_map/ppermute | solution.py:470
